TPU v7x, 32 devices: a whole 2x2x4 slice. The times are simulated.
32 devices in a mesh: view: 4 (over y, core), ctx: 8 (over z, x).
Axes of the slice: x: 2, y: 2, z: 4, core: 2. Of those that a mesh axis runs over, the one named last changes fastest.
Arguments:
- q_self: bfloat16 [4, 896, 1024], P('view', 'ctx'), may hold values from -16 to 16
- k_self: bfloat16 [4, 896, 1024], P('view', 'ctx'), may hold values from -16 to 16
- v_self: bfloat16 [4, 896, 1024], P('view', 'ctx'), may hold values from -6 to 6
- q_cross: bfloat16 [4, 896, 1024], P('view', 'ctx'), may hold values from -16 to 16
- k_cross: bfloat16 [4, 896, 1024], P('view', 'ctx'), may hold values from -16 to 16
- v_cross: bfloat16 [4, 896, 1024], P('view', 'ctx'), may hold values from -6 to 6
Outputs:
- block_out: bfloat16 [4, 896, 1024], P('view', 'ctx')
All inputs are finite; a program needn't handle non-finite values.
Results may differ from a plain program's by a relative error of at most 0.01.
Values may be sent and summed in bfloat16 or wider, within the bound.
No kernel may reach another device: no remote copies, remote signals or barrier semaphores. Data moves between devices by JAX's collectives and lax.ppermute only.
A program may use at most 128 MiB of HBM per device.

v0:
```python
import math

import jax
import jax.numpy as jnp
from jax import lax
from jax.sharding import PartitionSpec as P

HEAD = 128


def cross_attend(pieces):
    cross_query, key_four, value_four = pieces
    score_scale = 1.0 / math.sqrt(HEAD)
    cross_scores = (
        jnp.einsum("atnd,btnd->tnab", cross_query, key_four, preferred_element_type=jnp.float32)
        * score_scale
    )
    cross_scores = cross_scores - jnp.max(cross_scores, axis=-1, keepdims=True)
    weights_full = jnp.exp(cross_scores)
    cross_weights = (weights_full / jnp.sum(weights_full, axis=-1, keepdims=True)).astype(
        jnp.bfloat16
    )
    return jnp.einsum(
        "tnab,btnd->atnd", cross_weights, value_four, preferred_element_type=jnp.float32
    ).astype(jnp.bfloat16)


def start_state(view_count, head_count, row_count):
    return (
        jnp.full((view_count, head_count, row_count), -1e30, jnp.float32),
        jnp.zeros((view_count, head_count, row_count), jnp.float32),
        jnp.zeros((view_count, head_count, row_count, HEAD), jnp.float32),
    )


def online_update(queries, state_now, key_rows, value_rows):
    score_scale = 1.0 / math.sqrt(HEAD)
    running_max, running_sum, weighted = state_now
    scores = (
        jnp.einsum("aqhd,akhd->ahqk", queries, key_rows, preferred_element_type=jnp.float32)
        * score_scale
    )
    new_max = jnp.maximum(running_max, jnp.max(scores, axis=-1))
    weights_full = jnp.exp(scores - new_max[..., None])
    running_sum = jnp.sum(weights_full, axis=-1)
    update = jnp.einsum(
        "ahqk,akhd->ahqd",
        weights_full.astype(jnp.bfloat16),
        value_rows,
        preferred_element_type=jnp.float32,
    )
    weighted = update
    return (new_max, running_sum, weighted)


def finish_state(state_now):
    attended = state_now[2] / state_now[1][..., None]
    return jnp.transpose(attended, (0, 2, 1, 3)).astype(jnp.bfloat16)


def body(q_self, k_self, v_self, q_cross, k_cross, v_cross):
    view_count, row_count, feature_width = q_self.shape
    head_count = feature_width // HEAD
    queries = q_self.reshape(view_count, row_count, head_count, HEAD)
    initial = start_state(view_count, head_count, row_count)
    key_rows = lax.all_gather(k_self, "ctx", axis=1, tiled=True).reshape(
        view_count, -1, head_count, HEAD
    )
    value_rows = lax.all_gather(v_self, "ctx", axis=1, tiled=True).reshape(
        view_count, -1, head_count, HEAD
    )
    final_state = online_update(queries, initial, key_rows, value_rows)
    o_self = finish_state(final_state)
    merged = (
        q_cross.reshape(view_count, row_count, head_count, HEAD).astype(jnp.float32)
        + o_self.astype(jnp.float32)
    ).astype(jnp.bfloat16)
    key_four = k_cross.reshape(view_count, row_count, head_count, HEAD)
    value_four = v_cross.reshape(view_count, row_count, head_count, HEAD)
    mixed_out = cross_attend(
        (
            lax.all_to_all(merged, "view", split_axis=1, concat_axis=0, tiled=True),
            lax.all_to_all(key_four, "view", split_axis=1, concat_axis=0, tiled=True),
            lax.all_to_all(value_four, "view", split_axis=1, concat_axis=0, tiled=True),
        )
    )
    o_cross = lax.all_to_all(mixed_out, "view", split_axis=0, concat_axis=1, tiled=True)
    total_out = o_self.astype(jnp.float32) + o_cross.astype(jnp.float32)
    return total_out.reshape(view_count, row_count, feature_width).astype(jnp.bfloat16)


def solution(mesh):
    in_specs = (
        P("view", "ctx", None),
        P("view", "ctx", None),
        P("view", "ctx", None),
        P("view", "ctx", None),
        P("view", "ctx", None),
        P("view", "ctx", None),
    )
    out_specs = P("view", "ctx", None)
    return jax.shard_map(body, mesh=mesh, in_specs=in_specs, out_specs=out_specs, check_vma=False)
```

profile of v0, /device:TPU:0, one launch (start us, length us, event | category | flops | bytes accessed | tf_op | source)
XLA Modules:
  0.0 148.1 jit_solution(4887442943916707906)
XLA Ops:
  6.5 0.0 all-gather.3.cloned.1.call-start
  6.5 0.7 all-gather.3.cloned.1.call-update
  7.3 0.0 all-gather.5.cloned.1.call-start
  7.3 0.7 all-gather.5.cloned.1.call-update
  8.0 1.7 %copy.45 = bf16[14,8,8,128]{3,2,1,0:T(8,128)(2,1)} copy(bf16[14,8,8,128]{3,1,2,0:T(8,128)(2,1)} %bitcast.51) | data formatting | bytes 458752
  9.7 4.2 %all-to-all-start.1 = ((bf16[1,112,8,128]{3,2,0,1:T(8,128)(2,1)}), bf16[1,112,8,128]{3,2,0,1:T(8,128)(2,1)}, u32[]{:S(2)}, u32[]{:S(2)}) async-start(bf16[1,112,8,128]{3,2,0,1:T(8,128)(2,1)} %bitcast.25), calls=%async_computation.1 | async-start | bytes 458752 | tf_op jit(solution)/shard_map/all_to_all | solution.py:83
  13.9 1.0 copy.43
  14.9 1.0 convert_bitcast_fusion
  15.9 0.9 copy.44
  16.8 41.8 %all-gather.3.cloned.1.call-done = bf16[1,896,1024]{2,1,0:T(8,128)(2,1)} async-done(((bf16[1,112,1024]{2,1,0:T(8,128)(2,1)}), bf16[1,896,1024]{2,1,0:T(8,128)(2,1)}) %all-gather.3.cloned.1.call-update) | async-done | bytes 1835024 | tf_op jit(solution)/shard_map/all_gather | solution.py:66
  58.5 3.8 %copy.25 = bf16[1,896,1024]{1,2,0:T(8,128)(2,1)} copy(bf16[1,896,1024]{2,1,0:T(8,128)(2,1)} %all-gather.3.cloned.1.call-done) | data formatting | bytes 3670016 | tf_op jit(solution)/shard_map/all_gather | solution.py:66
  62.3 2.2 %multiply_reduce_fusion = (f32[8,112]{1,0:T(8,128)S(1)}, f32[8,112,896]{2,1,0:T(8,128)S(1)}) fusion(bf16[896,8,128]{0,2,1:T(8,128)(2,1)} %bitcast.46, bf16[112,8,128]{2,1,0:T(8,128)(2,1)S(1)} %bitcast.48), kind=kOutput, calls=%fused_computation.2 | convolution fusion | flops 207125632 | bytes 5279232 | tf_op jit(solution)/shard_map/aqhd,akhd->ahqk/dot_general | solution.py:40
  64.5 0.7 fusion.1
  65.2 40.8 %all-gather.5.cloned.1.call-done = bf16[1,896,1024]{2,1,0:T(8,128)(2,1)} async-done(((bf16[1,112,1024]{2,1,0:T(8,128)(2,1)}), bf16[1,896,1024]{2,1,0:T(8,128)(2,1)}) %all-gather.5.cloned.1.call-update) | async-done | bytes 1835024 | tf_op jit(solution)/shard_map/all_gather | solution.py:69
  106.0 3.8 %copy.28 = bf16[1,896,1024]{1,2,0:T(8,128)(2,1)} copy(bf16[1,896,1024]{2,1,0:T(8,128)(2,1)} %all-gather.5.cloned.1.call-done) | data formatting | bytes 3670016 | tf_op jit(solution)/shard_map/all_gather | solution.py:69
  109.8 0.0 copy-start.1
  109.8 3.2 %fusion.26 = (bf16[1,112,8,128]{3,1,2,0:T(8,128)(2,1)S(1)}, f32[1,112,8,128]{3,1,2,0:T(8,128)}) fusion(f32[1,112,8,128]{3,2,0,1:T(8,128)} %bitcast.50, f32[8,112]{1,0:T(8,128)S(1)} %fusion.1, bf16[896,8,128]{0,2,1:T(8,128)(2,1)} %bitcast.47, f32[8,112,896]{2,1,0:T(8,128)S(1)} %get-tuple-element.6, f32[8,112]{1,0:T(8,128)S(1)} %broadcast_maximum_fusion), kind=kOutput, calls=%fused_computation.21 | convolution fusion | flops 208502784 | bytes 6200320 | tf_op jit(solution)/shard_map/ahqk,akhd->ahqd/dot_general | solution.py:46
  113.0 0.7 copy.31
  113.8 0.0 all-to-all-done.1
  113.8 3.4 %all-to-all-start = ((bf16[1,112,8,128]{3,2,0,1:T(8,128)(2,1)}), bf16[1,112,8,128]{3,2,0,1:T(8,128)(2,1)S(1)}, u32[]{:S(2)}, u32[]{:S(2)}) async-start(bf16[1,112,8,128]{3,2,0,1:T(8,128)(2,1)} %copy.31), calls=%async_computation | async-start | bytes 458752 | tf_op jit(solution)/shard_map/all_to_all | solution.py:82
  117.2 0.0 copy-done.1
  117.2 0.7 copy.46
  117.9 4.9 %all-to-all-done = bf16[1,112,8,128]{3,2,0,1:T(8,128)(2,1)S(1)} async-done(((bf16[1,112,8,128]{3,2,0,1:T(8,128)(2,1)}), bf16[1,112,8,128]{3,2,0,1:T(8,128)(2,1)S(1)}, u32[]{:S(2)}, u32[]{:S(2)}) %all-to-all-start) | async-done | bytes 229408 | tf_op jit(solution)/shard_map/all_to_all | solution.py:82
  122.8 3.4 %all-to-all-start.2 = ((bf16[1,112,8,128]{3,2,0,1:T(8,128)(2,1)}), bf16[1,112,8,128]{3,2,0,1:T(8,128)(2,1)S(1)}, u32[]{:S(2)}, u32[]{:S(2)}) async-start(bf16[1,112,8,128]{3,2,0,1:T(8,128)(2,1)} %bitcast.30), calls=%async_computation.2 | async-start | bytes 458752 | tf_op jit(solution)/shard_map/all_to_all | solution.py:84
  126.2 1.8 %fusion.45 = (f32[28,8,4]{2,1,0:T(8,128)S(1)}, f32[28,8,4,4]{2,3,1,0:T(4,128)S(1)}) fusion(bf16[4,28,8,128]{3,2,1,0:T(8,128)(2,1)} %bitcast.6, bf16[4,28,8,128]{3,2,1,0:T(8,128)(2,1)S(1)} %bitcast.54), kind=kOutput, calls=%fused_computation.37 | convolution fusion | flops 928259 | bytes 476672 | tf_op jit(solution)/shard_map/sub | solution.py:18
  128.0 0.0 copy-start
  128.0 3.9 %all-to-all-done.2 = bf16[1,112,8,128]{3,2,0,1:T(8,128)(2,1)S(1)} async-done(((bf16[1,112,8,128]{3,2,0,1:T(8,128)(2,1)}), bf16[1,112,8,128]{3,2,0,1:T(8,128)(2,1)S(1)}, u32[]{:S(2)}, u32[]{:S(2)}) %all-to-all-start.2) | async-done | bytes 229408 | tf_op jit(solution)/shard_map/all_to_all | solution.py:84
  131.9 0.5 fusion.15
  132.4 8.1 %all_to_all.45 = bf16[4,28,8,128]{3,2,1,0:T(8,128)(2,1)S(1)} all-to-all(bf16[4,28,8,128]{3,2,1,0:T(8,128)(2,1)S(1)} %copy.36), channel_id=1, replica_groups=mesh['view'=4,'ctx'=8] {'view'}, dimensions={0} | all-to-all | bytes 458752 | tf_op jit(solution)/shard_map/all_to_all | solution.py:87
  140.5 0.0 copy-done
  140.5 0.8 copy_bitcast_fusion
  (3 shorter events, 0.1 us)
Async XLA Ops:
  6.5 52.0 %all-gather.3.cloned.1.call-start = ((), (), s32[]{:S(2)}) async-start(), calls=%async_computation.4 | async-start | bytes 2064384 | tf_op jit(solution)/shard_map/all_gather | solution.py:66
  7.3 98.8 %all-gather.5.cloned.1.call-start = ((), (), s32[]{:S(2)}) async-start(), calls=%async_computation.5 | async-start | bytes 2064384 | tf_op jit(solution)/shard_map/all_gather | solution.py:69
  9.7 104.1 %all-to-all-start.1 = ((bf16[1,112,8,128]{3,2,0,1:T(8,128)(2,1)}), bf16[1,112,8,128]{3,2,0,1:T(8,128)(2,1)}, u32[]{:S(2)}, u32[]{:S(2)}) async-start(bf16[1,112,8,128]{3,2,0,1:T(8,128)(2,1)} %bitcast.25), calls=%async_computation.1 | async-start | bytes 458752 | tf_op jit(solution)/shard_map/all_to_all | solution.py:83
  109.8 7.4 %copy-start.1 = (bf16[1,112,1024]{2,1,0:T(8,128)(2,1)S(1)}, bf16[1,112,1024]{2,1,0:T(8,128)(2,1)}, u32[]{:S(2)}) copy-start(bf16[1,112,1024]{2,1,0:T(8,128)(2,1)} %param.11) | copy-start | bytes 688132
  113.8 9.0 %all-to-all-start = ((bf16[1,112,8,128]{3,2,0,1:T(8,128)(2,1)}), bf16[1,112,8,128]{3,2,0,1:T(8,128)(2,1)S(1)}, u32[]{:S(2)}, u32[]{:S(2)}) async-start(bf16[1,112,8,128]{3,2,0,1:T(8,128)(2,1)} %copy.31), calls=%async_computation | async-start | bytes 458752 | tf_op jit(solution)/shard_map/all_to_all | solution.py:82
  122.8 9.0 %all-to-all-start.2 = ((bf16[1,112,8,128]{3,2,0,1:T(8,128)(2,1)}), bf16[1,112,8,128]{3,2,0,1:T(8,128)(2,1)S(1)}, u32[]{:S(2)}, u32[]{:S(2)}) async-start(bf16[1,112,8,128]{3,2,0,1:T(8,128)(2,1)} %bitcast.30), calls=%async_computation.2 | async-start | bytes 458752 | tf_op jit(solution)/shard_map/all_to_all | solution.py:84
  128.0 12.5 %copy-start = (f32[1,112,8,128]{3,1,2,0:T(8,128)S(1)}, f32[1,112,8,128]{3,1,2,0:T(8,128)}, u32[]{:S(2)}) copy-start(f32[1,112,8,128]{3,1,2,0:T(8,128)} %get-tuple-element.8) | copy-start | bytes 1376260
Sparse Core Ops, SparseCore 0:
  9.5 48.9 all-gather.2
  60.7 45.2 all-gather.4
where the time goes:
time: 149 us; the launch traced here: 148 us
  waiting for transfers between devices  92.7 us (62%)
  between operations  13.5 us (9%)
  local copies, waits for them, and re-layouts  12.6 us (8%)
  starting transfers between devices  11 us (7%)
  blocking collectives  8.06 us (5%)
  matrix products  7.67 us (5%)
  other arithmetic  2.5 us (2%)
    all_gather x1, waiting for transfers between devices, body(): lax.all_gather(k_self, 'ctx', axis=1, tiled=True)  41.8 us
    all_gather x1, waiting for transfers between devices, body(): lax.all_gather(v_self, 'ctx', axis=1, tiled=True)  40.8 us
    all_to_all x1, blocking collectives, body(): lax.all_to_all(mixed_out, 'view', split_axis=0, concat_axis=1, tiled=True)  8.06 us
    all_to_all x1, waiting for transfers between devices, body(): lax.all_to_all(merged, 'view', split_axis=1, concat_axis=0, tiled=True)  4.91 us
    unnamed x8, local copies, waits for them, and re-layouts  4.26 us
    all_to_all x1, starting transfers between devices, body(): lax.all_to_all(key_four, 'view', split_axis=1, concat_axis=0, tiled=True)  4.24 us
    all_to_all x1, waiting for transfers between devices, body(): lax.all_to_all(value_four, 'view', split_axis=1, concat_axis=0, tiled=True)  3.86 us
    all_gather x1, local copies, waits for them, and re-layouts, body(): lax.all_gather(v_self, 'ctx', axis=1, tiled=True)  3.81 us
  transfers between devices with their start and end apart: 5, of which 4 were waited for; matrix products, arithmetic and copies ran while one was open for 15% of the time, Pallas kernels for 0%

commit v1 on v0

v1 whole, which is shorter than its diff:
```python
import functools
import math

import jax
import jax.numpy as jnp
from jax import lax
from jax.experimental import pallas as pl
from jax.experimental.pallas import tpu as pltpu
from jax.sharding import PartitionSpec as P

HEAD = 128
SCALE = 1.0 / math.sqrt(HEAD)
EXP2_SCALE = SCALE * math.log2(math.e)
VMEM_LIMIT = 48 * 1024 * 1024


def pack_kernel(head_count, q_ref, k_ref, v_ref, out_ref):
    rows = q_ref.shape[0]
    for head in range(head_count):
        lanes = slice(head * HEAD, (head + 1) * HEAD)
        out_ref[head, 0:rows, :] = q_ref[:, lanes]
        out_ref[head, rows : 2 * rows, :] = k_ref[:, lanes]
        out_ref[head, 2 * rows : 3 * rows, :] = v_ref[:, lanes]


def attend(query, keys, values):
    scores = lax.dot_general(
        query, keys, (((1,), (1,)), ((), ())), preferred_element_type=jnp.float32
    )
    row_max = jnp.max(scores, axis=-1, keepdims=True)
    weights_full = jnp.exp2((scores - row_max) * EXP2_SCALE)
    total = jnp.sum(weights_full, axis=-1, keepdims=True)
    mixed = jnp.dot(
        weights_full.astype(jnp.bfloat16), values, preferred_element_type=jnp.float32
    )
    return (mixed / total).astype(jnp.bfloat16)


def packed_attention_kernel(rows, data_ref, out_ref):
    blocks = data_ref.shape[0]
    keys = data_ref[:, rows : 2 * rows, :].reshape(blocks * rows, HEAD)
    values = data_ref[:, 2 * rows : 3 * rows, :].reshape(blocks * rows, HEAD)
    for block in range(blocks):
        out_ref[block] = attend(data_ref[block, 0:rows, :], keys, values)


def attention_kernel(q_ref, k_ref, v_ref, out_ref):
    out_ref[...] = attend(q_ref[...], k_ref[...], v_ref[...])


def cross_kernel(head_count, o_ref, q_ref, *refs):
    out_ref = refs[-1]
    views = (len(refs) - 1) // 2
    key_refs, value_refs = refs[:views], refs[views : 2 * views]
    for head in range(head_count):
        lanes = slice(head * HEAD, (head + 1) * HEAD)
        o_self = o_ref[head].astype(jnp.float32)
        query = (q_ref[:, lanes].astype(jnp.float32) + o_self).astype(jnp.bfloat16).astype(jnp.float32)
        scores = [
            jnp.sum(query * key_ref[:, lanes].astype(jnp.float32), axis=-1, keepdims=True)
            for key_ref in key_refs
        ]
        top = functools.reduce(jnp.maximum, scores)
        weights = [jnp.exp2((score - top) * EXP2_SCALE) for score in scores]
        total = sum(weights[1:], weights[0])
        mixed = None
        for weight, value_ref in zip(weights, value_refs):
            rounded = (weight / total).astype(jnp.bfloat16).astype(jnp.float32)
            term = rounded * value_ref[:, lanes].astype(jnp.float32)
            mixed = term if mixed is None else mixed + term
        o_cross = mixed.astype(jnp.bfloat16).astype(jnp.float32)
        out_ref[:, lanes] = (o_self + o_cross).astype(jnp.bfloat16)


def kernel_params():
    return pltpu.CompilerParams(vmem_limit_bytes=VMEM_LIMIT)


def self_attention(q, k, v, ctx_size):
    rows, width = q.shape
    heads = width // HEAD
    parts = ctx_size // heads
    vmem = pl.BlockSpec(memory_space=pltpu.VMEM)
    if parts == 1:
        packed = pl.pallas_call(
            functools.partial(pack_kernel, heads),
            out_shape=jax.ShapeDtypeStruct((heads, 3 * rows, HEAD), q.dtype),
            in_specs=[vmem] * 3,
            out_specs=vmem,
            compiler_params=kernel_params(),
            name="pack_qkv",
        )(q, k, v)
        moved = lax.all_to_all(packed, "ctx", split_axis=0, concat_axis=0, tiled=True)
        own = pl.pallas_call(
            functools.partial(packed_attention_kernel, rows),
            out_shape=jax.ShapeDtypeStruct((heads, rows, HEAD), q.dtype),
            in_specs=[vmem],
            out_specs=vmem,
            compiler_params=kernel_params(),
            cost_estimate=pl.CostEstimate(
                flops=4 * rows * rows * heads * heads * HEAD,
                bytes_accessed=8 * rows * heads * HEAD,
                transcendentals=rows * rows * heads * heads,
            ),
            name="self_attention",
        )(moved)
        return lax.all_to_all(own, "ctx", split_axis=0, concat_axis=0, tiled=True)

    piece = rows // parts
    query = jnp.transpose(q.reshape(parts, piece, heads, HEAD), (2, 0, 1, 3)).reshape(
        ctx_size, piece, HEAD
    )
    key = jnp.repeat(jnp.transpose(k.reshape(rows, heads, HEAD), (1, 0, 2)), parts, axis=0)
    value = jnp.repeat(jnp.transpose(v.reshape(rows, heads, HEAD), (1, 0, 2)), parts, axis=0)
    packed = jnp.concatenate([query, key, value], axis=1)
    moved = lax.all_to_all(packed, "ctx", split_axis=0, concat_axis=0, tiled=True)
    query = moved[:, :piece].reshape(ctx_size * piece, HEAD)
    key = moved[:, piece : piece + rows].reshape(ctx_size * rows, HEAD)
    value = moved[:, piece + rows :].reshape(ctx_size * rows, HEAD)
    own = pl.pallas_call(
        attention_kernel,
        out_shape=jax.ShapeDtypeStruct((ctx_size * piece, HEAD), q.dtype),
        grid=(ctx_size * piece // rows,),
        in_specs=[
            pl.BlockSpec((rows, HEAD), lambda i: (i, 0)),
            pl.BlockSpec((ctx_size * rows, HEAD), lambda i: (0, 0)),
            pl.BlockSpec((ctx_size * rows, HEAD), lambda i: (0, 0)),
        ],
        out_specs=pl.BlockSpec((rows, HEAD), lambda i: (i, 0)),
        compiler_params=kernel_params(),
        name="self_attention",
    )(query, key, value)
    back = lax.all_to_all(
        own.reshape(ctx_size, piece, HEAD), "ctx", split_axis=0, concat_axis=0, tiled=True
    )
    return back.reshape(heads, rows, HEAD)


def gather_views(array, view_count):
    gathered = [array]
    step = view_count // 2
    while step:
        swap = [(i, i ^ step) for i in range(view_count)]
        gathered += [lax.ppermute(block, "view", swap) for block in gathered]
        step //= 2
    return gathered


def body(view_count, ctx_size, q_self, k_self, v_self, q_cross, k_cross, v_cross):
    _, rows, width = q_self.shape
    heads = width // HEAD
    keys = gather_views(k_cross[0], view_count)
    values = gather_views(v_cross[0], view_count)
    o_self = self_attention(q_self[0], k_self[0], v_self[0], ctx_size)
    vmem = pl.BlockSpec(memory_space=pltpu.VMEM)
    out = pl.pallas_call(
        functools.partial(cross_kernel, heads),
        out_shape=jax.ShapeDtypeStruct((rows, width), q_self.dtype),
        in_specs=[vmem] * (2 + 2 * view_count),
        out_specs=vmem,
        compiler_params=kernel_params(),
        name="cross_view",
    )(o_self, q_cross[0], *keys, *values)
    return out[None]


def solution(mesh):
    spec = P("view", "ctx", None)
    return jax.shard_map(
        functools.partial(body, mesh.shape["view"], mesh.shape["ctx"]),
        mesh=mesh,
        in_specs=(spec,) * 6,
        out_specs=spec,
        check_vma=False,
    )
```

time: 149 us -> 47.2 us (0.32)
  waiting for transfers between devices: 92.7 us -> 23.5 us
  between operations: 13.5 us -> 0.03 us
  local copies, waits for them, and re-layouts: 12.6 us -> 2.82 us
  blocking collectives: 8.06 us -> 0 us
  matrix products: 7.67 us -> 0 us
  Pallas kernels: 0 us -> 6.22 us
  starting transfers between devices: 11 us -> 14.3 us
  other arithmetic: 2.5 us -> 0 us
    all_gather x2 -> x0, waiting for transfers between devices: 82.5 us -> none  [the longest x1 41.8 us: body(): lax.all_gather(k_self, 'ctx', axis=1, tiled=True)]
    all_to_all x3 -> x2, waiting for transfers between devices: 8.77 us -> 22.1 us  [the longest x1 15.9 us: self_attention(): lax.all_to_all(packed, 'ctx', split_axis=0, concat_axis=0, tiled=True)]
    all_to_all x1 -> x0, blocking collectives: 8.06 us -> none  [body(): lax.all_to_all(mixed_out, 'view', split_axis=0, concat_axis=1, tiled=True)]
    all_gather x2 -> x0, local copies, waits for them, and re-layouts: 7.6 us -> none  [the longest x1 3.81 us: body(): lax.all_gather(v_self, 'ctx', axis=1, tiled=True)]
    pallas_call x0 -> x3, Pallas kernels: none -> 6.22 us  [the longest x1 3.57 us: self_attention(): pl.pallas_call(functools.partial(packed_attention_kernel, rows), out_shap...]
    dot_general x3 -> x0, matrix products: 5.9 us -> none  [the longest x1 3.23 us: online_update(): jnp.einsum('ahqk,akhd->ahqd', weights_full.astype(jnp.bfloat16), value_ro...]
    ppermute x0 -> x6, starting transfers between devices: none -> 3.11 us  [gather_views(): gathered += [lax.ppermute(block, 'view', swap) for block in gathered]]
    sub x1 -> x0, matrix products: 1.78 us -> none  [cross_attend(): cross_scores = cross_scores - jnp.max(cross_scores, axis=-1, keepdims=True)]
  transfers between devices with their start and end apart: 5 -> 8, of which waited for: 4 -> 6; matrix products, arithmetic and copies ran while one was open for 15% -> 0% of each run, Pallas kernels for 0% -> 8%
where the time goes in v1:
time: 47.2 us; the launch traced here: 46.8 us
  waiting for transfers between devices  23.5 us (50%)
  starting transfers between devices  14.3 us (30%)
  Pallas kernels  6.22 us (13%)
  local copies, waits for them, and re-layouts  2.82 us (6%)
    all_to_all x1, waiting for transfers between devices, self_attention(): lax.all_to_all(packed, 'ctx', split_axis=0, concat_axis=0, tiled=True)  15.9 us
    all_to_all x1, starting transfers between devices, self_attention(): lax.all_to_all(packed, 'ctx', split_axis=0, concat_axis=0, tiled=True)  7.38 us
    all_to_all x1, waiting for transfers between devices, self_attention(): return lax.all_to_all(own, 'ctx', split_axis=0, concat_axis=0, tiled=True)  6.16 us
    all_to_all x1, starting transfers between devices, self_attention(): return lax.all_to_all(own, 'ctx', split_axis=0, concat_axis=0, tiled=True)  3.78 us
    pallas_call x1, Pallas kernels, self_attention(): pl.pallas_call(functools.partial(packed_attention_kernel, rows), out_shap...  3.57 us
    ppermute x6, starting transfers between devices, gather_views(): gathered += [lax.ppermute(block, 'view', swap) for block in gathered]  3.11 us
    unnamed x12, local copies, waits for them, and re-layouts  2.82 us
    pallas_call x1, Pallas kernels, body(): pl.pallas_call(functools.partial(cross_kernel, heads), out_shape=jax.Shap...  1.67 us
  transfers between devices with their start and end apart: 8, of which 6 were waited for; matrix products, arithmetic and copies ran while one was open for 0% of the time, Pallas kernels for 8%

profile of v1, /device:TPU:0, one launch (start us, length us, event | category | flops | bytes accessed | tf_op | source)
XLA Modules:
  0.0 46.8 jit_solution(8065070686015139256)
XLA Ops:
  0.0 0.0 copy-start.3
  0.0 0.9 %copy-done.3 = bf16[1,112,1024]{2,1,0:T(8,128)(2,1)S(1)} copy-done((bf16[1,112,1024]{2,1,0:T(8,128)(2,1)S(1)}, bf16[1,112,1024]{2,1,0:T(8,128)(2,1)}, u32[]{:S(2)}) %copy-start.3) | copy-done | bytes 229400
  0.9 0.0 copy-start.4
  0.9 0.9 %copy-done.4 = bf16[1,112,1024]{2,1,0:T(8,128)(2,1)S(1)} copy-done((bf16[1,112,1024]{2,1,0:T(8,128)(2,1)S(1)}, bf16[1,112,1024]{2,1,0:T(8,128)(2,1)}, u32[]{:S(2)}) %copy-start.4) | copy-done | bytes 229400
  1.9 0.0 copy-start.5
  1.9 0.9 %copy-done.5 = bf16[1,112,1024]{2,1,0:T(8,128)(2,1)S(1)} copy-done((bf16[1,112,1024]{2,1,0:T(8,128)(2,1)S(1)}, bf16[1,112,1024]{2,1,0:T(8,128)(2,1)}, u32[]{:S(2)}) %copy-start.5) | copy-done | bytes 229400
  2.8 1.0 %pack_qkv.1 = bf16[8,336,128]{2,1,0:T(8,128)(2,1)} custom-call(bf16[112,1024]{1,0:T(8,128)(2,1)S(1)} %bitcast.14, bf16[112,1024]{1,0:T(8,128)(2,1)S(1)} %bitcast.15, bf16[112,1024]{1,0:T(8,128)(2,1)S(1)} %bitcast.16), custom_call_target="tpu_custom_call" | custom-call | tf_op jit(solution)/shard_map/pack_qkv/pallas_call | solution.py:85
  3.8 0.0 copy-start.1
  3.8 0.0 copy-start.2
  3.8 7.4 %all-to-all-start = ((bf16[8,336,128]{2,1,0:T(8,128)(2,1)}), bf16[8,336,128]{2,1,0:T(8,128)(2,1)S(1)}, u32[]{:S(2)}, u32[]{:S(2)}) async-start(bf16[8,336,128]{2,1,0:T(8,128)(2,1)} %pack_qkv.1), calls=%async_computation | async-start | bytes 1376256 | tf_op jit(solution)/shard_map/all_to_all | solution.py:93
  11.2 0.0 copy-done.1
  11.2 1.6 %collective-permute-start = (bf16[112,1024]{1,0:T(8,128)(2,1)S(1)}, bf16[112,1024]{1,0:T(8,128)(2,1)S(1)}, u32[]{:S(2)}, u32[]{:S(2)}) collective-permute-start(bf16[112,1024]{1,0:T(8,128)(2,1)S(1)} %bitcast.8), channel_id=1, source_target_pairs={{0,16},{8,24},{16,0},{24,8},{1,17},{9,25},{17,1},{25,9},{2,18},{10... | collective-permute-start | bytes 688136 | tf_op jit(solution)/shard_map/ppermute | solution.py:144
  12.8 0.0 copy-done.2
  12.8 0.5 %collective-permute-start.3 = (bf16[112,1024]{1,0:T(8,128)(2,1)S(1)}, bf16[112,1024]{1,0:T(8,128)(2,1)S(1)}, u32[]{:S(2)}, u32[]{:S(2)}) collective-permute-start(bf16[112,1024]{1,0:T(8,128)(2,1)S(1)} %bitcast.11), channel_id=1, source_target_pairs={{0,16},{8,24},{16,0},{24,8},{1,17},{9,25},{17,1},{25,9},{2,18},{10... | collective-permute-start | bytes 688136 | tf_op jit(solution)/shard_map/ppermute | solution.py:144
  13.3 15.9 %all-to-all-done.data_ref = bf16[8,336,128]{2,1,0:T(8,128)(2,1)S(1)} async-done(((bf16[8,336,128]{2,1,0:T(8,128)(2,1)}), bf16[8,336,128]{2,1,0:T(8,128)(2,1)S(1)}, u32[]{:S(2)}, u32[]{:S(2)}) %all-to-all-start) | async-done | bytes 688160 | tf_op jit(solution)/shard_map/all_to_all | solution.py:93
  29.2 3.6 %self_attention.1 = bf16[8,112,128]{2,1,0:T(8,128)(2,1)} custom-call(bf16[8,336,128]{2,1,0:T(8,128)(2,1)S(1)} %all-to-all-done.data_ref), custom_call_target="tpu_custom_call" | custom-call | flops 411041792 | bytes 917504 | tf_op jit(solution)/shard_map/self_attention/pallas_call | solution.py:94
  32.8 0.0 copy-start
  32.8 3.8 %all-to-all-start.1 = ((bf16[8,112,128]{2,1,0:T(8,128)(2,1)}), bf16[8,112,128]{2,1,0:T(8,128)(2,1)S(1)}, u32[]{:S(2)}, u32[]{:S(2)}) async-start(bf16[8,112,128]{2,1,0:T(8,128)(2,1)} %self_attention.1), calls=%async_computation.1 | async-start | bytes 458752 | tf_op jit(solution)/shard_map/all_to_all | solution.py:107
  36.5 0.0 collective-permute-start.1
  36.5 0.5 %collective-permute-start.4 = (bf16[112,1024]{1,0:T(8,128)(2,1)S(1)}, bf16[112,1024]{1,0:T(8,128)(2,1)S(1)}, u32[]{:S(2)}, u32[]{:S(2)}) collective-permute-start(bf16[112,1024]{1,0:T(8,128)(2,1)S(1)} %bitcast.12), channel_id=1, source_target_pairs={{0,8},{8,0},{16,24},{24,16},{1,9},{9,1},{17,25},{25,17},{2,10},{10... | collective-permute-start | bytes 688136 | tf_op jit(solution)/shard_map/ppermute | solution.py:144
  37.0 0.0 collective-permute-done.refs_1_
  37.1 0.1 collective-permute-start.2
  37.1 0.0 collective-permute-done.3.refs_5_
  37.1 0.4 collective-permute-start.5
  37.6 0.5 collective-permute-done.1.refs_2_
  38.0 0.3 collective-permute-done.4.refs_6_
  38.4 0.3 collective-permute-done.2.refs_3_
  38.7 0.3 collective-permute-done.5.refs_7_
  39.0 6.2 %all-to-all-done.1.o_ref = bf16[8,112,128]{2,1,0:T(8,128)(2,1)S(1)} async-done(((bf16[8,112,128]{2,1,0:T(8,128)(2,1)}), bf16[8,112,128]{2,1,0:T(8,128)(2,1)S(1)}, u32[]{:S(2)}, u32[]{:S(2)}) %all-to-all-start.1) | async-done | bytes 229408 | tf_op jit(solution)/shard_map/all_to_all | solution.py:107
  45.2 0.0 copy-done
  45.2 1.7 %cross_view.1 = bf16[112,1024]{1,0:T(8,128)(2,1)} custom-call(bf16[8,112,128]{2,1,0:T(8,128)(2,1)S(1)} %all-to-all-done.1.o_ref, bf16[112,1024]{1,0:T(8,128)(2,1)S(1)} %bitcast.7, bf16[112,1024]{1,0:T(8,128)(2,1)S(1)} %bitcast.10, bf16[112,1024]{1,0:T(8,128)(2,1)S(1)} %collective-permute-done.refs_1_, bf16[112,1024]{1,0:T(8,128)(2,1)S(1)} %collective-permute-done.1.refs_2_, ...), custom_call_target="tpu_custom_call" | custom-call | tf_op jit(solution)/shard_map/cross_view/pallas_call | solution.py:156
Async XLA Ops:
  0.0 0.9 %copy-start.3 = (bf16[1,112,1024]{2,1,0:T(8,128)(2,1)S(1)}, bf16[1,112,1024]{2,1,0:T(8,128)(2,1)}, u32[]{:S(2)}) copy-start(bf16[1,112,1024]{2,1,0:T(8,128)(2,1)} %param.6) | copy-start | bytes 688132
  0.9 0.9 %copy-start.4 = (bf16[1,112,1024]{2,1,0:T(8,128)(2,1)S(1)}, bf16[1,112,1024]{2,1,0:T(8,128)(2,1)}, u32[]{:S(2)}) copy-start(bf16[1,112,1024]{2,1,0:T(8,128)(2,1)} %param.7) | copy-start | bytes 688132
  1.9 0.9 %copy-start.5 = (bf16[1,112,1024]{2,1,0:T(8,128)(2,1)S(1)}, bf16[1,112,1024]{2,1,0:T(8,128)(2,1)}, u32[]{:S(2)}) copy-start(bf16[1,112,1024]{2,1,0:T(8,128)(2,1)} %param.8) | copy-start | bytes 688132
  3.8 7.4 %copy-start.1 = (bf16[1,112,1024]{2,1,0:T(8,128)(2,1)S(1)}, bf16[1,112,1024]{2,1,0:T(8,128)(2,1)}, u32[]{:S(2)}) copy-start(bf16[1,112,1024]{2,1,0:T(8,128)(2,1)} %param.10) | copy-start | bytes 688132
  3.8 9.0 %copy-start.2 = (bf16[1,112,1024]{2,1,0:T(8,128)(2,1)S(1)}, bf16[1,112,1024]{2,1,0:T(8,128)(2,1)}, u32[]{:S(2)}) copy-start(bf16[1,112,1024]{2,1,0:T(8,128)(2,1)} %param.11) | copy-start | bytes 688132
  3.8 25.4 %all-to-all-start = ((bf16[8,336,128]{2,1,0:T(8,128)(2,1)}), bf16[8,336,128]{2,1,0:T(8,128)(2,1)S(1)}, u32[]{:S(2)}, u32[]{:S(2)}) async-start(bf16[8,336,128]{2,1,0:T(8,128)(2,1)} %pack_qkv.1), calls=%async_computation | async-start | bytes 1376256 | tf_op jit(solution)/shard_map/all_to_all | solution.py:93
  11.2 25.9 %collective-permute-start = (bf16[112,1024]{1,0:T(8,128)(2,1)S(1)}, bf16[112,1024]{1,0:T(8,128)(2,1)S(1)}, u32[]{:S(2)}, u32[]{:S(2)}) collective-permute-start(bf16[112,1024]{1,0:T(8,128)(2,1)S(1)} %bitcast.8), channel_id=1, source_target_pairs={{0,16},{8,24},{16,0},{24,8},{1,17},{9,25},{17,1},{25,9},{2,18},{10... | collective-permute-start | bytes 688136 | tf_op jit(solution)/shard_map/ppermute | solution.py:144
  12.8 24.4 %collective-permute-start.3 = (bf16[112,1024]{1,0:T(8,128)(2,1)S(1)}, bf16[112,1024]{1,0:T(8,128)(2,1)S(1)}, u32[]{:S(2)}, u32[]{:S(2)}) collective-permute-start(bf16[112,1024]{1,0:T(8,128)(2,1)S(1)} %bitcast.11), channel_id=1, source_target_pairs={{0,16},{8,24},{16,0},{24,8},{1,17},{9,25},{17,1},{25,9},{2,18},{10... | collective-permute-start | bytes 688136 | tf_op jit(solution)/shard_map/ppermute | solution.py:144
  32.8 12.4 %copy-start = (bf16[1,112,1024]{2,1,0:T(8,128)(2,1)S(1)}, bf16[1,112,1024]{2,1,0:T(8,128)(2,1)}, u32[]{:S(2)}) copy-start(bf16[1,112,1024]{2,1,0:T(8,128)(2,1)} %param.9) | copy-start | bytes 688132
  32.8 12.4 %all-to-all-start.1 = ((bf16[8,112,128]{2,1,0:T(8,128)(2,1)}), bf16[8,112,128]{2,1,0:T(8,128)(2,1)S(1)}, u32[]{:S(2)}, u32[]{:S(2)}) async-start(bf16[8,112,128]{2,1,0:T(8,128)(2,1)} %self_attention.1), calls=%async_computation.1 | async-start | bytes 458752 | tf_op jit(solution)/shard_map/all_to_all | solution.py:107
  36.5 1.5 %collective-permute-start.1 = (bf16[112,1024]{1,0:T(8,128)(2,1)S(1)}, bf16[112,1024]{1,0:T(8,128)(2,1)S(1)}, u32[]{:S(2)}, u32[]{:S(2)}) collective-permute-start(bf16[112,1024]{1,0:T(8,128)(2,1)S(1)} %bitcast.9), channel_id=1, source_target_pairs={{0,8},{8,0},{16,24},{24,16},{1,9},{9,1},{17,25},{25,17},{2,10},{10... | collective-permute-start | bytes 688136 | tf_op jit(solution)/shard_map/ppermute | solution.py:144
  36.5 1.8 %collective-permute-start.4 = (bf16[112,1024]{1,0:T(8,128)(2,1)S(1)}, bf16[112,1024]{1,0:T(8,128)(2,1)S(1)}, u32[]{:S(2)}, u32[]{:S(2)}) collective-permute-start(bf16[112,1024]{1,0:T(8,128)(2,1)S(1)} %bitcast.12), channel_id=1, source_target_pairs={{0,8},{8,0},{16,24},{24,16},{1,9},{9,1},{17,25},{25,17},{2,10},{10... | collective-permute-start | bytes 688136 | tf_op jit(solution)/shard_map/ppermute | solution.py:144
  37.1 1.6 %collective-permute-start.2 = (bf16[112,1024]{1,0:T(8,128)(2,1)S(1)}, bf16[112,1024]{1,0:T(8,128)(2,1)S(1)}, u32[]{:S(2)}, u32[]{:S(2)}) collective-permute-start(bf16[112,1024]{1,0:T(8,128)(2,1)S(1)} %collective-permute-done.refs_1_), channel_id=1, source_target_pairs={{0,8},{8,0},{16,24},{24,16},{1,9},{9,1},{17,25},{25,17},{2,10},{10... | collective-permute-start | bytes 688136 | tf_op jit(solution)/shard_map/ppermute | solution.py:144
  37.1 1.9 %collective-permute-start.5 = (bf16[112,1024]{1,0:T(8,128)(2,1)S(1)}, bf16[112,1024]{1,0:T(8,128)(2,1)S(1)}, u32[]{:S(2)}, u32[]{:S(2)}) collective-permute-start(bf16[112,1024]{1,0:T(8,128)(2,1)S(1)} %collective-permute-done.3.refs_5_), channel_id=1, source_target_pairs={{0,8},{8,0},{16,24},{24,16},{1,9},{9,1},{17,25},{25,17},{2,10},{10... | collective-permute-start | bytes 688136 | tf_op jit(solution)/shard_map/ppermute | solution.py:144

commit v2 on v1

v2 whole, which is shorter than its diff:
```python
import functools
import math

import jax
import jax.numpy as jnp
from jax import lax
from jax.experimental import pallas as pl
from jax.experimental.pallas import tpu as pltpu
from jax.sharding import PartitionSpec as P

HEAD = 128
SCALE = 1.0 / math.sqrt(HEAD)
EXP2_SCALE = SCALE * math.log2(math.e)
MIB = 1024 * 1024


def pack_kernel(partners, q_ref, k_ref, v_ref, kc_ref, vc_ref, *refs):
    block_refs, pair_ref, sems = refs[: len(partners)], refs[-2], refs[-1]
    rows = q_ref.shape[0]
    me = lax.axis_index("ctx")
    copies = []

    def start(source, target):
        copy = pltpu.make_async_copy(source, target, sems.at[len(copies)])
        copy.start()
        copies.append(copy)

    for partner, block_ref in zip(partners, block_refs):
        lanes = pl.ds(pl.multiple_of((me ^ partner) * HEAD, HEAD), HEAD)
        for part, source in enumerate((q_ref, k_ref, v_ref)):
            start(source.at[:, lanes], block_ref.at[pl.ds(part * rows, rows)])
    for part, source in enumerate((kc_ref, vc_ref)):
        start(source, pair_ref.at[pl.ds(part * rows, rows)])
    for copy in copies:
        copy.wait()


def attend(query, keys, values):
    scores = lax.dot_general(
        query, keys, (((1,), (1,)), ((), ())), preferred_element_type=jnp.float32
    )
    row_max = jnp.max(scores, axis=-1, keepdims=True)
    weights_full = jnp.exp2((scores - row_max) * EXP2_SCALE)
    total = jnp.sum(weights_full, axis=-1, keepdims=True)
    mixed = jnp.dot(
        weights_full.astype(jnp.bfloat16), values, preferred_element_type=jnp.float32
    )
    return (mixed / total).astype(jnp.bfloat16)


def packed_attention_kernel(rows, *refs):
    blocks = len(refs) // 2
    in_refs, out_refs = refs[:blocks], refs[blocks:]
    keys = jnp.concatenate([ref[rows : 2 * rows] for ref in in_refs], axis=0)
    values = jnp.concatenate([ref[2 * rows : 3 * rows] for ref in in_refs], axis=0)
    for in_ref, out_ref in zip(in_refs, out_refs):
        out_ref[...] = attend(in_ref[0:rows], keys, values)


def attention_kernel(q_ref, k_ref, v_ref, out_ref):
    out_ref[...] = attend(q_ref[...], k_ref[...], v_ref[...])


def cross_head(rows, o_self, lanes, q_ref, pair_refs, out_ref):
    o_self = o_self.astype(jnp.float32)
    query = (q_ref[:, lanes].astype(jnp.float32) + o_self).astype(jnp.bfloat16).astype(jnp.float32)
    scores = [
        jnp.sum(query * ref[0:rows, lanes].astype(jnp.float32), axis=-1, keepdims=True)
        for ref in pair_refs
    ]
    top = functools.reduce(jnp.maximum, scores)
    weights = [jnp.exp2((score - top) * EXP2_SCALE) for score in scores]
    total = sum(weights[1:], weights[0])
    mixed = None
    for weight, ref in zip(weights, pair_refs):
        rounded = (weight / total).astype(jnp.bfloat16).astype(jnp.float32)
        term = rounded * ref[rows : 2 * rows, lanes].astype(jnp.float32)
        mixed = term if mixed is None else mixed + term
    o_cross = mixed.astype(jnp.bfloat16).astype(jnp.float32)
    out_ref[:, lanes] = (o_self + o_cross).astype(jnp.bfloat16)


def cross_kernel(head_count, view_count, partners, *refs):
    out_ref, refs = refs[-1], refs[:-1]
    pair_refs, refs = refs[-view_count:], refs[:-view_count]
    q_ref, o_refs = refs[-1], refs[:-1]
    rows = q_ref.shape[0]
    if partners is None:
        for head in range(head_count):
            lanes = slice(head * HEAD, (head + 1) * HEAD)
            cross_head(rows, o_refs[0][head], lanes, q_ref, pair_refs, out_ref)
    else:
        me = lax.axis_index("ctx")
        for partner, o_ref in zip(partners, o_refs):
            lanes = pl.ds(pl.multiple_of((me ^ partner) * HEAD, HEAD), HEAD)
            cross_head(rows, o_ref[...], lanes, q_ref, pair_refs, out_ref)


def kernel_params(grant=32):
    return pltpu.CompilerParams(vmem_limit_bytes=grant * MIB)


def swap(array, axis_name, axis_size, partner):
    return lax.ppermute(array, axis_name, [(i, i ^ partner) for i in range(axis_size)])


def gather_views(array, view_count, *after):
    gathered = [array]
    step = view_count // 2
    for earlier in after:
        gathered, _ = lax.optimization_barrier((gathered, earlier))
        gathered += [swap(block, "view", view_count, step) for block in gathered]
        step //= 2
    return gathered


def split_attention(q, k, v, k_cross, v_cross, ctx_size):
    rows, width = q.shape
    heads = width // HEAD
    partners = tuple(range(1, ctx_size)) + (0,)
    vmem = pl.BlockSpec(memory_space=pltpu.VMEM)
    hbm = pl.BlockSpec(memory_space=pltpu.HBM)
    block = jax.ShapeDtypeStruct((3 * rows, HEAD), q.dtype)
    *blocks, pair = pl.pallas_call(
        functools.partial(pack_kernel, partners),
        out_shape=[block] * heads + [jax.ShapeDtypeStruct((2 * rows, width), q.dtype)],
        in_specs=[hbm] * 5,
        out_specs=[vmem] * (heads + 1),
        scratch_shapes=[pltpu.SemaphoreType.DMA((3 * heads + 2,))],
        compiler_params=kernel_params(60),
        name="pack_qkv",
    )(q, k, v, k_cross, v_cross)
    moved = [
        swap(data, "ctx", ctx_size, partner) if partner else data
        for partner, data in zip(partners, blocks)
    ]
    own = pl.pallas_call(
        functools.partial(packed_attention_kernel, rows),
        out_shape=[jax.ShapeDtypeStruct((rows, HEAD), q.dtype)] * heads,
        in_specs=[vmem] * heads,
        out_specs=[vmem] * heads,
        compiler_params=kernel_params(),
        cost_estimate=pl.CostEstimate(
            flops=4 * rows * rows * heads * heads * HEAD,
            bytes_accessed=8 * rows * heads * HEAD,
            transcendentals=rows * rows * heads * heads,
        ),
        name="self_attention",
    )(*moved)
    back = [
        swap(data, "ctx", ctx_size, partner) if partner else data
        for partner, data in zip(partners, own)
    ]
    return back, (pair, moved[:3], own[0]), partners


def shared_attention(q, k, v, ctx_size):
    rows, width = q.shape
    heads = width // HEAD
    parts = ctx_size // heads
    piece = rows // parts
    query = jnp.transpose(q.reshape(parts, piece, heads, HEAD), (2, 0, 1, 3)).reshape(
        ctx_size, piece, HEAD
    )
    key = jnp.repeat(jnp.transpose(k.reshape(rows, heads, HEAD), (1, 0, 2)), parts, axis=0)
    value = jnp.repeat(jnp.transpose(v.reshape(rows, heads, HEAD), (1, 0, 2)), parts, axis=0)
    packed = jnp.concatenate([query, key, value], axis=1)
    moved = lax.all_to_all(packed, "ctx", split_axis=0, concat_axis=0, tiled=True)
    query = moved[:, :piece].reshape(ctx_size * piece, HEAD)
    key = moved[:, piece : piece + rows].reshape(ctx_size * rows, HEAD)
    value = moved[:, piece + rows :].reshape(ctx_size * rows, HEAD)
    own = pl.pallas_call(
        attention_kernel,
        out_shape=jax.ShapeDtypeStruct((ctx_size * piece, HEAD), q.dtype),
        grid=(ctx_size * piece // rows,),
        in_specs=[
            pl.BlockSpec((rows, HEAD), lambda i: (i, 0)),
            pl.BlockSpec((ctx_size * rows, HEAD), lambda i: (0, 0)),
            pl.BlockSpec((ctx_size * rows, HEAD), lambda i: (0, 0)),
        ],
        out_specs=pl.BlockSpec((rows, HEAD), lambda i: (i, 0)),
        compiler_params=kernel_params(),
        name="self_attention",
    )(query, key, value)
    back = lax.all_to_all(
        own.reshape(ctx_size, piece, HEAD), "ctx", split_axis=0, concat_axis=0, tiled=True
    )
    return back.reshape(heads, rows, HEAD)


def body(view_count, ctx_size, q_self, k_self, v_self, q_cross, k_cross, v_cross):
    _, rows, width = q_self.shape
    heads = width // HEAD
    if ctx_size == heads:
        o_self, (pair, *after), partners = split_attention(
            q_self[0], k_self[0], v_self[0], k_cross[0], v_cross[0], ctx_size
        )
    else:
        o_self = [shared_attention(q_self[0], k_self[0], v_self[0], ctx_size)]
        pair, partners = jnp.concatenate([k_cross[0], v_cross[0]], axis=0), None
        after = [pair] * (view_count.bit_length() - 1)
    pairs = gather_views(pair, view_count, *after)
    vmem = pl.BlockSpec(memory_space=pltpu.VMEM)
    out = pl.pallas_call(
        functools.partial(cross_kernel, heads, view_count, partners),
        out_shape=jax.ShapeDtypeStruct((rows, width), q_self.dtype),
        in_specs=[vmem] * (len(o_self) + 1 + view_count),
        out_specs=vmem,
        compiler_params=kernel_params(),
        name="cross_view",
    )(*o_self, q_cross[0], *pairs)
    return out[None]


def solution(mesh):
    spec = P("view", "ctx", None)
    return jax.shard_map(
        functools.partial(body, mesh.shape["view"], mesh.shape["ctx"]),
        mesh=mesh,
        in_specs=(spec,) * 6,
        out_specs=spec,
        check_vma=False,
    )
```

time: 47.2 us -> 52.6 us (1.11)
  starting transfers between devices: 14.3 us -> 28.2 us
  waiting for transfers between devices: 23.5 us -> 16 us
  local copies, waits for them, and re-layouts: 2.82 us -> 0.9 us
  Pallas kernels: 6.22 us -> 7.24 us
    ppermute x6 -> x17, starting transfers between devices: 3.11 us -> 28.2 us  [swap(): lax.ppermute(array, axis_name, [(i, i ^ partner) for i in range(axis_size)])]
    all_to_all x2 -> x0, waiting for transfers between devices: 22.1 us -> none  [the longest x1 15.9 us: self_attention(): lax.all_to_all(packed, 'ctx', split_axis=0, concat_axis=0, tiled=True)]
    ppermute x6 -> x17, waiting for transfers between devices: 1.45 us -> 16 us  [swap(): lax.ppermute(array, axis_name, [(i, i ^ partner) for i in range(axis_size)])]
    all_to_all x2 -> x0, starting transfers between devices: 11.2 us -> none  [the longest x1 7.38 us: self_attention(): lax.all_to_all(packed, 'ctx', split_axis=0, concat_axis=0, tiled=True)]
    unnamed x12 -> x6, local copies, waits for them, and re-layouts: 2.82 us -> 0.9 us
    pallas_call x3, Pallas kernels: 6.22 us -> 7.24 us  [the longest x1 2.9 us: split_attention(): pl.pallas_call(functools.partial(packed_attention_kernel, rows), out_shap...]
  transfers between devices with their start and end apart: 8 -> 17, of which waited for: 6 -> 7; matrix products, arithmetic and copies ran while one was open for 0% -> 0% of each run, Pallas kernels for 8% -> 6%
where the time goes in v2:
time: 52.6 us; the launch traced here: 52.4 us
  starting transfers between devices  28.2 us (54%)
  waiting for transfers between devices  16 us (30%)
  Pallas kernels  7.24 us (14%)
  local copies, waits for them, and re-layouts  0.9 us (2%)
    ppermute x17, starting transfers between devices, swap(): lax.ppermute(array, axis_name, [(i, i ^ partner) for i in range(axis_size)])  28.2 us
    ppermute x17, waiting for transfers between devices, swap(): lax.ppermute(array, axis_name, [(i, i ^ partner) for i in range(axis_size)])  16 us
    pallas_call x1, Pallas kernels, split_attention(): pl.pallas_call(functools.partial(packed_attention_kernel, rows), out_shap...  2.9 us
    pallas_call x1, Pallas kernels, split_attention(): pl.pallas_call(functools.partial(pack_kernel, partners), out_shape=[block...  2.6 us
    pallas_call x1, Pallas kernels, body(): pl.pallas_call(functools.partial(cross_kernel, heads, view_count, partner...  1.73 us
  transfers between devices with their start and end apart: 17, of which 7 were waited for; matrix products, arithmetic and copies ran while one was open for 0% of the time, Pallas kernels for 6%

profile of v2, /device:TPU:0, one launch (start us, length us, event | category | flops | bytes accessed | tf_op | source)
XLA Modules:
  0.0 52.4 jit_solution(7465773046359933124)
XLA Ops:
  0.0 2.6 %pack_qkv.1 = (bf16[336,128]{1,0:T(8,128)(2,1)}, bf16[336,128]{1,0:T(8,128)(2,1)}, bf16[336,128]{1,0:T(8,128)(2,1)}, bf16[336,128]{1,0:T(8,128)(2,1)}, bf16[336,...) custom-call(bf16[112,1024]{1,0:T(8,128)(2,1)} %bitcast.8, ...), custom_call_target="tpu_custom_call" | custom-call | tf_op jit(solution)/shard_map/pack_qkv/pallas_call | solution.py:124
  2.6 3.0 %collective-permute-start = (bf16[336,128]{1,0:T(8,128)(2,1)}, bf16[336,128]{1,0:T(8,128)(2,1)S(1)}, u32[]{:S(2)}, u32[]{:S(2)}) collective-permute-start(bf16[336,128]{1,0:T(8,128)(2,1)} %get-tuple-element.25), channel_id=1, source_target_pairs={{0,1},{1,0},{2,3},{3,2},{4,5},{5,4},{6,7},{7,6},{8,9},{9,8},{10,11... | collective-permute-start | bytes 258056 | tf_op jit(solution)/shard_map/ppermute | solution.py:104
  5.6 1.6 %collective-permute-start.1 = (bf16[336,128]{1,0:T(8,128)(2,1)}, bf16[336,128]{1,0:T(8,128)(2,1)S(1)}, u32[]{:S(2)}, u32[]{:S(2)}) collective-permute-start(bf16[336,128]{1,0:T(8,128)(2,1)} %get-tuple-element.26), channel_id=1, source_target_pairs={{0,2},{1,3},{2,0},{3,1},{4,6},{5,7},{6,4},{7,5},{8,10},{9,11},{10,... | collective-permute-start | bytes 258056 | tf_op jit(solution)/shard_map/ppermute | solution.py:104
  7.2 1.2 %collective-permute-done.refs_0_ = bf16[336,128]{1,0:T(8,128)(2,1)S(1)} collective-permute-done((bf16[336,128]{1,0:T(8,128)(2,1)}, bf16[336,128]{1,0:T(8,128)(2,1)S(1)}, u32[]{:S(2)}, u32[]{:S(2)}) %collective-permute-start) | collective-permute-done | bytes 86048 | tf_op jit(solution)/shard_map/ppermute | solution.py:104
  8.4 2.7 %collective-permute-done.1.refs_1_ = bf16[336,128]{1,0:T(8,128)(2,1)S(1)} collective-permute-done((bf16[336,128]{1,0:T(8,128)(2,1)}, bf16[336,128]{1,0:T(8,128)(2,1)S(1)}, u32[]{:S(2)}, u32[]{:S(2)}) %collective-permute-start.1) | collective-permute-done | bytes 86048 | tf_op jit(solution)/shard_map/ppermute | solution.py:104
  11.1 1.7 %collective-permute-done.2.refs_2_ = bf16[336,128]{1,0:T(8,128)(2,1)S(1)} collective-permute-done((bf16[336,128]{1,0:T(8,128)(2,1)}, bf16[336,128]{1,0:T(8,128)(2,1)S(1)}, u32[]{:S(2)}, u32[]{:S(2)}) %collective-permute-start.2) | collective-permute-done | bytes 86048 | tf_op jit(solution)/shard_map/ppermute | solution.py:104
  12.8 1.5 %collective-permute-start.14 = (bf16[224,1024]{1,0:T(8,128)(2,1)}, bf16[224,1024]{1,0:T(8,128)(2,1)S(1)}, u32[]{:S(2)}, u32[]{:S(2)}) collective-permute-start(bf16[224,1024]{1,0:T(8,128)(2,1)} %get-tuple-element.43.refs_9_), channel_id=1, source_target_pairs={{0,16},{8,24},{16,0},{24,8},{1,17},{9,25},{17,1},{25,9},{2,18},{10... | collective-permute-start | bytes 1376264 | tf_op jit(solution)/shard_map/ppermute | solution.py:104
  14.3 2.6 %collective-permute-start.3 = (bf16[336,128]{1,0:T(8,128)(2,1)}, bf16[336,128]{1,0:T(8,128)(2,1)S(1)}, u32[]{:S(2)}, u32[]{:S(2)}) collective-permute-start(bf16[336,128]{1,0:T(8,128)(2,1)} %get-tuple-element.28), channel_id=1, source_target_pairs={{0,4},{1,5},{2,6},{3,7},{4,0},{5,1},{6,2},{7,3},{8,12},{9,13},{10,... | collective-permute-start | bytes 258056 | tf_op jit(solution)/shard_map/ppermute | solution.py:104
  16.9 0.5 collective-permute-start.4
  17.4 3.3 %collective-permute-start.5 = (bf16[336,128]{1,0:T(8,128)(2,1)}, bf16[336,128]{1,0:T(8,128)(2,1)S(1)}, u32[]{:S(2)}, u32[]{:S(2)}) collective-permute-start(bf16[336,128]{1,0:T(8,128)(2,1)} %get-tuple-element.30), channel_id=1, source_target_pairs={{0,6},{1,7},{2,4},{3,5},{4,2},{5,3},{6,0},{7,1},{8,14},{9,15},{10,... | collective-permute-start | bytes 258056 | tf_op jit(solution)/shard_map/ppermute | solution.py:104
  20.6 1.3 %collective-permute-start.6 = (bf16[336,128]{1,0:T(8,128)(2,1)}, bf16[336,128]{1,0:T(8,128)(2,1)S(1)}, u32[]{:S(2)}, u32[]{:S(2)}) collective-permute-start(bf16[336,128]{1,0:T(8,128)(2,1)} %get-tuple-element.31), channel_id=1, source_target_pairs={{0,7},{1,6},{2,5},{3,4},{4,3},{5,2},{6,1},{7,0},{8,15},{9,14},{10,... | collective-permute-start | bytes 258056 | tf_op jit(solution)/shard_map/ppermute | solution.py:104
  22.0 4.4 %collective-permute-done.3.refs_3_ = bf16[336,128]{1,0:T(8,128)(2,1)S(1)} collective-permute-done((bf16[336,128]{1,0:T(8,128)(2,1)}, bf16[336,128]{1,0:T(8,128)(2,1)S(1)}, u32[]{:S(2)}, u32[]{:S(2)}) %collective-permute-start.3) | collective-permute-done | bytes 86048 | tf_op jit(solution)/shard_map/ppermute | solution.py:104
  26.4 2.8 %collective-permute-done.4.refs_4_ = bf16[336,128]{1,0:T(8,128)(2,1)S(1)} collective-permute-done((bf16[336,128]{1,0:T(8,128)(2,1)}, bf16[336,128]{1,0:T(8,128)(2,1)S(1)}, u32[]{:S(2)}, u32[]{:S(2)}) %collective-permute-start.4) | collective-permute-done | bytes 86048 | tf_op jit(solution)/shard_map/ppermute | solution.py:104
  29.2 0.0 collective-permute-done.5.refs_5_
  29.2 0.0 collective-permute-done.6.refs_6_
  29.2 0.9 %copy-done.2 = bf16[336,128]{1,0:T(8,128)(2,1)S(1)} copy-done((bf16[336,128]{1,0:T(8,128)(2,1)S(1)}, bf16[336,128]{1,0:T(8,128)(2,1)}, u32[]{:S(2)}) %copy-start.2) | copy-done | bytes 86040
  30.1 2.9 %self_attention.1 = (bf16[112,128]{1,0:T(8,128)(2,1)S(1)}, bf16[112,128]{1,0:T(8,128)(2,1)S(1)}, bf16[112,128]{1,0:T(8,128)(2,1)S(1)}, bf16[112,128]{1,0:T(8,128...) custom-call(bf16[336,128]{1,0:T(8,128)(2,1)S(1)} %collective-permute, ...), custom_call_target="tpu_custom_call" | custom-call | flops 411041792 | bytes 917504 | tf_op jit(solution)/shard_map/self_attention/pallas_call | solution.py:137
  33.0 0.0 collective-permute-done.14.refs_10_
  33.0 0.1 collective-permute-start.15
  33.1 0.5 collective-permute-start.16
  33.6 3.4 %collective-permute-start.8 = (bf16[112,128]{1,0:T(8,128)(2,1)S(1)}, bf16[112,128]{1,0:T(8,128)(2,1)S(1)}, u32[]{:S(2)}, u32[]{:S(2)}) collective-permute-start(bf16[112,128]{1,0:T(8,128)(2,1)S(1)} %get-tuple-element.34), channel_id=1, source_target_pairs={{0,2},{1,3},{2,0},{3,1},{4,6},{5,7},{6,4},{7,5},{8,10},{9,11},{10,... | collective-permute-start | bytes 86024 | tf_op jit(solution)/shard_map/ppermute | solution.py:104
  37.0 0.7 %collective-permute-start.9 = (bf16[112,128]{1,0:T(8,128)(2,1)S(1)}, bf16[112,128]{1,0:T(8,128)(2,1)S(1)}, u32[]{:S(2)}, u32[]{:S(2)}) collective-permute-start(bf16[112,128]{1,0:T(8,128)(2,1)S(1)} %get-tuple-element.35), channel_id=1, source_target_pairs={{0,3},{1,2},{2,1},{3,0},{4,7},{5,6},{6,5},{7,4},{8,11},{9,10},{10,... | collective-permute-start | bytes 86024 | tf_op jit(solution)/shard_map/ppermute | solution.py:104
  37.7 2.4 %collective-permute-start.10 = (bf16[112,128]{1,0:T(8,128)(2,1)S(1)}, bf16[112,128]{1,0:T(8,128)(2,1)S(1)}, u32[]{:S(2)}, u32[]{:S(2)}) collective-permute-start(bf16[112,128]{1,0:T(8,128)(2,1)S(1)} %get-tuple-element.36), channel_id=1, source_target_pairs={{0,4},{1,5},{2,6},{3,7},{4,0},{5,1},{6,2},{7,3},{8,12},{9,13},{10,... | collective-permute-start | bytes 86024 | tf_op jit(solution)/shard_map/ppermute | solution.py:104
  40.1 1.8 %collective-permute-start.11 = (bf16[112,128]{1,0:T(8,128)(2,1)S(1)}, bf16[112,128]{1,0:T(8,128)(2,1)S(1)}, u32[]{:S(2)}, u32[]{:S(2)}) collective-permute-start(bf16[112,128]{1,0:T(8,128)(2,1)S(1)} %get-tuple-element.37), channel_id=1, source_target_pairs={{0,5},{1,4},{2,7},{3,6},{4,1},{5,0},{6,3},{7,2},{8,13},{9,12},{10,... | collective-permute-start | bytes 86024 | tf_op jit(solution)/shard_map/ppermute | solution.py:104
  41.9 2.0 %collective-permute-start.12 = (bf16[112,128]{1,0:T(8,128)(2,1)S(1)}, bf16[112,128]{1,0:T(8,128)(2,1)S(1)}, u32[]{:S(2)}, u32[]{:S(2)}) collective-permute-start(bf16[112,128]{1,0:T(8,128)(2,1)S(1)} %get-tuple-element.38), channel_id=1, source_target_pairs={{0,6},{1,7},{2,4},{3,5},{4,2},{5,3},{6,0},{7,1},{8,14},{9,15},{10,... | collective-permute-start | bytes 86024 | tf_op jit(solution)/shard_map/ppermute | solution.py:104
  44.0 2.3 %collective-permute-start.13 = (bf16[112,128]{1,0:T(8,128)(2,1)S(1)}, bf16[112,128]{1,0:T(8,128)(2,1)S(1)}, u32[]{:S(2)}, u32[]{:S(2)}) collective-permute-start(bf16[112,128]{1,0:T(8,128)(2,1)S(1)} %get-tuple-element.39), channel_id=1, source_target_pairs={{0,7},{1,6},{2,5},{3,4},{4,3},{5,2},{6,1},{7,0},{8,15},{9,14},{10,... | collective-permute-start | bytes 86024 | tf_op jit(solution)/shard_map/ppermute | solution.py:104
  46.3 0.2 collective-permute-done.11.refs_4_
  46.5 1.1 %collective-permute-start.7 = (bf16[112,128]{1,0:T(8,128)(2,1)S(1)}, bf16[112,128]{1,0:T(8,128)(2,1)S(1)}, u32[]{:S(2)}, u32[]{:S(2)}) collective-permute-start(bf16[112,128]{1,0:T(8,128)(2,1)S(1)} %get-tuple-element.33), channel_id=1, source_target_pairs={{0,1},{1,0},{2,3},{3,2},{4,5},{5,4},{6,7},{7,6},{8,9},{9,8},{10,11... | collective-permute-start | bytes 86024 | tf_op jit(solution)/shard_map/ppermute | solution.py:104
  47.7 0.0 collective-permute-done.12.refs_5_
  47.7 3.0 %collective-permute-done.13.refs_6_ = bf16[112,128]{1,0:T(8,128)(2,1)S(1)} collective-permute-done((bf16[112,128]{1,0:T(8,128)(2,1)S(1)}, bf16[112,128]{1,0:T(8,128)(2,1)S(1)}, u32[]{:S(2)}, u32[]{:S(2)}) %collective-permute-start.13) | collective-permute-done | bytes 28704 | tf_op jit(solution)/shard_map/ppermute | solution.py:104
  50.7 0.0 collective-permute-done.7.refs_0_
  50.7 1.7 %cross_view.1 = bf16[112,1024]{1,0:T(8,128)(2,1)} custom-call(bf16[112,128]{1,0:T(8,128)(2,1)S(1)} %collective-permute-done.7.refs_0_, bf16[112,128]{1,0:T(8,128)(2,1)S(1)} %collective-permute-done.8.refs_1_, bf16[112,128]{1,0:T(8,128)(2,1)S(1)} %collective-permute-done.9.refs_2_, bf16[112,128]{1,0:T(8,128)(2,1)S(1)} %collective-permute-done.10.refs_3_, ...), custom_call_target="tpu_custom_call" | custom-call | tf_op jit(solution)/shard_map/cross_view/pallas_call | solution.py:204
  (11 shorter events, 0.0 us)
Async XLA Ops:
  2.6 5.7 %collective-permute-start = (bf16[336,128]{1,0:T(8,128)(2,1)}, bf16[336,128]{1,0:T(8,128)(2,1)S(1)}, u32[]{:S(2)}, u32[]{:S(2)}) collective-permute-start(bf16[336,128]{1,0:T(8,128)(2,1)} %get-tuple-element.25), channel_id=1, source_target_pairs={{0,1},{1,0},{2,3},{3,2},{4,5},{5,4},{6,7},{7,6},{8,9},{9,8},{10,11... | collective-permute-start | bytes 258056 | tf_op jit(solution)/shard_map/ppermute | solution.py:104
  5.6 5.5 %collective-permute-start.1 = (bf16[336,128]{1,0:T(8,128)(2,1)}, bf16[336,128]{1,0:T(8,128)(2,1)S(1)}, u32[]{:S(2)}, u32[]{:S(2)}) collective-permute-start(bf16[336,128]{1,0:T(8,128)(2,1)} %get-tuple-element.26), channel_id=1, source_target_pairs={{0,2},{1,3},{2,0},{3,1},{4,6},{5,7},{6,4},{7,5},{8,10},{9,11},{10,... | collective-permute-start | bytes 258056 | tf_op jit(solution)/shard_map/ppermute | solution.py:104
  7.2 5.6 %collective-permute-start.2 = (bf16[336,128]{1,0:T(8,128)(2,1)}, bf16[336,128]{1,0:T(8,128)(2,1)S(1)}, u32[]{:S(2)}, u32[]{:S(2)}) collective-permute-start(bf16[336,128]{1,0:T(8,128)(2,1)} %get-tuple-element.27), channel_id=1, source_target_pairs={{0,3},{1,2},{2,1},{3,0},{4,7},{5,6},{6,5},{7,4},{8,11},{9,10},{10,... | collective-permute-start | bytes 258056 | tf_op jit(solution)/shard_map/ppermute | solution.py:104
  12.8 20.2 %collective-permute-start.14 = (bf16[224,1024]{1,0:T(8,128)(2,1)}, bf16[224,1024]{1,0:T(8,128)(2,1)S(1)}, u32[]{:S(2)}, u32[]{:S(2)}) collective-permute-start(bf16[224,1024]{1,0:T(8,128)(2,1)} %get-tuple-element.43.refs_9_), channel_id=1, source_target_pairs={{0,16},{8,24},{16,0},{24,8},{1,17},{9,25},{17,1},{25,9},{2,18},{10... | collective-permute-start | bytes 1376264 | tf_op jit(solution)/shard_map/ppermute | solution.py:104
  14.3 12.1 %collective-permute-start.3 = (bf16[336,128]{1,0:T(8,128)(2,1)}, bf16[336,128]{1,0:T(8,128)(2,1)S(1)}, u32[]{:S(2)}, u32[]{:S(2)}) collective-permute-start(bf16[336,128]{1,0:T(8,128)(2,1)} %get-tuple-element.28), channel_id=1, source_target_pairs={{0,4},{1,5},{2,6},{3,7},{4,0},{5,1},{6,2},{7,3},{8,12},{9,13},{10,... | collective-permute-start | bytes 258056 | tf_op jit(solution)/shard_map/ppermute | solution.py:104
  16.9 12.3 %collective-permute-start.4 = (bf16[336,128]{1,0:T(8,128)(2,1)}, bf16[336,128]{1,0:T(8,128)(2,1)S(1)}, u32[]{:S(2)}, u32[]{:S(2)}) collective-permute-start(bf16[336,128]{1,0:T(8,128)(2,1)} %get-tuple-element.29), channel_id=1, source_target_pairs={{0,5},{1,4},{2,7},{3,6},{4,1},{5,0},{6,3},{7,2},{8,13},{9,12},{10,... | collective-permute-start | bytes 258056 | tf_op jit(solution)/shard_map/ppermute | solution.py:104
  17.4 11.8 %collective-permute-start.5 = (bf16[336,128]{1,0:T(8,128)(2,1)}, bf16[336,128]{1,0:T(8,128)(2,1)S(1)}, u32[]{:S(2)}, u32[]{:S(2)}) collective-permute-start(bf16[336,128]{1,0:T(8,128)(2,1)} %get-tuple-element.30), channel_id=1, source_target_pairs={{0,6},{1,7},{2,4},{3,5},{4,2},{5,3},{6,0},{7,1},{8,14},{9,15},{10,... | collective-permute-start | bytes 258056 | tf_op jit(solution)/shard_map/ppermute | solution.py:104
  20.6 8.6 %collective-permute-start.6 = (bf16[336,128]{1,0:T(8,128)(2,1)}, bf16[336,128]{1,0:T(8,128)(2,1)S(1)}, u32[]{:S(2)}, u32[]{:S(2)}) collective-permute-start(bf16[336,128]{1,0:T(8,128)(2,1)} %get-tuple-element.31), channel_id=1, source_target_pairs={{0,7},{1,6},{2,5},{3,4},{4,3},{5,2},{6,1},{7,0},{8,15},{9,14},{10,... | collective-permute-start | bytes 258056 | tf_op jit(solution)/shard_map/ppermute | solution.py:104
  29.2 0.9 %copy-start.2 = (bf16[336,128]{1,0:T(8,128)(2,1)S(1)}, bf16[336,128]{1,0:T(8,128)(2,1)}, u32[]{:S(2)}) copy-start(bf16[336,128]{1,0:T(8,128)(2,1)} %get-tuple-element.32.refs_7_) | copy-start | bytes 258052
  30.1 2.9 %copy-start = (bf16[224,1024]{1,0:T(8,128)(2,1)S(1)}, bf16[224,1024]{1,0:T(8,128)(2,1)}, u32[]{:S(2)}) copy-start(bf16[224,1024]{1,0:T(8,128)(2,1)} %get-tuple-element.43.refs_9_) | copy-start | bytes 1376260
  30.1 20.6 %copy-start.1 = (bf16[1,112,1024]{2,1,0:T(8,128)(2,1)S(1)}, bf16[1,112,1024]{2,1,0:T(8,128)(2,1)}, u32[]{:S(2)}) copy-start(bf16[1,112,1024]{2,1,0:T(8,128)(2,1)} %param.9) | copy-start | bytes 688132
  33.0 17.7 %collective-permute-start.15 = (bf16[224,1024]{1,0:T(8,128)(2,1)S(1)}, bf16[224,1024]{1,0:T(8,128)(2,1)S(1)}, u32[]{:S(2)}, u32[]{:S(2)}) collective-permute-start(bf16[224,1024]{1,0:T(8,128)(2,1)S(1)} %copy-done), channel_id=1, source_target_pairs={{0,8},{8,0},{16,24},{24,16},{1,9},{9,1},{17,25},{25,17},{2,10},{10... | collective-permute-start | bytes 1376264 | tf_op jit(solution)/shard_map/ppermute | solution.py:104
  33.1 17.6 %collective-permute-start.16 = (bf16[224,1024]{1,0:T(8,128)(2,1)S(1)}, bf16[224,1024]{1,0:T(8,128)(2,1)S(1)}, u32[]{:S(2)}, u32[]{:S(2)}) collective-permute-start(bf16[224,1024]{1,0:T(8,128)(2,1)S(1)} %collective-permute-done.14.refs_10_), channel_id=1, source_target_pairs={{0,8},{8,0},{16,24},{24,16},{1,9},{9,1},{17,25},{25,17},{2,10},{10... | collective-permute-start | bytes 1376264 | tf_op jit(solution)/shard_map/ppermute | solution.py:104
  33.6 6.5 %collective-permute-start.8 = (bf16[112,128]{1,0:T(8,128)(2,1)S(1)}, bf16[112,128]{1,0:T(8,128)(2,1)S(1)}, u32[]{:S(2)}, u32[]{:S(2)}) collective-permute-start(bf16[112,128]{1,0:T(8,128)(2,1)S(1)} %get-tuple-element.34), channel_id=1, source_target_pairs={{0,2},{1,3},{2,0},{3,1},{4,6},{5,7},{6,4},{7,5},{8,10},{9,11},{10,... | collective-permute-start | bytes 86024 | tf_op jit(solution)/shard_map/ppermute | solution.py:104
  37.0 5.0 %collective-permute-start.9 = (bf16[112,128]{1,0:T(8,128)(2,1)S(1)}, bf16[112,128]{1,0:T(8,128)(2,1)S(1)}, u32[]{:S(2)}, u32[]{:S(2)}) collective-permute-start(bf16[112,128]{1,0:T(8,128)(2,1)S(1)} %get-tuple-element.35), channel_id=1, source_target_pairs={{0,3},{1,2},{2,1},{3,0},{4,7},{5,6},{6,5},{7,4},{8,11},{9,10},{10,... | collective-permute-start | bytes 86024 | tf_op jit(solution)/shard_map/ppermute | solution.py:104
  37.7 6.3 %collective-permute-start.10 = (bf16[112,128]{1,0:T(8,128)(2,1)S(1)}, bf16[112,128]{1,0:T(8,128)(2,1)S(1)}, u32[]{:S(2)}, u32[]{:S(2)}) collective-permute-start(bf16[112,128]{1,0:T(8,128)(2,1)S(1)} %get-tuple-element.36), channel_id=1, source_target_pairs={{0,4},{1,5},{2,6},{3,7},{4,0},{5,1},{6,2},{7,3},{8,12},{9,13},{10,... | collective-permute-start | bytes 86024 | tf_op jit(solution)/shard_map/ppermute | solution.py:104
  40.1 6.4 %collective-permute-start.11 = (bf16[112,128]{1,0:T(8,128)(2,1)S(1)}, bf16[112,128]{1,0:T(8,128)(2,1)S(1)}, u32[]{:S(2)}, u32[]{:S(2)}) collective-permute-start(bf16[112,128]{1,0:T(8,128)(2,1)S(1)} %get-tuple-element.37), channel_id=1, source_target_pairs={{0,5},{1,4},{2,7},{3,6},{4,1},{5,0},{6,3},{7,2},{8,13},{9,12},{10,... | collective-permute-start | bytes 86024 | tf_op jit(solution)/shard_map/ppermute | solution.py:104
  41.9 5.7 %collective-permute-start.12 = (bf16[112,128]{1,0:T(8,128)(2,1)S(1)}, bf16[112,128]{1,0:T(8,128)(2,1)S(1)}, u32[]{:S(2)}, u32[]{:S(2)}) collective-permute-start(bf16[112,128]{1,0:T(8,128)(2,1)S(1)} %get-tuple-element.38), channel_id=1, source_target_pairs={{0,6},{1,7},{2,4},{3,5},{4,2},{5,3},{6,0},{7,1},{8,14},{9,15},{10,... | collective-permute-start | bytes 86024 | tf_op jit(solution)/shard_map/ppermute | solution.py:104
  44.0 6.7 %collective-permute-start.13 = (bf16[112,128]{1,0:T(8,128)(2,1)S(1)}, bf16[112,128]{1,0:T(8,128)(2,1)S(1)}, u32[]{:S(2)}, u32[]{:S(2)}) collective-permute-start(bf16[112,128]{1,0:T(8,128)(2,1)S(1)} %get-tuple-element.39), channel_id=1, source_target_pairs={{0,7},{1,6},{2,5},{3,4},{4,3},{5,2},{6,1},{7,0},{8,15},{9,14},{10,... | collective-permute-start | bytes 86024 | tf_op jit(solution)/shard_map/ppermute | solution.py:104
  46.5 4.2 %collective-permute-start.7 = (bf16[112,128]{1,0:T(8,128)(2,1)S(1)}, bf16[112,128]{1,0:T(8,128)(2,1)S(1)}, u32[]{:S(2)}, u32[]{:S(2)}) collective-permute-start(bf16[112,128]{1,0:T(8,128)(2,1)S(1)} %get-tuple-element.33), channel_id=1, source_target_pairs={{0,1},{1,0},{2,3},{3,2},{4,5},{5,4},{6,7},{7,6},{8,9},{9,8},{10,11... | collective-permute-start | bytes 86024 | tf_op jit(solution)/shard_map/ppermute | solution.py:104

commit v3 on v1

--- a/solution.py
+++ b/solution.py
@@ -11,16 +11,20 @@
 HEAD = 128
 SCALE = 1.0 / math.sqrt(HEAD)
 EXP2_SCALE = SCALE * math.log2(math.e)
-VMEM_LIMIT = 48 * 1024 * 1024
+MIB = 1024 * 1024
 
 
-def pack_kernel(head_count, q_ref, k_ref, v_ref, out_ref):
+def pack_kernel(head_count, q_ref, k_ref, v_ref, out_ref, sems):
     rows = q_ref.shape[0]
+    copies = []
     for head in range(head_count):
-        lanes = slice(head * HEAD, (head + 1) * HEAD)
-        out_ref[head, 0:rows, :] = q_ref[:, lanes]
-        out_ref[head, rows : 2 * rows, :] = k_ref[:, lanes]
-        out_ref[head, 2 * rows : 3 * rows, :] = v_ref[:, lanes]
+        lanes = pl.ds(head * HEAD, HEAD)
+        for part, source in enumerate((q_ref, k_ref, v_ref)):
+            target = out_ref.at[head, pl.ds(part * rows, rows)]
+            copies.append(pltpu.make_async_copy(source.at[:, lanes], target, sems.at[len(copies)]))
+            copies[-1].start()
+    for copy in copies:
+        copy.wait()
 
 
 def attend(query, keys, values):
@@ -28,24 +32,35 @@
         query, keys, (((1,), (1,)), ((), ())), preferred_element_type=jnp.float32
     )
     row_max = jnp.max(scores, axis=-1, keepdims=True)
-    weights_full = jnp.exp2((scores - row_max) * EXP2_SCALE)
-    total = jnp.sum(weights_full, axis=-1, keepdims=True)
-    mixed = jnp.dot(
-        weights_full.astype(jnp.bfloat16), values, preferred_element_type=jnp.float32
-    )
-    return (mixed / total).astype(jnp.bfloat16)
+    weights_raw = jnp.exp2((scores - row_max) * EXP2_SCALE).astype(jnp.bfloat16)
+    values_ones = jnp.concatenate([values, jnp.ones_like(values)], axis=1)
+    mixed = jnp.dot(weights_raw, values_ones, preferred_element_type=jnp.float32)
+    return (mixed[:, :HEAD] / mixed[:, HEAD:]).astype(jnp.bfloat16)
 
 
-def packed_attention_kernel(rows, data_ref, out_ref):
+def packed_attention_kernel(rows, group, data_ref, out_ref):
     blocks = data_ref.shape[0]
-    keys = data_ref[:, rows : 2 * rows, :].reshape(blocks * rows, HEAD)
-    values = data_ref[:, 2 * rows : 3 * rows, :].reshape(blocks * rows, HEAD)
-    for block in range(blocks):
-        out_ref[block] = attend(data_ref[block, 0:rows, :], keys, values)
+    keys = jnp.concatenate([data_ref[i, rows : 2 * rows] for i in range(blocks)], axis=0)
+    values = jnp.concatenate([data_ref[i, 2 * rows : 3 * rows] for i in range(blocks)], axis=0)
+    for first in range(0, blocks, group):
+        query = jnp.concatenate(
+            [data_ref[first + i, 0:rows] for i in range(group)], axis=0
+        )
+        mixed = attend(query, keys, values)
+        for i in range(group):
+            out_ref[first + i] = mixed[i * rows : (i + 1) * rows]
 
 
 def attention_kernel(q_ref, k_ref, v_ref, out_ref):
     out_ref[...] = attend(q_ref[...], k_ref[...], v_ref[...])
+
+
+def lane_sums(products):
+    high = products.astype(jnp.bfloat16)
+    low = (products - high.astype(jnp.float32)).astype(jnp.bfloat16)
+    halves = jnp.concatenate([high, low], axis=1)
+    ones = jnp.ones((2 * HEAD, HEAD), jnp.bfloat16)
+    return jnp.dot(halves, ones, preferred_element_type=jnp.float32)
 
 
 def cross_kernel(head_count, o_ref, q_ref, *refs):
@@ -57,42 +72,44 @@
         o_self = o_ref[head].astype(jnp.float32)
         query = (q_ref[:, lanes].astype(jnp.float32) + o_self).astype(jnp.bfloat16).astype(jnp.float32)
         scores = [
-            jnp.sum(query * key_ref[:, lanes].astype(jnp.float32), axis=-1, keepdims=True)
-            for key_ref in key_refs
+            lane_sums(query * key_ref[:, lanes].astype(jnp.float32)) for key_ref in key_refs
         ]
         top = functools.reduce(jnp.maximum, scores)
         weights = [jnp.exp2((score - top) * EXP2_SCALE) for score in scores]
-        total = sum(weights[1:], weights[0])
+        inverse = 1.0 / sum(weights[1:], weights[0])
         mixed = None
         for weight, value_ref in zip(weights, value_refs):
-            rounded = (weight / total).astype(jnp.bfloat16).astype(jnp.float32)
+            rounded = (weight * inverse).astype(jnp.bfloat16).astype(jnp.float32)
             term = rounded * value_ref[:, lanes].astype(jnp.float32)
             mixed = term if mixed is None else mixed + term
         o_cross = mixed.astype(jnp.bfloat16).astype(jnp.float32)
         out_ref[:, lanes] = (o_self + o_cross).astype(jnp.bfloat16)
 
 
-def kernel_params():
-    return pltpu.CompilerParams(vmem_limit_bytes=VMEM_LIMIT)
+def kernel_params(grant=32):
+    return pltpu.CompilerParams(vmem_limit_bytes=grant * MIB)
 
 
-def self_attention(q, k, v, ctx_size):
+def self_attention(q, k, v, pairs, ctx_size):
     rows, width = q.shape
     heads = width // HEAD
     parts = ctx_size // heads
     vmem = pl.BlockSpec(memory_space=pltpu.VMEM)
+    hbm = pl.BlockSpec(memory_space=pl.ANY)
     if parts == 1:
         packed = pl.pallas_call(
             functools.partial(pack_kernel, heads),
             out_shape=jax.ShapeDtypeStruct((heads, 3 * rows, HEAD), q.dtype),
-            in_specs=[vmem] * 3,
-            out_specs=vmem,
-            compiler_params=kernel_params(),
+            in_specs=[hbm] * 3,
+            out_specs=hbm,
+            scratch_shapes=[pltpu.SemaphoreType.DMA((3 * heads,))],
+            compiler_params=kernel_params(60),
             name="pack_qkv",
         )(q, k, v)
         moved = lax.all_to_all(packed, "ctx", split_axis=0, concat_axis=0, tiled=True)
+        moved, pairs = lax.optimization_barrier((moved, pairs))
         own = pl.pallas_call(
-            functools.partial(packed_attention_kernel, rows),
+            functools.partial(packed_attention_kernel, rows, max(heads // 4, 1)),
             out_shape=jax.ShapeDtypeStruct((heads, rows, HEAD), q.dtype),
             in_specs=[vmem],
             out_specs=vmem,
@@ -104,7 +121,8 @@
             ),
             name="self_attention",
         )(moved)
-        return lax.all_to_all(own, "ctx", split_axis=0, concat_axis=0, tiled=True)
+        back = lax.all_to_all(own, "ctx", split_axis=0, concat_axis=0, tiled=True)
+        return back, pairs
 
     piece = rows // parts
     query = jnp.transpose(q.reshape(parts, piece, heads, HEAD), (2, 0, 1, 3)).reshape(
@@ -133,7 +151,7 @@
     back = lax.all_to_all(
         own.reshape(ctx_size, piece, HEAD), "ctx", split_axis=0, concat_axis=0, tiled=True
     )
-    return back.reshape(heads, rows, HEAD)
+    return back.reshape(heads, rows, HEAD), pairs
 
 
 def gather_views(array, view_count):
@@ -151,7 +169,9 @@
     heads = width // HEAD
     keys = gather_views(k_cross[0], view_count)
     values = gather_views(v_cross[0], view_count)
-    o_self = self_attention(q_self[0], k_self[0], v_self[0], ctx_size)
+    o_self, (keys, values) = self_attention(
+        q_self[0], k_self[0], v_self[0], (keys, values), ctx_size
+    )
     vmem = pl.BlockSpec(memory_space=pltpu.VMEM)
     out = pl.pallas_call(
         functools.partial(cross_kernel, heads),

time: 47.2 us -> 63.5 us (1.35)
  Pallas kernels: 6.22 us -> 25.6 us
  blocking collectives: 0 us -> 12.2 us
  waiting for transfers between devices: 23.5 us -> 15.4 us
  starting transfers between devices: 14.3 us -> 10 us
  local copies, waits for them, and re-layouts: 2.82 us -> 0.02 us
    pallas_call x1, Pallas kernels: 0.98 us -> 22.2 us  [self_attention(): pl.pallas_call(functools.partial(pack_kernel, heads), out_shape=jax.Shape...]
    all_to_all x0 -> x1, blocking collectives: none -> 12.2 us  [self_attention(): back = lax.all_to_all(own, 'ctx', split_axis=0, concat_axis=0, tiled=True)]
    all_to_all x1, waiting for transfers between devices: 15.9 us -> 4.46 us  [self_attention(): lax.all_to_all(packed, 'ctx', split_axis=0, concat_axis=0, tiled=True)]
    ppermute x6, waiting for transfers between devices: 1.45 us -> 10.9 us  [gather_views(): gathered += [lax.ppermute(block, 'view', swap) for block in gathered]]
    all_to_all x1 -> x0, waiting for transfers between devices: 6.16 us -> none  [self_attention(): return lax.all_to_all(own, 'ctx', split_axis=0, concat_axis=0, tiled=True)]
    all_to_all x1 -> x0, starting transfers between devices: 3.78 us -> none  [self_attention(): return lax.all_to_all(own, 'ctx', split_axis=0, concat_axis=0, tiled=True)]
    unnamed x12 -> x6, local copies, waits for them, and re-layouts: 2.82 us -> 0.02 us
    pallas_call x1, Pallas kernels: 3.57 us -> 1.55 us  [self_attention(): pl.pallas_call(functools.partial(packed_attention_kernel, rows, max(heads...]
  transfers between devices with their start and end apart: 8 -> 7, of which waited for: 6 -> 4; matrix products, arithmetic and copies ran while one was open for 0% -> 0% of each run, Pallas kernels for 8% -> 0%
where the time goes in v3:
time: 63.5 us; the launch traced here: 63.3 us
  Pallas kernels  25.6 us (40%)
  waiting for transfers between devices  15.4 us (24%)
  blocking collectives  12.2 us (19%)
  starting transfers between devices  10 us (16%)
    pallas_call x1, Pallas kernels, self_attention(): pl.pallas_call(functools.partial(pack_kernel, heads), out_shape=jax.Shape...  22.2 us
    all_to_all x1, blocking collectives, self_attention(): back = lax.all_to_all(own, 'ctx', split_axis=0, concat_axis=0, tiled=True)  12.2 us
    ppermute x6, waiting for transfers between devices, gather_views(): gathered += [lax.ppermute(block, 'view', swap) for block in gathered]  10.9 us
    all_to_all x1, starting transfers between devices, self_attention(): lax.all_to_all(packed, 'ctx', split_axis=0, concat_axis=0, tiled=True)  7.4 us
    all_to_all x1, waiting for transfers between devices, self_attention(): lax.all_to_all(packed, 'ctx', split_axis=0, concat_axis=0, tiled=True)  4.46 us
    ppermute x6, starting transfers between devices, gather_views(): gathered += [lax.ppermute(block, 'view', swap) for block in gathered]  2.61 us
    pallas_call x1, Pallas kernels, body(): pl.pallas_call(functools.partial(cross_kernel, heads), out_shape=jax.Shap...  1.93 us
    pallas_call x1, Pallas kernels, self_attention(): pl.pallas_call(functools.partial(packed_attention_kernel, rows, max(heads...  1.55 us
  transfers between devices with their start and end apart: 7, of which 4 were waited for; matrix products, arithmetic and copies ran while one was open for 0% of the time, Pallas kernels for 0%

profile of v3, /device:TPU:0, one launch (start us, length us, event | category | flops | bytes accessed | tf_op | source)
XLA Modules:
  0.0 63.3 jit_solution(12194906858344391370)
XLA Ops:
  0.0 22.2 %pack_qkv.1 = bf16[8,336,128]{2,1,0:T(8,128)(2,1)} custom-call(bf16[112,1024]{1,0:T(8,128)(2,1)} %bitcast.14, bf16[112,1024]{1,0:T(8,128)(2,1)} %bitcast.15, bf16[112,1024]{1,0:T(8,128)(2,1)} %bitcast.16), custom_call_target="tpu_custom_call" | custom-call | tf_op jit(solution)/shard_map/pack_qkv/pallas_call | solution.py:100
  22.2 0.0 copy-start.1
  22.2 0.0 copy-start.2
  22.2 7.4 %all-to-all-start = ((bf16[8,336,128]{2,1,0:T(8,128)(2,1)}), bf16[8,336,128]{2,1,0:T(8,128)(2,1)S(1)}, u32[]{:S(2)}, u32[]{:S(2)}) async-start(bf16[8,336,128]{2,1,0:T(8,128)(2,1)} %pack_qkv.1), calls=%async_computation | async-start | bytes 1376256 | tf_op jit(solution)/shard_map/all_to_all | solution.py:109
  29.6 0.0 copy-done.1
  29.6 1.6 %collective-permute-start = (bf16[112,1024]{1,0:T(8,128)(2,1)S(1)}, bf16[112,1024]{1,0:T(8,128)(2,1)S(1)}, u32[]{:S(2)}, u32[]{:S(2)}) collective-permute-start(bf16[112,1024]{1,0:T(8,128)(2,1)S(1)} %bitcast.8), channel_id=1, source_target_pairs={{0,16},{8,24},{16,0},{24,8},{1,17},{9,25},{17,1},{25,9},{2,18},{10... | collective-permute-start | bytes 688136 | tf_op jit(solution)/shard_map/ppermute | solution.py:162
  31.2 0.0 copy-done.2
  31.2 0.5 collective-permute-start.3
  31.7 0.0 collective-permute-start.1
  31.7 0.5 collective-permute-start.4
  32.2 6.0 %collective-permute-done.refs_1_ = bf16[112,1024]{1,0:T(8,128)(2,1)S(1)} collective-permute-done((bf16[112,1024]{1,0:T(8,128)(2,1)S(1)}, bf16[112,1024]{1,0:T(8,128)(2,1)S(1)}, u32[]{:S(2)}, u32[]{:S(2)}) %collective-permute-start) | collective-permute-done | bytes 229408 | tf_op jit(solution)/shard_map/ppermute | solution.py:162
  38.2 0.0 collective-permute-start.2
  38.2 3.4 %collective-permute-done.3.refs_5_ = bf16[112,1024]{1,0:T(8,128)(2,1)S(1)} collective-permute-done((bf16[112,1024]{1,0:T(8,128)(2,1)S(1)}, bf16[112,1024]{1,0:T(8,128)(2,1)S(1)}, u32[]{:S(2)}, u32[]{:S(2)}) %collective-permute-start.3) | collective-permute-done | bytes 229408 | tf_op jit(solution)/shard_map/ppermute | solution.py:162
  41.6 0.0 collective-permute-start.5
  41.7 0.0 collective-permute-done.1.refs_2_
  41.7 0.0 collective-permute-done.4.refs_6_
  41.7 0.0 collective-permute-done.2.refs_3_
  41.7 1.5 %collective-permute-done.5.refs_7_ = bf16[112,1024]{1,0:T(8,128)(2,1)S(1)} collective-permute-done((bf16[112,1024]{1,0:T(8,128)(2,1)S(1)}, bf16[112,1024]{1,0:T(8,128)(2,1)S(1)}, u32[]{:S(2)}, u32[]{:S(2)}) %collective-permute-start.5) | collective-permute-done | bytes 229408 | tf_op jit(solution)/shard_map/ppermute | solution.py:162
  43.1 4.5 %all-to-all-done.data_ref = bf16[8,336,128]{2,1,0:T(8,128)(2,1)S(1)} async-done(((bf16[8,336,128]{2,1,0:T(8,128)(2,1)}), bf16[8,336,128]{2,1,0:T(8,128)(2,1)S(1)}, u32[]{:S(2)}, u32[]{:S(2)}) %all-to-all-start) | async-done | bytes 688160 | tf_op jit(solution)/shard_map/all_to_all | solution.py:109
  47.6 1.5 %self_attention.1 = bf16[8,112,128]{2,1,0:T(8,128)(2,1)S(1)} custom-call(bf16[8,336,128]{2,1,0:T(8,128)(2,1)S(1)} %all-to-all-done.data_ref), custom_call_target="tpu_custom_call" | custom-call | flops 411041792 | bytes 917504 | tf_op jit(solution)/shard_map/self_attention/pallas_call | solution.py:111
  49.1 0.0 copy-start
  49.2 12.2 %all_to_all.10.o_ref = bf16[8,112,128]{2,1,0:T(8,128)(2,1)S(1)} all-to-all(bf16[8,112,128]{2,1,0:T(8,128)(2,1)S(1)} %self_attention.1), channel_id=1, replica_groups=mesh['view'=4,'ctx'=8] {'ctx'}, dimensions={0} | all-to-all | bytes 458752 | tf_op jit(solution)/shard_map/all_to_all | solution.py:124
  61.3 0.0 copy-done
  61.3 1.9 %cross_view.1 = bf16[112,1024]{1,0:T(8,128)(2,1)} custom-call(bf16[8,112,128]{2,1,0:T(8,128)(2,1)S(1)} %all_to_all.10.o_ref, bf16[112,1024]{1,0:T(8,128)(2,1)S(1)} %bitcast.7, bf16[112,1024]{1,0:T(8,128)(2,1)S(1)} %bitcast.10, bf16[112,1024]{1,0:T(8,128)(2,1)S(1)} %collective-permute-done.refs_1_, bf16[112,1024]{1,0:T(8,128)(2,1)S(1)} %collective-permute-done.1.refs_2_, ...), custom_call_target="tpu_custom_call" | custom-call | tf_op jit(solution)/shard_map/cross_view/pallas_call | solution.py:176
Async XLA Ops:
  22.2 7.4 %copy-start.1 = (bf16[1,112,1024]{2,1,0:T(8,128)(2,1)S(1)}, bf16[1,112,1024]{2,1,0:T(8,128)(2,1)}, u32[]{:S(2)}) copy-start(bf16[1,112,1024]{2,1,0:T(8,128)(2,1)} %param.10) | copy-start | bytes 688132
  22.2 9.0 %copy-start.2 = (bf16[1,112,1024]{2,1,0:T(8,128)(2,1)S(1)}, bf16[1,112,1024]{2,1,0:T(8,128)(2,1)}, u32[]{:S(2)}) copy-start(bf16[1,112,1024]{2,1,0:T(8,128)(2,1)} %param.11) | copy-start | bytes 688132
  22.2 25.4 %all-to-all-start = ((bf16[8,336,128]{2,1,0:T(8,128)(2,1)}), bf16[8,336,128]{2,1,0:T(8,128)(2,1)S(1)}, u32[]{:S(2)}, u32[]{:S(2)}) async-start(bf16[8,336,128]{2,1,0:T(8,128)(2,1)} %pack_qkv.1), calls=%async_computation | async-start | bytes 1376256 | tf_op jit(solution)/shard_map/all_to_all | solution.py:109
  29.6 8.6 %collective-permute-start = (bf16[112,1024]{1,0:T(8,128)(2,1)S(1)}, bf16[112,1024]{1,0:T(8,128)(2,1)S(1)}, u32[]{:S(2)}, u32[]{:S(2)}) collective-permute-start(bf16[112,1024]{1,0:T(8,128)(2,1)S(1)} %bitcast.8), channel_id=1, source_target_pairs={{0,16},{8,24},{16,0},{24,8},{1,17},{9,25},{17,1},{25,9},{2,18},{10... | collective-permute-start | bytes 688136 | tf_op jit(solution)/shard_map/ppermute | solution.py:162
  31.2 10.5 %collective-permute-start.3 = (bf16[112,1024]{1,0:T(8,128)(2,1)S(1)}, bf16[112,1024]{1,0:T(8,128)(2,1)S(1)}, u32[]{:S(2)}, u32[]{:S(2)}) collective-permute-start(bf16[112,1024]{1,0:T(8,128)(2,1)S(1)} %bitcast.11), channel_id=1, source_target_pairs={{0,16},{8,24},{16,0},{24,8},{1,17},{9,25},{17,1},{25,9},{2,18},{10... | collective-permute-start | bytes 688136 | tf_op jit(solution)/shard_map/ppermute | solution.py:162
  31.7 10.0 %collective-permute-start.1 = (bf16[112,1024]{1,0:T(8,128)(2,1)S(1)}, bf16[112,1024]{1,0:T(8,128)(2,1)S(1)}, u32[]{:S(2)}, u32[]{:S(2)}) collective-permute-start(bf16[112,1024]{1,0:T(8,128)(2,1)S(1)} %bitcast.9), channel_id=1, source_target_pairs={{0,8},{8,0},{16,24},{24,16},{1,9},{9,1},{17,25},{25,17},{2,10},{10... | collective-permute-start | bytes 688136 | tf_op jit(solution)/shard_map/ppermute | solution.py:162
  31.7 10.0 %collective-permute-start.4 = (bf16[112,1024]{1,0:T(8,128)(2,1)S(1)}, bf16[112,1024]{1,0:T(8,128)(2,1)S(1)}, u32[]{:S(2)}, u32[]{:S(2)}) collective-permute-start(bf16[112,1024]{1,0:T(8,128)(2,1)S(1)} %bitcast.12), channel_id=1, source_target_pairs={{0,8},{8,0},{16,24},{24,16},{1,9},{9,1},{17,25},{25,17},{2,10},{10... | collective-permute-start | bytes 688136 | tf_op jit(solution)/shard_map/ppermute | solution.py:162
  38.2 3.5 %collective-permute-start.2 = (bf16[112,1024]{1,0:T(8,128)(2,1)S(1)}, bf16[112,1024]{1,0:T(8,128)(2,1)S(1)}, u32[]{:S(2)}, u32[]{:S(2)}) collective-permute-start(bf16[112,1024]{1,0:T(8,128)(2,1)S(1)} %collective-permute-done.refs_1_), channel_id=1, source_target_pairs={{0,8},{8,0},{16,24},{24,16},{1,9},{9,1},{17,25},{25,17},{2,10},{10... | collective-permute-start | bytes 688136 | tf_op jit(solution)/shard_map/ppermute | solution.py:162
  41.6 1.5 %collective-permute-start.5 = (bf16[112,1024]{1,0:T(8,128)(2,1)S(1)}, bf16[112,1024]{1,0:T(8,128)(2,1)S(1)}, u32[]{:S(2)}, u32[]{:S(2)}) collective-permute-start(bf16[112,1024]{1,0:T(8,128)(2,1)S(1)} %collective-permute-done.3.refs_5_), channel_id=1, source_target_pairs={{0,8},{8,0},{16,24},{24,16},{1,9},{9,1},{17,25},{25,17},{2,10},{10... | collective-permute-start | bytes 688136 | tf_op jit(solution)/shard_map/ppermute | solution.py:162
  49.1 12.2 %copy-start = (bf16[1,112,1024]{2,1,0:T(8,128)(2,1)S(1)}, bf16[1,112,1024]{2,1,0:T(8,128)(2,1)}, u32[]{:S(2)}) copy-start(bf16[1,112,1024]{2,1,0:T(8,128)(2,1)} %param.9) | copy-start | bytes 688132

commit v4 on v2

--- a/solution.py
+++ b/solution.py
@@ -40,60 +40,49 @@
         query, keys, (((1,), (1,)), ((), ())), preferred_element_type=jnp.float32
     )
     row_max = jnp.max(scores, axis=-1, keepdims=True)
-    weights_full = jnp.exp2((scores - row_max) * EXP2_SCALE)
-    total = jnp.sum(weights_full, axis=-1, keepdims=True)
-    mixed = jnp.dot(
-        weights_full.astype(jnp.bfloat16), values, preferred_element_type=jnp.float32
-    )
-    return (mixed / total).astype(jnp.bfloat16)
-
-
-def packed_attention_kernel(rows, *refs):
-    blocks = len(refs) // 2
-    in_refs, out_refs = refs[:blocks], refs[blocks:]
+    weights_raw = jnp.exp2((scores - row_max) * EXP2_SCALE).astype(jnp.bfloat16)
+    values_ones = jnp.concatenate([values, jnp.ones_like(values)], axis=1)
+    mixed = jnp.dot(weights_raw, values_ones, preferred_element_type=jnp.float32)
+    return (mixed[:, :HEAD] / mixed[:, HEAD:]).astype(jnp.bfloat16)
+
+
+def packed_attention_kernel(partners, rows, group, *refs):
+    *in_refs, out_ref = refs
+    me = lax.axis_index("ctx")
     keys = jnp.concatenate([ref[rows : 2 * rows] for ref in in_refs], axis=0)
     values = jnp.concatenate([ref[2 * rows : 3 * rows] for ref in in_refs], axis=0)
-    for in_ref, out_ref in zip(in_refs, out_refs):
-        out_ref[...] = attend(in_ref[0:rows], keys, values)
+    for first in range(0, len(in_refs), group):
+        query = jnp.concatenate([ref[0:rows] for ref in in_refs[first : first + group]], axis=0)
+        mixed = attend(query, keys, values)
+        for i in range(group):
+            out_ref[me ^ partners[first + i]] = mixed[i * rows : (i + 1) * rows]
 
 
 def attention_kernel(q_ref, k_ref, v_ref, out_ref):
     out_ref[...] = attend(q_ref[...], k_ref[...], v_ref[...])
 
 
-def cross_head(rows, o_self, lanes, q_ref, pair_refs, out_ref):
-    o_self = o_self.astype(jnp.float32)
-    query = (q_ref[:, lanes].astype(jnp.float32) + o_self).astype(jnp.bfloat16).astype(jnp.float32)
-    scores = [
-        jnp.sum(query * ref[0:rows, lanes].astype(jnp.float32), axis=-1, keepdims=True)
-        for ref in pair_refs
-    ]
-    top = functools.reduce(jnp.maximum, scores)
-    weights = [jnp.exp2((score - top) * EXP2_SCALE) for score in scores]
-    total = sum(weights[1:], weights[0])
-    mixed = None
-    for weight, ref in zip(weights, pair_refs):
-        rounded = (weight / total).astype(jnp.bfloat16).astype(jnp.float32)
-        term = rounded * ref[rows : 2 * rows, lanes].astype(jnp.float32)
-        mixed = term if mixed is None else mixed + term
-    o_cross = mixed.astype(jnp.bfloat16).astype(jnp.float32)
-    out_ref[:, lanes] = (o_self + o_cross).astype(jnp.bfloat16)
-
-
-def cross_kernel(head_count, view_count, partners, *refs):
-    out_ref, refs = refs[-1], refs[:-1]
-    pair_refs, refs = refs[-view_count:], refs[:-view_count]
-    q_ref, o_refs = refs[-1], refs[:-1]
+def cross_kernel(head_count, o_ref, q_ref, *refs):
+    *pair_refs, out_ref = refs
     rows = q_ref.shape[0]
-    if partners is None:
-        for head in range(head_count):
-            lanes = slice(head * HEAD, (head + 1) * HEAD)
-            cross_head(rows, o_refs[0][head], lanes, q_ref, pair_refs, out_ref)
-    else:
-        me = lax.axis_index("ctx")
-        for partner, o_ref in zip(partners, o_refs):
-            lanes = pl.ds(pl.multiple_of((me ^ partner) * HEAD, HEAD), HEAD)
-            cross_head(rows, o_ref[...], lanes, q_ref, pair_refs, out_ref)
+    for head in range(head_count):
+        lanes = slice(head * HEAD, (head + 1) * HEAD)
+        o_self = o_ref[head].astype(jnp.float32)
+        query = (q_ref[:, lanes].astype(jnp.float32) + o_self).astype(jnp.bfloat16).astype(jnp.float32)
+        scores = [
+            jnp.sum(query * ref[0:rows, lanes].astype(jnp.float32), axis=-1, keepdims=True)
+            for ref in pair_refs
+        ]
+        top = functools.reduce(jnp.maximum, scores)
+        weights = [jnp.exp2((score - top) * EXP2_SCALE) for score in scores]
+        total = sum(weights[1:], weights[0])
+        mixed = None
+        for weight, ref in zip(weights, pair_refs):
+            rounded = (weight / total).astype(jnp.bfloat16).astype(jnp.float32)
+            term = rounded * ref[rows : 2 * rows, lanes].astype(jnp.float32)
+            mixed = term if mixed is None else mixed + term
+        o_cross = mixed.astype(jnp.bfloat16).astype(jnp.float32)
+        out_ref[:, lanes] = (o_self + o_cross).astype(jnp.bfloat16)
 
 
 def kernel_params(grant=32):
@@ -117,9 +106,10 @@
 def split_attention(q, k, v, k_cross, v_cross, ctx_size):
     rows, width = q.shape
     heads = width // HEAD
-    partners = tuple(range(1, ctx_size)) + (0,)
+    partners = tuple(range(ctx_size - 1, -1, -1))
     vmem = pl.BlockSpec(memory_space=pltpu.VMEM)
     hbm = pl.BlockSpec(memory_space=pltpu.HBM)
+    sources = [pltpu.with_memory_space_constraint(x, pltpu.HBM) for x in (q, k, v, k_cross, v_cross)]
     block = jax.ShapeDtypeStruct((3 * rows, HEAD), q.dtype)
     *blocks, pair = pl.pallas_call(
         functools.partial(pack_kernel, partners),
@@ -127,18 +117,18 @@
         in_specs=[hbm] * 5,
         out_specs=[vmem] * (heads + 1),
         scratch_shapes=[pltpu.SemaphoreType.DMA((3 * heads + 2,))],
-        compiler_params=kernel_params(60),
+        compiler_params=kernel_params(),
         name="pack_qkv",
-    )(q, k, v, k_cross, v_cross)
+    )(*sources)
     moved = [
         swap(data, "ctx", ctx_size, partner) if partner else data
         for partner, data in zip(partners, blocks)
     ]
     own = pl.pallas_call(
-        functools.partial(packed_attention_kernel, rows),
-        out_shape=[jax.ShapeDtypeStruct((rows, HEAD), q.dtype)] * heads,
+        functools.partial(packed_attention_kernel, partners, rows, max(heads // 4, 1)),
+        out_shape=jax.ShapeDtypeStruct((heads, rows, HEAD), q.dtype),
         in_specs=[vmem] * heads,
-        out_specs=[vmem] * heads,
+        out_specs=vmem,
         compiler_params=kernel_params(),
         cost_estimate=pl.CostEstimate(
             flops=4 * rows * rows * heads * heads * HEAD,
@@ -147,11 +137,8 @@
         ),
         name="self_attention",
     )(*moved)
-    back = [
-        swap(data, "ctx", ctx_size, partner) if partner else data
-        for partner, data in zip(partners, own)
-    ]
-    return back, (pair, moved[:3], own[0]), partners
+    back = lax.all_to_all(own, "ctx", split_axis=0, concat_axis=0, tiled=True)
+    return back, pair, (moved, own)
 
 
 def shared_attention(q, k, v, ctx_size):
@@ -192,23 +179,23 @@
     _, rows, width = q_self.shape
     heads = width // HEAD
     if ctx_size == heads:
-        o_self, (pair, *after), partners = split_attention(
+        o_self, pair, after = split_attention(
             q_self[0], k_self[0], v_self[0], k_cross[0], v_cross[0], ctx_size
         )
     else:
-        o_self = [shared_attention(q_self[0], k_self[0], v_self[0], ctx_size)]
-        pair, partners = jnp.concatenate([k_cross[0], v_cross[0]], axis=0), None
+        o_self = shared_attention(q_self[0], k_self[0], v_self[0], ctx_size)
+        pair = jnp.concatenate([k_cross[0], v_cross[0]], axis=0)
         after = [pair] * (view_count.bit_length() - 1)
     pairs = gather_views(pair, view_count, *after)
     vmem = pl.BlockSpec(memory_space=pltpu.VMEM)
     out = pl.pallas_call(
-        functools.partial(cross_kernel, heads, view_count, partners),
+        functools.partial(cross_kernel, heads),
         out_shape=jax.ShapeDtypeStruct((rows, width), q_self.dtype),
-        in_specs=[vmem] * (len(o_self) + 1 + view_count),
+        in_specs=[vmem] * (2 + view_count),
         out_specs=vmem,
         compiler_params=kernel_params(),
         name="cross_view",
-    )(*o_self, q_cross[0], *pairs)
+    )(o_self, q_cross[0], *pairs)
     return out[None]
 
 

time: 52.6 us -> 48.2 us (0.916)
  blocking collectives: 0 us -> 11.8 us
  starting transfers between devices: 28.2 us -> 19.3 us
  waiting for transfers between devices: 16 us -> 12 us
  Pallas kernels: 7.24 us -> 4.86 us
  local copies, waits for them, and re-layouts: 0.9 us -> 0.01 us
    all_to_all x0 -> x1, blocking collectives: none -> 11.8 us  [split_attention(): back = lax.all_to_all(own, 'ctx', split_axis=0, concat_axis=0, tiled=True)]
    ppermute x17 -> x10, starting transfers between devices: 28.2 us -> 19.3 us  [swap(): lax.ppermute(array, axis_name, [(i, i ^ partner) for i in range(axis_size)])]
    ppermute x17 -> x10, waiting for transfers between devices: 16 us -> 12 us  [swap(): lax.ppermute(array, axis_name, [(i, i ^ partner) for i in range(axis_size)])]
    pallas_call x2, Pallas kernels: 4.63 us -> 3.25 us  [the longest x1 1.68 us: body(): pl.pallas_call(functools.partial(cross_kernel, heads), out_shape=jax.Shap...]
    pallas_call x1, Pallas kernels: 2.6 us -> 1.61 us  [split_attention(): pl.pallas_call(functools.partial(pack_kernel, partners), out_shape=[block...]
    unnamed x6 -> x2, local copies, waits for them, and re-layouts: 0.9 us -> 0.01 us
  transfers between devices with their start and end apart: 17 -> 10, of which waited for: 7 -> 4; matrix products, arithmetic and copies ran while one was open for 0% -> 0% of each run, Pallas kernels for 6% -> 3%
where the time goes in v4:
time: 48.2 us; the launch traced here: 48.1 us
  starting transfers between devices  19.3 us (40%)
  waiting for transfers between devices  12 us (25%)
  blocking collectives  11.8 us (24%)
  Pallas kernels  4.86 us (10%)
    ppermute x10, starting transfers between devices, swap(): lax.ppermute(array, axis_name, [(i, i ^ partner) for i in range(axis_size)])  19.3 us
    ppermute x10, waiting for transfers between devices, swap(): lax.ppermute(array, axis_name, [(i, i ^ partner) for i in range(axis_size)])  12 us
    all_to_all x1, blocking collectives, split_attention(): back = lax.all_to_all(own, 'ctx', split_axis=0, concat_axis=0, tiled=True)  11.8 us
    pallas_call x1, Pallas kernels, body(): pl.pallas_call(functools.partial(cross_kernel, heads), out_shape=jax.Shap...  1.68 us
    pallas_call x1, Pallas kernels, split_attention(): pl.pallas_call(functools.partial(pack_kernel, partners), out_shape=[block...  1.61 us
    pallas_call x1, Pallas kernels, split_attention(): pl.pallas_call(functools.partial(packed_attention_kernel, partners, rows,...  1.57 us
  transfers between devices with their start and end apart: 10, of which 4 were waited for; matrix products, arithmetic and copies ran while one was open for 0% of the time, Pallas kernels for 3%

profile of v4, /device:TPU:0, one launch (start us, length us, event | category | flops | bytes accessed | tf_op | source)
XLA Modules:
  0.0 48.1 jit_solution(14155738790300578886)
XLA Ops:
  0.0 1.6 %pack_qkv.1 = (bf16[336,128]{1,0:T(8,128)(2,1)S(1)}, bf16[336,128]{1,0:T(8,128)(2,1)S(1)}, bf16[336,128]{1,0:T(8,128)(2,1)S(1)}, bf16[336,128]{1,0:T(8,128)(2,1)...) custom-call(bf16[112,1024]{1,0:T(8,128)(2,1)} %bitcast.8, ...), custom_call_target="tpu_custom_call" | custom-call | tf_op jit(solution)/shard_map/pack_qkv/pallas_call | solution.py:114
  1.6 6.0 %collective-permute-start = (bf16[336,128]{1,0:T(8,128)(2,1)S(1)}, bf16[336,128]{1,0:T(8,128)(2,1)S(1)}, u32[]{:S(2)}, u32[]{:S(2)}) collective-permute-start(bf16[336,128]{1,0:T(8,128)(2,1)S(1)} %get-tuple-element.17), channel_id=1, source_target_pairs={{0,7},{1,6},{2,5},{3,4},{4,3},{5,2},{6,1},{7,0},{8,15},{9,14},{10,... | collective-permute-start | bytes 258056 | tf_op jit(solution)/shard_map/ppermute | solution.py:93
  7.7 0.2 collective-permute-start.1
  7.9 0.8 %collective-permute-start.2 = (bf16[336,128]{1,0:T(8,128)(2,1)S(1)}, bf16[336,128]{1,0:T(8,128)(2,1)S(1)}, u32[]{:S(2)}, u32[]{:S(2)}) collective-permute-start(bf16[336,128]{1,0:T(8,128)(2,1)S(1)} %get-tuple-element.19), channel_id=1, source_target_pairs={{0,5},{1,4},{2,7},{3,6},{4,1},{5,0},{6,3},{7,2},{8,13},{9,12},{10,... | collective-permute-start | bytes 258056 | tf_op jit(solution)/shard_map/ppermute | solution.py:93
  8.6 2.0 %collective-permute-start.3 = (bf16[336,128]{1,0:T(8,128)(2,1)S(1)}, bf16[336,128]{1,0:T(8,128)(2,1)S(1)}, u32[]{:S(2)}, u32[]{:S(2)}) collective-permute-start(bf16[336,128]{1,0:T(8,128)(2,1)S(1)} %get-tuple-element.20), channel_id=1, source_target_pairs={{0,4},{1,5},{2,6},{3,7},{4,0},{5,1},{6,2},{7,3},{8,12},{9,13},{10,... | collective-permute-start | bytes 258056 | tf_op jit(solution)/shard_map/ppermute | solution.py:93
  10.7 2.3 %collective-permute-start.4 = (bf16[336,128]{1,0:T(8,128)(2,1)S(1)}, bf16[336,128]{1,0:T(8,128)(2,1)S(1)}, u32[]{:S(2)}, u32[]{:S(2)}) collective-permute-start(bf16[336,128]{1,0:T(8,128)(2,1)S(1)} %get-tuple-element.21), channel_id=1, source_target_pairs={{0,3},{1,2},{2,1},{3,0},{4,7},{5,6},{6,5},{7,4},{8,11},{9,10},{10,... | collective-permute-start | bytes 258056 | tf_op jit(solution)/shard_map/ppermute | solution.py:93
  13.0 0.0 collective-permute-done.refs_0_
  13.0 4.3 %collective-permute-start.5 = (bf16[336,128]{1,0:T(8,128)(2,1)S(1)}, bf16[336,128]{1,0:T(8,128)(2,1)S(1)}, u32[]{:S(2)}, u32[]{:S(2)}) collective-permute-start(bf16[336,128]{1,0:T(8,128)(2,1)S(1)} %get-tuple-element.22), channel_id=1, source_target_pairs={{0,2},{1,3},{2,0},{3,1},{4,6},{5,7},{6,4},{7,5},{8,10},{9,11},{10,... | collective-permute-start | bytes 258056 | tf_op jit(solution)/shard_map/ppermute | solution.py:93
  17.2 0.0 collective-permute-done.1.refs_1_
  17.2 1.6 %collective-permute-start.6 = (bf16[336,128]{1,0:T(8,128)(2,1)S(1)}, bf16[336,128]{1,0:T(8,128)(2,1)S(1)}, u32[]{:S(2)}, u32[]{:S(2)}) collective-permute-start(bf16[336,128]{1,0:T(8,128)(2,1)S(1)} %get-tuple-element.23), channel_id=1, source_target_pairs={{0,1},{1,0},{2,3},{3,2},{4,5},{5,4},{6,7},{7,6},{8,9},{9,8},{10,11... | collective-permute-start | bytes 258056 | tf_op jit(solution)/shard_map/ppermute | solution.py:93
  18.9 2.5 %collective-permute-done.2.refs_2_ = bf16[336,128]{1,0:T(8,128)(2,1)S(1)} collective-permute-done((bf16[336,128]{1,0:T(8,128)(2,1)S(1)}, bf16[336,128]{1,0:T(8,128)(2,1)S(1)}, u32[]{:S(2)}, u32[]{:S(2)}) %collective-permute-start.2) | collective-permute-done | bytes 86048 | tf_op jit(solution)/shard_map/ppermute | solution.py:93
  21.4 1.0 %collective-permute-done.3.refs_3_ = bf16[336,128]{1,0:T(8,128)(2,1)S(1)} collective-permute-done((bf16[336,128]{1,0:T(8,128)(2,1)S(1)}, bf16[336,128]{1,0:T(8,128)(2,1)S(1)}, u32[]{:S(2)}, u32[]{:S(2)}) %collective-permute-start.3) | collective-permute-done | bytes 86048 | tf_op jit(solution)/shard_map/ppermute | solution.py:93
  22.4 0.0 collective-permute-done.4.refs_4_
  22.4 0.5 collective-permute-done.5.refs_5_
  22.8 0.0 collective-permute-done.6.refs_6_
  22.8 1.5 %collective-permute-start.7 = (bf16[224,1024]{1,0:T(8,128)(2,1)S(1)}, bf16[224,1024]{1,0:T(8,128)(2,1)S(1)}, u32[]{:S(2)}, u32[]{:S(2)}) collective-permute-start(bf16[224,1024]{1,0:T(8,128)(2,1)S(1)} %get-tuple-element.27.refs_0_), channel_id=1, source_target_pairs={{0,16},{8,24},{16,0},{24,8},{1,17},{9,25},{17,1},{25,9},{2,18},{10... | collective-permute-start | bytes 1376264 | tf_op jit(solution)/shard_map/ppermute | solution.py:93
  24.3 1.6 %self_attention.1 = bf16[8,112,128]{2,1,0:T(8,128)(2,1)S(1)} custom-call(bf16[336,128]{1,0:T(8,128)(2,1)S(1)} %collective-permute-done.refs_0_, bf16[336,128]{1,0:T(8,128)(2,1)S(1)} %collective-permute-done.1.refs_1_, bf16[336,128]{1,0:T(8,128)(2,1)S(1)} %collective-permute-done.2.refs_2_, bf16[336,128]{1,0:T(8,128)(2,1)S(1)} %collective-permute-done.3.refs_3_, ...), custom_call_target="tpu_custom_call" | custom-call | flops 411041792 | bytes 917504 | tf_op jit(solution)/shard_map/self_attention/pallas_call | solution.py:127
  25.9 0.0 copy-start
  25.9 8.1 %collective-permute-done.7.refs_1_ = bf16[224,1024]{1,0:T(8,128)(2,1)S(1)} collective-permute-done((bf16[224,1024]{1,0:T(8,128)(2,1)S(1)}, bf16[224,1024]{1,0:T(8,128)(2,1)S(1)}, u32[]{:S(2)}, u32[]{:S(2)}) %collective-permute-start.7) | collective-permute-done | bytes 458784 | tf_op jit(solution)/shard_map/ppermute | solution.py:93
  34.0 0.0 collective-permute-start.8
  34.0 0.5 %collective-permute-start.9 = (bf16[224,1024]{1,0:T(8,128)(2,1)S(1)}, bf16[224,1024]{1,0:T(8,128)(2,1)S(1)}, u32[]{:S(2)}, u32[]{:S(2)}) collective-permute-start(bf16[224,1024]{1,0:T(8,128)(2,1)S(1)} %collective-permute-done.7.refs_1_), channel_id=1, source_target_pairs={{0,8},{8,0},{16,24},{24,16},{1,9},{9,1},{17,25},{25,17},{2,10},{10... | collective-permute-start | bytes 1376264 | tf_op jit(solution)/shard_map/ppermute | solution.py:93
  34.5 11.8 %all_to_all.5.o_ref = bf16[8,112,128]{2,1,0:T(8,128)(2,1)S(1)} all-to-all(bf16[8,112,128]{2,1,0:T(8,128)(2,1)S(1)} %self_attention.1), channel_id=1, replica_groups=mesh['view'=4,'ctx'=8] {'ctx'}, dimensions={0} | all-to-all | bytes 458752 | tf_op jit(solution)/shard_map/all_to_all | solution.py:140
  46.4 0.0 collective-permute-done.8.refs_2_
  46.4 0.0 collective-permute-done.9.refs_3_
  46.4 0.0 copy-done
  46.4 1.7 %cross_view.1 = bf16[112,1024]{1,0:T(8,128)(2,1)} custom-call(bf16[8,112,128]{2,1,0:T(8,128)(2,1)S(1)} %all_to_all.5.o_ref, bf16[112,1024]{1,0:T(8,128)(2,1)S(1)} %bitcast.7, bf16[224,1024]{1,0:T(8,128)(2,1)S(1)} %get-tuple-element.27.refs_0_, bf16[224,1024]{1,0:T(8,128)(2,1)S(1)} %collective-permute-done.7.refs_1_, ...), custom_call_target="tpu_custom_call" | custom-call | tf_op jit(solution)/shard_map/cross_view/pallas_call | solution.py:191
Async XLA Ops:
  1.6 11.3 %collective-permute-start = (bf16[336,128]{1,0:T(8,128)(2,1)S(1)}, bf16[336,128]{1,0:T(8,128)(2,1)S(1)}, u32[]{:S(2)}, u32[]{:S(2)}) collective-permute-start(bf16[336,128]{1,0:T(8,128)(2,1)S(1)} %get-tuple-element.17), channel_id=1, source_target_pairs={{0,7},{1,6},{2,5},{3,4},{4,3},{5,2},{6,1},{7,0},{8,15},{9,14},{10,... | collective-permute-start | bytes 258056 | tf_op jit(solution)/shard_map/ppermute | solution.py:93
  7.7 9.6 %collective-permute-start.1 = (bf16[336,128]{1,0:T(8,128)(2,1)S(1)}, bf16[336,128]{1,0:T(8,128)(2,1)S(1)}, u32[]{:S(2)}, u32[]{:S(2)}) collective-permute-start(bf16[336,128]{1,0:T(8,128)(2,1)S(1)} %get-tuple-element.18), channel_id=1, source_target_pairs={{0,6},{1,7},{2,4},{3,5},{4,2},{5,3},{6,0},{7,1},{8,14},{9,15},{10,... | collective-permute-start | bytes 258056 | tf_op jit(solution)/shard_map/ppermute | solution.py:93
  7.9 13.5 %collective-permute-start.2 = (bf16[336,128]{1,0:T(8,128)(2,1)S(1)}, bf16[336,128]{1,0:T(8,128)(2,1)S(1)}, u32[]{:S(2)}, u32[]{:S(2)}) collective-permute-start(bf16[336,128]{1,0:T(8,128)(2,1)S(1)} %get-tuple-element.19), channel_id=1, source_target_pairs={{0,5},{1,4},{2,7},{3,6},{4,1},{5,0},{6,3},{7,2},{8,13},{9,12},{10,... | collective-permute-start | bytes 258056 | tf_op jit(solution)/shard_map/ppermute | solution.py:93
  8.6 13.7 %collective-permute-start.3 = (bf16[336,128]{1,0:T(8,128)(2,1)S(1)}, bf16[336,128]{1,0:T(8,128)(2,1)S(1)}, u32[]{:S(2)}, u32[]{:S(2)}) collective-permute-start(bf16[336,128]{1,0:T(8,128)(2,1)S(1)} %get-tuple-element.20), channel_id=1, source_target_pairs={{0,4},{1,5},{2,6},{3,7},{4,0},{5,1},{6,2},{7,3},{8,12},{9,13},{10,... | collective-permute-start | bytes 258056 | tf_op jit(solution)/shard_map/ppermute | solution.py:93
  10.7 11.7 %collective-permute-start.4 = (bf16[336,128]{1,0:T(8,128)(2,1)S(1)}, bf16[336,128]{1,0:T(8,128)(2,1)S(1)}, u32[]{:S(2)}, u32[]{:S(2)}) collective-permute-start(bf16[336,128]{1,0:T(8,128)(2,1)S(1)} %get-tuple-element.21), channel_id=1, source_target_pairs={{0,3},{1,2},{2,1},{3,0},{4,7},{5,6},{6,5},{7,4},{8,11},{9,10},{10,... | collective-permute-start | bytes 258056 | tf_op jit(solution)/shard_map/ppermute | solution.py:93
  13.0 9.9 %collective-permute-start.5 = (bf16[336,128]{1,0:T(8,128)(2,1)S(1)}, bf16[336,128]{1,0:T(8,128)(2,1)S(1)}, u32[]{:S(2)}, u32[]{:S(2)}) collective-permute-start(bf16[336,128]{1,0:T(8,128)(2,1)S(1)} %get-tuple-element.22), channel_id=1, source_target_pairs={{0,2},{1,3},{2,0},{3,1},{4,6},{5,7},{6,4},{7,5},{8,10},{9,11},{10,... | collective-permute-start | bytes 258056 | tf_op jit(solution)/shard_map/ppermute | solution.py:93
  17.2 5.6 %collective-permute-start.6 = (bf16[336,128]{1,0:T(8,128)(2,1)S(1)}, bf16[336,128]{1,0:T(8,128)(2,1)S(1)}, u32[]{:S(2)}, u32[]{:S(2)}) collective-permute-start(bf16[336,128]{1,0:T(8,128)(2,1)S(1)} %get-tuple-element.23), channel_id=1, source_target_pairs={{0,1},{1,0},{2,3},{3,2},{4,5},{5,4},{6,7},{7,6},{8,9},{9,8},{10,11... | collective-permute-start | bytes 258056 | tf_op jit(solution)/shard_map/ppermute | solution.py:93
  22.8 11.2 %collective-permute-start.7 = (bf16[224,1024]{1,0:T(8,128)(2,1)S(1)}, bf16[224,1024]{1,0:T(8,128)(2,1)S(1)}, u32[]{:S(2)}, u32[]{:S(2)}) collective-permute-start(bf16[224,1024]{1,0:T(8,128)(2,1)S(1)} %get-tuple-element.27.refs_0_), channel_id=1, source_target_pairs={{0,16},{8,24},{16,0},{24,8},{1,17},{9,25},{17,1},{25,9},{2,18},{10... | collective-permute-start | bytes 1376264 | tf_op jit(solution)/shard_map/ppermute | solution.py:93
  25.9 20.4 %copy-start = (bf16[1,112,1024]{2,1,0:T(8,128)(2,1)S(1)}, bf16[1,112,1024]{2,1,0:T(8,128)(2,1)}, u32[]{:S(2)}) copy-start(bf16[1,112,1024]{2,1,0:T(8,128)(2,1)} %param.9) | copy-start | bytes 688132
  34.0 12.4 %collective-permute-start.8 = (bf16[224,1024]{1,0:T(8,128)(2,1)S(1)}, bf16[224,1024]{1,0:T(8,128)(2,1)S(1)}, u32[]{:S(2)}, u32[]{:S(2)}) collective-permute-start(bf16[224,1024]{1,0:T(8,128)(2,1)S(1)} %get-tuple-element.27.refs_0_), channel_id=1, source_target_pairs={{0,8},{8,0},{16,24},{24,16},{1,9},{9,1},{17,25},{25,17},{2,10},{10... | collective-permute-start | bytes 1376264 | tf_op jit(solution)/shard_map/ppermute | solution.py:93
  34.0 12.4 %collective-permute-start.9 = (bf16[224,1024]{1,0:T(8,128)(2,1)S(1)}, bf16[224,1024]{1,0:T(8,128)(2,1)S(1)}, u32[]{:S(2)}, u32[]{:S(2)}) collective-permute-start(bf16[224,1024]{1,0:T(8,128)(2,1)S(1)} %collective-permute-done.7.refs_1_), channel_id=1, source_target_pairs={{0,8},{8,0},{16,24},{24,16},{1,9},{9,1},{17,25},{25,17},{2,10},{10... | collective-permute-start | bytes 1376264 | tf_op jit(solution)/shard_map/ppermute | solution.py:93

commit v5 on v4

--- a/solution.py
+++ b/solution.py
@@ -138,7 +138,7 @@
         name="self_attention",
     )(*moved)
     back = lax.all_to_all(own, "ctx", split_axis=0, concat_axis=0, tiled=True)
-    return back, pair, (moved, own)
+    return back, pair, (pair, moved)
 
 
 def shared_attention(q, k, v, ctx_size):

time: 48.2 us -> 44.3 us (0.919)
  waiting for transfers between devices: 12 us -> 4.34 us
  starting transfers between devices: 19.3 us -> 21.7 us
  blocking collectives: 11.8 us -> 13.2 us
    ppermute x10, waiting for transfers between devices: 12 us -> 4.34 us  [swap(): lax.ppermute(array, axis_name, [(i, i ^ partner) for i in range(axis_size)])]
    ppermute x10, starting transfers between devices: 19.3 us -> 21.7 us  [swap(): lax.ppermute(array, axis_name, [(i, i ^ partner) for i in range(axis_size)])]
    all_to_all x1, blocking collectives: 11.8 us -> 13.2 us  [split_attention(): back = lax.all_to_all(own, 'ctx', split_axis=0, concat_axis=0, tiled=True)]
  transfers between devices with their start and end apart: 10 -> 10, of which waited for: 4 -> 4; matrix products, arithmetic and copies ran while one was open for 0% -> 0% of each run, Pallas kernels for 3% -> 4%
where the time goes in v5:
time: 44.3 us; the launch traced here: 44.1 us
  starting transfers between devices  21.7 us (49%)
  blocking collectives  13.2 us (30%)
  Pallas kernels  4.85 us (11%)
  waiting for transfers between devices  4.34 us (10%)
    ppermute x10, starting transfers between devices, swap(): lax.ppermute(array, axis_name, [(i, i ^ partner) for i in range(axis_size)])  21.7 us
    all_to_all x1, blocking collectives, split_attention(): back = lax.all_to_all(own, 'ctx', split_axis=0, concat_axis=0, tiled=True)  13.2 us
    ppermute x10, waiting for transfers between devices, swap(): lax.ppermute(array, axis_name, [(i, i ^ partner) for i in range(axis_size)])  4.34 us
    pallas_call x1, Pallas kernels, body(): pl.pallas_call(functools.partial(cross_kernel, heads), out_shape=jax.Shap...  1.68 us
    pallas_call x1, Pallas kernels, split_attention(): pl.pallas_call(functools.partial(pack_kernel, partners), out_shape=[block...  1.61 us
    pallas_call x1, Pallas kernels, split_attention(): pl.pallas_call(functools.partial(packed_attention_kernel, partners, rows,...  1.57 us
  transfers between devices with their start and end apart: 10, of which 4 were waited for; matrix products, arithmetic and copies ran while one was open for 0% of the time, Pallas kernels for 4%

profile of v5, /device:TPU:0, one launch (start us, length us, event | category | flops | bytes accessed | tf_op | source)
XLA Modules:
  0.0 44.1 jit_solution(15348968931192729386)
XLA Ops:
  0.0 1.6 %pack_qkv.1 = (bf16[336,128]{1,0:T(8,128)(2,1)S(1)}, bf16[336,128]{1,0:T(8,128)(2,1)S(1)}, bf16[336,128]{1,0:T(8,128)(2,1)S(1)}, bf16[336,128]{1,0:T(8,128)(2,1)...) custom-call(bf16[112,1024]{1,0:T(8,128)(2,1)} %bitcast.8, ...), custom_call_target="tpu_custom_call" | custom-call | tf_op jit(solution)/shard_map/pack_qkv/pallas_call | solution.py:114
  1.6 3.0 %collective-permute-start.7 = (bf16[224,1024]{1,0:T(8,128)(2,1)S(1)}, bf16[224,1024]{1,0:T(8,128)(2,1)S(1)}, u32[]{:S(2)}, u32[]{:S(2)}) collective-permute-start(bf16[224,1024]{1,0:T(8,128)(2,1)S(1)} %get-tuple-element.25.refs_0_), channel_id=1, source_target_pairs={{0,16},{8,24},{16,0},{24,8},{1,17},{9,25},{17,1},{25,9},{2,18},{10... | collective-permute-start | bytes 1376264 | tf_op jit(solution)/shard_map/ppermute | solution.py:93
  4.7 4.5 %collective-permute-start = (bf16[336,128]{1,0:T(8,128)(2,1)S(1)}, bf16[336,128]{1,0:T(8,128)(2,1)S(1)}, u32[]{:S(2)}, u32[]{:S(2)}) collective-permute-start(bf16[336,128]{1,0:T(8,128)(2,1)S(1)} %get-tuple-element.16), channel_id=1, source_target_pairs={{0,7},{1,6},{2,5},{3,4},{4,3},{5,2},{6,1},{7,0},{8,15},{9,14},{10,... | collective-permute-start | bytes 258056 | tf_op jit(solution)/shard_map/ppermute | solution.py:93
  9.2 0.2 collective-permute-start.1
  9.4 0.8 %collective-permute-start.2 = (bf16[336,128]{1,0:T(8,128)(2,1)S(1)}, bf16[336,128]{1,0:T(8,128)(2,1)S(1)}, u32[]{:S(2)}, u32[]{:S(2)}) collective-permute-start(bf16[336,128]{1,0:T(8,128)(2,1)S(1)} %get-tuple-element.18), channel_id=1, source_target_pairs={{0,5},{1,4},{2,7},{3,6},{4,1},{5,0},{6,3},{7,2},{8,13},{9,12},{10,... | collective-permute-start | bytes 258056 | tf_op jit(solution)/shard_map/ppermute | solution.py:93
  10.2 2.1 %collective-permute-start.3 = (bf16[336,128]{1,0:T(8,128)(2,1)S(1)}, bf16[336,128]{1,0:T(8,128)(2,1)S(1)}, u32[]{:S(2)}, u32[]{:S(2)}) collective-permute-start(bf16[336,128]{1,0:T(8,128)(2,1)S(1)} %get-tuple-element.19), channel_id=1, source_target_pairs={{0,4},{1,5},{2,6},{3,7},{4,0},{5,1},{6,2},{7,3},{8,12},{9,13},{10,... | collective-permute-start | bytes 258056 | tf_op jit(solution)/shard_map/ppermute | solution.py:93
  12.3 0.0 collective-permute-done.refs_0_
  12.3 7.3 %collective-permute-start.4 = (bf16[336,128]{1,0:T(8,128)(2,1)S(1)}, bf16[336,128]{1,0:T(8,128)(2,1)S(1)}, u32[]{:S(2)}, u32[]{:S(2)}) collective-permute-start(bf16[336,128]{1,0:T(8,128)(2,1)S(1)} %get-tuple-element.20), channel_id=1, source_target_pairs={{0,3},{1,2},{2,1},{3,0},{4,7},{5,6},{6,5},{7,4},{8,11},{9,10},{10,... | collective-permute-start | bytes 258056 | tf_op jit(solution)/shard_map/ppermute | solution.py:93
  19.6 0.0 collective-permute-done.1.refs_1_
  19.6 1.7 %collective-permute-start.5 = (bf16[336,128]{1,0:T(8,128)(2,1)S(1)}, bf16[336,128]{1,0:T(8,128)(2,1)S(1)}, u32[]{:S(2)}, u32[]{:S(2)}) collective-permute-start(bf16[336,128]{1,0:T(8,128)(2,1)S(1)} %get-tuple-element.21), channel_id=1, source_target_pairs={{0,2},{1,3},{2,0},{3,1},{4,6},{5,7},{6,4},{7,5},{8,10},{9,11},{10,... | collective-permute-start | bytes 258056 | tf_op jit(solution)/shard_map/ppermute | solution.py:93
  21.3 1.3 %collective-permute-done.2.refs_2_ = bf16[336,128]{1,0:T(8,128)(2,1)S(1)} collective-permute-done((bf16[336,128]{1,0:T(8,128)(2,1)S(1)}, bf16[336,128]{1,0:T(8,128)(2,1)S(1)}, u32[]{:S(2)}, u32[]{:S(2)}) %collective-permute-start.2) | collective-permute-done | bytes 86048 | tf_op jit(solution)/shard_map/ppermute | solution.py:93
  22.6 1.5 %collective-permute-start.6 = (bf16[336,128]{1,0:T(8,128)(2,1)S(1)}, bf16[336,128]{1,0:T(8,128)(2,1)S(1)}, u32[]{:S(2)}, u32[]{:S(2)}) collective-permute-start(bf16[336,128]{1,0:T(8,128)(2,1)S(1)} %get-tuple-element.22), channel_id=1, source_target_pairs={{0,1},{1,0},{2,3},{3,2},{4,5},{5,4},{6,7},{7,6},{8,9},{9,8},{10,11... | collective-permute-start | bytes 258056 | tf_op jit(solution)/shard_map/ppermute | solution.py:93
  24.1 0.0 collective-permute-done.3.refs_3_
  24.1 0.6 %collective-permute-done.4.refs_4_ = bf16[336,128]{1,0:T(8,128)(2,1)S(1)} collective-permute-done((bf16[336,128]{1,0:T(8,128)(2,1)S(1)}, bf16[336,128]{1,0:T(8,128)(2,1)S(1)}, u32[]{:S(2)}, u32[]{:S(2)}) %collective-permute-start.4) | collective-permute-done | bytes 86048 | tf_op jit(solution)/shard_map/ppermute | solution.py:93
  24.8 0.8 %collective-permute-done.5.refs_5_ = bf16[336,128]{1,0:T(8,128)(2,1)S(1)} collective-permute-done((bf16[336,128]{1,0:T(8,128)(2,1)S(1)}, bf16[336,128]{1,0:T(8,128)(2,1)S(1)}, u32[]{:S(2)}, u32[]{:S(2)}) %collective-permute-start.5) | collective-permute-done | bytes 86048 | tf_op jit(solution)/shard_map/ppermute | solution.py:93
  25.6 1.6 %collective-permute-done.6.refs_6_ = bf16[336,128]{1,0:T(8,128)(2,1)S(1)} collective-permute-done((bf16[336,128]{1,0:T(8,128)(2,1)S(1)}, bf16[336,128]{1,0:T(8,128)(2,1)S(1)}, u32[]{:S(2)}, u32[]{:S(2)}) %collective-permute-start.6) | collective-permute-done | bytes 86048 | tf_op jit(solution)/shard_map/ppermute | solution.py:93
  27.1 0.0 collective-permute-done.7.refs_1_
  27.1 0.0 collective-permute-start.8
  27.1 0.5 %collective-permute-start.9 = (bf16[224,1024]{1,0:T(8,128)(2,1)S(1)}, bf16[224,1024]{1,0:T(8,128)(2,1)S(1)}, u32[]{:S(2)}, u32[]{:S(2)}) collective-permute-start(bf16[224,1024]{1,0:T(8,128)(2,1)S(1)} %collective-permute-done.7.refs_1_), channel_id=1, source_target_pairs={{0,8},{8,0},{16,24},{24,16},{1,9},{9,1},{17,25},{25,17},{2,10},{10... | collective-permute-start | bytes 1376264 | tf_op jit(solution)/shard_map/ppermute | solution.py:93
  27.6 1.6 %self_attention.1 = bf16[8,112,128]{2,1,0:T(8,128)(2,1)S(1)} custom-call(bf16[336,128]{1,0:T(8,128)(2,1)S(1)} %collective-permute-done.refs_0_, bf16[336,128]{1,0:T(8,128)(2,1)S(1)} %collective-permute-done.1.refs_1_, bf16[336,128]{1,0:T(8,128)(2,1)S(1)} %collective-permute-done.2.refs_2_, bf16[336,128]{1,0:T(8,128)(2,1)S(1)} %collective-permute-done.3.refs_3_, ...), custom_call_target="tpu_custom_call" | custom-call | flops 411041792 | bytes 917504 | tf_op jit(solution)/shard_map/self_attention/pallas_call | solution.py:127
  29.2 0.0 copy-start
  29.2 13.2 %all_to_all.5.o_ref = bf16[8,112,128]{2,1,0:T(8,128)(2,1)S(1)} all-to-all(bf16[8,112,128]{2,1,0:T(8,128)(2,1)S(1)} %self_attention.1), channel_id=1, replica_groups=mesh['view'=4,'ctx'=8] {'ctx'}, dimensions={0} | all-to-all | bytes 458752 | tf_op jit(solution)/shard_map/all_to_all | solution.py:140
  42.4 0.0 collective-permute-done.8.refs_2_
  42.4 0.0 collective-permute-done.9.refs_3_
  42.4 0.0 copy-done
  42.5 1.7 %cross_view.1 = bf16[112,1024]{1,0:T(8,128)(2,1)} custom-call(bf16[8,112,128]{2,1,0:T(8,128)(2,1)S(1)} %all_to_all.5.o_ref, bf16[112,1024]{1,0:T(8,128)(2,1)S(1)} %bitcast.7, bf16[224,1024]{1,0:T(8,128)(2,1)S(1)} %get-tuple-element.25.refs_0_, bf16[224,1024]{1,0:T(8,128)(2,1)S(1)} %collective-permute-done.7.refs_1_, ...), custom_call_target="tpu_custom_call" | custom-call | tf_op jit(solution)/shard_map/cross_view/pallas_call | solution.py:191
Async XLA Ops:
  1.6 25.5 %collective-permute-start.7 = (bf16[224,1024]{1,0:T(8,128)(2,1)S(1)}, bf16[224,1024]{1,0:T(8,128)(2,1)S(1)}, u32[]{:S(2)}, u32[]{:S(2)}) collective-permute-start(bf16[224,1024]{1,0:T(8,128)(2,1)S(1)} %get-tuple-element.25.refs_0_), channel_id=1, source_target_pairs={{0,16},{8,24},{16,0},{24,8},{1,17},{9,25},{17,1},{25,9},{2,18},{10... | collective-permute-start | bytes 1376264 | tf_op jit(solution)/shard_map/ppermute | solution.py:93
  4.7 7.7 %collective-permute-start = (bf16[336,128]{1,0:T(8,128)(2,1)S(1)}, bf16[336,128]{1,0:T(8,128)(2,1)S(1)}, u32[]{:S(2)}, u32[]{:S(2)}) collective-permute-start(bf16[336,128]{1,0:T(8,128)(2,1)S(1)} %get-tuple-element.16), channel_id=1, source_target_pairs={{0,7},{1,6},{2,5},{3,4},{4,3},{5,2},{6,1},{7,0},{8,15},{9,14},{10,... | collective-permute-start | bytes 258056 | tf_op jit(solution)/shard_map/ppermute | solution.py:93
  9.2 10.4 %collective-permute-start.1 = (bf16[336,128]{1,0:T(8,128)(2,1)S(1)}, bf16[336,128]{1,0:T(8,128)(2,1)S(1)}, u32[]{:S(2)}, u32[]{:S(2)}) collective-permute-start(bf16[336,128]{1,0:T(8,128)(2,1)S(1)} %get-tuple-element.17), channel_id=1, source_target_pairs={{0,6},{1,7},{2,4},{3,5},{4,2},{5,3},{6,0},{7,1},{8,14},{9,15},{10,... | collective-permute-start | bytes 258056 | tf_op jit(solution)/shard_map/ppermute | solution.py:93
  9.4 13.2 %collective-permute-start.2 = (bf16[336,128]{1,0:T(8,128)(2,1)S(1)}, bf16[336,128]{1,0:T(8,128)(2,1)S(1)}, u32[]{:S(2)}, u32[]{:S(2)}) collective-permute-start(bf16[336,128]{1,0:T(8,128)(2,1)S(1)} %get-tuple-element.18), channel_id=1, source_target_pairs={{0,5},{1,4},{2,7},{3,6},{4,1},{5,0},{6,3},{7,2},{8,13},{9,12},{10,... | collective-permute-start | bytes 258056 | tf_op jit(solution)/shard_map/ppermute | solution.py:93
  10.2 14.0 %collective-permute-start.3 = (bf16[336,128]{1,0:T(8,128)(2,1)S(1)}, bf16[336,128]{1,0:T(8,128)(2,1)S(1)}, u32[]{:S(2)}, u32[]{:S(2)}) collective-permute-start(bf16[336,128]{1,0:T(8,128)(2,1)S(1)} %get-tuple-element.19), channel_id=1, source_target_pairs={{0,4},{1,5},{2,6},{3,7},{4,0},{5,1},{6,2},{7,3},{8,12},{9,13},{10,... | collective-permute-start | bytes 258056 | tf_op jit(solution)/shard_map/ppermute | solution.py:93
  12.3 12.5 %collective-permute-start.4 = (bf16[336,128]{1,0:T(8,128)(2,1)S(1)}, bf16[336,128]{1,0:T(8,128)(2,1)S(1)}, u32[]{:S(2)}, u32[]{:S(2)}) collective-permute-start(bf16[336,128]{1,0:T(8,128)(2,1)S(1)} %get-tuple-element.20), channel_id=1, source_target_pairs={{0,3},{1,2},{2,1},{3,0},{4,7},{5,6},{6,5},{7,4},{8,11},{9,10},{10,... | collective-permute-start | bytes 258056 | tf_op jit(solution)/shard_map/ppermute | solution.py:93
  19.6 6.0 %collective-permute-start.5 = (bf16[336,128]{1,0:T(8,128)(2,1)S(1)}, bf16[336,128]{1,0:T(8,128)(2,1)S(1)}, u32[]{:S(2)}, u32[]{:S(2)}) collective-permute-start(bf16[336,128]{1,0:T(8,128)(2,1)S(1)} %get-tuple-element.21), channel_id=1, source_target_pairs={{0,2},{1,3},{2,0},{3,1},{4,6},{5,7},{6,4},{7,5},{8,10},{9,11},{10,... | collective-permute-start | bytes 258056 | tf_op jit(solution)/shard_map/ppermute | solution.py:93
  22.6 4.5 %collective-permute-start.6 = (bf16[336,128]{1,0:T(8,128)(2,1)S(1)}, bf16[336,128]{1,0:T(8,128)(2,1)S(1)}, u32[]{:S(2)}, u32[]{:S(2)}) collective-permute-start(bf16[336,128]{1,0:T(8,128)(2,1)S(1)} %get-tuple-element.22), channel_id=1, source_target_pairs={{0,1},{1,0},{2,3},{3,2},{4,5},{5,4},{6,7},{7,6},{8,9},{9,8},{10,11... | collective-permute-start | bytes 258056 | tf_op jit(solution)/shard_map/ppermute | solution.py:93
  27.1 15.3 %collective-permute-start.8 = (bf16[224,1024]{1,0:T(8,128)(2,1)S(1)}, bf16[224,1024]{1,0:T(8,128)(2,1)S(1)}, u32[]{:S(2)}, u32[]{:S(2)}) collective-permute-start(bf16[224,1024]{1,0:T(8,128)(2,1)S(1)} %get-tuple-element.25.refs_0_), channel_id=1, source_target_pairs={{0,8},{8,0},{16,24},{24,16},{1,9},{9,1},{17,25},{25,17},{2,10},{10... | collective-permute-start | bytes 1376264 | tf_op jit(solution)/shard_map/ppermute | solution.py:93
  27.1 15.3 %collective-permute-start.9 = (bf16[224,1024]{1,0:T(8,128)(2,1)S(1)}, bf16[224,1024]{1,0:T(8,128)(2,1)S(1)}, u32[]{:S(2)}, u32[]{:S(2)}) collective-permute-start(bf16[224,1024]{1,0:T(8,128)(2,1)S(1)} %collective-permute-done.7.refs_1_), channel_id=1, source_target_pairs={{0,8},{8,0},{16,24},{24,16},{1,9},{9,1},{17,25},{25,17},{2,10},{10... | collective-permute-start | bytes 1376264 | tf_op jit(solution)/shard_map/ppermute | solution.py:93
  29.2 13.2 %copy-start = (bf16[1,112,1024]{2,1,0:T(8,128)(2,1)S(1)}, bf16[1,112,1024]{2,1,0:T(8,128)(2,1)}, u32[]{:S(2)}) copy-start(bf16[1,112,1024]{2,1,0:T(8,128)(2,1)} %param.9) | copy-start | bytes 688132

commit v6 on v3

--- a/solution.py
+++ b/solution.py
@@ -55,14 +55,6 @@
     out_ref[...] = attend(q_ref[...], k_ref[...], v_ref[...])
 
 
-def lane_sums(products):
-    high = products.astype(jnp.bfloat16)
-    low = (products - high.astype(jnp.float32)).astype(jnp.bfloat16)
-    halves = jnp.concatenate([high, low], axis=1)
-    ones = jnp.ones((2 * HEAD, HEAD), jnp.bfloat16)
-    return jnp.dot(halves, ones, preferred_element_type=jnp.float32)
-
-
 def cross_kernel(head_count, o_ref, q_ref, *refs):
     out_ref = refs[-1]
     views = (len(refs) - 1) // 2
@@ -72,14 +64,15 @@
         o_self = o_ref[head].astype(jnp.float32)
         query = (q_ref[:, lanes].astype(jnp.float32) + o_self).astype(jnp.bfloat16).astype(jnp.float32)
         scores = [
-            lane_sums(query * key_ref[:, lanes].astype(jnp.float32)) for key_ref in key_refs
+            jnp.sum(query * key_ref[:, lanes].astype(jnp.float32), axis=-1, keepdims=True)
+            for key_ref in key_refs
         ]
         top = functools.reduce(jnp.maximum, scores)
         weights = [jnp.exp2((score - top) * EXP2_SCALE) for score in scores]
-        inverse = 1.0 / sum(weights[1:], weights[0])
+        total = sum(weights[1:], weights[0])
         mixed = None
         for weight, value_ref in zip(weights, value_refs):
-            rounded = (weight * inverse).astype(jnp.bfloat16).astype(jnp.float32)
+            rounded = (weight / total).astype(jnp.bfloat16).astype(jnp.float32)
             term = rounded * value_ref[:, lanes].astype(jnp.float32)
             mixed = term if mixed is None else mixed + term
         o_cross = mixed.astype(jnp.bfloat16).astype(jnp.float32)
@@ -95,17 +88,17 @@
     heads = width // HEAD
     parts = ctx_size // heads
     vmem = pl.BlockSpec(memory_space=pltpu.VMEM)
-    hbm = pl.BlockSpec(memory_space=pl.ANY)
+    hbm = pl.BlockSpec(memory_space=pltpu.HBM)
     if parts == 1:
         packed = pl.pallas_call(
             functools.partial(pack_kernel, heads),
             out_shape=jax.ShapeDtypeStruct((heads, 3 * rows, HEAD), q.dtype),
             in_specs=[hbm] * 3,
-            out_specs=hbm,
+            out_specs=vmem,
             scratch_shapes=[pltpu.SemaphoreType.DMA((3 * heads,))],
-            compiler_params=kernel_params(60),
+            compiler_params=kernel_params(),
             name="pack_qkv",
-        )(q, k, v)
+        )(*[pltpu.with_memory_space_constraint(x, pltpu.HBM) for x in (q, k, v)])
         moved = lax.all_to_all(packed, "ctx", split_axis=0, concat_axis=0, tiled=True)
         moved, pairs = lax.optimization_barrier((moved, pairs))
         own = pl.pallas_call(

time: 63.5 us -> 43.3 us (0.68)
  Pallas kernels: 25.6 us -> 5.36 us
    pallas_call x1, Pallas kernels: 22.2 us -> 2.14 us  [self_attention(): pl.pallas_call(functools.partial(pack_kernel, heads), out_shape=jax.Shape...]
where the time goes in v6:
time: 43.3 us; the launch traced here: 43 us
  waiting for transfers between devices  15.4 us (36%)
  blocking collectives  12.2 us (28%)
  starting transfers between devices  10 us (23%)
  Pallas kernels  5.36 us (12%)
    all_to_all x1, blocking collectives, self_attention(): back = lax.all_to_all(own, 'ctx', split_axis=0, concat_axis=0, tiled=True)  12.2 us
    ppermute x6, waiting for transfers between devices, gather_views(): gathered += [lax.ppermute(block, 'view', swap) for block in gathered]  10.9 us
    all_to_all x1, starting transfers between devices, self_attention(): lax.all_to_all(packed, 'ctx', split_axis=0, concat_axis=0, tiled=True)  7.4 us
    all_to_all x1, waiting for transfers between devices, self_attention(): lax.all_to_all(packed, 'ctx', split_axis=0, concat_axis=0, tiled=True)  4.46 us
    ppermute x6, starting transfers between devices, gather_views(): gathered += [lax.ppermute(block, 'view', swap) for block in gathered]  2.61 us
    pallas_call x1, Pallas kernels, self_attention(): pl.pallas_call(functools.partial(pack_kernel, heads), out_shape=jax.Shape...  2.14 us
    pallas_call x1, Pallas kernels, body(): pl.pallas_call(functools.partial(cross_kernel, heads), out_shape=jax.Shap...  1.67 us
    pallas_call x1, Pallas kernels, self_attention(): pl.pallas_call(functools.partial(packed_attention_kernel, rows, max(heads...  1.55 us
  transfers between devices with their start and end apart: 7, of which 4 were waited for; matrix products, arithmetic and copies ran while one was open for 0% of the time, Pallas kernels for 0%

profile of v6, /device:TPU:0, one launch (start us, length us, event | category | flops | bytes accessed | tf_op | source)
XLA Modules:
  0.0 43.0 jit_solution(12135161890122419674)
XLA Ops:
  0.0 2.1 %pack_qkv.1 = bf16[8,336,128]{2,1,0:T(8,128)(2,1)} custom-call(bf16[112,1024]{1,0:T(8,128)(2,1)} %bitcast.14, bf16[112,1024]{1,0:T(8,128)(2,1)} %bitcast.15, bf16[112,1024]{1,0:T(8,128)(2,1)} %bitcast.16), custom_call_target="tpu_custom_call" | custom-call | tf_op jit(solution)/shard_map/pack_qkv/pallas_call | solution.py:93
  2.1 0.0 copy-start.1
  2.2 0.0 copy-start.2
  2.2 7.4 %all-to-all-start = ((bf16[8,336,128]{2,1,0:T(8,128)(2,1)}), bf16[8,336,128]{2,1,0:T(8,128)(2,1)S(1)}, u32[]{:S(2)}, u32[]{:S(2)}) async-start(bf16[8,336,128]{2,1,0:T(8,128)(2,1)} %pack_qkv.1), calls=%async_computation | async-start | bytes 1376256 | tf_op jit(solution)/shard_map/all_to_all | solution.py:102
  9.6 0.0 copy-done.1
  9.6 1.6 %collective-permute-start = (bf16[112,1024]{1,0:T(8,128)(2,1)S(1)}, bf16[112,1024]{1,0:T(8,128)(2,1)S(1)}, u32[]{:S(2)}, u32[]{:S(2)}) collective-permute-start(bf16[112,1024]{1,0:T(8,128)(2,1)S(1)} %bitcast.8), channel_id=1, source_target_pairs={{0,16},{8,24},{16,0},{24,8},{1,17},{9,25},{17,1},{25,9},{2,18},{10... | collective-permute-start | bytes 688136 | tf_op jit(solution)/shard_map/ppermute | solution.py:155
  11.2 0.0 copy-done.2
  11.2 0.5 %collective-permute-start.3 = (bf16[112,1024]{1,0:T(8,128)(2,1)S(1)}, bf16[112,1024]{1,0:T(8,128)(2,1)S(1)}, u32[]{:S(2)}, u32[]{:S(2)}) collective-permute-start(bf16[112,1024]{1,0:T(8,128)(2,1)S(1)} %bitcast.11), channel_id=1, source_target_pairs={{0,16},{8,24},{16,0},{24,8},{1,17},{9,25},{17,1},{25,9},{2,18},{10... | collective-permute-start | bytes 688136 | tf_op jit(solution)/shard_map/ppermute | solution.py:155
  11.7 0.0 collective-permute-start.1
  11.7 0.5 %collective-permute-start.4 = (bf16[112,1024]{1,0:T(8,128)(2,1)S(1)}, bf16[112,1024]{1,0:T(8,128)(2,1)S(1)}, u32[]{:S(2)}, u32[]{:S(2)}) collective-permute-start(bf16[112,1024]{1,0:T(8,128)(2,1)S(1)} %bitcast.12), channel_id=1, source_target_pairs={{0,8},{8,0},{16,24},{24,16},{1,9},{9,1},{17,25},{25,17},{2,10},{10... | collective-permute-start | bytes 688136 | tf_op jit(solution)/shard_map/ppermute | solution.py:155
  12.2 6.0 %collective-permute-done.refs_1_ = bf16[112,1024]{1,0:T(8,128)(2,1)S(1)} collective-permute-done((bf16[112,1024]{1,0:T(8,128)(2,1)S(1)}, bf16[112,1024]{1,0:T(8,128)(2,1)S(1)}, u32[]{:S(2)}, u32[]{:S(2)}) %collective-permute-start) | collective-permute-done | bytes 229408 | tf_op jit(solution)/shard_map/ppermute | solution.py:155
  18.2 0.0 collective-permute-start.2
  18.2 3.4 %collective-permute-done.3.refs_5_ = bf16[112,1024]{1,0:T(8,128)(2,1)S(1)} collective-permute-done((bf16[112,1024]{1,0:T(8,128)(2,1)S(1)}, bf16[112,1024]{1,0:T(8,128)(2,1)S(1)}, u32[]{:S(2)}, u32[]{:S(2)}) %collective-permute-start.3) | collective-permute-done | bytes 229408 | tf_op jit(solution)/shard_map/ppermute | solution.py:155
  21.6 0.0 collective-permute-start.5
  21.6 0.0 collective-permute-done.1.refs_2_
  21.6 0.0 collective-permute-done.4.refs_6_
  21.6 0.0 collective-permute-done.2.refs_3_
  21.6 1.5 %collective-permute-done.5.refs_7_ = bf16[112,1024]{1,0:T(8,128)(2,1)S(1)} collective-permute-done((bf16[112,1024]{1,0:T(8,128)(2,1)S(1)}, bf16[112,1024]{1,0:T(8,128)(2,1)S(1)}, u32[]{:S(2)}, u32[]{:S(2)}) %collective-permute-start.5) | collective-permute-done | bytes 229408 | tf_op jit(solution)/shard_map/ppermute | solution.py:155
  23.1 4.5 %all-to-all-done.data_ref = bf16[8,336,128]{2,1,0:T(8,128)(2,1)S(1)} async-done(((bf16[8,336,128]{2,1,0:T(8,128)(2,1)}), bf16[8,336,128]{2,1,0:T(8,128)(2,1)S(1)}, u32[]{:S(2)}, u32[]{:S(2)}) %all-to-all-start) | async-done | bytes 688160 | tf_op jit(solution)/shard_map/all_to_all | solution.py:102
  27.6 1.6 %self_attention.1 = bf16[8,112,128]{2,1,0:T(8,128)(2,1)S(1)} custom-call(bf16[8,336,128]{2,1,0:T(8,128)(2,1)S(1)} %all-to-all-done.data_ref), custom_call_target="tpu_custom_call" | custom-call | flops 411041792 | bytes 917504 | tf_op jit(solution)/shard_map/self_attention/pallas_call | solution.py:104
  29.1 0.0 copy-start
  29.1 12.2 %all_to_all.10.o_ref = bf16[8,112,128]{2,1,0:T(8,128)(2,1)S(1)} all-to-all(bf16[8,112,128]{2,1,0:T(8,128)(2,1)S(1)} %self_attention.1), channel_id=1, replica_groups=mesh['view'=4,'ctx'=8] {'ctx'}, dimensions={0} | all-to-all | bytes 458752 | tf_op jit(solution)/shard_map/all_to_all | solution.py:117
  41.3 0.0 copy-done
  41.3 1.7 %cross_view.1 = bf16[112,1024]{1,0:T(8,128)(2,1)} custom-call(bf16[8,112,128]{2,1,0:T(8,128)(2,1)S(1)} %all_to_all.10.o_ref, bf16[112,1024]{1,0:T(8,128)(2,1)S(1)} %bitcast.7, bf16[112,1024]{1,0:T(8,128)(2,1)S(1)} %bitcast.10, bf16[112,1024]{1,0:T(8,128)(2,1)S(1)} %collective-permute-done.refs_1_, bf16[112,1024]{1,0:T(8,128)(2,1)S(1)} %collective-permute-done.1.refs_2_, ...), custom_call_target="tpu_custom_call" | custom-call | tf_op jit(solution)/shard_map/cross_view/pallas_call | solution.py:169
Async XLA Ops:
  2.1 7.4 %copy-start.1 = (bf16[1,112,1024]{2,1,0:T(8,128)(2,1)S(1)}, bf16[1,112,1024]{2,1,0:T(8,128)(2,1)}, u32[]{:S(2)}) copy-start(bf16[1,112,1024]{2,1,0:T(8,128)(2,1)} %param.10) | copy-start | bytes 688132
  2.2 9.0 %copy-start.2 = (bf16[1,112,1024]{2,1,0:T(8,128)(2,1)S(1)}, bf16[1,112,1024]{2,1,0:T(8,128)(2,1)}, u32[]{:S(2)}) copy-start(bf16[1,112,1024]{2,1,0:T(8,128)(2,1)} %param.11) | copy-start | bytes 688132
  2.2 25.4 %all-to-all-start = ((bf16[8,336,128]{2,1,0:T(8,128)(2,1)}), bf16[8,336,128]{2,1,0:T(8,128)(2,1)S(1)}, u32[]{:S(2)}, u32[]{:S(2)}) async-start(bf16[8,336,128]{2,1,0:T(8,128)(2,1)} %pack_qkv.1), calls=%async_computation | async-start | bytes 1376256 | tf_op jit(solution)/shard_map/all_to_all | solution.py:102
  9.6 8.6 %collective-permute-start = (bf16[112,1024]{1,0:T(8,128)(2,1)S(1)}, bf16[112,1024]{1,0:T(8,128)(2,1)S(1)}, u32[]{:S(2)}, u32[]{:S(2)}) collective-permute-start(bf16[112,1024]{1,0:T(8,128)(2,1)S(1)} %bitcast.8), channel_id=1, source_target_pairs={{0,16},{8,24},{16,0},{24,8},{1,17},{9,25},{17,1},{25,9},{2,18},{10... | collective-permute-start | bytes 688136 | tf_op jit(solution)/shard_map/ppermute | solution.py:155
  11.2 10.5 %collective-permute-start.3 = (bf16[112,1024]{1,0:T(8,128)(2,1)S(1)}, bf16[112,1024]{1,0:T(8,128)(2,1)S(1)}, u32[]{:S(2)}, u32[]{:S(2)}) collective-permute-start(bf16[112,1024]{1,0:T(8,128)(2,1)S(1)} %bitcast.11), channel_id=1, source_target_pairs={{0,16},{8,24},{16,0},{24,8},{1,17},{9,25},{17,1},{25,9},{2,18},{10... | collective-permute-start | bytes 688136 | tf_op jit(solution)/shard_map/ppermute | solution.py:155
  11.7 10.0 %collective-permute-start.1 = (bf16[112,1024]{1,0:T(8,128)(2,1)S(1)}, bf16[112,1024]{1,0:T(8,128)(2,1)S(1)}, u32[]{:S(2)}, u32[]{:S(2)}) collective-permute-start(bf16[112,1024]{1,0:T(8,128)(2,1)S(1)} %bitcast.9), channel_id=1, source_target_pairs={{0,8},{8,0},{16,24},{24,16},{1,9},{9,1},{17,25},{25,17},{2,10},{10... | collective-permute-start | bytes 688136 | tf_op jit(solution)/shard_map/ppermute | solution.py:155
  11.7 10.0 %collective-permute-start.4 = (bf16[112,1024]{1,0:T(8,128)(2,1)S(1)}, bf16[112,1024]{1,0:T(8,128)(2,1)S(1)}, u32[]{:S(2)}, u32[]{:S(2)}) collective-permute-start(bf16[112,1024]{1,0:T(8,128)(2,1)S(1)} %bitcast.12), channel_id=1, source_target_pairs={{0,8},{8,0},{16,24},{24,16},{1,9},{9,1},{17,25},{25,17},{2,10},{10... | collective-permute-start | bytes 688136 | tf_op jit(solution)/shard_map/ppermute | solution.py:155
  18.2 3.5 %collective-permute-start.2 = (bf16[112,1024]{1,0:T(8,128)(2,1)S(1)}, bf16[112,1024]{1,0:T(8,128)(2,1)S(1)}, u32[]{:S(2)}, u32[]{:S(2)}) collective-permute-start(bf16[112,1024]{1,0:T(8,128)(2,1)S(1)} %collective-permute-done.refs_1_), channel_id=1, source_target_pairs={{0,8},{8,0},{16,24},{24,16},{1,9},{9,1},{17,25},{25,17},{2,10},{10... | collective-permute-start | bytes 688136 | tf_op jit(solution)/shard_map/ppermute | solution.py:155
  21.6 1.5 %collective-permute-start.5 = (bf16[112,1024]{1,0:T(8,128)(2,1)S(1)}, bf16[112,1024]{1,0:T(8,128)(2,1)S(1)}, u32[]{:S(2)}, u32[]{:S(2)}) collective-permute-start(bf16[112,1024]{1,0:T(8,128)(2,1)S(1)} %collective-permute-done.3.refs_5_), channel_id=1, source_target_pairs={{0,8},{8,0},{16,24},{24,16},{1,9},{9,1},{17,25},{25,17},{2,10},{10... | collective-permute-start | bytes 688136 | tf_op jit(solution)/shard_map/ppermute | solution.py:155
  29.1 12.2 %copy-start = (bf16[1,112,1024]{2,1,0:T(8,128)(2,1)S(1)}, bf16[1,112,1024]{2,1,0:T(8,128)(2,1)}, u32[]{:S(2)}) copy-start(bf16[1,112,1024]{2,1,0:T(8,128)(2,1)} %param.9) | copy-start | bytes 688132

commit v7 on v5

--- a/solution.py
+++ b/solution.py
@@ -15,8 +15,9 @@
 
 
 def pack_kernel(partners, q_ref, k_ref, v_ref, kc_ref, vc_ref, *refs):
-    block_refs, pair_ref, sems = refs[: len(partners)], refs[-2], refs[-1]
+    *far_refs, near_ref, pair_ref, sems = refs
     rows = q_ref.shape[0]
+    group = near_ref.shape[0]
     me = lax.axis_index("ctx")
     copies = []
 
@@ -25,12 +26,17 @@
         copy.start()
         copies.append(copy)
 
-    for partner, block_ref in zip(partners, block_refs):
-        lanes = pl.ds(pl.multiple_of((me ^ partner) * HEAD, HEAD), HEAD)
+    def pack(head, target):
+        lanes = pl.ds(pl.multiple_of(head * HEAD, HEAD), HEAD)
         for part, source in enumerate((q_ref, k_ref, v_ref)):
-            start(source.at[:, lanes], block_ref.at[pl.ds(part * rows, rows)])
+            start(source.at[:, lanes], target.at[pl.ds(part * rows, rows)])
+
+    for partner, far_ref in zip(partners, far_refs):
+        pack(me ^ partner, far_ref)
     for part, source in enumerate((kc_ref, vc_ref)):
         start(source, pair_ref.at[pl.ds(part * rows, rows)])
+    for member in range(group):
+        pack((me // group) * group + member, near_ref.at[member])
     for copy in copies:
         copy.wait()
 
@@ -46,16 +52,20 @@
     return (mixed[:, :HEAD] / mixed[:, HEAD:]).astype(jnp.bfloat16)
 
 
-def packed_attention_kernel(partners, rows, group, *refs):
-    *in_refs, out_ref = refs
+def packed_attention_kernel(partners, rows, *refs):
+    *far_refs, near_ref, out_ref = refs
+    group = near_ref.shape[0]
     me = lax.axis_index("ctx")
-    keys = jnp.concatenate([ref[rows : 2 * rows] for ref in in_refs], axis=0)
-    values = jnp.concatenate([ref[2 * rows : 3 * rows] for ref in in_refs], axis=0)
-    for first in range(0, len(in_refs), group):
-        query = jnp.concatenate([ref[0:rows] for ref in in_refs[first : first + group]], axis=0)
+    blocks = [(me ^ partner, ref) for partner, ref in zip(partners, far_refs)]
+    blocks += [((me // group) * group + i, near_ref.at[i]) for i in range(group)]
+    keys = jnp.concatenate([ref[rows : 2 * rows] for _, ref in blocks], axis=0)
+    values = jnp.concatenate([ref[2 * rows : 3 * rows] for _, ref in blocks], axis=0)
+    for first in range(0, len(blocks), 2):
+        chunk = blocks[first : first + 2]
+        query = jnp.concatenate([ref[0:rows] for _, ref in chunk], axis=0)
         mixed = attend(query, keys, values)
-        for i in range(group):
-            out_ref[me ^ partners[first + i]] = mixed[i * rows : (i + 1) * rows]
+        for i, (source, _) in enumerate(chunk):
+            out_ref[source] = mixed[i * rows : (i + 1) * rows]
 
 
 def attention_kernel(q_ref, k_ref, v_ref, out_ref):
@@ -106,28 +116,37 @@
 def split_attention(q, k, v, k_cross, v_cross, ctx_size):
     rows, width = q.shape
     heads = width // HEAD
-    partners = tuple(range(ctx_size - 1, -1, -1))
+    group = ctx_size // 2
+    partners = tuple(range(ctx_size - 1, group - 1, -1))
     vmem = pl.BlockSpec(memory_space=pltpu.VMEM)
     hbm = pl.BlockSpec(memory_space=pltpu.HBM)
     sources = [pltpu.with_memory_space_constraint(x, pltpu.HBM) for x in (q, k, v, k_cross, v_cross)]
-    block = jax.ShapeDtypeStruct((3 * rows, HEAD), q.dtype)
-    *blocks, pair = pl.pallas_call(
+    *far, near, pair = pl.pallas_call(
         functools.partial(pack_kernel, partners),
-        out_shape=[block] * heads + [jax.ShapeDtypeStruct((2 * rows, width), q.dtype)],
+        out_shape=[jax.ShapeDtypeStruct((3 * rows, HEAD), q.dtype)] * len(partners)
+        + [
+            jax.ShapeDtypeStruct((group, 3 * rows, HEAD), q.dtype),
+            jax.ShapeDtypeStruct((2 * rows, width), q.dtype),
+        ],
         in_specs=[hbm] * 5,
-        out_specs=[vmem] * (heads + 1),
+        out_specs=[vmem] * (len(partners) + 2),
         scratch_shapes=[pltpu.SemaphoreType.DMA((3 * heads + 2,))],
         compiler_params=kernel_params(),
         name="pack_qkv",
     )(*sources)
-    moved = [
-        swap(data, "ctx", ctx_size, partner) if partner else data
-        for partner, data in zip(partners, blocks)
-    ]
+    far = [swap(data, "ctx", ctx_size, partner) for partner, data in zip(partners, far)]
+    near = lax.all_to_all(
+        near,
+        "ctx",
+        split_axis=0,
+        concat_axis=0,
+        tiled=True,
+        axis_index_groups=[list(range(group)), list(range(group, ctx_size))],
+    )
     own = pl.pallas_call(
-        functools.partial(packed_attention_kernel, partners, rows, max(heads // 4, 1)),
+        functools.partial(packed_attention_kernel, partners, rows),
         out_shape=jax.ShapeDtypeStruct((heads, rows, HEAD), q.dtype),
-        in_specs=[vmem] * heads,
+        in_specs=[vmem] * (len(partners) + 1),
         out_specs=vmem,
         compiler_params=kernel_params(),
         cost_estimate=pl.CostEstimate(
@@ -136,9 +155,9 @@
             transcendentals=rows * rows * heads * heads,
         ),
         name="self_attention",
-    )(*moved)
+    )(*far, near)
     back = lax.all_to_all(own, "ctx", split_axis=0, concat_axis=0, tiled=True)
-    return back, pair, (pair, moved)
+    return back, pair, (pair, near)
 
 
 def shared_attention(q, k, v, ctx_size):

time: 44.3 us -> 43 us (0.971)
  starting transfers between devices: 21.7 us -> 15 us
  waiting for transfers between devices: 4.34 us -> 10.7 us
  blocking collectives: 13.2 us -> 11.4 us
  Pallas kernels: 4.85 us -> 5.48 us
    ppermute x10 -> x7, starting transfers between devices: 21.7 us -> 9.82 us  [swap(): lax.ppermute(array, axis_name, [(i, i ^ partner) for i in range(axis_size)])]
    ppermute x10 -> x7, waiting for transfers between devices: 4.34 us -> 10.7 us  [swap(): lax.ppermute(array, axis_name, [(i, i ^ partner) for i in range(axis_size)])]
    all_to_all x0 -> x1, starting transfers between devices: none -> 5.23 us  [split_attention(): lax.all_to_all(near, 'ctx', split_axis=0, concat_axis=0, tiled=True, axis...]
    all_to_all x1, blocking collectives: 13.2 us -> 11.4 us  [split_attention(): back = lax.all_to_all(own, 'ctx', split_axis=0, concat_axis=0, tiled=True)]
    pallas_call x2, Pallas kernels: 3.17 us -> 3.8 us  [the longest x1 2.24 us: split_attention(): pl.pallas_call(functools.partial(pack_kernel, partners), out_shape=[jax.S...]
  transfers between devices with their start and end apart: 10 -> 8, of which waited for: 4 -> 5; matrix products, arithmetic and copies ran while one was open for 0% -> 0% of each run, Pallas kernels for 4% -> 4%
where the time goes in v7:
time: 43 us; the launch traced here: 42.8 us
  starting transfers between devices  15 us (35%)
  blocking collectives  11.4 us (27%)
  waiting for transfers between devices  10.7 us (25%)
  Pallas kernels  5.48 us (13%)
    all_to_all x1, blocking collectives, split_attention(): back = lax.all_to_all(own, 'ctx', split_axis=0, concat_axis=0, tiled=True)  11.4 us
    ppermute x7, waiting for transfers between devices, swap(): lax.ppermute(array, axis_name, [(i, i ^ partner) for i in range(axis_size)])  10.7 us
    ppermute x7, starting transfers between devices, swap(): lax.ppermute(array, axis_name, [(i, i ^ partner) for i in range(axis_size)])  9.82 us
    all_to_all x1, starting transfers between devices, split_attention(): lax.all_to_all(near, 'ctx', split_axis=0, concat_axis=0, tiled=True, axis...  5.23 us
    pallas_call x1, Pallas kernels, split_attention(): pl.pallas_call(functools.partial(pack_kernel, partners), out_shape=[jax.S...  2.24 us
    pallas_call x1, Pallas kernels, body(): pl.pallas_call(functools.partial(cross_kernel, heads), out_shape=jax.Shap...  1.68 us
    pallas_call x1, Pallas kernels, split_attention(): pl.pallas_call(functools.partial(packed_attention_kernel, partners, rows)...  1.56 us
  transfers between devices with their start and end apart: 8, of which 5 were waited for; matrix products, arithmetic and copies ran while one was open for 0% of the time, Pallas kernels for 4%

profile of v7, /device:TPU:0, one launch (start us, length us, event | category | flops | bytes accessed | tf_op | source)
XLA Modules:
  0.0 42.8 jit_solution(15396945683106678463)
XLA Ops:
  0.0 2.2 %pack_qkv.1 = (bf16[336,128]{1,0:T(8,128)(2,1)S(1)}, bf16[336,128]{1,0:T(8,128)(2,1)S(1)}, bf16[336,128]{1,0:T(8,128)(2,1)S(1)}, bf16[336,128]{1,0:T(8,128)(2,1)...) custom-call(bf16[112,1024]{1,0:T(8,128)(2,1)} %bitcast.8, bf16[112,1024]{1,0:T(8,128)(2,1)} %bitcast.9, ...), custom_call_target="tpu_custom_call" | custom-call | tf_op jit(solution)/shard_map/pack_qkv/pallas_call | solution.py:124
  2.3 5.2 %all-to-all-start = ((bf16[4,336,128]{2,1,0:T(8,128)(2,1)}), bf16[4,336,128]{2,1,0:T(8,128)(2,1)S(1)}, u32[]{:S(2)}, u32[]{:S(2)}) async-start(bf16[4,336,128]{2,1,0:T(8,128)(2,1)} %get-tuple-element.17), calls=%async_computation | async-start | bytes 688128 | tf_op jit(solution)/shard_map/all_to_all | solution.py:138
  7.5 1.5 %collective-permute-start.4 = (bf16[224,1024]{1,0:T(8,128)(2,1)S(1)}, bf16[224,1024]{1,0:T(8,128)(2,1)S(1)}, u32[]{:S(2)}, u32[]{:S(2)}) collective-permute-start(bf16[224,1024]{1,0:T(8,128)(2,1)S(1)} %get-tuple-element.19.refs_0_), channel_id=1, source_target_pairs={{0,16},{8,24},{16,0},{24,8},{1,17},{9,25},{17,1},{25,9},{2,18},{10... | collective-permute-start | bytes 1376264 | tf_op jit(solution)/shard_map/ppermute | solution.py:103
  9.0 4.9 %collective-permute-start = (bf16[336,128]{1,0:T(8,128)(2,1)S(1)}, bf16[336,128]{1,0:T(8,128)(2,1)S(1)}, u32[]{:S(2)}, u32[]{:S(2)}) collective-permute-start(bf16[336,128]{1,0:T(8,128)(2,1)S(1)} %get-tuple-element.13), channel_id=1, source_target_pairs={{0,7},{1,6},{2,5},{3,4},{4,3},{5,2},{6,1},{7,0},{8,15},{9,14},{10,... | collective-permute-start | bytes 258056 | tf_op jit(solution)/shard_map/ppermute | solution.py:103
  14.0 0.3 collective-permute-start.1
  14.3 0.2 collective-permute-start.2
  14.5 2.4 %collective-permute-start.3 = (bf16[336,128]{1,0:T(8,128)(2,1)S(1)}, bf16[336,128]{1,0:T(8,128)(2,1)S(1)}, u32[]{:S(2)}, u32[]{:S(2)}) collective-permute-start(bf16[336,128]{1,0:T(8,128)(2,1)S(1)} %get-tuple-element.16), channel_id=1, source_target_pairs={{0,4},{1,5},{2,6},{3,7},{4,0},{5,1},{6,2},{7,3},{8,12},{9,13},{10,... | collective-permute-start | bytes 258056 | tf_op jit(solution)/shard_map/ppermute | solution.py:103
  16.9 2.6 %collective-permute-done.4.refs_1_ = bf16[224,1024]{1,0:T(8,128)(2,1)S(1)} collective-permute-done((bf16[224,1024]{1,0:T(8,128)(2,1)S(1)}, bf16[224,1024]{1,0:T(8,128)(2,1)S(1)}, u32[]{:S(2)}, u32[]{:S(2)}) %collective-permute-start.4) | collective-permute-done | bytes 458784 | tf_op jit(solution)/shard_map/ppermute | solution.py:103
  19.5 0.0 all-to-all-done.refs_4_
  19.5 0.0 collective-permute-start.5
  19.5 0.1 collective-permute-done.refs_0_
  19.6 0.4 collective-permute-start.6
  20.0 1.1 %collective-permute-done.1.refs_1_ = bf16[336,128]{1,0:T(8,128)(2,1)S(1)} collective-permute-done((bf16[336,128]{1,0:T(8,128)(2,1)S(1)}, bf16[336,128]{1,0:T(8,128)(2,1)S(1)}, u32[]{:S(2)}, u32[]{:S(2)}) %collective-permute-start.1) | collective-permute-done | bytes 86048 | tf_op jit(solution)/shard_map/ppermute | solution.py:103
  21.1 5.7 %collective-permute-done.2.refs_2_ = bf16[336,128]{1,0:T(8,128)(2,1)S(1)} collective-permute-done((bf16[336,128]{1,0:T(8,128)(2,1)S(1)}, bf16[336,128]{1,0:T(8,128)(2,1)S(1)}, u32[]{:S(2)}, u32[]{:S(2)}) %collective-permute-start.2) | collective-permute-done | bytes 86048 | tf_op jit(solution)/shard_map/ppermute | solution.py:103
  26.7 1.3 %collective-permute-done.3.refs_3_ = bf16[336,128]{1,0:T(8,128)(2,1)S(1)} collective-permute-done((bf16[336,128]{1,0:T(8,128)(2,1)S(1)}, bf16[336,128]{1,0:T(8,128)(2,1)S(1)}, u32[]{:S(2)}, u32[]{:S(2)}) %collective-permute-start.3) | collective-permute-done | bytes 86048 | tf_op jit(solution)/shard_map/ppermute | solution.py:103
  28.0 1.6 %self_attention.1 = bf16[8,112,128]{2,1,0:T(8,128)(2,1)S(1)} custom-call(bf16[336,128]{1,0:T(8,128)(2,1)S(1)} %collective-permute-done.refs_0_, bf16[336,128]{1,0:T(8,128)(2,1)S(1)} %collective-permute-done.1.refs_1_, bf16[336,128]{1,0:T(8,128)(2,1)S(1)} %collective-permute-done.2.refs_2_, bf16[336,128]{1,0:T(8,128)(2,1)S(1)} %collective-permute-done.3.refs_3_, ...), custom_call_target="tpu_custom_call" | custom-call | flops 411041792 | bytes 917504 | tf_op jit(solution)/shard_map/self_attention/pallas_call | solution.py:146
  29.6 0.0 copy-start
  29.6 11.4 %all_to_all.10.o_ref = bf16[8,112,128]{2,1,0:T(8,128)(2,1)S(1)} all-to-all(bf16[8,112,128]{2,1,0:T(8,128)(2,1)S(1)} %self_attention.1), channel_id=1, replica_groups=mesh['view'=4,'ctx'=8] {'ctx'}, dimensions={0} | all-to-all | bytes 458752 | tf_op jit(solution)/shard_map/all_to_all | solution.py:159
  41.1 0.0 collective-permute-done.5.refs_2_
  41.1 0.0 collective-permute-done.6.refs_3_
  41.1 0.0 copy-done
  41.1 1.7 %cross_view.1 = bf16[112,1024]{1,0:T(8,128)(2,1)} custom-call(bf16[8,112,128]{2,1,0:T(8,128)(2,1)S(1)} %all_to_all.10.o_ref, bf16[112,1024]{1,0:T(8,128)(2,1)S(1)} %bitcast.7, bf16[224,1024]{1,0:T(8,128)(2,1)S(1)} %get-tuple-element.19.refs_0_, bf16[224,1024]{1,0:T(8,128)(2,1)S(1)} %collective-permute-done.4.refs_1_, ...), custom_call_target="tpu_custom_call" | custom-call | tf_op jit(solution)/shard_map/cross_view/pallas_call | solution.py:210
Async XLA Ops:
  2.3 17.2 %all-to-all-start = ((bf16[4,336,128]{2,1,0:T(8,128)(2,1)}), bf16[4,336,128]{2,1,0:T(8,128)(2,1)S(1)}, u32[]{:S(2)}, u32[]{:S(2)}) async-start(bf16[4,336,128]{2,1,0:T(8,128)(2,1)} %get-tuple-element.17), calls=%async_computation | async-start | bytes 688128 | tf_op jit(solution)/shard_map/all_to_all | solution.py:138
  7.5 12.0 %collective-permute-start.4 = (bf16[224,1024]{1,0:T(8,128)(2,1)S(1)}, bf16[224,1024]{1,0:T(8,128)(2,1)S(1)}, u32[]{:S(2)}, u32[]{:S(2)}) collective-permute-start(bf16[224,1024]{1,0:T(8,128)(2,1)S(1)} %get-tuple-element.19.refs_0_), channel_id=1, source_target_pairs={{0,16},{8,24},{16,0},{24,8},{1,17},{9,25},{17,1},{25,9},{2,18},{10... | collective-permute-start | bytes 1376264 | tf_op jit(solution)/shard_map/ppermute | solution.py:103
  9.0 10.6 %collective-permute-start = (bf16[336,128]{1,0:T(8,128)(2,1)S(1)}, bf16[336,128]{1,0:T(8,128)(2,1)S(1)}, u32[]{:S(2)}, u32[]{:S(2)}) collective-permute-start(bf16[336,128]{1,0:T(8,128)(2,1)S(1)} %get-tuple-element.13), channel_id=1, source_target_pairs={{0,7},{1,6},{2,5},{3,4},{4,3},{5,2},{6,1},{7,0},{8,15},{9,14},{10,... | collective-permute-start | bytes 258056 | tf_op jit(solution)/shard_map/ppermute | solution.py:103
  14.0 7.1 %collective-permute-start.1 = (bf16[336,128]{1,0:T(8,128)(2,1)S(1)}, bf16[336,128]{1,0:T(8,128)(2,1)S(1)}, u32[]{:S(2)}, u32[]{:S(2)}) collective-permute-start(bf16[336,128]{1,0:T(8,128)(2,1)S(1)} %get-tuple-element.14), channel_id=1, source_target_pairs={{0,6},{1,7},{2,4},{3,5},{4,2},{5,3},{6,0},{7,1},{8,14},{9,15},{10,... | collective-permute-start | bytes 258056 | tf_op jit(solution)/shard_map/ppermute | solution.py:103
  14.3 12.4 %collective-permute-start.2 = (bf16[336,128]{1,0:T(8,128)(2,1)S(1)}, bf16[336,128]{1,0:T(8,128)(2,1)S(1)}, u32[]{:S(2)}, u32[]{:S(2)}) collective-permute-start(bf16[336,128]{1,0:T(8,128)(2,1)S(1)} %get-tuple-element.15), channel_id=1, source_target_pairs={{0,5},{1,4},{2,7},{3,6},{4,1},{5,0},{6,3},{7,2},{8,13},{9,12},{10,... | collective-permute-start | bytes 258056 | tf_op jit(solution)/shard_map/ppermute | solution.py:103
  14.5 13.5 %collective-permute-start.3 = (bf16[336,128]{1,0:T(8,128)(2,1)S(1)}, bf16[336,128]{1,0:T(8,128)(2,1)S(1)}, u32[]{:S(2)}, u32[]{:S(2)}) collective-permute-start(bf16[336,128]{1,0:T(8,128)(2,1)S(1)} %get-tuple-element.16), channel_id=1, source_target_pairs={{0,4},{1,5},{2,6},{3,7},{4,0},{5,1},{6,2},{7,3},{8,12},{9,13},{10,... | collective-permute-start | bytes 258056 | tf_op jit(solution)/shard_map/ppermute | solution.py:103
  19.5 21.6 %collective-permute-start.5 = (bf16[224,1024]{1,0:T(8,128)(2,1)S(1)}, bf16[224,1024]{1,0:T(8,128)(2,1)S(1)}, u32[]{:S(2)}, u32[]{:S(2)}) collective-permute-start(bf16[224,1024]{1,0:T(8,128)(2,1)S(1)} %get-tuple-element.19.refs_0_), channel_id=1, source_target_pairs={{0,8},{8,0},{16,24},{24,16},{1,9},{9,1},{17,25},{25,17},{2,10},{10... | collective-permute-start | bytes 1376264 | tf_op jit(solution)/shard_map/ppermute | solution.py:103
  19.6 21.5 %collective-permute-start.6 = (bf16[224,1024]{1,0:T(8,128)(2,1)S(1)}, bf16[224,1024]{1,0:T(8,128)(2,1)S(1)}, u32[]{:S(2)}, u32[]{:S(2)}) collective-permute-start(bf16[224,1024]{1,0:T(8,128)(2,1)S(1)} %collective-permute-done.4.refs_1_), channel_id=1, source_target_pairs={{0,8},{8,0},{16,24},{24,16},{1,9},{9,1},{17,25},{25,17},{2,10},{10... | collective-permute-start | bytes 1376264 | tf_op jit(solution)/shard_map/ppermute | solution.py:103
  29.6 11.5 %copy-start = (bf16[1,112,1024]{2,1,0:T(8,128)(2,1)S(1)}, bf16[1,112,1024]{2,1,0:T(8,128)(2,1)}, u32[]{:S(2)}) copy-start(bf16[1,112,1024]{2,1,0:T(8,128)(2,1)} %param.9) | copy-start | bytes 688132

commit v8 on v5

--- a/solution.py
+++ b/solution.py
@@ -106,7 +106,9 @@
 def split_attention(q, k, v, k_cross, v_cross, ctx_size):
     rows, width = q.shape
     heads = width // HEAD
-    partners = tuple(range(ctx_size - 1, -1, -1))
+    far = list(range(ctx_size - 1, ctx_size // 2 - 1, -1))
+    near = list(range(ctx_size // 2 - 1, -1, -1))
+    partners = tuple(far[:3] + near[:1] + far[3:] + near[1:])
     vmem = pl.BlockSpec(memory_space=pltpu.VMEM)
     hbm = pl.BlockSpec(memory_space=pltpu.HBM)
     sources = [pltpu.with_memory_space_constraint(x, pltpu.HBM) for x in (q, k, v, k_cross, v_cross)]

time: 44.3 us -> 43.3 us (0.977)
  blocking collectives: 13.2 us -> 12.3 us
  starting transfers between devices: 21.7 us -> 20.9 us
  waiting for transfers between devices: 4.34 us -> 5.06 us
    all_to_all x1, blocking collectives: 13.2 us -> 12.3 us  [split_attention(): back = lax.all_to_all(own, 'ctx', split_axis=0, concat_axis=0, tiled=True)]
    ppermute x10, starting transfers between devices: 21.7 us -> 20.9 us  [swap(): lax.ppermute(array, axis_name, [(i, i ^ partner) for i in range(axis_size)])]
    ppermute x10, waiting for transfers between devices: 4.34 us -> 5.06 us  [swap(): lax.ppermute(array, axis_name, [(i, i ^ partner) for i in range(axis_size)])]
  transfers between devices with their start and end apart: 10 -> 10, of which waited for: 4 -> 3; matrix products, arithmetic and copies ran while one was open for 0% -> 0% of each run, Pallas kernels for 4% -> 4%
where the time goes in v8:
time: 43.3 us; the launch traced here: 43.1 us
  starting transfers between devices  20.9 us (48%)
  blocking collectives  12.3 us (28%)
  waiting for transfers between devices  5.06 us (12%)
  Pallas kernels  4.85 us (11%)
    ppermute x10, starting transfers between devices, swap(): lax.ppermute(array, axis_name, [(i, i ^ partner) for i in range(axis_size)])  20.9 us
    all_to_all x1, blocking collectives, split_attention(): back = lax.all_to_all(own, 'ctx', split_axis=0, concat_axis=0, tiled=True)  12.3 us
    ppermute x10, waiting for transfers between devices, swap(): lax.ppermute(array, axis_name, [(i, i ^ partner) for i in range(axis_size)])  5.06 us
    pallas_call x1, Pallas kernels, body(): pl.pallas_call(functools.partial(cross_kernel, heads), out_shape=jax.Shap...  1.68 us
    pallas_call x1, Pallas kernels, split_attention(): pl.pallas_call(functools.partial(pack_kernel, partners), out_shape=[block...  1.61 us
    pallas_call x1, Pallas kernels, split_attention(): pl.pallas_call(functools.partial(packed_attention_kernel, partners, rows,...  1.56 us
  transfers between devices with their start and end apart: 10, of which 3 were waited for; matrix products, arithmetic and copies ran while one was open for 0% of the time, Pallas kernels for 4%

profile of v8, /device:TPU:0, one launch (start us, length us, event | category | flops | bytes accessed | tf_op | source)
XLA Modules:
  0.0 43.1 jit_solution(14061768408475308114)
XLA Ops:
  0.0 1.6 %pack_qkv.1 = (bf16[336,128]{1,0:T(8,128)(2,1)S(1)}, bf16[336,128]{1,0:T(8,128)(2,1)S(1)}, bf16[336,128]{1,0:T(8,128)(2,1)S(1)}, bf16[336,128]{1,0:T(8,128)(2,1)...) custom-call(bf16[112,1024]{1,0:T(8,128)(2,1)} %bitcast.8, ...), custom_call_target="tpu_custom_call" | custom-call | tf_op jit(solution)/shard_map/pack_qkv/pallas_call | solution.py:116
  1.6 3.0 %collective-permute-start.7 = (bf16[224,1024]{1,0:T(8,128)(2,1)S(1)}, bf16[224,1024]{1,0:T(8,128)(2,1)S(1)}, u32[]{:S(2)}, u32[]{:S(2)}) collective-permute-start(bf16[224,1024]{1,0:T(8,128)(2,1)S(1)} %get-tuple-element.25.refs_0_), channel_id=1, source_target_pairs={{0,16},{8,24},{16,0},{24,8},{1,17},{9,25},{17,1},{25,9},{2,18},{10... | collective-permute-start | bytes 1376264 | tf_op jit(solution)/shard_map/ppermute | solution.py:93
  4.7 4.5 %collective-permute-start = (bf16[336,128]{1,0:T(8,128)(2,1)S(1)}, bf16[336,128]{1,0:T(8,128)(2,1)S(1)}, u32[]{:S(2)}, u32[]{:S(2)}) collective-permute-start(bf16[336,128]{1,0:T(8,128)(2,1)S(1)} %get-tuple-element.16), channel_id=1, source_target_pairs={{0,7},{1,6},{2,5},{3,4},{4,3},{5,2},{6,1},{7,0},{8,15},{9,14},{10,... | collective-permute-start | bytes 258056 | tf_op jit(solution)/shard_map/ppermute | solution.py:93
  9.2 0.2 collective-permute-start.1
  9.4 0.8 %collective-permute-start.2 = (bf16[336,128]{1,0:T(8,128)(2,1)S(1)}, bf16[336,128]{1,0:T(8,128)(2,1)S(1)}, u32[]{:S(2)}, u32[]{:S(2)}) collective-permute-start(bf16[336,128]{1,0:T(8,128)(2,1)S(1)} %get-tuple-element.18), channel_id=1, source_target_pairs={{0,5},{1,4},{2,7},{3,6},{4,1},{5,0},{6,3},{7,2},{8,13},{9,12},{10,... | collective-permute-start | bytes 258056 | tf_op jit(solution)/shard_map/ppermute | solution.py:93
  10.2 4.3 %collective-permute-start.3 = (bf16[336,128]{1,0:T(8,128)(2,1)S(1)}, bf16[336,128]{1,0:T(8,128)(2,1)S(1)}, u32[]{:S(2)}, u32[]{:S(2)}) collective-permute-start(bf16[336,128]{1,0:T(8,128)(2,1)S(1)} %get-tuple-element.19), channel_id=1, source_target_pairs={{0,3},{1,2},{2,1},{3,0},{4,7},{5,6},{6,5},{7,4},{8,11},{9,10},{10,... | collective-permute-start | bytes 258056 | tf_op jit(solution)/shard_map/ppermute | solution.py:93
  14.5 0.0 collective-permute-done.refs_0_
  14.5 5.5 %collective-permute-start.4 = (bf16[336,128]{1,0:T(8,128)(2,1)S(1)}, bf16[336,128]{1,0:T(8,128)(2,1)S(1)}, u32[]{:S(2)}, u32[]{:S(2)}) collective-permute-start(bf16[336,128]{1,0:T(8,128)(2,1)S(1)} %get-tuple-element.20), channel_id=1, source_target_pairs={{0,4},{1,5},{2,6},{3,7},{4,0},{5,1},{6,2},{7,3},{8,12},{9,13},{10,... | collective-permute-start | bytes 258056 | tf_op jit(solution)/shard_map/ppermute | solution.py:93
  20.0 0.0 collective-permute-done.1.refs_1_
  20.0 0.4 collective-permute-start.5
  20.4 2.2 %collective-permute-done.2.refs_2_ = bf16[336,128]{1,0:T(8,128)(2,1)S(1)} collective-permute-done((bf16[336,128]{1,0:T(8,128)(2,1)S(1)}, bf16[336,128]{1,0:T(8,128)(2,1)S(1)}, u32[]{:S(2)}, u32[]{:S(2)}) %collective-permute-start.2) | collective-permute-done | bytes 86048 | tf_op jit(solution)/shard_map/ppermute | solution.py:93
  22.5 1.6 %collective-permute-start.6 = (bf16[336,128]{1,0:T(8,128)(2,1)S(1)}, bf16[336,128]{1,0:T(8,128)(2,1)S(1)}, u32[]{:S(2)}, u32[]{:S(2)}) collective-permute-start(bf16[336,128]{1,0:T(8,128)(2,1)S(1)} %get-tuple-element.22), channel_id=1, source_target_pairs={{0,1},{1,0},{2,3},{3,2},{4,5},{5,4},{6,7},{7,6},{8,9},{9,8},{10,11... | collective-permute-start | bytes 258056 | tf_op jit(solution)/shard_map/ppermute | solution.py:93
  24.1 0.0 collective-permute-done.3.refs_3_
  24.1 0.0 collective-permute-done.4.refs_4_
  24.1 0.4 collective-permute-done.5.refs_5_
  24.5 2.5 %collective-permute-done.6.refs_6_ = bf16[336,128]{1,0:T(8,128)(2,1)S(1)} collective-permute-done((bf16[336,128]{1,0:T(8,128)(2,1)S(1)}, bf16[336,128]{1,0:T(8,128)(2,1)S(1)}, u32[]{:S(2)}, u32[]{:S(2)}) %collective-permute-start.6) | collective-permute-done | bytes 86048 | tf_op jit(solution)/shard_map/ppermute | solution.py:93
  27.0 0.0 collective-permute-done.7.refs_1_
  27.0 0.0 collective-permute-start.8
  27.0 0.5 %collective-permute-start.9 = (bf16[224,1024]{1,0:T(8,128)(2,1)S(1)}, bf16[224,1024]{1,0:T(8,128)(2,1)S(1)}, u32[]{:S(2)}, u32[]{:S(2)}) collective-permute-start(bf16[224,1024]{1,0:T(8,128)(2,1)S(1)} %collective-permute-done.7.refs_1_), channel_id=1, source_target_pairs={{0,8},{8,0},{16,24},{24,16},{1,9},{9,1},{17,25},{25,17},{2,10},{10... | collective-permute-start | bytes 1376264 | tf_op jit(solution)/shard_map/ppermute | solution.py:93
  27.5 1.6 %self_attention.1 = bf16[8,112,128]{2,1,0:T(8,128)(2,1)S(1)} custom-call(bf16[336,128]{1,0:T(8,128)(2,1)S(1)} %collective-permute-done.refs_0_, bf16[336,128]{1,0:T(8,128)(2,1)S(1)} %collective-permute-done.1.refs_1_, bf16[336,128]{1,0:T(8,128)(2,1)S(1)} %collective-permute-done.2.refs_2_, bf16[336,128]{1,0:T(8,128)(2,1)S(1)} %collective-permute-done.3.refs_3_, ...), custom_call_target="tpu_custom_call" | custom-call | flops 411041792 | bytes 917504 | tf_op jit(solution)/shard_map/self_attention/pallas_call | solution.py:129
  29.1 0.0 copy-start
  29.1 12.3 %all_to_all.5.o_ref = bf16[8,112,128]{2,1,0:T(8,128)(2,1)S(1)} all-to-all(bf16[8,112,128]{2,1,0:T(8,128)(2,1)S(1)} %self_attention.1), channel_id=1, replica_groups=mesh['view'=4,'ctx'=8] {'ctx'}, dimensions={0} | all-to-all | bytes 458752 | tf_op jit(solution)/shard_map/all_to_all | solution.py:142
  41.4 0.0 collective-permute-done.8.refs_2_
  41.4 0.0 collective-permute-done.9.refs_3_
  41.4 0.0 copy-done
  41.4 1.7 %cross_view.1 = bf16[112,1024]{1,0:T(8,128)(2,1)} custom-call(bf16[8,112,128]{2,1,0:T(8,128)(2,1)S(1)} %all_to_all.5.o_ref, bf16[112,1024]{1,0:T(8,128)(2,1)S(1)} %bitcast.7, bf16[224,1024]{1,0:T(8,128)(2,1)S(1)} %get-tuple-element.25.refs_0_, bf16[224,1024]{1,0:T(8,128)(2,1)S(1)} %collective-permute-done.7.refs_1_, ...), custom_call_target="tpu_custom_call" | custom-call | tf_op jit(solution)/shard_map/cross_view/pallas_call | solution.py:193
Async XLA Ops:
  1.6 25.4 %collective-permute-start.7 = (bf16[224,1024]{1,0:T(8,128)(2,1)S(1)}, bf16[224,1024]{1,0:T(8,128)(2,1)S(1)}, u32[]{:S(2)}, u32[]{:S(2)}) collective-permute-start(bf16[224,1024]{1,0:T(8,128)(2,1)S(1)} %get-tuple-element.25.refs_0_), channel_id=1, source_target_pairs={{0,16},{8,24},{16,0},{24,8},{1,17},{9,25},{17,1},{25,9},{2,18},{10... | collective-permute-start | bytes 1376264 | tf_op jit(solution)/shard_map/ppermute | solution.py:93
  4.7 9.8 %collective-permute-start = (bf16[336,128]{1,0:T(8,128)(2,1)S(1)}, bf16[336,128]{1,0:T(8,128)(2,1)S(1)}, u32[]{:S(2)}, u32[]{:S(2)}) collective-permute-start(bf16[336,128]{1,0:T(8,128)(2,1)S(1)} %get-tuple-element.16), channel_id=1, source_target_pairs={{0,7},{1,6},{2,5},{3,4},{4,3},{5,2},{6,1},{7,0},{8,15},{9,14},{10,... | collective-permute-start | bytes 258056 | tf_op jit(solution)/shard_map/ppermute | solution.py:93
  9.2 10.8 %collective-permute-start.1 = (bf16[336,128]{1,0:T(8,128)(2,1)S(1)}, bf16[336,128]{1,0:T(8,128)(2,1)S(1)}, u32[]{:S(2)}, u32[]{:S(2)}) collective-permute-start(bf16[336,128]{1,0:T(8,128)(2,1)S(1)} %get-tuple-element.17), channel_id=1, source_target_pairs={{0,6},{1,7},{2,4},{3,5},{4,2},{5,3},{6,0},{7,1},{8,14},{9,15},{10,... | collective-permute-start | bytes 258056 | tf_op jit(solution)/shard_map/ppermute | solution.py:93
  9.4 13.1 %collective-permute-start.2 = (bf16[336,128]{1,0:T(8,128)(2,1)S(1)}, bf16[336,128]{1,0:T(8,128)(2,1)S(1)}, u32[]{:S(2)}, u32[]{:S(2)}) collective-permute-start(bf16[336,128]{1,0:T(8,128)(2,1)S(1)} %get-tuple-element.18), channel_id=1, source_target_pairs={{0,5},{1,4},{2,7},{3,6},{4,1},{5,0},{6,3},{7,2},{8,13},{9,12},{10,... | collective-permute-start | bytes 258056 | tf_op jit(solution)/shard_map/ppermute | solution.py:93
  10.2 14.0 %collective-permute-start.3 = (bf16[336,128]{1,0:T(8,128)(2,1)S(1)}, bf16[336,128]{1,0:T(8,128)(2,1)S(1)}, u32[]{:S(2)}, u32[]{:S(2)}) collective-permute-start(bf16[336,128]{1,0:T(8,128)(2,1)S(1)} %get-tuple-element.19), channel_id=1, source_target_pairs={{0,3},{1,2},{2,1},{3,0},{4,7},{5,6},{6,5},{7,4},{8,11},{9,10},{10,... | collective-permute-start | bytes 258056 | tf_op jit(solution)/shard_map/ppermute | solution.py:93
  14.5 9.7 %collective-permute-start.4 = (bf16[336,128]{1,0:T(8,128)(2,1)S(1)}, bf16[336,128]{1,0:T(8,128)(2,1)S(1)}, u32[]{:S(2)}, u32[]{:S(2)}) collective-permute-start(bf16[336,128]{1,0:T(8,128)(2,1)S(1)} %get-tuple-element.20), channel_id=1, source_target_pairs={{0,4},{1,5},{2,6},{3,7},{4,0},{5,1},{6,2},{7,3},{8,12},{9,13},{10,... | collective-permute-start | bytes 258056 | tf_op jit(solution)/shard_map/ppermute | solution.py:93
  20.0 4.5 %collective-permute-start.5 = (bf16[336,128]{1,0:T(8,128)(2,1)S(1)}, bf16[336,128]{1,0:T(8,128)(2,1)S(1)}, u32[]{:S(2)}, u32[]{:S(2)}) collective-permute-start(bf16[336,128]{1,0:T(8,128)(2,1)S(1)} %get-tuple-element.21), channel_id=1, source_target_pairs={{0,2},{1,3},{2,0},{3,1},{4,6},{5,7},{6,4},{7,5},{8,10},{9,11},{10,... | collective-permute-start | bytes 258056 | tf_op jit(solution)/shard_map/ppermute | solution.py:93
  22.5 4.5 %collective-permute-start.6 = (bf16[336,128]{1,0:T(8,128)(2,1)S(1)}, bf16[336,128]{1,0:T(8,128)(2,1)S(1)}, u32[]{:S(2)}, u32[]{:S(2)}) collective-permute-start(bf16[336,128]{1,0:T(8,128)(2,1)S(1)} %get-tuple-element.22), channel_id=1, source_target_pairs={{0,1},{1,0},{2,3},{3,2},{4,5},{5,4},{6,7},{7,6},{8,9},{9,8},{10,11... | collective-permute-start | bytes 258056 | tf_op jit(solution)/shard_map/ppermute | solution.py:93
  27.0 14.4 %collective-permute-start.8 = (bf16[224,1024]{1,0:T(8,128)(2,1)S(1)}, bf16[224,1024]{1,0:T(8,128)(2,1)S(1)}, u32[]{:S(2)}, u32[]{:S(2)}) collective-permute-start(bf16[224,1024]{1,0:T(8,128)(2,1)S(1)} %get-tuple-element.25.refs_0_), channel_id=1, source_target_pairs={{0,8},{8,0},{16,24},{24,16},{1,9},{9,1},{17,25},{25,17},{2,10},{10... | collective-permute-start | bytes 1376264 | tf_op jit(solution)/shard_map/ppermute | solution.py:93
  27.0 14.4 %collective-permute-start.9 = (bf16[224,1024]{1,0:T(8,128)(2,1)S(1)}, bf16[224,1024]{1,0:T(8,128)(2,1)S(1)}, u32[]{:S(2)}, u32[]{:S(2)}) collective-permute-start(bf16[224,1024]{1,0:T(8,128)(2,1)S(1)} %collective-permute-done.7.refs_1_), channel_id=1, source_target_pairs={{0,8},{8,0},{16,24},{24,16},{1,9},{9,1},{17,25},{25,17},{2,10},{10... | collective-permute-start | bytes 1376264 | tf_op jit(solution)/shard_map/ppermute | solution.py:93
  29.1 12.3 %copy-start = (bf16[1,112,1024]{2,1,0:T(8,128)(2,1)S(1)}, bf16[1,112,1024]{2,1,0:T(8,128)(2,1)}, u32[]{:S(2)}) copy-start(bf16[1,112,1024]{2,1,0:T(8,128)(2,1)} %param.9) | copy-start | bytes 688132

commit v9 on v5

--- a/solution.py
+++ b/solution.py
@@ -14,8 +14,8 @@
 MIB = 1024 * 1024
 
 
-def pack_kernel(partners, q_ref, k_ref, v_ref, kc_ref, vc_ref, *refs):
-    block_refs, pair_ref, sems = refs[: len(partners)], refs[-2], refs[-1]
+def pack_kernel(far, q_ref, k_ref, v_ref, kc_ref, vc_ref, *refs):
+    *far_refs, across_ref, along_ref, own_ref, pair_ref, sems = refs
     rows = q_ref.shape[0]
     me = lax.axis_index("ctx")
     copies = []
@@ -25,10 +25,12 @@
         copy.start()
         copies.append(copy)
 
-    for partner, block_ref in zip(partners, block_refs):
+    blocks = list(zip(far, far_refs))
+    blocks += [(1, across_ref.at[0]), (3, across_ref.at[1]), (2, along_ref), (0, own_ref)]
+    for partner, target in blocks:
         lanes = pl.ds(pl.multiple_of((me ^ partner) * HEAD, HEAD), HEAD)
         for part, source in enumerate((q_ref, k_ref, v_ref)):
-            start(source.at[:, lanes], block_ref.at[pl.ds(part * rows, rows)])
+            start(source.at[:, lanes], target.at[pl.ds(part * rows, rows)])
     for part, source in enumerate((kc_ref, vc_ref)):
         start(source, pair_ref.at[pl.ds(part * rows, rows)])
     for copy in copies:
@@ -46,16 +48,19 @@
     return (mixed[:, :HEAD] / mixed[:, HEAD:]).astype(jnp.bfloat16)
 
 
-def packed_attention_kernel(partners, rows, group, *refs):
-    *in_refs, out_ref = refs
+def packed_attention_kernel(far, rows, *refs):
+    *far_refs, across_ref, along_ref, own_ref, out_ref = refs
     me = lax.axis_index("ctx")
-    keys = jnp.concatenate([ref[rows : 2 * rows] for ref in in_refs], axis=0)
-    values = jnp.concatenate([ref[2 * rows : 3 * rows] for ref in in_refs], axis=0)
-    for first in range(0, len(in_refs), group):
-        query = jnp.concatenate([ref[0:rows] for ref in in_refs[first : first + group]], axis=0)
+    blocks = list(zip(far, far_refs))
+    blocks += [(0, own_ref), (1, across_ref.at[0]), (2, along_ref.at[0]), (3, along_ref.at[1])]
+    keys = jnp.concatenate([ref[rows : 2 * rows] for _, ref in blocks], axis=0)
+    values = jnp.concatenate([ref[2 * rows : 3 * rows] for _, ref in blocks], axis=0)
+    for first in range(0, len(blocks), 2):
+        chunk = blocks[first : first + 2]
+        query = jnp.concatenate([ref[0:rows] for _, ref in chunk], axis=0)
         mixed = attend(query, keys, values)
-        for i in range(group):
-            out_ref[me ^ partners[first + i]] = mixed[i * rows : (i + 1) * rows]
+        for i, (partner, _) in enumerate(chunk):
+            out_ref[me ^ partner] = mixed[i * rows : (i + 1) * rows]
 
 
 def attention_kernel(q_ref, k_ref, v_ref, out_ref):
@@ -106,28 +111,30 @@
 def split_attention(q, k, v, k_cross, v_cross, ctx_size):
     rows, width = q.shape
     heads = width // HEAD
-    partners = tuple(range(ctx_size - 1, -1, -1))
+    far = (7, 6, 5, 4)
     vmem = pl.BlockSpec(memory_space=pltpu.VMEM)
     hbm = pl.BlockSpec(memory_space=pltpu.HBM)
     sources = [pltpu.with_memory_space_constraint(x, pltpu.HBM) for x in (q, k, v, k_cross, v_cross)]
     block = jax.ShapeDtypeStruct((3 * rows, HEAD), q.dtype)
-    *blocks, pair = pl.pallas_call(
-        functools.partial(pack_kernel, partners),
-        out_shape=[block] * heads + [jax.ShapeDtypeStruct((2 * rows, width), q.dtype)],
+    two_blocks = jax.ShapeDtypeStruct((2, 3 * rows, HEAD), q.dtype)
+    *far_blocks, across, along, own, pair = pl.pallas_call(
+        functools.partial(pack_kernel, far),
+        out_shape=[block] * len(far)
+        + [two_blocks, block, block, jax.ShapeDtypeStruct((2 * rows, width), q.dtype)],
         in_specs=[hbm] * 5,
-        out_specs=[vmem] * (heads + 1),
+        out_specs=[vmem] * (len(far) + 4),
         scratch_shapes=[pltpu.SemaphoreType.DMA((3 * heads + 2,))],
         compiler_params=kernel_params(),
         name="pack_qkv",
     )(*sources)
-    moved = [
-        swap(data, "ctx", ctx_size, partner) if partner else data
-        for partner, data in zip(partners, blocks)
-    ]
-    own = pl.pallas_call(
-        functools.partial(packed_attention_kernel, partners, rows, max(heads // 4, 1)),
+    across = swap(across, "ctx", ctx_size, 1)
+    moved = [swap(data, "ctx", ctx_size, partner) for partner, data in zip(far, far_blocks)]
+    along = swap(jnp.stack([along, across[1]]), "ctx", ctx_size, 2)
+    moved += [across, along, own]
+    own_heads = pl.pallas_call(
+        functools.partial(packed_attention_kernel, far, rows),
         out_shape=jax.ShapeDtypeStruct((heads, rows, HEAD), q.dtype),
-        in_specs=[vmem] * heads,
+        in_specs=[vmem] * len(moved),
         out_specs=vmem,
         compiler_params=kernel_params(),
         cost_estimate=pl.CostEstimate(
@@ -137,7 +144,7 @@
         ),
         name="self_attention",
     )(*moved)
-    back = lax.all_to_all(own, "ctx", split_axis=0, concat_axis=0, tiled=True)
+    back = lax.all_to_all(own_heads, "ctx", split_axis=0, concat_axis=0, tiled=True)
     return back, pair, (pair, moved)
 
 
@@ -178,7 +185,7 @@
 def body(view_count, ctx_size, q_self, k_self, v_self, q_cross, k_cross, v_cross):
     _, rows, width = q_self.shape
     heads = width // HEAD
-    if ctx_size == heads:
+    if ctx_size == heads == 8:
         o_self, pair, after = split_attention(
             q_self[0], k_self[0], v_self[0], k_cross[0], v_cross[0], ctx_size
         )

time: 44.3 us -> 42.1 us (0.950)
  starting transfers between devices: 21.7 us -> 17.4 us
  waiting for transfers between devices: 4.34 us -> 6.93 us
  blocking collectives: 13.2 us -> 12.6 us
    ppermute x10 -> x9, starting transfers between devices: 21.7 us -> 17.4 us  [swap(): lax.ppermute(array, axis_name, [(i, i ^ partner) for i in range(axis_size)])]
    ppermute x10 -> x9, waiting for transfers between devices: 4.34 us -> 6.93 us  [swap(): lax.ppermute(array, axis_name, [(i, i ^ partner) for i in range(axis_size)])]
    all_to_all x1, blocking collectives: 13.2 us -> 12.6 us  [split_attention(): lax.all_to_all(own_heads, 'ctx', split_axis=0, concat_axis=0, tiled=True)]
  transfers between devices with their start and end apart: 10 -> 9, of which waited for: 4 -> 2; matrix products, arithmetic and copies ran while one was open for 0% -> 0% of each run, Pallas kernels for 4% -> 4%
where the time goes in v9:
time: 42.1 us; the launch traced here: 41.9 us
  starting transfers between devices  17.4 us (41%)
  blocking collectives  12.6 us (30%)
  waiting for transfers between devices  6.93 us (16%)
  Pallas kernels  4.88 us (12%)
    ppermute x9, starting transfers between devices, swap(): lax.ppermute(array, axis_name, [(i, i ^ partner) for i in range(axis_size)])  17.4 us
    all_to_all x1, blocking collectives, split_attention(): lax.all_to_all(own_heads, 'ctx', split_axis=0, concat_axis=0, tiled=True)  12.6 us
    ppermute x9, waiting for transfers between devices, swap(): lax.ppermute(array, axis_name, [(i, i ^ partner) for i in range(axis_size)])  6.93 us
    pallas_call x1, Pallas kernels, body(): pl.pallas_call(functools.partial(cross_kernel, heads), out_shape=jax.Shap...  1.69 us
    pallas_call x1, Pallas kernels, split_attention(): pl.pallas_call(functools.partial(pack_kernel, far), out_shape=[block] * l...  1.61 us
    pallas_call x1, Pallas kernels, split_attention(): pl.pallas_call(functools.partial(packed_attention_kernel, far, rows), out...  1.57 us
  transfers between devices with their start and end apart: 9, of which 2 were waited for; matrix products, arithmetic and copies ran while one was open for 0% of the time, Pallas kernels for 4%

profile of v9, /device:TPU:0, one launch (start us, length us, event | category | flops | bytes accessed | tf_op | source)
XLA Modules:
  0.0 41.9 jit_solution(10913523240907827469)
XLA Ops:
  0.0 1.6 %pack_qkv.1 = (bf16[336,128]{1,0:T(8,128)(2,1)S(1)}, bf16[336,128]{1,0:T(8,128)(2,1)S(1)}, bf16[336,128]{1,0:T(8,128)(2,1)S(1)}, bf16[336,128]{1,0:T(8,128)(2,1)...) custom-call(bf16[112,1024]{1,0:T(8,128)(2,1)} %bitcast.10, ...), custom_call_target="tpu_custom_call" | custom-call | tf_op jit(solution)/shard_map/pack_qkv/pallas_call | solution.py:120
  1.6 3.0 %collective-permute-start.4 = (bf16[2,336,128]{2,1,0:T(8,128)(2,1)S(1)}, bf16[2,336,128]{2,1,0:T(8,128)(2,1)S(1)}, u32[]{:S(2)}, u32[]{:S(2)}) collective-permute-start(bf16[2,336,128]{2,1,0:T(8,128)(2,1)S(1)} %get-tuple-element.19), channel_id=1, source_target_pairs={{0,1},{1,0},{2,3},{3,2},{4,5},{5,4},{6,7},{7,6},{8,9},{9,8},{10,11... | collective-permute-start | bytes 516104 | tf_op jit(solution)/shard_map/ppermute | solution.py:98
  4.6 1.5 %collective-permute-start.6 = (bf16[224,1024]{1,0:T(8,128)(2,1)S(1)}, bf16[224,1024]{1,0:T(8,128)(2,1)S(1)}, u32[]{:S(2)}, u32[]{:S(2)}) collective-permute-start(bf16[224,1024]{1,0:T(8,128)(2,1)S(1)} %get-tuple-element.23.refs_0_), channel_id=1, source_target_pairs={{0,16},{8,24},{16,0},{24,8},{1,17},{9,25},{17,1},{25,9},{2,18},{10... | collective-permute-start | bytes 1376264 | tf_op jit(solution)/shard_map/ppermute | solution.py:98
  6.1 3.6 %collective-permute-start = (bf16[336,128]{1,0:T(8,128)(2,1)S(1)}, bf16[336,128]{1,0:T(8,128)(2,1)S(1)}, u32[]{:S(2)}, u32[]{:S(2)}) collective-permute-start(bf16[336,128]{1,0:T(8,128)(2,1)S(1)} %get-tuple-element.15), channel_id=1, source_target_pairs={{0,7},{1,6},{2,5},{3,4},{4,3},{5,2},{6,1},{7,0},{8,15},{9,14},{10,... | collective-permute-start | bytes 258056 | tf_op jit(solution)/shard_map/ppermute | solution.py:98
  9.7 0.0 collective-permute-done.4.refs_4_
  9.8 2.1 %collective-permute-start.5 = (bf16[2,336,128]{2,1,0:T(8,128)(2,1)S(1)}, bf16[2,336,128]{2,1,0:T(8,128)(2,1)S(1)}, u32[]{:S(2)}, u32[]{:S(2)}) collective-permute-start(bf16[2,336,128]{2,1,0:T(8,128)(2,1)S(1)} %pad_maximum_fusion), channel_id=1, source_target_pairs={{0,2},{1,3},{2,0},{3,1},{4,6},{5,7},{6,4},{7,5},{8,10},{9,11},{10,... | collective-permute-start | bytes 516104 | tf_op jit(solution)/shard_map/ppermute | solution.py:98
  11.8 2.5 %collective-permute-start.1 = (bf16[336,128]{1,0:T(8,128)(2,1)S(1)}, bf16[336,128]{1,0:T(8,128)(2,1)S(1)}, u32[]{:S(2)}, u32[]{:S(2)}) collective-permute-start(bf16[336,128]{1,0:T(8,128)(2,1)S(1)} %get-tuple-element.16), channel_id=1, source_target_pairs={{0,6},{1,7},{2,4},{3,5},{4,2},{5,3},{6,0},{7,1},{8,14},{9,15},{10,... | collective-permute-start | bytes 258056 | tf_op jit(solution)/shard_map/ppermute | solution.py:98
  14.3 0.7 %collective-permute-start.2 = (bf16[336,128]{1,0:T(8,128)(2,1)S(1)}, bf16[336,128]{1,0:T(8,128)(2,1)S(1)}, u32[]{:S(2)}, u32[]{:S(2)}) collective-permute-start(bf16[336,128]{1,0:T(8,128)(2,1)S(1)} %get-tuple-element.17), channel_id=1, source_target_pairs={{0,5},{1,4},{2,7},{3,6},{4,1},{5,0},{6,3},{7,2},{8,13},{9,12},{10,... | collective-permute-start | bytes 258056 | tf_op jit(solution)/shard_map/ppermute | solution.py:98
  15.0 0.0 collective-permute-done.refs_0_
  15.1 3.4 %collective-permute-start.3 = (bf16[336,128]{1,0:T(8,128)(2,1)S(1)}, bf16[336,128]{1,0:T(8,128)(2,1)S(1)}, u32[]{:S(2)}, u32[]{:S(2)}) collective-permute-start(bf16[336,128]{1,0:T(8,128)(2,1)S(1)} %get-tuple-element.18), channel_id=1, source_target_pairs={{0,4},{1,5},{2,6},{3,7},{4,0},{5,1},{6,2},{7,3},{8,12},{9,13},{10,... | collective-permute-start | bytes 258056 | tf_op jit(solution)/shard_map/ppermute | solution.py:98
  18.5 2.0 %collective-permute-done.1.refs_1_ = bf16[336,128]{1,0:T(8,128)(2,1)S(1)} collective-permute-done((bf16[336,128]{1,0:T(8,128)(2,1)S(1)}, bf16[336,128]{1,0:T(8,128)(2,1)S(1)}, u32[]{:S(2)}, u32[]{:S(2)}) %collective-permute-start.1) | collective-permute-done | bytes 86048 | tf_op jit(solution)/shard_map/ppermute | solution.py:98
  20.5 4.9 %collective-permute-done.2.refs_2_ = bf16[336,128]{1,0:T(8,128)(2,1)S(1)} collective-permute-done((bf16[336,128]{1,0:T(8,128)(2,1)S(1)}, bf16[336,128]{1,0:T(8,128)(2,1)S(1)}, u32[]{:S(2)}, u32[]{:S(2)}) %collective-permute-start.2) | collective-permute-done | bytes 86048 | tf_op jit(solution)/shard_map/ppermute | solution.py:98
  25.4 0.0 collective-permute-done.3.refs_3_
  25.4 0.0 collective-permute-done.5.refs_5_
  25.4 0.0 collective-permute-done.6.refs_1_
  25.4 0.1 collective-permute-start.7
  25.5 0.5 %collective-permute-start.8 = (bf16[224,1024]{1,0:T(8,128)(2,1)S(1)}, bf16[224,1024]{1,0:T(8,128)(2,1)S(1)}, u32[]{:S(2)}, u32[]{:S(2)}) collective-permute-start(bf16[224,1024]{1,0:T(8,128)(2,1)S(1)} %collective-permute-done.6.refs_1_), channel_id=1, source_target_pairs={{0,8},{8,0},{16,24},{24,16},{1,9},{9,1},{17,25},{25,17},{2,10},{10... | collective-permute-start | bytes 1376264 | tf_op jit(solution)/shard_map/ppermute | solution.py:98
  26.0 1.6 %self_attention.1 = bf16[8,112,128]{2,1,0:T(8,128)(2,1)S(1)} custom-call(bf16[336,128]{1,0:T(8,128)(2,1)S(1)} %collective-permute-done.refs_0_, bf16[336,128]{1,0:T(8,128)(2,1)S(1)} %collective-permute-done.1.refs_1_, bf16[336,128]{1,0:T(8,128)(2,1)S(1)} %collective-permute-done.2.refs_2_, bf16[336,128]{1,0:T(8,128)(2,1)S(1)} %collective-permute-done.3.refs_3_, ...), custom_call_target="tpu_custom_call" | custom-call | flops 411041792 | bytes 917504 | tf_op jit(solution)/shard_map/self_attention/pallas_call | solution.py:134
  27.6 0.0 copy-start
  27.6 12.6 %all_to_all.5.o_ref = bf16[8,112,128]{2,1,0:T(8,128)(2,1)S(1)} all-to-all(bf16[8,112,128]{2,1,0:T(8,128)(2,1)S(1)} %self_attention.1), channel_id=1, replica_groups=mesh['view'=4,'ctx'=8] {'ctx'}, dimensions={0} | all-to-all | bytes 458752 | tf_op jit(solution)/shard_map/all_to_all | solution.py:147
  40.2 0.0 collective-permute-done.7.refs_2_
  40.2 0.0 collective-permute-done.8.refs_3_
  40.2 0.0 copy-done
  40.2 1.7 %cross_view.1 = bf16[112,1024]{1,0:T(8,128)(2,1)} custom-call(bf16[8,112,128]{2,1,0:T(8,128)(2,1)S(1)} %all_to_all.5.o_ref, bf16[112,1024]{1,0:T(8,128)(2,1)S(1)} %bitcast.8, bf16[224,1024]{1,0:T(8,128)(2,1)S(1)} %get-tuple-element.23.refs_0_, bf16[224,1024]{1,0:T(8,128)(2,1)S(1)} %collective-permute-done.6.refs_1_, ...), custom_call_target="tpu_custom_call" | custom-call | tf_op jit(solution)/shard_map/cross_view/pallas_call | solution.py:198
  (2 shorter events, 0.0 us)
Async XLA Ops:
  1.6 8.1 %collective-permute-start.4 = (bf16[2,336,128]{2,1,0:T(8,128)(2,1)S(1)}, bf16[2,336,128]{2,1,0:T(8,128)(2,1)S(1)}, u32[]{:S(2)}, u32[]{:S(2)}) collective-permute-start(bf16[2,336,128]{2,1,0:T(8,128)(2,1)S(1)} %get-tuple-element.19), channel_id=1, source_target_pairs={{0,1},{1,0},{2,3},{3,2},{4,5},{5,4},{6,7},{7,6},{8,9},{9,8},{10,11... | collective-permute-start | bytes 516104 | tf_op jit(solution)/shard_map/ppermute | solution.py:98
  4.6 20.8 %collective-permute-start.6 = (bf16[224,1024]{1,0:T(8,128)(2,1)S(1)}, bf16[224,1024]{1,0:T(8,128)(2,1)S(1)}, u32[]{:S(2)}, u32[]{:S(2)}) collective-permute-start(bf16[224,1024]{1,0:T(8,128)(2,1)S(1)} %get-tuple-element.23.refs_0_), channel_id=1, source_target_pairs={{0,16},{8,24},{16,0},{24,8},{1,17},{9,25},{17,1},{25,9},{2,18},{10... | collective-permute-start | bytes 1376264 | tf_op jit(solution)/shard_map/ppermute | solution.py:98
  6.1 8.9 %collective-permute-start = (bf16[336,128]{1,0:T(8,128)(2,1)S(1)}, bf16[336,128]{1,0:T(8,128)(2,1)S(1)}, u32[]{:S(2)}, u32[]{:S(2)}) collective-permute-start(bf16[336,128]{1,0:T(8,128)(2,1)S(1)} %get-tuple-element.15), channel_id=1, source_target_pairs={{0,7},{1,6},{2,5},{3,4},{4,3},{5,2},{6,1},{7,0},{8,15},{9,14},{10,... | collective-permute-start | bytes 258056 | tf_op jit(solution)/shard_map/ppermute | solution.py:98
  9.8 15.7 %collective-permute-start.5 = (bf16[2,336,128]{2,1,0:T(8,128)(2,1)S(1)}, bf16[2,336,128]{2,1,0:T(8,128)(2,1)S(1)}, u32[]{:S(2)}, u32[]{:S(2)}) collective-permute-start(bf16[2,336,128]{2,1,0:T(8,128)(2,1)S(1)} %pad_maximum_fusion), channel_id=1, source_target_pairs={{0,2},{1,3},{2,0},{3,1},{4,6},{5,7},{6,4},{7,5},{8,10},{9,11},{10,... | collective-permute-start | bytes 516104 | tf_op jit(solution)/shard_map/ppermute | solution.py:98
  11.8 8.7 %collective-permute-start.1 = (bf16[336,128]{1,0:T(8,128)(2,1)S(1)}, bf16[336,128]{1,0:T(8,128)(2,1)S(1)}, u32[]{:S(2)}, u32[]{:S(2)}) collective-permute-start(bf16[336,128]{1,0:T(8,128)(2,1)S(1)} %get-tuple-element.16), channel_id=1, source_target_pairs={{0,6},{1,7},{2,4},{3,5},{4,2},{5,3},{6,0},{7,1},{8,14},{9,15},{10,... | collective-permute-start | bytes 258056 | tf_op jit(solution)/shard_map/ppermute | solution.py:98
  14.3 11.1 %collective-permute-start.2 = (bf16[336,128]{1,0:T(8,128)(2,1)S(1)}, bf16[336,128]{1,0:T(8,128)(2,1)S(1)}, u32[]{:S(2)}, u32[]{:S(2)}) collective-permute-start(bf16[336,128]{1,0:T(8,128)(2,1)S(1)} %get-tuple-element.17), channel_id=1, source_target_pairs={{0,5},{1,4},{2,7},{3,6},{4,1},{5,0},{6,3},{7,2},{8,13},{9,12},{10,... | collective-permute-start | bytes 258056 | tf_op jit(solution)/shard_map/ppermute | solution.py:98
  15.1 10.4 %collective-permute-start.3 = (bf16[336,128]{1,0:T(8,128)(2,1)S(1)}, bf16[336,128]{1,0:T(8,128)(2,1)S(1)}, u32[]{:S(2)}, u32[]{:S(2)}) collective-permute-start(bf16[336,128]{1,0:T(8,128)(2,1)S(1)} %get-tuple-element.18), channel_id=1, source_target_pairs={{0,4},{1,5},{2,6},{3,7},{4,0},{5,1},{6,2},{7,3},{8,12},{9,13},{10,... | collective-permute-start | bytes 258056 | tf_op jit(solution)/shard_map/ppermute | solution.py:98
  25.4 14.8 %collective-permute-start.7 = (bf16[224,1024]{1,0:T(8,128)(2,1)S(1)}, bf16[224,1024]{1,0:T(8,128)(2,1)S(1)}, u32[]{:S(2)}, u32[]{:S(2)}) collective-permute-start(bf16[224,1024]{1,0:T(8,128)(2,1)S(1)} %get-tuple-element.23.refs_0_), channel_id=1, source_target_pairs={{0,8},{8,0},{16,24},{24,16},{1,9},{9,1},{17,25},{25,17},{2,10},{10... | collective-permute-start | bytes 1376264 | tf_op jit(solution)/shard_map/ppermute | solution.py:98
  25.5 14.7 %collective-permute-start.8 = (bf16[224,1024]{1,0:T(8,128)(2,1)S(1)}, bf16[224,1024]{1,0:T(8,128)(2,1)S(1)}, u32[]{:S(2)}, u32[]{:S(2)}) collective-permute-start(bf16[224,1024]{1,0:T(8,128)(2,1)S(1)} %collective-permute-done.6.refs_1_), channel_id=1, source_target_pairs={{0,8},{8,0},{16,24},{24,16},{1,9},{9,1},{17,25},{25,17},{2,10},{10... | collective-permute-start | bytes 1376264 | tf_op jit(solution)/shard_map/ppermute | solution.py:98
  27.6 12.7 %copy-start = (bf16[1,112,1024]{2,1,0:T(8,128)(2,1)S(1)}, bf16[1,112,1024]{2,1,0:T(8,128)(2,1)}, u32[]{:S(2)}) copy-start(bf16[1,112,1024]{2,1,0:T(8,128)(2,1)} %param.9) | copy-start | bytes 688132

commit v10 on v5

--- a/solution.py
+++ b/solution.py
@@ -75,10 +75,10 @@
         ]
         top = functools.reduce(jnp.maximum, scores)
         weights = [jnp.exp2((score - top) * EXP2_SCALE) for score in scores]
-        total = sum(weights[1:], weights[0])
+        inverse = 1.0 / sum(weights[1:], weights[0])
         mixed = None
         for weight, ref in zip(weights, pair_refs):
-            rounded = (weight / total).astype(jnp.bfloat16).astype(jnp.float32)
+            rounded = (weight * inverse).astype(jnp.bfloat16).astype(jnp.float32)
             term = rounded * ref[rows : 2 * rows, lanes].astype(jnp.float32)
             mixed = term if mixed is None else mixed + term
         o_cross = mixed.astype(jnp.bfloat16).astype(jnp.float32)
@@ -106,7 +106,7 @@
 def split_attention(q, k, v, k_cross, v_cross, ctx_size):
     rows, width = q.shape
     heads = width // HEAD
-    partners = tuple(range(ctx_size - 1, -1, -1))
+    partners = (3, 7, 6, 2, 5, 4, 1, 0)
     vmem = pl.BlockSpec(memory_space=pltpu.VMEM)
     hbm = pl.BlockSpec(memory_space=pltpu.HBM)
     sources = [pltpu.with_memory_space_constraint(x, pltpu.HBM) for x in (q, k, v, k_cross, v_cross)]
@@ -138,7 +138,7 @@
         name="self_attention",
     )(*moved)
     back = lax.all_to_all(own, "ctx", split_axis=0, concat_axis=0, tiled=True)
-    return back, pair, (pair, moved)
+    return back, pair, (pair, moved[:4])
 
 
 def shared_attention(q, k, v, ctx_size):
@@ -178,7 +178,7 @@
 def body(view_count, ctx_size, q_self, k_self, v_self, q_cross, k_cross, v_cross):
     _, rows, width = q_self.shape
     heads = width // HEAD
-    if ctx_size == heads:
+    if ctx_size == heads == 8:
         o_self, pair, after = split_attention(
             q_self[0], k_self[0], v_self[0], k_cross[0], v_cross[0], ctx_size
         )

time: 44.3 us -> 40.7 us (0.919)
  blocking collectives: 13.2 us -> 11 us
  waiting for transfers between devices: 4.34 us -> 3.33 us
    all_to_all x1, blocking collectives: 13.2 us -> 11 us  [split_attention(): back = lax.all_to_all(own, 'ctx', split_axis=0, concat_axis=0, tiled=True)]
    ppermute x10, waiting for transfers between devices: 4.34 us -> 3.33 us  [swap(): lax.ppermute(array, axis_name, [(i, i ^ partner) for i in range(axis_size)])]
  transfers between devices with their start and end apart: 10 -> 10, of which waited for: 4 -> 3; matrix products, arithmetic and copies ran while one was open for 0% -> 0% of each run, Pallas kernels for 4% -> 4%
where the time goes in v10:
time: 40.7 us; the launch traced here: 40.6 us
  starting transfers between devices  21.3 us (52%)
  blocking collectives  11 us (27%)
  Pallas kernels  4.85 us (12%)
  waiting for transfers between devices  3.33 us (8%)
    ppermute x10, starting transfers between devices, swap(): lax.ppermute(array, axis_name, [(i, i ^ partner) for i in range(axis_size)])  21.3 us
    all_to_all x1, blocking collectives, split_attention(): back = lax.all_to_all(own, 'ctx', split_axis=0, concat_axis=0, tiled=True)  11 us
    ppermute x10, waiting for transfers between devices, swap(): lax.ppermute(array, axis_name, [(i, i ^ partner) for i in range(axis_size)])  3.33 us
    pallas_call x1, Pallas kernels, body(): pl.pallas_call(functools.partial(cross_kernel, heads), out_shape=jax.Shap...  1.68 us
    pallas_call x1, Pallas kernels, split_attention(): pl.pallas_call(functools.partial(pack_kernel, partners), out_shape=[block...  1.61 us
    pallas_call x1, Pallas kernels, split_attention(): pl.pallas_call(functools.partial(packed_attention_kernel, partners, rows,...  1.57 us
  transfers between devices with their start and end apart: 10, of which 3 were waited for; matrix products, arithmetic and copies ran while one was open for 0% of the time, Pallas kernels for 4%

profile of v10, /device:TPU:0, one launch (start us, length us, event | category | flops | bytes accessed | tf_op | source)
XLA Modules:
  0.0 40.6 jit_solution(4048430655908675187)
XLA Ops:
  0.0 1.6 %pack_qkv.1 = (bf16[336,128]{1,0:T(8,128)(2,1)S(1)}, bf16[336,128]{1,0:T(8,128)(2,1)S(1)}, bf16[336,128]{1,0:T(8,128)(2,1)S(1)}, bf16[336,128]{1,0:T(8,128)(2,1)...) custom-call(bf16[112,1024]{1,0:T(8,128)(2,1)} %bitcast.8, ...), custom_call_target="tpu_custom_call" | custom-call | tf_op jit(solution)/shard_map/pack_qkv/pallas_call | solution.py:114
  1.6 3.0 %collective-permute-start.7 = (bf16[224,1024]{1,0:T(8,128)(2,1)S(1)}, bf16[224,1024]{1,0:T(8,128)(2,1)S(1)}, u32[]{:S(2)}, u32[]{:S(2)}) collective-permute-start(bf16[224,1024]{1,0:T(8,128)(2,1)S(1)} %get-tuple-element.25.refs_0_), channel_id=1, source_target_pairs={{0,16},{8,24},{16,0},{24,8},{1,17},{9,25},{17,1},{25,9},{2,18},{10... | collective-permute-start | bytes 1376264 | tf_op jit(solution)/shard_map/ppermute | solution.py:93
  4.7 2.5 %collective-permute-start = (bf16[336,128]{1,0:T(8,128)(2,1)S(1)}, bf16[336,128]{1,0:T(8,128)(2,1)S(1)}, u32[]{:S(2)}, u32[]{:S(2)}) collective-permute-start(bf16[336,128]{1,0:T(8,128)(2,1)S(1)} %get-tuple-element.16), channel_id=1, source_target_pairs={{0,3},{1,2},{2,1},{3,0},{4,7},{5,6},{6,5},{7,4},{8,11},{9,10},{10,... | collective-permute-start | bytes 258056 | tf_op jit(solution)/shard_map/ppermute | solution.py:93
  7.2 2.4 %collective-permute-start.1 = (bf16[336,128]{1,0:T(8,128)(2,1)S(1)}, bf16[336,128]{1,0:T(8,128)(2,1)S(1)}, u32[]{:S(2)}, u32[]{:S(2)}) collective-permute-start(bf16[336,128]{1,0:T(8,128)(2,1)S(1)} %get-tuple-element.17), channel_id=1, source_target_pairs={{0,7},{1,6},{2,5},{3,4},{4,3},{5,2},{6,1},{7,0},{8,15},{9,14},{10,... | collective-permute-start | bytes 258056 | tf_op jit(solution)/shard_map/ppermute | solution.py:93
  9.6 1.3 %collective-permute-start.2 = (bf16[336,128]{1,0:T(8,128)(2,1)S(1)}, bf16[336,128]{1,0:T(8,128)(2,1)S(1)}, u32[]{:S(2)}, u32[]{:S(2)}) collective-permute-start(bf16[336,128]{1,0:T(8,128)(2,1)S(1)} %get-tuple-element.18), channel_id=1, source_target_pairs={{0,6},{1,7},{2,4},{3,5},{4,2},{5,3},{6,0},{7,1},{8,14},{9,15},{10,... | collective-permute-start | bytes 258056 | tf_op jit(solution)/shard_map/ppermute | solution.py:93
  11.0 0.0 collective-permute-start.3
  11.0 0.0 collective-permute-done.refs_0_
  11.0 4.0 %collective-permute-start.4 = (bf16[336,128]{1,0:T(8,128)(2,1)S(1)}, bf16[336,128]{1,0:T(8,128)(2,1)S(1)}, u32[]{:S(2)}, u32[]{:S(2)}) collective-permute-start(bf16[336,128]{1,0:T(8,128)(2,1)S(1)} %get-tuple-element.20), channel_id=1, source_target_pairs={{0,5},{1,4},{2,7},{3,6},{4,1},{5,0},{6,3},{7,2},{8,13},{9,12},{10,... | collective-permute-start | bytes 258056 | tf_op jit(solution)/shard_map/ppermute | solution.py:93
  14.9 0.0 collective-permute-done.1.refs_1_
  14.9 6.8 %collective-permute-start.5 = (bf16[336,128]{1,0:T(8,128)(2,1)S(1)}, bf16[336,128]{1,0:T(8,128)(2,1)S(1)}, u32[]{:S(2)}, u32[]{:S(2)}) collective-permute-start(bf16[336,128]{1,0:T(8,128)(2,1)S(1)} %get-tuple-element.21), channel_id=1, source_target_pairs={{0,4},{1,5},{2,6},{3,7},{4,0},{5,1},{6,2},{7,3},{8,12},{9,13},{10,... | collective-permute-start | bytes 258056 | tf_op jit(solution)/shard_map/ppermute | solution.py:93
  21.8 0.0 collective-permute-done.2.refs_2_
  21.8 0.7 %collective-permute-start.6 = (bf16[336,128]{1,0:T(8,128)(2,1)S(1)}, bf16[336,128]{1,0:T(8,128)(2,1)S(1)}, u32[]{:S(2)}, u32[]{:S(2)}) collective-permute-start(bf16[336,128]{1,0:T(8,128)(2,1)S(1)} %get-tuple-element.22), channel_id=1, source_target_pairs={{0,1},{1,0},{2,3},{3,2},{4,5},{5,4},{6,7},{7,6},{8,9},{9,8},{10,11... | collective-permute-start | bytes 258056 | tf_op jit(solution)/shard_map/ppermute | solution.py:93
  22.4 0.0 collective-permute-done.3.refs_3_
  22.4 0.0 collective-permute-done.7.refs_1_
  22.4 0.0 collective-permute-start.8
  22.4 0.5 %collective-permute-start.9 = (bf16[224,1024]{1,0:T(8,128)(2,1)S(1)}, bf16[224,1024]{1,0:T(8,128)(2,1)S(1)}, u32[]{:S(2)}, u32[]{:S(2)}) collective-permute-start(bf16[224,1024]{1,0:T(8,128)(2,1)S(1)} %collective-permute-done.7.refs_1_), channel_id=1, source_target_pairs={{0,8},{8,0},{16,24},{24,16},{1,9},{9,1},{17,25},{25,17},{2,10},{10... | collective-permute-start | bytes 1376264 | tf_op jit(solution)/shard_map/ppermute | solution.py:93
  22.9 1.1 %collective-permute-done.4.refs_4_ = bf16[336,128]{1,0:T(8,128)(2,1)S(1)} collective-permute-done((bf16[336,128]{1,0:T(8,128)(2,1)S(1)}, bf16[336,128]{1,0:T(8,128)(2,1)S(1)}, u32[]{:S(2)}, u32[]{:S(2)}) %collective-permute-start.4) | collective-permute-done | bytes 86048 | tf_op jit(solution)/shard_map/ppermute | solution.py:93
  24.0 0.7 %collective-permute-done.5.refs_5_ = bf16[336,128]{1,0:T(8,128)(2,1)S(1)} collective-permute-done((bf16[336,128]{1,0:T(8,128)(2,1)S(1)}, bf16[336,128]{1,0:T(8,128)(2,1)S(1)}, u32[]{:S(2)}, u32[]{:S(2)}) %collective-permute-start.5) | collective-permute-done | bytes 86048 | tf_op jit(solution)/shard_map/ppermute | solution.py:93
  24.7 1.5 %collective-permute-done.6.refs_6_ = bf16[336,128]{1,0:T(8,128)(2,1)S(1)} collective-permute-done((bf16[336,128]{1,0:T(8,128)(2,1)S(1)}, bf16[336,128]{1,0:T(8,128)(2,1)S(1)}, u32[]{:S(2)}, u32[]{:S(2)}) %collective-permute-start.6) | collective-permute-done | bytes 86048 | tf_op jit(solution)/shard_map/ppermute | solution.py:93
  26.2 1.6 %self_attention.1 = bf16[8,112,128]{2,1,0:T(8,128)(2,1)S(1)} custom-call(bf16[336,128]{1,0:T(8,128)(2,1)S(1)} %collective-permute-done.refs_0_, bf16[336,128]{1,0:T(8,128)(2,1)S(1)} %collective-permute-done.1.refs_1_, bf16[336,128]{1,0:T(8,128)(2,1)S(1)} %collective-permute-done.2.refs_2_, bf16[336,128]{1,0:T(8,128)(2,1)S(1)} %collective-permute-done.3.refs_3_, ...), custom_call_target="tpu_custom_call" | custom-call | flops 411041792 | bytes 917504 | tf_op jit(solution)/shard_map/self_attention/pallas_call | solution.py:127
  27.8 0.0 copy-start
  27.8 11.0 %all_to_all.5.o_ref = bf16[8,112,128]{2,1,0:T(8,128)(2,1)S(1)} all-to-all(bf16[8,112,128]{2,1,0:T(8,128)(2,1)S(1)} %self_attention.1), channel_id=1, replica_groups=mesh['view'=4,'ctx'=8] {'ctx'}, dimensions={0} | all-to-all | bytes 458752 | tf_op jit(solution)/shard_map/all_to_all | solution.py:140
  38.9 0.0 collective-permute-done.8.refs_2_
  38.9 0.0 collective-permute-done.9.refs_3_
  38.9 0.0 copy-done
  38.9 1.7 %cross_view.1 = bf16[112,1024]{1,0:T(8,128)(2,1)} custom-call(bf16[8,112,128]{2,1,0:T(8,128)(2,1)S(1)} %all_to_all.5.o_ref, bf16[112,1024]{1,0:T(8,128)(2,1)S(1)} %bitcast.7, bf16[224,1024]{1,0:T(8,128)(2,1)S(1)} %get-tuple-element.25.refs_0_, bf16[224,1024]{1,0:T(8,128)(2,1)S(1)} %collective-permute-done.7.refs_1_, ...), custom_call_target="tpu_custom_call" | custom-call | tf_op jit(solution)/shard_map/cross_view/pallas_call | solution.py:191
Async XLA Ops:
  1.6 20.8 %collective-permute-start.7 = (bf16[224,1024]{1,0:T(8,128)(2,1)S(1)}, bf16[224,1024]{1,0:T(8,128)(2,1)S(1)}, u32[]{:S(2)}, u32[]{:S(2)}) collective-permute-start(bf16[224,1024]{1,0:T(8,128)(2,1)S(1)} %get-tuple-element.25.refs_0_), channel_id=1, source_target_pairs={{0,16},{8,24},{16,0},{24,8},{1,17},{9,25},{17,1},{25,9},{2,18},{10... | collective-permute-start | bytes 1376264 | tf_op jit(solution)/shard_map/ppermute | solution.py:93
  4.7 6.3 %collective-permute-start = (bf16[336,128]{1,0:T(8,128)(2,1)S(1)}, bf16[336,128]{1,0:T(8,128)(2,1)S(1)}, u32[]{:S(2)}, u32[]{:S(2)}) collective-permute-start(bf16[336,128]{1,0:T(8,128)(2,1)S(1)} %get-tuple-element.16), channel_id=1, source_target_pairs={{0,3},{1,2},{2,1},{3,0},{4,7},{5,6},{6,5},{7,4},{8,11},{9,10},{10,... | collective-permute-start | bytes 258056 | tf_op jit(solution)/shard_map/ppermute | solution.py:93
  7.2 7.8 %collective-permute-start.1 = (bf16[336,128]{1,0:T(8,128)(2,1)S(1)}, bf16[336,128]{1,0:T(8,128)(2,1)S(1)}, u32[]{:S(2)}, u32[]{:S(2)}) collective-permute-start(bf16[336,128]{1,0:T(8,128)(2,1)S(1)} %get-tuple-element.17), channel_id=1, source_target_pairs={{0,7},{1,6},{2,5},{3,4},{4,3},{5,2},{6,1},{7,0},{8,15},{9,14},{10,... | collective-permute-start | bytes 258056 | tf_op jit(solution)/shard_map/ppermute | solution.py:93
  9.6 12.2 %collective-permute-start.2 = (bf16[336,128]{1,0:T(8,128)(2,1)S(1)}, bf16[336,128]{1,0:T(8,128)(2,1)S(1)}, u32[]{:S(2)}, u32[]{:S(2)}) collective-permute-start(bf16[336,128]{1,0:T(8,128)(2,1)S(1)} %get-tuple-element.18), channel_id=1, source_target_pairs={{0,6},{1,7},{2,4},{3,5},{4,2},{5,3},{6,0},{7,1},{8,14},{9,15},{10,... | collective-permute-start | bytes 258056 | tf_op jit(solution)/shard_map/ppermute | solution.py:93
  11.0 11.5 %collective-permute-start.3 = (bf16[336,128]{1,0:T(8,128)(2,1)S(1)}, bf16[336,128]{1,0:T(8,128)(2,1)S(1)}, u32[]{:S(2)}, u32[]{:S(2)}) collective-permute-start(bf16[336,128]{1,0:T(8,128)(2,1)S(1)} %get-tuple-element.19), channel_id=1, source_target_pairs={{0,2},{1,3},{2,0},{3,1},{4,6},{5,7},{6,4},{7,5},{8,10},{9,11},{10,... | collective-permute-start | bytes 258056 | tf_op jit(solution)/shard_map/ppermute | solution.py:93
  11.0 13.0 %collective-permute-start.4 = (bf16[336,128]{1,0:T(8,128)(2,1)S(1)}, bf16[336,128]{1,0:T(8,128)(2,1)S(1)}, u32[]{:S(2)}, u32[]{:S(2)}) collective-permute-start(bf16[336,128]{1,0:T(8,128)(2,1)S(1)} %get-tuple-element.20), channel_id=1, source_target_pairs={{0,5},{1,4},{2,7},{3,6},{4,1},{5,0},{6,3},{7,2},{8,13},{9,12},{10,... | collective-permute-start | bytes 258056 | tf_op jit(solution)/shard_map/ppermute | solution.py:93
  14.9 9.8 %collective-permute-start.5 = (bf16[336,128]{1,0:T(8,128)(2,1)S(1)}, bf16[336,128]{1,0:T(8,128)(2,1)S(1)}, u32[]{:S(2)}, u32[]{:S(2)}) collective-permute-start(bf16[336,128]{1,0:T(8,128)(2,1)S(1)} %get-tuple-element.21), channel_id=1, source_target_pairs={{0,4},{1,5},{2,6},{3,7},{4,0},{5,1},{6,2},{7,3},{8,12},{9,13},{10,... | collective-permute-start | bytes 258056 | tf_op jit(solution)/shard_map/ppermute | solution.py:93
  21.8 4.5 %collective-permute-start.6 = (bf16[336,128]{1,0:T(8,128)(2,1)S(1)}, bf16[336,128]{1,0:T(8,128)(2,1)S(1)}, u32[]{:S(2)}, u32[]{:S(2)}) collective-permute-start(bf16[336,128]{1,0:T(8,128)(2,1)S(1)} %get-tuple-element.22), channel_id=1, source_target_pairs={{0,1},{1,0},{2,3},{3,2},{4,5},{5,4},{6,7},{7,6},{8,9},{9,8},{10,11... | collective-permute-start | bytes 258056 | tf_op jit(solution)/shard_map/ppermute | solution.py:93
  22.4 16.5 %collective-permute-start.8 = (bf16[224,1024]{1,0:T(8,128)(2,1)S(1)}, bf16[224,1024]{1,0:T(8,128)(2,1)S(1)}, u32[]{:S(2)}, u32[]{:S(2)}) collective-permute-start(bf16[224,1024]{1,0:T(8,128)(2,1)S(1)} %get-tuple-element.25.refs_0_), channel_id=1, source_target_pairs={{0,8},{8,0},{16,24},{24,16},{1,9},{9,1},{17,25},{25,17},{2,10},{10... | collective-permute-start | bytes 1376264 | tf_op jit(solution)/shard_map/ppermute | solution.py:93
  22.4 16.5 %collective-permute-start.9 = (bf16[224,1024]{1,0:T(8,128)(2,1)S(1)}, bf16[224,1024]{1,0:T(8,128)(2,1)S(1)}, u32[]{:S(2)}, u32[]{:S(2)}) collective-permute-start(bf16[224,1024]{1,0:T(8,128)(2,1)S(1)} %collective-permute-done.7.refs_1_), channel_id=1, source_target_pairs={{0,8},{8,0},{16,24},{24,16},{1,9},{9,1},{17,25},{25,17},{2,10},{10... | collective-permute-start | bytes 1376264 | tf_op jit(solution)/shard_map/ppermute | solution.py:93
  27.8 11.1 %copy-start = (bf16[1,112,1024]{2,1,0:T(8,128)(2,1)S(1)}, bf16[1,112,1024]{2,1,0:T(8,128)(2,1)}, u32[]{:S(2)}) copy-start(bf16[1,112,1024]{2,1,0:T(8,128)(2,1)} %param.9) | copy-start | bytes 688132

commit v11 on v7

--- a/solution.py
+++ b/solution.py
@@ -85,10 +85,10 @@
         ]
         top = functools.reduce(jnp.maximum, scores)
         weights = [jnp.exp2((score - top) * EXP2_SCALE) for score in scores]
-        total = sum(weights[1:], weights[0])
+        inverse = 1.0 / sum(weights[1:], weights[0])
         mixed = None
         for weight, ref in zip(weights, pair_refs):
-            rounded = (weight / total).astype(jnp.bfloat16).astype(jnp.float32)
+            rounded = (weight * inverse).astype(jnp.bfloat16).astype(jnp.float32)
             term = rounded * ref[rows : 2 * rows, lanes].astype(jnp.float32)
             mixed = term if mixed is None else mixed + term
         o_cross = mixed.astype(jnp.bfloat16).astype(jnp.float32)
@@ -103,17 +103,7 @@
     return lax.ppermute(array, axis_name, [(i, i ^ partner) for i in range(axis_size)])
 
 
-def gather_views(array, view_count, *after):
-    gathered = [array]
-    step = view_count // 2
-    for earlier in after:
-        gathered, _ = lax.optimization_barrier((gathered, earlier))
-        gathered += [swap(block, "view", view_count, step) for block in gathered]
-        step //= 2
-    return gathered
-
-
-def split_attention(q, k, v, k_cross, v_cross, ctx_size):
+def split_attention(q, k, v, k_cross, v_cross, ctx_size, view_count):
     rows, width = q.shape
     heads = width // HEAD
     group = ctx_size // 2
@@ -135,6 +125,8 @@
         name="pack_qkv",
     )(*sources)
     far = [swap(data, "ctx", ctx_size, partner) for partner, data in zip(partners, far)]
+    mate = swap(pair, "view", view_count, 1)
+    near, _ = lax.optimization_barrier((near, mate))
     near = lax.all_to_all(
         near,
         "ctx",
@@ -157,7 +149,7 @@
         name="self_attention",
     )(*far, near)
     back = lax.all_to_all(own, "ctx", split_axis=0, concat_axis=0, tiled=True)
-    return back, pair, (pair, near)
+    return back, [pair, mate], [near, far[0]]
 
 
 def shared_attention(q, k, v, ctx_size):
@@ -197,15 +189,17 @@
 def body(view_count, ctx_size, q_self, k_self, v_self, q_cross, k_cross, v_cross):
     _, rows, width = q_self.shape
     heads = width // HEAD
-    if ctx_size == heads:
-        o_self, pair, after = split_attention(
-            q_self[0], k_self[0], v_self[0], k_cross[0], v_cross[0], ctx_size
+    if ctx_size == heads == 8:
+        o_self, (pair, mate), after = split_attention(
+            q_self[0], k_self[0], v_self[0], k_cross[0], v_cross[0], ctx_size, view_count
         )
     else:
         o_self = shared_attention(q_self[0], k_self[0], v_self[0], ctx_size)
-        pair = jnp.concatenate([k_cross[0], v_cross[0]], axis=0)
-        after = [pair] * (view_count.bit_length() - 1)
-    pairs = gather_views(pair, view_count, *after)
+        pair = after = jnp.concatenate([k_cross[0], v_cross[0]], axis=0)
+        mate = swap(pair, "view", view_count, 1)
+    far = swap(pair, "view", view_count, 2)
+    far, _ = lax.optimization_barrier((far, after))
+    pairs = [pair, mate, far, swap(far, "view", view_count, 1)]
     vmem = pl.BlockSpec(memory_space=pltpu.VMEM)
     out = pl.pallas_call(
         functools.partial(cross_kernel, heads),

time: 43 us -> 45.2 us (1.051)
  waiting for transfers between devices: 10.7 us -> 13 us
    ppermute x7, waiting for transfers between devices: 10.7 us -> 13 us  [swap(): lax.ppermute(array, axis_name, [(i, i ^ partner) for i in range(axis_size)])]
  transfers between devices with their start and end apart: 8 -> 8, of which waited for: 5 -> 5; matrix products, arithmetic and copies ran while one was open for 0% -> 0% of each run, Pallas kernels for 4% -> 3%
where the time goes in v11:
time: 45.2 us; the launch traced here: 44.9 us
  starting transfers between devices  15.1 us (33%)
  waiting for transfers between devices  13 us (29%)
  blocking collectives  11.3 us (25%)
  Pallas kernels  5.47 us (12%)
    ppermute x7, waiting for transfers between devices, swap(): lax.ppermute(array, axis_name, [(i, i ^ partner) for i in range(axis_size)])  13 us
    all_to_all x1, blocking collectives, split_attention(): back = lax.all_to_all(own, 'ctx', split_axis=0, concat_axis=0, tiled=True)  11.3 us
    ppermute x7, starting transfers between devices, swap(): lax.ppermute(array, axis_name, [(i, i ^ partner) for i in range(axis_size)])  9.92 us
    all_to_all x1, starting transfers between devices, split_attention(): lax.all_to_all(near, 'ctx', split_axis=0, concat_axis=0, tiled=True, axis...  5.14 us
    pallas_call x1, Pallas kernels, split_attention(): pl.pallas_call(functools.partial(pack_kernel, partners), out_shape=[jax.S...  2.24 us
    pallas_call x1, Pallas kernels, body(): pl.pallas_call(functools.partial(cross_kernel, heads), out_shape=jax.Shap...  1.68 us
    pallas_call x1, Pallas kernels, split_attention(): pl.pallas_call(functools.partial(packed_attention_kernel, partners, rows)...  1.55 us
  transfers between devices with their start and end apart: 8, of which 5 were waited for; matrix products, arithmetic and copies ran while one was open for 0% of the time, Pallas kernels for 3%

profile of v11, /device:TPU:0, one launch (start us, length us, event | category | flops | bytes accessed | tf_op | source)
XLA Modules:
  0.0 44.9 jit_solution(14923956115179871135)
XLA Ops:
  0.0 2.2 %pack_qkv.1 = (bf16[336,128]{1,0:T(8,128)(2,1)S(1)}, bf16[336,128]{1,0:T(8,128)(2,1)S(1)}, bf16[336,128]{1,0:T(8,128)(2,1)S(1)}, bf16[336,128]{1,0:T(8,128)(2,1)...) custom-call(bf16[112,1024]{1,0:T(8,128)(2,1)} %bitcast.8, bf16[112,1024]{1,0:T(8,128)(2,1)} %bitcast.9, ...), custom_call_target="tpu_custom_call" | custom-call | tf_op jit(solution)/shard_map/pack_qkv/pallas_call | solution.py:114
  2.3 0.5 %collective-permute-start.4 = (bf16[224,1024]{1,0:T(8,128)(2,1)S(1)}, bf16[224,1024]{1,0:T(8,128)(2,1)S(1)}, u32[]{:S(2)}, u32[]{:S(2)}) collective-permute-start(bf16[224,1024]{1,0:T(8,128)(2,1)S(1)} %get-tuple-element.18.refs_0_), channel_id=1, source_target_pairs={{0,8},{8,0},{16,24},{24,16},{1,9},{9,1},{17,25},{25,17},{2,10},{10... | collective-permute-start | bytes 1376264 | tf_op jit(solution)/shard_map/ppermute | solution.py:103
  2.8 1.4 %collective-permute-done.4.refs_1_ = bf16[224,1024]{1,0:T(8,128)(2,1)S(1)} collective-permute-done((bf16[224,1024]{1,0:T(8,128)(2,1)S(1)}, bf16[224,1024]{1,0:T(8,128)(2,1)S(1)}, u32[]{:S(2)}, u32[]{:S(2)}) %collective-permute-start.4) | collective-permute-done | bytes 458784 | tf_op jit(solution)/shard_map/ppermute | solution.py:103
  4.2 5.1 %all-to-all-start = ((bf16[4,336,128]{2,1,0:T(8,128)(2,1)}), bf16[4,336,128]{2,1,0:T(8,128)(2,1)S(1)}, u32[]{:S(2)}, u32[]{:S(2)}) async-start(bf16[4,336,128]{2,1,0:T(8,128)(2,1)} %get-tuple-element.19), calls=%async_computation | async-start | bytes 688128 | tf_op jit(solution)/shard_map/all_to_all | solution.py:130
  9.4 1.5 %collective-permute-start.5 = (bf16[224,1024]{1,0:T(8,128)(2,1)S(1)}, bf16[224,1024]{1,0:T(8,128)(2,1)S(1)}, u32[]{:S(2)}, u32[]{:S(2)}) collective-permute-start(bf16[224,1024]{1,0:T(8,128)(2,1)S(1)} %get-tuple-element.18.refs_0_), channel_id=1, source_target_pairs={{0,16},{8,24},{16,0},{24,8},{1,17},{9,25},{17,1},{25,9},{2,18},{10... | collective-permute-start | bytes 1376264 | tf_op jit(solution)/shard_map/ppermute | solution.py:103
  10.9 4.9 %collective-permute-start = (bf16[336,128]{1,0:T(8,128)(2,1)S(1)}, bf16[336,128]{1,0:T(8,128)(2,1)S(1)}, u32[]{:S(2)}, u32[]{:S(2)}) collective-permute-start(bf16[336,128]{1,0:T(8,128)(2,1)S(1)} %get-tuple-element.13), channel_id=1, source_target_pairs={{0,7},{1,6},{2,5},{3,4},{4,3},{5,2},{6,1},{7,0},{8,15},{9,14},{10,... | collective-permute-start | bytes 258056 | tf_op jit(solution)/shard_map/ppermute | solution.py:103
  15.8 0.3 collective-permute-start.1
  16.2 0.2 collective-permute-start.2
  16.4 2.4 %collective-permute-start.3 = (bf16[336,128]{1,0:T(8,128)(2,1)S(1)}, bf16[336,128]{1,0:T(8,128)(2,1)S(1)}, u32[]{:S(2)}, u32[]{:S(2)}) collective-permute-start(bf16[336,128]{1,0:T(8,128)(2,1)S(1)} %get-tuple-element.16), channel_id=1, source_target_pairs={{0,4},{1,5},{2,6},{3,7},{4,0},{5,1},{6,2},{7,3},{8,12},{9,13},{10,... | collective-permute-start | bytes 258056 | tf_op jit(solution)/shard_map/ppermute | solution.py:103
  18.8 2.9 %collective-permute-done.refs_0_ = bf16[336,128]{1,0:T(8,128)(2,1)S(1)} collective-permute-done((bf16[336,128]{1,0:T(8,128)(2,1)S(1)}, bf16[336,128]{1,0:T(8,128)(2,1)S(1)}, u32[]{:S(2)}, u32[]{:S(2)}) %collective-permute-start) | collective-permute-done | bytes 86048 | tf_op jit(solution)/shard_map/ppermute | solution.py:103
  21.7 0.0 collective-permute-done.5.refs_2_
  21.7 0.0 all-to-all-done.refs_4_
  21.7 0.0 collective-permute-start.6
  21.7 1.4 %collective-permute-done.1.refs_1_ = bf16[336,128]{1,0:T(8,128)(2,1)S(1)} collective-permute-done((bf16[336,128]{1,0:T(8,128)(2,1)S(1)}, bf16[336,128]{1,0:T(8,128)(2,1)S(1)}, u32[]{:S(2)}, u32[]{:S(2)}) %collective-permute-start.1) | collective-permute-done | bytes 86048 | tf_op jit(solution)/shard_map/ppermute | solution.py:103
  23.2 5.7 %collective-permute-done.2.refs_2_ = bf16[336,128]{1,0:T(8,128)(2,1)S(1)} collective-permute-done((bf16[336,128]{1,0:T(8,128)(2,1)S(1)}, bf16[336,128]{1,0:T(8,128)(2,1)S(1)}, u32[]{:S(2)}, u32[]{:S(2)}) %collective-permute-start.2) | collective-permute-done | bytes 86048 | tf_op jit(solution)/shard_map/ppermute | solution.py:103
  28.9 1.5 %collective-permute-done.3.refs_3_ = bf16[336,128]{1,0:T(8,128)(2,1)S(1)} collective-permute-done((bf16[336,128]{1,0:T(8,128)(2,1)S(1)}, bf16[336,128]{1,0:T(8,128)(2,1)S(1)}, u32[]{:S(2)}, u32[]{:S(2)}) %collective-permute-start.3) | collective-permute-done | bytes 86048 | tf_op jit(solution)/shard_map/ppermute | solution.py:103
  30.4 1.6 %self_attention.1 = bf16[8,112,128]{2,1,0:T(8,128)(2,1)S(1)} custom-call(bf16[336,128]{1,0:T(8,128)(2,1)S(1)} %collective-permute-done.refs_0_, bf16[336,128]{1,0:T(8,128)(2,1)S(1)} %collective-permute-done.1.refs_1_, bf16[336,128]{1,0:T(8,128)(2,1)S(1)} %collective-permute-done.2.refs_2_, bf16[336,128]{1,0:T(8,128)(2,1)S(1)} %collective-permute-done.3.refs_3_, ...), custom_call_target="tpu_custom_call" | custom-call | flops 411041792 | bytes 917504 | tf_op jit(solution)/shard_map/self_attention/pallas_call | solution.py:138
  31.9 0.0 copy-start
  31.9 11.3 %all_to_all.10.o_ref = bf16[8,112,128]{2,1,0:T(8,128)(2,1)S(1)} all-to-all(bf16[8,112,128]{2,1,0:T(8,128)(2,1)S(1)} %self_attention.1), channel_id=1, replica_groups=mesh['view'=4,'ctx'=8] {'ctx'}, dimensions={0} | all-to-all | bytes 458752 | tf_op jit(solution)/shard_map/all_to_all | solution.py:151
  43.2 0.0 collective-permute-done.6.refs_3_
  43.2 0.0 copy-done
  43.2 1.7 %cross_view.1 = bf16[112,1024]{1,0:T(8,128)(2,1)} custom-call(bf16[8,112,128]{2,1,0:T(8,128)(2,1)S(1)} %all_to_all.10.o_ref, bf16[112,1024]{1,0:T(8,128)(2,1)S(1)} %bitcast.7, bf16[224,1024]{1,0:T(8,128)(2,1)S(1)} %get-tuple-element.18.refs_0_, bf16[224,1024]{1,0:T(8,128)(2,1)S(1)} %collective-permute-done.4.refs_1_, ...), custom_call_target="tpu_custom_call" | custom-call | tf_op jit(solution)/shard_map/cross_view/pallas_call | solution.py:204
Async XLA Ops:
  2.3 2.0 %collective-permute-start.4 = (bf16[224,1024]{1,0:T(8,128)(2,1)S(1)}, bf16[224,1024]{1,0:T(8,128)(2,1)S(1)}, u32[]{:S(2)}, u32[]{:S(2)}) collective-permute-start(bf16[224,1024]{1,0:T(8,128)(2,1)S(1)} %get-tuple-element.18.refs_0_), channel_id=1, source_target_pairs={{0,8},{8,0},{16,24},{24,16},{1,9},{9,1},{17,25},{25,17},{2,10},{10... | collective-permute-start | bytes 1376264 | tf_op jit(solution)/shard_map/ppermute | solution.py:103
  4.2 17.5 %all-to-all-start = ((bf16[4,336,128]{2,1,0:T(8,128)(2,1)}), bf16[4,336,128]{2,1,0:T(8,128)(2,1)S(1)}, u32[]{:S(2)}, u32[]{:S(2)}) async-start(bf16[4,336,128]{2,1,0:T(8,128)(2,1)} %get-tuple-element.19), calls=%async_computation | async-start | bytes 688128 | tf_op jit(solution)/shard_map/all_to_all | solution.py:130
  9.4 12.3 %collective-permute-start.5 = (bf16[224,1024]{1,0:T(8,128)(2,1)S(1)}, bf16[224,1024]{1,0:T(8,128)(2,1)S(1)}, u32[]{:S(2)}, u32[]{:S(2)}) collective-permute-start(bf16[224,1024]{1,0:T(8,128)(2,1)S(1)} %get-tuple-element.18.refs_0_), channel_id=1, source_target_pairs={{0,16},{8,24},{16,0},{24,8},{1,17},{9,25},{17,1},{25,9},{2,18},{10... | collective-permute-start | bytes 1376264 | tf_op jit(solution)/shard_map/ppermute | solution.py:103
  10.9 10.8 %collective-permute-start = (bf16[336,128]{1,0:T(8,128)(2,1)S(1)}, bf16[336,128]{1,0:T(8,128)(2,1)S(1)}, u32[]{:S(2)}, u32[]{:S(2)}) collective-permute-start(bf16[336,128]{1,0:T(8,128)(2,1)S(1)} %get-tuple-element.13), channel_id=1, source_target_pairs={{0,7},{1,6},{2,5},{3,4},{4,3},{5,2},{6,1},{7,0},{8,15},{9,14},{10,... | collective-permute-start | bytes 258056 | tf_op jit(solution)/shard_map/ppermute | solution.py:103
  15.8 7.3 %collective-permute-start.1 = (bf16[336,128]{1,0:T(8,128)(2,1)S(1)}, bf16[336,128]{1,0:T(8,128)(2,1)S(1)}, u32[]{:S(2)}, u32[]{:S(2)}) collective-permute-start(bf16[336,128]{1,0:T(8,128)(2,1)S(1)} %get-tuple-element.14), channel_id=1, source_target_pairs={{0,6},{1,7},{2,4},{3,5},{4,2},{5,3},{6,0},{7,1},{8,14},{9,15},{10,... | collective-permute-start | bytes 258056 | tf_op jit(solution)/shard_map/ppermute | solution.py:103
  16.2 12.7 %collective-permute-start.2 = (bf16[336,128]{1,0:T(8,128)(2,1)S(1)}, bf16[336,128]{1,0:T(8,128)(2,1)S(1)}, u32[]{:S(2)}, u32[]{:S(2)}) collective-permute-start(bf16[336,128]{1,0:T(8,128)(2,1)S(1)} %get-tuple-element.15), channel_id=1, source_target_pairs={{0,5},{1,4},{2,7},{3,6},{4,1},{5,0},{6,3},{7,2},{8,13},{9,12},{10,... | collective-permute-start | bytes 258056 | tf_op jit(solution)/shard_map/ppermute | solution.py:103
  16.4 14.0 %collective-permute-start.3 = (bf16[336,128]{1,0:T(8,128)(2,1)S(1)}, bf16[336,128]{1,0:T(8,128)(2,1)S(1)}, u32[]{:S(2)}, u32[]{:S(2)}) collective-permute-start(bf16[336,128]{1,0:T(8,128)(2,1)S(1)} %get-tuple-element.16), channel_id=1, source_target_pairs={{0,4},{1,5},{2,6},{3,7},{4,0},{5,1},{6,2},{7,3},{8,12},{9,13},{10,... | collective-permute-start | bytes 258056 | tf_op jit(solution)/shard_map/ppermute | solution.py:103
  21.7 21.5 %collective-permute-start.6 = (bf16[224,1024]{1,0:T(8,128)(2,1)S(1)}, bf16[224,1024]{1,0:T(8,128)(2,1)S(1)}, u32[]{:S(2)}, u32[]{:S(2)}) collective-permute-start(bf16[224,1024]{1,0:T(8,128)(2,1)S(1)} %collective-permute-done.5.refs_2_), channel_id=1, source_target_pairs={{0,8},{8,0},{16,24},{24,16},{1,9},{9,1},{17,25},{25,17},{2,10},{10... | collective-permute-start | bytes 1376264 | tf_op jit(solution)/shard_map/ppermute | solution.py:103
  31.9 11.3 %copy-start = (bf16[1,112,1024]{2,1,0:T(8,128)(2,1)S(1)}, bf16[1,112,1024]{2,1,0:T(8,128)(2,1)}, u32[]{:S(2)}) copy-start(bf16[1,112,1024]{2,1,0:T(8,128)(2,1)} %param.9) | copy-start | bytes 688132

commit v12 on v10

--- a/solution.py
+++ b/solution.py
@@ -106,7 +106,7 @@
 def split_attention(q, k, v, k_cross, v_cross, ctx_size):
     rows, width = q.shape
     heads = width // HEAD
-    partners = (3, 7, 6, 2, 5, 4, 1, 0)
+    partners = (3, 2, 7, 6, 5, 4, 1, 0)
     vmem = pl.BlockSpec(memory_space=pltpu.VMEM)
     hbm = pl.BlockSpec(memory_space=pltpu.HBM)
     sources = [pltpu.with_memory_space_constraint(x, pltpu.HBM) for x in (q, k, v, k_cross, v_cross)]

time: 40.7 us -> 41.1 us (level)
  starting transfers between devices: 21.3 us -> 16.5 us
  waiting for transfers between devices: 3.33 us -> 7.21 us
  blocking collectives: 11 us -> 12.3 us
    ppermute x10, starting transfers between devices: 21.3 us -> 16.5 us  [swap(): lax.ppermute(array, axis_name, [(i, i ^ partner) for i in range(axis_size)])]
    ppermute x10, waiting for transfers between devices: 3.33 us -> 7.21 us  [swap(): lax.ppermute(array, axis_name, [(i, i ^ partner) for i in range(axis_size)])]
    all_to_all x1, blocking collectives: 11 us -> 12.3 us  [split_attention(): back = lax.all_to_all(own, 'ctx', split_axis=0, concat_axis=0, tiled=True)]
where the time goes in v12:
time: 41.1 us; the launch traced here: 40.9 us
  starting transfers between devices  16.5 us (40%)
  blocking collectives  12.3 us (30%)
  waiting for transfers between devices  7.21 us (18%)
  Pallas kernels  4.85 us (12%)
    ppermute x10, starting transfers between devices, swap(): lax.ppermute(array, axis_name, [(i, i ^ partner) for i in range(axis_size)])  16.5 us
    all_to_all x1, blocking collectives, split_attention(): back = lax.all_to_all(own, 'ctx', split_axis=0, concat_axis=0, tiled=True)  12.3 us
    ppermute x10, waiting for transfers between devices, swap(): lax.ppermute(array, axis_name, [(i, i ^ partner) for i in range(axis_size)])  7.21 us
    pallas_call x1, Pallas kernels, body(): pl.pallas_call(functools.partial(cross_kernel, heads), out_shape=jax.Shap...  1.68 us
    pallas_call x1, Pallas kernels, split_attention(): pl.pallas_call(functools.partial(pack_kernel, partners), out_shape=[block...  1.61 us
    pallas_call x1, Pallas kernels, split_attention(): pl.pallas_call(functools.partial(packed_attention_kernel, partners, rows,...  1.57 us
  transfers between devices with their start and end apart: 10, of which 3 were waited for; matrix products, arithmetic and copies ran while one was open for 0% of the time, Pallas kernels for 4%

profile of v12, /device:TPU:0, one launch (start us, length us, event | category | flops | bytes accessed | tf_op | source)
XLA Modules:
  0.0 40.9 jit_solution(10713733361586756171)
XLA Ops:
  0.0 1.6 %pack_qkv.1 = (bf16[336,128]{1,0:T(8,128)(2,1)S(1)}, bf16[336,128]{1,0:T(8,128)(2,1)S(1)}, bf16[336,128]{1,0:T(8,128)(2,1)S(1)}, bf16[336,128]{1,0:T(8,128)(2,1)...) custom-call(bf16[112,1024]{1,0:T(8,128)(2,1)} %bitcast.8, ...), custom_call_target="tpu_custom_call" | custom-call | tf_op jit(solution)/shard_map/pack_qkv/pallas_call | solution.py:114
  1.6 3.0 %collective-permute-start.7 = (bf16[224,1024]{1,0:T(8,128)(2,1)S(1)}, bf16[224,1024]{1,0:T(8,128)(2,1)S(1)}, u32[]{:S(2)}, u32[]{:S(2)}) collective-permute-start(bf16[224,1024]{1,0:T(8,128)(2,1)S(1)} %get-tuple-element.25.refs_0_), channel_id=1, source_target_pairs={{0,16},{8,24},{16,0},{24,8},{1,17},{9,25},{17,1},{25,9},{2,18},{10... | collective-permute-start | bytes 1376264 | tf_op jit(solution)/shard_map/ppermute | solution.py:93
  4.7 2.5 %collective-permute-start = (bf16[336,128]{1,0:T(8,128)(2,1)S(1)}, bf16[336,128]{1,0:T(8,128)(2,1)S(1)}, u32[]{:S(2)}, u32[]{:S(2)}) collective-permute-start(bf16[336,128]{1,0:T(8,128)(2,1)S(1)} %get-tuple-element.16), channel_id=1, source_target_pairs={{0,3},{1,2},{2,1},{3,0},{4,7},{5,6},{6,5},{7,4},{8,11},{9,10},{10,... | collective-permute-start | bytes 258056 | tf_op jit(solution)/shard_map/ppermute | solution.py:93
  7.2 0.4 %collective-permute-start.1 = (bf16[336,128]{1,0:T(8,128)(2,1)S(1)}, bf16[336,128]{1,0:T(8,128)(2,1)S(1)}, u32[]{:S(2)}, u32[]{:S(2)}) collective-permute-start(bf16[336,128]{1,0:T(8,128)(2,1)S(1)} %get-tuple-element.17), channel_id=1, source_target_pairs={{0,2},{1,3},{2,0},{3,1},{4,6},{5,7},{6,4},{7,5},{8,10},{9,11},{10,... | collective-permute-start | bytes 258056 | tf_op jit(solution)/shard_map/ppermute | solution.py:93
  7.6 3.6 %collective-permute-start.2 = (bf16[336,128]{1,0:T(8,128)(2,1)S(1)}, bf16[336,128]{1,0:T(8,128)(2,1)S(1)}, u32[]{:S(2)}, u32[]{:S(2)}) collective-permute-start(bf16[336,128]{1,0:T(8,128)(2,1)S(1)} %get-tuple-element.18), channel_id=1, source_target_pairs={{0,7},{1,6},{2,5},{3,4},{4,3},{5,2},{6,1},{7,0},{8,15},{9,14},{10,... | collective-permute-start | bytes 258056 | tf_op jit(solution)/shard_map/ppermute | solution.py:93
  11.2 0.2 collective-permute-start.3
  11.4 0.0 collective-permute-done.refs_0_
  11.4 3.1 %collective-permute-start.4 = (bf16[336,128]{1,0:T(8,128)(2,1)S(1)}, bf16[336,128]{1,0:T(8,128)(2,1)S(1)}, u32[]{:S(2)}, u32[]{:S(2)}) collective-permute-start(bf16[336,128]{1,0:T(8,128)(2,1)S(1)} %get-tuple-element.20), channel_id=1, source_target_pairs={{0,5},{1,4},{2,7},{3,6},{4,1},{5,0},{6,3},{7,2},{8,13},{9,12},{10,... | collective-permute-start | bytes 258056 | tf_op jit(solution)/shard_map/ppermute | solution.py:93
  14.5 0.0 collective-permute-done.1.refs_1_
  14.5 0.9 %collective-permute-start.5 = (bf16[336,128]{1,0:T(8,128)(2,1)S(1)}, bf16[336,128]{1,0:T(8,128)(2,1)S(1)}, u32[]{:S(2)}, u32[]{:S(2)}) collective-permute-start(bf16[336,128]{1,0:T(8,128)(2,1)S(1)} %get-tuple-element.21), channel_id=1, source_target_pairs={{0,4},{1,5},{2,6},{3,7},{4,0},{5,1},{6,2},{7,3},{8,12},{9,13},{10,... | collective-permute-start | bytes 258056 | tf_op jit(solution)/shard_map/ppermute | solution.py:93
  15.4 0.7 %collective-permute-done.2.refs_2_ = bf16[336,128]{1,0:T(8,128)(2,1)S(1)} collective-permute-done((bf16[336,128]{1,0:T(8,128)(2,1)S(1)}, bf16[336,128]{1,0:T(8,128)(2,1)S(1)}, u32[]{:S(2)}, u32[]{:S(2)}) %collective-permute-start.2) | collective-permute-done | bytes 86048 | tf_op jit(solution)/shard_map/ppermute | solution.py:93
  16.1 2.2 %collective-permute-start.6 = (bf16[336,128]{1,0:T(8,128)(2,1)S(1)}, bf16[336,128]{1,0:T(8,128)(2,1)S(1)}, u32[]{:S(2)}, u32[]{:S(2)}) collective-permute-start(bf16[336,128]{1,0:T(8,128)(2,1)S(1)} %get-tuple-element.22), channel_id=1, source_target_pairs={{0,1},{1,0},{2,3},{3,2},{4,5},{5,4},{6,7},{7,6},{8,9},{9,8},{10,11... | collective-permute-start | bytes 258056 | tf_op jit(solution)/shard_map/ppermute | solution.py:93
  18.3 0.4 collective-permute-done.3.refs_3_
  18.6 0.0 collective-permute-done.7.refs_1_
  18.6 0.0 collective-permute-start.8
  18.6 0.5 %collective-permute-start.9 = (bf16[224,1024]{1,0:T(8,128)(2,1)S(1)}, bf16[224,1024]{1,0:T(8,128)(2,1)S(1)}, u32[]{:S(2)}, u32[]{:S(2)}) collective-permute-start(bf16[224,1024]{1,0:T(8,128)(2,1)S(1)} %collective-permute-done.7.refs_1_), channel_id=1, source_target_pairs={{0,8},{8,0},{16,24},{24,16},{1,9},{9,1},{17,25},{25,17},{2,10},{10... | collective-permute-start | bytes 1376264 | tf_op jit(solution)/shard_map/ppermute | solution.py:93
  19.2 6.1 %collective-permute-done.4.refs_4_ = bf16[336,128]{1,0:T(8,128)(2,1)S(1)} collective-permute-done((bf16[336,128]{1,0:T(8,128)(2,1)S(1)}, bf16[336,128]{1,0:T(8,128)(2,1)S(1)}, u32[]{:S(2)}, u32[]{:S(2)}) %collective-permute-start.4) | collective-permute-done | bytes 86048 | tf_op jit(solution)/shard_map/ppermute | solution.py:93
  25.3 0.0 collective-permute-done.5.refs_5_
  25.3 0.0 collective-permute-done.6.refs_6_
  25.3 1.6 %self_attention.1 = bf16[8,112,128]{2,1,0:T(8,128)(2,1)S(1)} custom-call(bf16[336,128]{1,0:T(8,128)(2,1)S(1)} %collective-permute-done.refs_0_, bf16[336,128]{1,0:T(8,128)(2,1)S(1)} %collective-permute-done.1.refs_1_, bf16[336,128]{1,0:T(8,128)(2,1)S(1)} %collective-permute-done.2.refs_2_, bf16[336,128]{1,0:T(8,128)(2,1)S(1)} %collective-permute-done.3.refs_3_, ...), custom_call_target="tpu_custom_call" | custom-call | flops 411041792 | bytes 917504 | tf_op jit(solution)/shard_map/self_attention/pallas_call | solution.py:127
  26.9 0.0 copy-start
  26.9 12.3 %all_to_all.5.o_ref = bf16[8,112,128]{2,1,0:T(8,128)(2,1)S(1)} all-to-all(bf16[8,112,128]{2,1,0:T(8,128)(2,1)S(1)} %self_attention.1), channel_id=1, replica_groups=mesh['view'=4,'ctx'=8] {'ctx'}, dimensions={0} | all-to-all | bytes 458752 | tf_op jit(solution)/shard_map/all_to_all | solution.py:140
  39.2 0.0 collective-permute-done.8.refs_2_
  39.2 0.0 collective-permute-done.9.refs_3_
  39.2 0.0 copy-done
  39.2 1.7 %cross_view.1 = bf16[112,1024]{1,0:T(8,128)(2,1)} custom-call(bf16[8,112,128]{2,1,0:T(8,128)(2,1)S(1)} %all_to_all.5.o_ref, bf16[112,1024]{1,0:T(8,128)(2,1)S(1)} %bitcast.7, bf16[224,1024]{1,0:T(8,128)(2,1)S(1)} %get-tuple-element.25.refs_0_, bf16[224,1024]{1,0:T(8,128)(2,1)S(1)} %collective-permute-done.7.refs_1_, ...), custom_call_target="tpu_custom_call" | custom-call | tf_op jit(solution)/shard_map/cross_view/pallas_call | solution.py:191
Async XLA Ops:
  1.6 17.0 %collective-permute-start.7 = (bf16[224,1024]{1,0:T(8,128)(2,1)S(1)}, bf16[224,1024]{1,0:T(8,128)(2,1)S(1)}, u32[]{:S(2)}, u32[]{:S(2)}) collective-permute-start(bf16[224,1024]{1,0:T(8,128)(2,1)S(1)} %get-tuple-element.25.refs_0_), channel_id=1, source_target_pairs={{0,16},{8,24},{16,0},{24,8},{1,17},{9,25},{17,1},{25,9},{2,18},{10... | collective-permute-start | bytes 1376264 | tf_op jit(solution)/shard_map/ppermute | solution.py:93
  4.7 6.8 %collective-permute-start = (bf16[336,128]{1,0:T(8,128)(2,1)S(1)}, bf16[336,128]{1,0:T(8,128)(2,1)S(1)}, u32[]{:S(2)}, u32[]{:S(2)}) collective-permute-start(bf16[336,128]{1,0:T(8,128)(2,1)S(1)} %get-tuple-element.16), channel_id=1, source_target_pairs={{0,3},{1,2},{2,1},{3,0},{4,7},{5,6},{6,5},{7,4},{8,11},{9,10},{10,... | collective-permute-start | bytes 258056 | tf_op jit(solution)/shard_map/ppermute | solution.py:93
  7.2 7.3 %collective-permute-start.1 = (bf16[336,128]{1,0:T(8,128)(2,1)S(1)}, bf16[336,128]{1,0:T(8,128)(2,1)S(1)}, u32[]{:S(2)}, u32[]{:S(2)}) collective-permute-start(bf16[336,128]{1,0:T(8,128)(2,1)S(1)} %get-tuple-element.17), channel_id=1, source_target_pairs={{0,2},{1,3},{2,0},{3,1},{4,6},{5,7},{6,4},{7,5},{8,10},{9,11},{10,... | collective-permute-start | bytes 258056 | tf_op jit(solution)/shard_map/ppermute | solution.py:93
  7.6 8.5 %collective-permute-start.2 = (bf16[336,128]{1,0:T(8,128)(2,1)S(1)}, bf16[336,128]{1,0:T(8,128)(2,1)S(1)}, u32[]{:S(2)}, u32[]{:S(2)}) collective-permute-start(bf16[336,128]{1,0:T(8,128)(2,1)S(1)} %get-tuple-element.18), channel_id=1, source_target_pairs={{0,7},{1,6},{2,5},{3,4},{4,3},{5,2},{6,1},{7,0},{8,15},{9,14},{10,... | collective-permute-start | bytes 258056 | tf_op jit(solution)/shard_map/ppermute | solution.py:93
  11.2 7.5 %collective-permute-start.3 = (bf16[336,128]{1,0:T(8,128)(2,1)S(1)}, bf16[336,128]{1,0:T(8,128)(2,1)S(1)}, u32[]{:S(2)}, u32[]{:S(2)}) collective-permute-start(bf16[336,128]{1,0:T(8,128)(2,1)S(1)} %get-tuple-element.19), channel_id=1, source_target_pairs={{0,6},{1,7},{2,4},{3,5},{4,2},{5,3},{6,0},{7,1},{8,14},{9,15},{10,... | collective-permute-start | bytes 258056 | tf_op jit(solution)/shard_map/ppermute | solution.py:93
  11.4 13.9 %collective-permute-start.4 = (bf16[336,128]{1,0:T(8,128)(2,1)S(1)}, bf16[336,128]{1,0:T(8,128)(2,1)S(1)}, u32[]{:S(2)}, u32[]{:S(2)}) collective-permute-start(bf16[336,128]{1,0:T(8,128)(2,1)S(1)} %get-tuple-element.20), channel_id=1, source_target_pairs={{0,5},{1,4},{2,7},{3,6},{4,1},{5,0},{6,3},{7,2},{8,13},{9,12},{10,... | collective-permute-start | bytes 258056 | tf_op jit(solution)/shard_map/ppermute | solution.py:93
  14.5 10.8 %collective-permute-start.5 = (bf16[336,128]{1,0:T(8,128)(2,1)S(1)}, bf16[336,128]{1,0:T(8,128)(2,1)S(1)}, u32[]{:S(2)}, u32[]{:S(2)}) collective-permute-start(bf16[336,128]{1,0:T(8,128)(2,1)S(1)} %get-tuple-element.21), channel_id=1, source_target_pairs={{0,4},{1,5},{2,6},{3,7},{4,0},{5,1},{6,2},{7,3},{8,12},{9,13},{10,... | collective-permute-start | bytes 258056 | tf_op jit(solution)/shard_map/ppermute | solution.py:93
  16.1 9.2 %collective-permute-start.6 = (bf16[336,128]{1,0:T(8,128)(2,1)S(1)}, bf16[336,128]{1,0:T(8,128)(2,1)S(1)}, u32[]{:S(2)}, u32[]{:S(2)}) collective-permute-start(bf16[336,128]{1,0:T(8,128)(2,1)S(1)} %get-tuple-element.22), channel_id=1, source_target_pairs={{0,1},{1,0},{2,3},{3,2},{4,5},{5,4},{6,7},{7,6},{8,9},{9,8},{10,11... | collective-permute-start | bytes 258056 | tf_op jit(solution)/shard_map/ppermute | solution.py:93
  18.6 20.6 %collective-permute-start.8 = (bf16[224,1024]{1,0:T(8,128)(2,1)S(1)}, bf16[224,1024]{1,0:T(8,128)(2,1)S(1)}, u32[]{:S(2)}, u32[]{:S(2)}) collective-permute-start(bf16[224,1024]{1,0:T(8,128)(2,1)S(1)} %get-tuple-element.25.refs_0_), channel_id=1, source_target_pairs={{0,8},{8,0},{16,24},{24,16},{1,9},{9,1},{17,25},{25,17},{2,10},{10... | collective-permute-start | bytes 1376264 | tf_op jit(solution)/shard_map/ppermute | solution.py:93
  18.6 20.6 %collective-permute-start.9 = (bf16[224,1024]{1,0:T(8,128)(2,1)S(1)}, bf16[224,1024]{1,0:T(8,128)(2,1)S(1)}, u32[]{:S(2)}, u32[]{:S(2)}) collective-permute-start(bf16[224,1024]{1,0:T(8,128)(2,1)S(1)} %collective-permute-done.7.refs_1_), channel_id=1, source_target_pairs={{0,8},{8,0},{16,24},{24,16},{1,9},{9,1},{17,25},{25,17},{2,10},{10... | collective-permute-start | bytes 1376264 | tf_op jit(solution)/shard_map/ppermute | solution.py:93
  26.9 12.3 %copy-start = (bf16[1,112,1024]{2,1,0:T(8,128)(2,1)S(1)}, bf16[1,112,1024]{2,1,0:T(8,128)(2,1)}, u32[]{:S(2)}) copy-start(bf16[1,112,1024]{2,1,0:T(8,128)(2,1)} %param.9) | copy-start | bytes 688132

commit v13 on v9

--- a/solution.py
+++ b/solution.py
@@ -80,10 +80,10 @@
         ]
         top = functools.reduce(jnp.maximum, scores)
         weights = [jnp.exp2((score - top) * EXP2_SCALE) for score in scores]
-        total = sum(weights[1:], weights[0])
+        inverse = 1.0 / sum(weights[1:], weights[0])
         mixed = None
         for weight, ref in zip(weights, pair_refs):
-            rounded = (weight / total).astype(jnp.bfloat16).astype(jnp.float32)
+            rounded = (weight * inverse).astype(jnp.bfloat16).astype(jnp.float32)
             term = rounded * ref[rows : 2 * rows, lanes].astype(jnp.float32)
             mixed = term if mixed is None else mixed + term
         o_cross = mixed.astype(jnp.bfloat16).astype(jnp.float32)
@@ -145,7 +145,7 @@
         name="self_attention",
     )(*moved)
     back = lax.all_to_all(own_heads, "ctx", split_axis=0, concat_axis=0, tiled=True)
-    return back, pair, (pair, moved)
+    return back, pair, (pair, moved[:2])
 
 
 def shared_attention(q, k, v, ctx_size):

time: 42.1 us -> 42.2 us (level)
  blocking collectives: 12.6 us -> 11.5 us
  starting transfers between devices: 17.4 us -> 18.4 us
    all_to_all x1, blocking collectives: 12.6 us -> 11.5 us  [split_attention(): lax.all_to_all(own_heads, 'ctx', split_axis=0, concat_axis=0, tiled=True)]
    ppermute x9, starting transfers between devices: 17.4 us -> 18.4 us  [swap(): lax.ppermute(array, axis_name, [(i, i ^ partner) for i in range(axis_size)])]
  transfers between devices with their start and end apart: 9 -> 9, of which waited for: 2 -> 3; matrix products, arithmetic and copies ran while one was open for 0% -> 0% of each run, Pallas kernels for 4% -> 4%
where the time goes in v13:
time: 42.2 us; the launch traced here: 42 us
  starting transfers between devices  18.4 us (44%)
  blocking collectives  11.5 us (27%)
  waiting for transfers between devices  7.17 us (17%)
  Pallas kernels  4.87 us (12%)
    ppermute x9, starting transfers between devices, swap(): lax.ppermute(array, axis_name, [(i, i ^ partner) for i in range(axis_size)])  18.4 us
    all_to_all x1, blocking collectives, split_attention(): lax.all_to_all(own_heads, 'ctx', split_axis=0, concat_axis=0, tiled=True)  11.5 us
    ppermute x9, waiting for transfers between devices, swap(): lax.ppermute(array, axis_name, [(i, i ^ partner) for i in range(axis_size)])  7.17 us
    pallas_call x1, Pallas kernels, body(): pl.pallas_call(functools.partial(cross_kernel, heads), out_shape=jax.Shap...  1.69 us
    pallas_call x1, Pallas kernels, split_attention(): pl.pallas_call(functools.partial(pack_kernel, far), out_shape=[block] * l...  1.61 us
    pallas_call x1, Pallas kernels, split_attention(): pl.pallas_call(functools.partial(packed_attention_kernel, far, rows), out...  1.57 us
  transfers between devices with their start and end apart: 9, of which 3 were waited for; matrix products, arithmetic and copies ran while one was open for 0% of the time, Pallas kernels for 4%

profile of v13, /device:TPU:0, one launch (start us, length us, event | category | flops | bytes accessed | tf_op | source)
XLA Modules:
  0.0 42.0 jit_solution(15766212608464194855)
XLA Ops:
  0.0 1.6 %pack_qkv.1 = (bf16[336,128]{1,0:T(8,128)(2,1)S(1)}, bf16[336,128]{1,0:T(8,128)(2,1)S(1)}, bf16[336,128]{1,0:T(8,128)(2,1)S(1)}, bf16[336,128]{1,0:T(8,128)(2,1)...) custom-call(bf16[112,1024]{1,0:T(8,128)(2,1)} %bitcast.10, ...), custom_call_target="tpu_custom_call" | custom-call | tf_op jit(solution)/shard_map/pack_qkv/pallas_call | solution.py:120
  1.6 3.0 %collective-permute-start.6 = (bf16[224,1024]{1,0:T(8,128)(2,1)S(1)}, bf16[224,1024]{1,0:T(8,128)(2,1)S(1)}, u32[]{:S(2)}, u32[]{:S(2)}) collective-permute-start(bf16[224,1024]{1,0:T(8,128)(2,1)S(1)} %get-tuple-element.23.refs_0_), channel_id=1, source_target_pairs={{0,16},{8,24},{16,0},{24,8},{1,17},{9,25},{17,1},{25,9},{2,18},{10... | collective-permute-start | bytes 1376264 | tf_op jit(solution)/shard_map/ppermute | solution.py:98
  4.7 1.5 %collective-permute-start.4 = (bf16[2,336,128]{2,1,0:T(8,128)(2,1)S(1)}, bf16[2,336,128]{2,1,0:T(8,128)(2,1)S(1)}, u32[]{:S(2)}, u32[]{:S(2)}) collective-permute-start(bf16[2,336,128]{2,1,0:T(8,128)(2,1)S(1)} %get-tuple-element.19), channel_id=1, source_target_pairs={{0,1},{1,0},{2,3},{3,2},{4,5},{5,4},{6,7},{7,6},{8,9},{9,8},{10,11... | collective-permute-start | bytes 516104 | tf_op jit(solution)/shard_map/ppermute | solution.py:98
  6.1 3.6 %collective-permute-start = (bf16[336,128]{1,0:T(8,128)(2,1)S(1)}, bf16[336,128]{1,0:T(8,128)(2,1)S(1)}, u32[]{:S(2)}, u32[]{:S(2)}) collective-permute-start(bf16[336,128]{1,0:T(8,128)(2,1)S(1)} %get-tuple-element.15), channel_id=1, source_target_pairs={{0,7},{1,6},{2,5},{3,4},{4,3},{5,2},{6,1},{7,0},{8,15},{9,14},{10,... | collective-permute-start | bytes 258056 | tf_op jit(solution)/shard_map/ppermute | solution.py:98
  9.7 0.8 %collective-permute-done.4.refs_4_ = bf16[2,336,128]{2,1,0:T(8,128)(2,1)S(1)} collective-permute-done((bf16[2,336,128]{2,1,0:T(8,128)(2,1)S(1)}, bf16[2,336,128]{2,1,0:T(8,128)(2,1)S(1)}, u32[]{:S(2)}, u32[]{:S(2)}) %collective-permute-start.4) | collective-permute-done | bytes 172064 | tf_op jit(solution)/shard_map/ppermute | solution.py:98
  10.5 3.3 %collective-permute-start.5 = (bf16[2,336,128]{2,1,0:T(8,128)(2,1)S(1)}, bf16[2,336,128]{2,1,0:T(8,128)(2,1)S(1)}, u32[]{:S(2)}, u32[]{:S(2)}) collective-permute-start(bf16[2,336,128]{2,1,0:T(8,128)(2,1)S(1)} %pad_maximum_fusion), channel_id=1, source_target_pairs={{0,2},{1,3},{2,0},{3,1},{4,6},{5,7},{6,4},{7,5},{8,10},{9,11},{10,... | collective-permute-start | bytes 516104 | tf_op jit(solution)/shard_map/ppermute | solution.py:98
  13.8 2.1 %collective-permute-start.1 = (bf16[336,128]{1,0:T(8,128)(2,1)S(1)}, bf16[336,128]{1,0:T(8,128)(2,1)S(1)}, u32[]{:S(2)}, u32[]{:S(2)}) collective-permute-start(bf16[336,128]{1,0:T(8,128)(2,1)S(1)} %get-tuple-element.16), channel_id=1, source_target_pairs={{0,6},{1,7},{2,4},{3,5},{4,2},{5,3},{6,0},{7,1},{8,14},{9,15},{10,... | collective-permute-start | bytes 258056 | tf_op jit(solution)/shard_map/ppermute | solution.py:98
  15.9 0.7 %collective-permute-start.2 = (bf16[336,128]{1,0:T(8,128)(2,1)S(1)}, bf16[336,128]{1,0:T(8,128)(2,1)S(1)}, u32[]{:S(2)}, u32[]{:S(2)}) collective-permute-start(bf16[336,128]{1,0:T(8,128)(2,1)S(1)} %get-tuple-element.17), channel_id=1, source_target_pairs={{0,5},{1,4},{2,7},{3,6},{4,1},{5,0},{6,3},{7,2},{8,13},{9,12},{10,... | collective-permute-start | bytes 258056 | tf_op jit(solution)/shard_map/ppermute | solution.py:98
  16.6 0.0 collective-permute-done.refs_0_
  16.6 3.7 %collective-permute-start.3 = (bf16[336,128]{1,0:T(8,128)(2,1)S(1)}, bf16[336,128]{1,0:T(8,128)(2,1)S(1)}, u32[]{:S(2)}, u32[]{:S(2)}) collective-permute-start(bf16[336,128]{1,0:T(8,128)(2,1)S(1)} %get-tuple-element.18), channel_id=1, source_target_pairs={{0,4},{1,5},{2,6},{3,7},{4,0},{5,1},{6,2},{7,3},{8,12},{9,13},{10,... | collective-permute-start | bytes 258056 | tf_op jit(solution)/shard_map/ppermute | solution.py:98
  20.3 1.9 %collective-permute-done.1.refs_1_ = bf16[336,128]{1,0:T(8,128)(2,1)S(1)} collective-permute-done((bf16[336,128]{1,0:T(8,128)(2,1)S(1)}, bf16[336,128]{1,0:T(8,128)(2,1)S(1)}, u32[]{:S(2)}, u32[]{:S(2)}) %collective-permute-start.1) | collective-permute-done | bytes 86048 | tf_op jit(solution)/shard_map/ppermute | solution.py:98
  22.2 0.0 collective-permute-done.6.refs_1_
  22.2 0.0 collective-permute-start.7
  22.2 0.5 %collective-permute-start.8 = (bf16[224,1024]{1,0:T(8,128)(2,1)S(1)}, bf16[224,1024]{1,0:T(8,128)(2,1)S(1)}, u32[]{:S(2)}, u32[]{:S(2)}) collective-permute-start(bf16[224,1024]{1,0:T(8,128)(2,1)S(1)} %collective-permute-done.6.refs_1_), channel_id=1, source_target_pairs={{0,8},{8,0},{16,24},{24,16},{1,9},{9,1},{17,25},{25,17},{2,10},{10... | collective-permute-start | bytes 1376264 | tf_op jit(solution)/shard_map/ppermute | solution.py:98
  22.7 4.5 %collective-permute-done.2.refs_2_ = bf16[336,128]{1,0:T(8,128)(2,1)S(1)} collective-permute-done((bf16[336,128]{1,0:T(8,128)(2,1)S(1)}, bf16[336,128]{1,0:T(8,128)(2,1)S(1)}, u32[]{:S(2)}, u32[]{:S(2)}) %collective-permute-start.2) | collective-permute-done | bytes 86048 | tf_op jit(solution)/shard_map/ppermute | solution.py:98
  27.2 0.0 collective-permute-done.3.refs_3_
  27.2 0.0 collective-permute-done.5.refs_5_
  27.2 1.6 %self_attention.1 = bf16[8,112,128]{2,1,0:T(8,128)(2,1)S(1)} custom-call(bf16[336,128]{1,0:T(8,128)(2,1)S(1)} %collective-permute-done.refs_0_, bf16[336,128]{1,0:T(8,128)(2,1)S(1)} %collective-permute-done.1.refs_1_, bf16[336,128]{1,0:T(8,128)(2,1)S(1)} %collective-permute-done.2.refs_2_, bf16[336,128]{1,0:T(8,128)(2,1)S(1)} %collective-permute-done.3.refs_3_, ...), custom_call_target="tpu_custom_call" | custom-call | flops 411041792 | bytes 917504 | tf_op jit(solution)/shard_map/self_attention/pallas_call | solution.py:134
  28.8 0.0 copy-start
  28.8 11.5 %all_to_all.5.o_ref = bf16[8,112,128]{2,1,0:T(8,128)(2,1)S(1)} all-to-all(bf16[8,112,128]{2,1,0:T(8,128)(2,1)S(1)} %self_attention.1), channel_id=1, replica_groups=mesh['view'=4,'ctx'=8] {'ctx'}, dimensions={0} | all-to-all | bytes 458752 | tf_op jit(solution)/shard_map/all_to_all | solution.py:147
  40.3 0.0 collective-permute-done.7.refs_2_
  40.3 0.0 collective-permute-done.8.refs_3_
  40.3 0.0 copy-done
  40.3 1.7 %cross_view.1 = bf16[112,1024]{1,0:T(8,128)(2,1)} custom-call(bf16[8,112,128]{2,1,0:T(8,128)(2,1)S(1)} %all_to_all.5.o_ref, bf16[112,1024]{1,0:T(8,128)(2,1)S(1)} %bitcast.8, bf16[224,1024]{1,0:T(8,128)(2,1)S(1)} %get-tuple-element.23.refs_0_, bf16[224,1024]{1,0:T(8,128)(2,1)S(1)} %collective-permute-done.6.refs_1_, ...), custom_call_target="tpu_custom_call" | custom-call | tf_op jit(solution)/shard_map/cross_view/pallas_call | solution.py:198
  (2 shorter events, 0.0 us)
Async XLA Ops:
  1.6 20.6 %collective-permute-start.6 = (bf16[224,1024]{1,0:T(8,128)(2,1)S(1)}, bf16[224,1024]{1,0:T(8,128)(2,1)S(1)}, u32[]{:S(2)}, u32[]{:S(2)}) collective-permute-start(bf16[224,1024]{1,0:T(8,128)(2,1)S(1)} %get-tuple-element.23.refs_0_), channel_id=1, source_target_pairs={{0,16},{8,24},{16,0},{24,8},{1,17},{9,25},{17,1},{25,9},{2,18},{10... | collective-permute-start | bytes 1376264 | tf_op jit(solution)/shard_map/ppermute | solution.py:98
  4.7 5.8 %collective-permute-start.4 = (bf16[2,336,128]{2,1,0:T(8,128)(2,1)S(1)}, bf16[2,336,128]{2,1,0:T(8,128)(2,1)S(1)}, u32[]{:S(2)}, u32[]{:S(2)}) collective-permute-start(bf16[2,336,128]{2,1,0:T(8,128)(2,1)S(1)} %get-tuple-element.19), channel_id=1, source_target_pairs={{0,1},{1,0},{2,3},{3,2},{4,5},{5,4},{6,7},{7,6},{8,9},{9,8},{10,11... | collective-permute-start | bytes 516104 | tf_op jit(solution)/shard_map/ppermute | solution.py:98
  6.1 10.5 %collective-permute-start = (bf16[336,128]{1,0:T(8,128)(2,1)S(1)}, bf16[336,128]{1,0:T(8,128)(2,1)S(1)}, u32[]{:S(2)}, u32[]{:S(2)}) collective-permute-start(bf16[336,128]{1,0:T(8,128)(2,1)S(1)} %get-tuple-element.15), channel_id=1, source_target_pairs={{0,7},{1,6},{2,5},{3,4},{4,3},{5,2},{6,1},{7,0},{8,15},{9,14},{10,... | collective-permute-start | bytes 258056 | tf_op jit(solution)/shard_map/ppermute | solution.py:98
  10.5 16.7 %collective-permute-start.5 = (bf16[2,336,128]{2,1,0:T(8,128)(2,1)S(1)}, bf16[2,336,128]{2,1,0:T(8,128)(2,1)S(1)}, u32[]{:S(2)}, u32[]{:S(2)}) collective-permute-start(bf16[2,336,128]{2,1,0:T(8,128)(2,1)S(1)} %pad_maximum_fusion), channel_id=1, source_target_pairs={{0,2},{1,3},{2,0},{3,1},{4,6},{5,7},{6,4},{7,5},{8,10},{9,11},{10,... | collective-permute-start | bytes 516104 | tf_op jit(solution)/shard_map/ppermute | solution.py:98
  13.8 8.4 %collective-permute-start.1 = (bf16[336,128]{1,0:T(8,128)(2,1)S(1)}, bf16[336,128]{1,0:T(8,128)(2,1)S(1)}, u32[]{:S(2)}, u32[]{:S(2)}) collective-permute-start(bf16[336,128]{1,0:T(8,128)(2,1)S(1)} %get-tuple-element.16), channel_id=1, source_target_pairs={{0,6},{1,7},{2,4},{3,5},{4,2},{5,3},{6,0},{7,1},{8,14},{9,15},{10,... | collective-permute-start | bytes 258056 | tf_op jit(solution)/shard_map/ppermute | solution.py:98
  15.9 11.4 %collective-permute-start.2 = (bf16[336,128]{1,0:T(8,128)(2,1)S(1)}, bf16[336,128]{1,0:T(8,128)(2,1)S(1)}, u32[]{:S(2)}, u32[]{:S(2)}) collective-permute-start(bf16[336,128]{1,0:T(8,128)(2,1)S(1)} %get-tuple-element.17), channel_id=1, source_target_pairs={{0,5},{1,4},{2,7},{3,6},{4,1},{5,0},{6,3},{7,2},{8,13},{9,12},{10,... | collective-permute-start | bytes 258056 | tf_op jit(solution)/shard_map/ppermute | solution.py:98
  16.6 10.6 %collective-permute-start.3 = (bf16[336,128]{1,0:T(8,128)(2,1)S(1)}, bf16[336,128]{1,0:T(8,128)(2,1)S(1)}, u32[]{:S(2)}, u32[]{:S(2)}) collective-permute-start(bf16[336,128]{1,0:T(8,128)(2,1)S(1)} %get-tuple-element.18), channel_id=1, source_target_pairs={{0,4},{1,5},{2,6},{3,7},{4,0},{5,1},{6,2},{7,3},{8,12},{9,13},{10,... | collective-permute-start | bytes 258056 | tf_op jit(solution)/shard_map/ppermute | solution.py:98
  22.2 18.1 %collective-permute-start.7 = (bf16[224,1024]{1,0:T(8,128)(2,1)S(1)}, bf16[224,1024]{1,0:T(8,128)(2,1)S(1)}, u32[]{:S(2)}, u32[]{:S(2)}) collective-permute-start(bf16[224,1024]{1,0:T(8,128)(2,1)S(1)} %get-tuple-element.23.refs_0_), channel_id=1, source_target_pairs={{0,8},{8,0},{16,24},{24,16},{1,9},{9,1},{17,25},{25,17},{2,10},{10... | collective-permute-start | bytes 1376264 | tf_op jit(solution)/shard_map/ppermute | solution.py:98
  22.2 18.1 %collective-permute-start.8 = (bf16[224,1024]{1,0:T(8,128)(2,1)S(1)}, bf16[224,1024]{1,0:T(8,128)(2,1)S(1)}, u32[]{:S(2)}, u32[]{:S(2)}) collective-permute-start(bf16[224,1024]{1,0:T(8,128)(2,1)S(1)} %collective-permute-done.6.refs_1_), channel_id=1, source_target_pairs={{0,8},{8,0},{16,24},{24,16},{1,9},{9,1},{17,25},{25,17},{2,10},{10... | collective-permute-start | bytes 1376264 | tf_op jit(solution)/shard_map/ppermute | solution.py:98
  28.8 11.5 %copy-start = (bf16[1,112,1024]{2,1,0:T(8,128)(2,1)S(1)}, bf16[1,112,1024]{2,1,0:T(8,128)(2,1)}, u32[]{:S(2)}) copy-start(bf16[1,112,1024]{2,1,0:T(8,128)(2,1)} %param.9) | copy-start | bytes 688132

commit v14 on v12

--- a/solution.py
+++ b/solution.py
@@ -106,7 +106,7 @@
 def split_attention(q, k, v, k_cross, v_cross, ctx_size):
     rows, width = q.shape
     heads = width // HEAD
-    partners = (3, 2, 7, 6, 5, 4, 1, 0)
+    partners = (3, 2, 1, 7, 6, 5, 4, 0)
     vmem = pl.BlockSpec(memory_space=pltpu.VMEM)
     hbm = pl.BlockSpec(memory_space=pltpu.HBM)
     sources = [pltpu.with_memory_space_constraint(x, pltpu.HBM) for x in (q, k, v, k_cross, v_cross)]

time: 41.1 us -> 42 us (1.022)
  waiting for transfers between devices: 7.21 us -> 8.06 us
    ppermute x10, waiting for transfers between devices: 7.21 us -> 8.06 us  [swap(): lax.ppermute(array, axis_name, [(i, i ^ partner) for i in range(axis_size)])]
where the time goes in v14:
time: 42 us; the launch traced here: 41.8 us
  starting transfers between devices  16.8 us (40%)
  blocking collectives  12 us (29%)
  waiting for transfers between devices  8.06 us (19%)
  Pallas kernels  4.85 us (12%)
    ppermute x10, starting transfers between devices, swap(): lax.ppermute(array, axis_name, [(i, i ^ partner) for i in range(axis_size)])  16.8 us
    all_to_all x1, blocking collectives, split_attention(): back = lax.all_to_all(own, 'ctx', split_axis=0, concat_axis=0, tiled=True)  12 us
    ppermute x10, waiting for transfers between devices, swap(): lax.ppermute(array, axis_name, [(i, i ^ partner) for i in range(axis_size)])  8.06 us
    pallas_call x1, Pallas kernels, body(): pl.pallas_call(functools.partial(cross_kernel, heads), out_shape=jax.Shap...  1.68 us
    pallas_call x1, Pallas kernels, split_attention(): pl.pallas_call(functools.partial(pack_kernel, partners), out_shape=[block...  1.61 us
    pallas_call x1, Pallas kernels, split_attention(): pl.pallas_call(functools.partial(packed_attention_kernel, partners, rows,...  1.57 us
  transfers between devices with their start and end apart: 10, of which 3 were waited for; matrix products, arithmetic and copies ran while one was open for 0% of the time, Pallas kernels for 4%

profile of v14, /device:TPU:0, one launch (start us, length us, event | category | flops | bytes accessed | tf_op | source)
XLA Modules:
  0.0 41.8 jit_solution(7661426337365733369)
XLA Ops:
  0.0 1.6 %pack_qkv.1 = (bf16[336,128]{1,0:T(8,128)(2,1)S(1)}, bf16[336,128]{1,0:T(8,128)(2,1)S(1)}, bf16[336,128]{1,0:T(8,128)(2,1)S(1)}, bf16[336,128]{1,0:T(8,128)(2,1)...) custom-call(bf16[112,1024]{1,0:T(8,128)(2,1)} %bitcast.8, ...), custom_call_target="tpu_custom_call" | custom-call | tf_op jit(solution)/shard_map/pack_qkv/pallas_call | solution.py:114
  1.6 3.0 %collective-permute-start.7 = (bf16[224,1024]{1,0:T(8,128)(2,1)S(1)}, bf16[224,1024]{1,0:T(8,128)(2,1)S(1)}, u32[]{:S(2)}, u32[]{:S(2)}) collective-permute-start(bf16[224,1024]{1,0:T(8,128)(2,1)S(1)} %get-tuple-element.25.refs_0_), channel_id=1, source_target_pairs={{0,16},{8,24},{16,0},{24,8},{1,17},{9,25},{17,1},{25,9},{2,18},{10... | collective-permute-start | bytes 1376264 | tf_op jit(solution)/shard_map/ppermute | solution.py:93
  4.7 2.5 %collective-permute-start = (bf16[336,128]{1,0:T(8,128)(2,1)S(1)}, bf16[336,128]{1,0:T(8,128)(2,1)S(1)}, u32[]{:S(2)}, u32[]{:S(2)}) collective-permute-start(bf16[336,128]{1,0:T(8,128)(2,1)S(1)} %get-tuple-element.16), channel_id=1, source_target_pairs={{0,3},{1,2},{2,1},{3,0},{4,7},{5,6},{6,5},{7,4},{8,11},{9,10},{10,... | collective-permute-start | bytes 258056 | tf_op jit(solution)/shard_map/ppermute | solution.py:93
  7.2 0.4 %collective-permute-start.1 = (bf16[336,128]{1,0:T(8,128)(2,1)S(1)}, bf16[336,128]{1,0:T(8,128)(2,1)S(1)}, u32[]{:S(2)}, u32[]{:S(2)}) collective-permute-start(bf16[336,128]{1,0:T(8,128)(2,1)S(1)} %get-tuple-element.17), channel_id=1, source_target_pairs={{0,2},{1,3},{2,0},{3,1},{4,6},{5,7},{6,4},{7,5},{8,10},{9,11},{10,... | collective-permute-start | bytes 258056 | tf_op jit(solution)/shard_map/ppermute | solution.py:93
  7.6 0.5 %collective-permute-start.2 = (bf16[336,128]{1,0:T(8,128)(2,1)S(1)}, bf16[336,128]{1,0:T(8,128)(2,1)S(1)}, u32[]{:S(2)}, u32[]{:S(2)}) collective-permute-start(bf16[336,128]{1,0:T(8,128)(2,1)S(1)} %get-tuple-element.18), channel_id=1, source_target_pairs={{0,1},{1,0},{2,3},{3,2},{4,5},{5,4},{6,7},{7,6},{8,9},{9,8},{10,11... | collective-permute-start | bytes 258056 | tf_op jit(solution)/shard_map/ppermute | solution.py:93
  8.1 4.5 %collective-permute-start.3 = (bf16[336,128]{1,0:T(8,128)(2,1)S(1)}, bf16[336,128]{1,0:T(8,128)(2,1)S(1)}, u32[]{:S(2)}, u32[]{:S(2)}) collective-permute-start(bf16[336,128]{1,0:T(8,128)(2,1)S(1)} %get-tuple-element.19), channel_id=1, source_target_pairs={{0,7},{1,6},{2,5},{3,4},{4,3},{5,2},{6,1},{7,0},{8,15},{9,14},{10,... | collective-permute-start | bytes 258056 | tf_op jit(solution)/shard_map/ppermute | solution.py:93
  12.7 0.0 collective-permute-done.refs_0_
  12.7 1.5 %collective-permute-start.4 = (bf16[336,128]{1,0:T(8,128)(2,1)S(1)}, bf16[336,128]{1,0:T(8,128)(2,1)S(1)}, u32[]{:S(2)}, u32[]{:S(2)}) collective-permute-start(bf16[336,128]{1,0:T(8,128)(2,1)S(1)} %get-tuple-element.20), channel_id=1, source_target_pairs={{0,6},{1,7},{2,4},{3,5},{4,2},{5,3},{6,0},{7,1},{8,14},{9,15},{10,... | collective-permute-start | bytes 258056 | tf_op jit(solution)/shard_map/ppermute | solution.py:93
  14.2 0.0 collective-permute-done.1.refs_1_
  14.2 1.1 %collective-permute-start.5 = (bf16[336,128]{1,0:T(8,128)(2,1)S(1)}, bf16[336,128]{1,0:T(8,128)(2,1)S(1)}, u32[]{:S(2)}, u32[]{:S(2)}) collective-permute-start(bf16[336,128]{1,0:T(8,128)(2,1)S(1)} %get-tuple-element.21), channel_id=1, source_target_pairs={{0,5},{1,4},{2,7},{3,6},{4,1},{5,0},{6,3},{7,2},{8,13},{9,12},{10,... | collective-permute-start | bytes 258056 | tf_op jit(solution)/shard_map/ppermute | solution.py:93
  15.3 0.0 collective-permute-done.2.refs_2_
  15.3 2.7 %collective-permute-start.6 = (bf16[336,128]{1,0:T(8,128)(2,1)S(1)}, bf16[336,128]{1,0:T(8,128)(2,1)S(1)}, u32[]{:S(2)}, u32[]{:S(2)}) collective-permute-start(bf16[336,128]{1,0:T(8,128)(2,1)S(1)} %get-tuple-element.22), channel_id=1, source_target_pairs={{0,4},{1,5},{2,6},{3,7},{4,0},{5,1},{6,2},{7,3},{8,12},{9,13},{10,... | collective-permute-start | bytes 258056 | tf_op jit(solution)/shard_map/ppermute | solution.py:93
  17.9 0.0 collective-permute-done.3.refs_3_
  18.0 0.0 collective-permute-done.7.refs_1_
  18.0 0.0 collective-permute-start.8
  18.0 0.5 %collective-permute-start.9 = (bf16[224,1024]{1,0:T(8,128)(2,1)S(1)}, bf16[224,1024]{1,0:T(8,128)(2,1)S(1)}, u32[]{:S(2)}, u32[]{:S(2)}) collective-permute-start(bf16[224,1024]{1,0:T(8,128)(2,1)S(1)} %collective-permute-done.7.refs_1_), channel_id=1, source_target_pairs={{0,8},{8,0},{16,24},{24,16},{1,9},{9,1},{17,25},{25,17},{2,10},{10... | collective-permute-start | bytes 1376264 | tf_op jit(solution)/shard_map/ppermute | solution.py:93
  18.5 1.2 %collective-permute-done.4.refs_4_ = bf16[336,128]{1,0:T(8,128)(2,1)S(1)} collective-permute-done((bf16[336,128]{1,0:T(8,128)(2,1)S(1)}, bf16[336,128]{1,0:T(8,128)(2,1)S(1)}, u32[]{:S(2)}, u32[]{:S(2)}) %collective-permute-start.4) | collective-permute-done | bytes 86048 | tf_op jit(solution)/shard_map/ppermute | solution.py:93
  19.7 6.1 %collective-permute-done.5.refs_5_ = bf16[336,128]{1,0:T(8,128)(2,1)S(1)} collective-permute-done((bf16[336,128]{1,0:T(8,128)(2,1)S(1)}, bf16[336,128]{1,0:T(8,128)(2,1)S(1)}, u32[]{:S(2)}, u32[]{:S(2)}) %collective-permute-start.5) | collective-permute-done | bytes 86048 | tf_op jit(solution)/shard_map/ppermute | solution.py:93
  25.8 0.7 %collective-permute-done.6.refs_6_ = bf16[336,128]{1,0:T(8,128)(2,1)S(1)} collective-permute-done((bf16[336,128]{1,0:T(8,128)(2,1)S(1)}, bf16[336,128]{1,0:T(8,128)(2,1)S(1)}, u32[]{:S(2)}, u32[]{:S(2)}) %collective-permute-start.6) | collective-permute-done | bytes 86048 | tf_op jit(solution)/shard_map/ppermute | solution.py:93
  26.5 1.6 %self_attention.1 = bf16[8,112,128]{2,1,0:T(8,128)(2,1)S(1)} custom-call(bf16[336,128]{1,0:T(8,128)(2,1)S(1)} %collective-permute-done.refs_0_, bf16[336,128]{1,0:T(8,128)(2,1)S(1)} %collective-permute-done.1.refs_1_, bf16[336,128]{1,0:T(8,128)(2,1)S(1)} %collective-permute-done.2.refs_2_, bf16[336,128]{1,0:T(8,128)(2,1)S(1)} %collective-permute-done.3.refs_3_, ...), custom_call_target="tpu_custom_call" | custom-call | flops 411041792 | bytes 917504 | tf_op jit(solution)/shard_map/self_attention/pallas_call | solution.py:127
  28.1 0.0 copy-start
  28.1 12.0 %all_to_all.5.o_ref = bf16[8,112,128]{2,1,0:T(8,128)(2,1)S(1)} all-to-all(bf16[8,112,128]{2,1,0:T(8,128)(2,1)S(1)} %self_attention.1), channel_id=1, replica_groups=mesh['view'=4,'ctx'=8] {'ctx'}, dimensions={0} | all-to-all | bytes 458752 | tf_op jit(solution)/shard_map/all_to_all | solution.py:140
  40.1 0.0 collective-permute-done.8.refs_2_
  40.1 0.0 collective-permute-done.9.refs_3_
  40.1 0.0 copy-done
  40.1 1.7 %cross_view.1 = bf16[112,1024]{1,0:T(8,128)(2,1)} custom-call(bf16[8,112,128]{2,1,0:T(8,128)(2,1)S(1)} %all_to_all.5.o_ref, bf16[112,1024]{1,0:T(8,128)(2,1)S(1)} %bitcast.7, bf16[224,1024]{1,0:T(8,128)(2,1)S(1)} %get-tuple-element.25.refs_0_, bf16[224,1024]{1,0:T(8,128)(2,1)S(1)} %collective-permute-done.7.refs_1_, ...), custom_call_target="tpu_custom_call" | custom-call | tf_op jit(solution)/shard_map/cross_view/pallas_call | solution.py:191
Async XLA Ops:
  1.6 16.3 %collective-permute-start.7 = (bf16[224,1024]{1,0:T(8,128)(2,1)S(1)}, bf16[224,1024]{1,0:T(8,128)(2,1)S(1)}, u32[]{:S(2)}, u32[]{:S(2)}) collective-permute-start(bf16[224,1024]{1,0:T(8,128)(2,1)S(1)} %get-tuple-element.25.refs_0_), channel_id=1, source_target_pairs={{0,16},{8,24},{16,0},{24,8},{1,17},{9,25},{17,1},{25,9},{2,18},{10... | collective-permute-start | bytes 1376264 | tf_op jit(solution)/shard_map/ppermute | solution.py:93
  4.7 8.0 %collective-permute-start = (bf16[336,128]{1,0:T(8,128)(2,1)S(1)}, bf16[336,128]{1,0:T(8,128)(2,1)S(1)}, u32[]{:S(2)}, u32[]{:S(2)}) collective-permute-start(bf16[336,128]{1,0:T(8,128)(2,1)S(1)} %get-tuple-element.16), channel_id=1, source_target_pairs={{0,3},{1,2},{2,1},{3,0},{4,7},{5,6},{6,5},{7,4},{8,11},{9,10},{10,... | collective-permute-start | bytes 258056 | tf_op jit(solution)/shard_map/ppermute | solution.py:93
  7.2 7.0 %collective-permute-start.1 = (bf16[336,128]{1,0:T(8,128)(2,1)S(1)}, bf16[336,128]{1,0:T(8,128)(2,1)S(1)}, u32[]{:S(2)}, u32[]{:S(2)}) collective-permute-start(bf16[336,128]{1,0:T(8,128)(2,1)S(1)} %get-tuple-element.17), channel_id=1, source_target_pairs={{0,2},{1,3},{2,0},{3,1},{4,6},{5,7},{6,4},{7,5},{8,10},{9,11},{10,... | collective-permute-start | bytes 258056 | tf_op jit(solution)/shard_map/ppermute | solution.py:93
  7.6 7.7 %collective-permute-start.2 = (bf16[336,128]{1,0:T(8,128)(2,1)S(1)}, bf16[336,128]{1,0:T(8,128)(2,1)S(1)}, u32[]{:S(2)}, u32[]{:S(2)}) collective-permute-start(bf16[336,128]{1,0:T(8,128)(2,1)S(1)} %get-tuple-element.18), channel_id=1, source_target_pairs={{0,1},{1,0},{2,3},{3,2},{4,5},{5,4},{6,7},{7,6},{8,9},{9,8},{10,11... | collective-permute-start | bytes 258056 | tf_op jit(solution)/shard_map/ppermute | solution.py:93
  8.1 9.8 %collective-permute-start.3 = (bf16[336,128]{1,0:T(8,128)(2,1)S(1)}, bf16[336,128]{1,0:T(8,128)(2,1)S(1)}, u32[]{:S(2)}, u32[]{:S(2)}) collective-permute-start(bf16[336,128]{1,0:T(8,128)(2,1)S(1)} %get-tuple-element.19), channel_id=1, source_target_pairs={{0,7},{1,6},{2,5},{3,4},{4,3},{5,2},{6,1},{7,0},{8,15},{9,14},{10,... | collective-permute-start | bytes 258056 | tf_op jit(solution)/shard_map/ppermute | solution.py:93
  12.7 7.0 %collective-permute-start.4 = (bf16[336,128]{1,0:T(8,128)(2,1)S(1)}, bf16[336,128]{1,0:T(8,128)(2,1)S(1)}, u32[]{:S(2)}, u32[]{:S(2)}) collective-permute-start(bf16[336,128]{1,0:T(8,128)(2,1)S(1)} %get-tuple-element.20), channel_id=1, source_target_pairs={{0,6},{1,7},{2,4},{3,5},{4,2},{5,3},{6,0},{7,1},{8,14},{9,15},{10,... | collective-permute-start | bytes 258056 | tf_op jit(solution)/shard_map/ppermute | solution.py:93
  14.2 11.6 %collective-permute-start.5 = (bf16[336,128]{1,0:T(8,128)(2,1)S(1)}, bf16[336,128]{1,0:T(8,128)(2,1)S(1)}, u32[]{:S(2)}, u32[]{:S(2)}) collective-permute-start(bf16[336,128]{1,0:T(8,128)(2,1)S(1)} %get-tuple-element.21), channel_id=1, source_target_pairs={{0,5},{1,4},{2,7},{3,6},{4,1},{5,0},{6,3},{7,2},{8,13},{9,12},{10,... | collective-permute-start | bytes 258056 | tf_op jit(solution)/shard_map/ppermute | solution.py:93
  15.3 11.2 %collective-permute-start.6 = (bf16[336,128]{1,0:T(8,128)(2,1)S(1)}, bf16[336,128]{1,0:T(8,128)(2,1)S(1)}, u32[]{:S(2)}, u32[]{:S(2)}) collective-permute-start(bf16[336,128]{1,0:T(8,128)(2,1)S(1)} %get-tuple-element.22), channel_id=1, source_target_pairs={{0,4},{1,5},{2,6},{3,7},{4,0},{5,1},{6,2},{7,3},{8,12},{9,13},{10,... | collective-permute-start | bytes 258056 | tf_op jit(solution)/shard_map/ppermute | solution.py:93
  18.0 22.2 %collective-permute-start.8 = (bf16[224,1024]{1,0:T(8,128)(2,1)S(1)}, bf16[224,1024]{1,0:T(8,128)(2,1)S(1)}, u32[]{:S(2)}, u32[]{:S(2)}) collective-permute-start(bf16[224,1024]{1,0:T(8,128)(2,1)S(1)} %get-tuple-element.25.refs_0_), channel_id=1, source_target_pairs={{0,8},{8,0},{16,24},{24,16},{1,9},{9,1},{17,25},{25,17},{2,10},{10... | collective-permute-start | bytes 1376264 | tf_op jit(solution)/shard_map/ppermute | solution.py:93
  18.0 22.1 %collective-permute-start.9 = (bf16[224,1024]{1,0:T(8,128)(2,1)S(1)}, bf16[224,1024]{1,0:T(8,128)(2,1)S(1)}, u32[]{:S(2)}, u32[]{:S(2)}) collective-permute-start(bf16[224,1024]{1,0:T(8,128)(2,1)S(1)} %collective-permute-done.7.refs_1_), channel_id=1, source_target_pairs={{0,8},{8,0},{16,24},{24,16},{1,9},{9,1},{17,25},{25,17},{2,10},{10... | collective-permute-start | bytes 1376264 | tf_op jit(solution)/shard_map/ppermute | solution.py:93
  28.1 12.0 %copy-start = (bf16[1,112,1024]{2,1,0:T(8,128)(2,1)S(1)}, bf16[1,112,1024]{2,1,0:T(8,128)(2,1)}, u32[]{:S(2)}) copy-start(bf16[1,112,1024]{2,1,0:T(8,128)(2,1)} %param.9) | copy-start | bytes 688132

commit v15 on v14

--- a/solution.py
+++ b/solution.py
@@ -12,12 +12,18 @@
 SCALE = 1.0 / math.sqrt(HEAD)
 EXP2_SCALE = SCALE * math.log2(math.e)
 MIB = 1024 * 1024
+PARTNERS = tuple(zip((7, 6, 5, 3, 4, 2, 1, 0), (3, 2, 1, 7, 6, 5, 4, 0)))
+
+
+def partner_of(orders):
+    core = lax.rem(lax.axis_index("view"), 2)
+    first, second = orders
+    return lax.axis_index("ctx") ^ (first + core * (second - first))
 
 
 def pack_kernel(partners, q_ref, k_ref, v_ref, kc_ref, vc_ref, *refs):
     block_refs, pair_ref, sems = refs[: len(partners)], refs[-2], refs[-1]
     rows = q_ref.shape[0]
-    me = lax.axis_index("ctx")
     copies = []
 
     def start(source, target):
@@ -26,7 +32,7 @@
         copies.append(copy)
 
     for partner, block_ref in zip(partners, block_refs):
-        lanes = pl.ds(pl.multiple_of((me ^ partner) * HEAD, HEAD), HEAD)
+        lanes = pl.ds(pl.multiple_of(partner_of(partner) * HEAD, HEAD), HEAD)
         for part, source in enumerate((q_ref, k_ref, v_ref)):
             start(source.at[:, lanes], block_ref.at[pl.ds(part * rows, rows)])
     for part, source in enumerate((kc_ref, vc_ref)):
@@ -48,14 +54,13 @@
 
 def packed_attention_kernel(partners, rows, group, *refs):
     *in_refs, out_ref = refs
-    me = lax.axis_index("ctx")
     keys = jnp.concatenate([ref[rows : 2 * rows] for ref in in_refs], axis=0)
     values = jnp.concatenate([ref[2 * rows : 3 * rows] for ref in in_refs], axis=0)
     for first in range(0, len(in_refs), group):
         query = jnp.concatenate([ref[0:rows] for ref in in_refs[first : first + group]], axis=0)
         mixed = attend(query, keys, values)
         for i in range(group):
-            out_ref[me ^ partners[first + i]] = mixed[i * rows : (i + 1) * rows]
+            out_ref[partner_of(partners[first + i])] = mixed[i * rows : (i + 1) * rows]
 
 
 def attention_kernel(q_ref, k_ref, v_ref, out_ref):
@@ -93,6 +98,15 @@
     return lax.ppermute(array, axis_name, [(i, i ^ partner) for i in range(axis_size)])
 
 
+def exchange(array, view_count, ctx_size, orders):
+    pairs = [
+        (view * ctx_size + i, view * ctx_size + (i ^ orders[view % 2]))
+        for view in range(view_count)
+        for i in range(ctx_size)
+    ]
+    return lax.ppermute(array, ("view", "ctx"), pairs)
+
+
 def gather_views(array, view_count, *after):
     gathered = [array]
     step = view_count // 2
@@ -103,10 +117,10 @@
     return gathered
 
 
-def split_attention(q, k, v, k_cross, v_cross, ctx_size):
+def split_attention(q, k, v, k_cross, v_cross, view_count, ctx_size):
     rows, width = q.shape
     heads = width // HEAD
-    partners = (3, 2, 1, 7, 6, 5, 4, 0)
+    partners = PARTNERS
     vmem = pl.BlockSpec(memory_space=pltpu.VMEM)
     hbm = pl.BlockSpec(memory_space=pltpu.HBM)
     sources = [pltpu.with_memory_space_constraint(x, pltpu.HBM) for x in (q, k, v, k_cross, v_cross)]
@@ -121,7 +135,7 @@
         name="pack_qkv",
     )(*sources)
     moved = [
-        swap(data, "ctx", ctx_size, partner) if partner else data
+        exchange(data, view_count, ctx_size, partner) if any(partner) else data
         for partner, data in zip(partners, blocks)
     ]
     own = pl.pallas_call(
@@ -180,7 +194,7 @@
     heads = width // HEAD
     if ctx_size == heads == 8:
         o_self, pair, after = split_attention(
-            q_self[0], k_self[0], v_self[0], k_cross[0], v_cross[0], ctx_size
+            q_self[0], k_self[0], v_self[0], k_cross[0], v_cross[0], view_count, ctx_size
         )
     else:
         o_self = shared_attention(q_self[0], k_self[0], v_self[0], ctx_size)

time: 42 us -> 42.3 us (level)
  starting transfers between devices: 16.8 us -> 17.9 us
  waiting for transfers between devices: 8.06 us -> 7.3 us
    ppermute x0 -> x7, starting transfers between devices: none -> 14.3 us  [exchange(): return lax.ppermute(array, ('view', 'ctx'), pairs)]
    ppermute x10 -> x3, starting transfers between devices: 16.8 us -> 3.54 us  [swap(): lax.ppermute(array, axis_name, [(i, i ^ partner) for i in range(axis_size)])]
    ppermute x10 -> x3, waiting for transfers between devices: 8.06 us -> 0.01 us  [swap(): lax.ppermute(array, axis_name, [(i, i ^ partner) for i in range(axis_size)])]
    ppermute x0 -> x7, waiting for transfers between devices: none -> 7.29 us  [exchange(): return lax.ppermute(array, ('view', 'ctx'), pairs)]
where the time goes in v15:
time: 42.3 us; the launch traced here: 42.1 us
  starting transfers between devices  17.9 us (42%)
  blocking collectives  12.1 us (29%)
  waiting for transfers between devices  7.3 us (17%)
  Pallas kernels  4.86 us (11%)
    ppermute x7, starting transfers between devices, exchange(): return lax.ppermute(array, ('view', 'ctx'), pairs)  14.3 us
    all_to_all x1, blocking collectives, split_attention(): back = lax.all_to_all(own, 'ctx', split_axis=0, concat_axis=0, tiled=True)  12.1 us
    ppermute x7, waiting for transfers between devices, exchange(): return lax.ppermute(array, ('view', 'ctx'), pairs)  7.29 us
    ppermute x3, starting transfers between devices, swap(): lax.ppermute(array, axis_name, [(i, i ^ partner) for i in range(axis_size)])  3.54 us
    pallas_call x1, Pallas kernels, body(): pl.pallas_call(functools.partial(cross_kernel, heads), out_shape=jax.Shap...  1.68 us
    pallas_call x1, Pallas kernels, split_attention(): pl.pallas_call(functools.partial(pack_kernel, partners), out_shape=[block...  1.61 us
    pallas_call x1, Pallas kernels, split_attention(): pl.pallas_call(functools.partial(packed_attention_kernel, partners, rows,...  1.57 us
  transfers between devices with their start and end apart: 10, of which 3 were waited for; matrix products, arithmetic and copies ran while one was open for 0% of the time, Pallas kernels for 4%

profile of v15, /device:TPU:0, one launch (start us, length us, event | category | flops | bytes accessed | tf_op | source)
XLA Modules:
  0.0 42.1 jit_solution(15264150312283513418)
XLA Ops:
  0.0 1.6 %pack_qkv.1 = (bf16[336,128]{1,0:T(8,128)(2,1)S(1)}, bf16[336,128]{1,0:T(8,128)(2,1)S(1)}, bf16[336,128]{1,0:T(8,128)(2,1)S(1)}, bf16[336,128]{1,0:T(8,128)(2,1)...) custom-call(bf16[112,1024]{1,0:T(8,128)(2,1)} %bitcast.8, ...), custom_call_target="tpu_custom_call" | custom-call | tf_op jit(solution)/shard_map/pack_qkv/pallas_call | solution.py:128
  1.6 3.0 %collective-permute-start.7 = (bf16[224,1024]{1,0:T(8,128)(2,1)S(1)}, bf16[224,1024]{1,0:T(8,128)(2,1)S(1)}, u32[]{:S(2)}, u32[]{:S(2)}) collective-permute-start(bf16[224,1024]{1,0:T(8,128)(2,1)S(1)} %get-tuple-element.25.refs_0_), channel_id=1, source_target_pairs={{0,16},{8,24},{16,0},{24,8},{1,17},{9,25},{17,1},{25,9},{2,18},{10... | collective-permute-start | bytes 1376264 | tf_op jit(solution)/shard_map/ppermute | solution.py:98
  4.7 4.5 %collective-permute-start = (bf16[336,128]{1,0:T(8,128)(2,1)S(1)}, bf16[336,128]{1,0:T(8,128)(2,1)S(1)}, u32[]{:S(2)}, u32[]{:S(2)}) collective-permute-start(bf16[336,128]{1,0:T(8,128)(2,1)S(1)} %get-tuple-element.16), channel_id=1, source_target_pairs={{0,7},{1,6},{2,5},{3,4},{4,3},{5,2},{6,1},{7,0},{8,11},{9,10},{10,... | collective-permute-start | bytes 258056 | tf_op jit(solution)/shard_map/ppermute | solution.py:107
  9.2 0.2 collective-permute-start.1
  9.4 0.8 %collective-permute-start.2 = (bf16[336,128]{1,0:T(8,128)(2,1)S(1)}, bf16[336,128]{1,0:T(8,128)(2,1)S(1)}, u32[]{:S(2)}, u32[]{:S(2)}) collective-permute-start(bf16[336,128]{1,0:T(8,128)(2,1)S(1)} %get-tuple-element.18), channel_id=1, source_target_pairs={{0,5},{1,4},{2,7},{3,6},{4,1},{5,0},{6,3},{7,2},{8,9},{9,8},{10,11... | collective-permute-start | bytes 258056 | tf_op jit(solution)/shard_map/ppermute | solution.py:107
  10.2 4.3 %collective-permute-start.3 = (bf16[336,128]{1,0:T(8,128)(2,1)S(1)}, bf16[336,128]{1,0:T(8,128)(2,1)S(1)}, u32[]{:S(2)}, u32[]{:S(2)}) collective-permute-start(bf16[336,128]{1,0:T(8,128)(2,1)S(1)} %get-tuple-element.19), channel_id=1, source_target_pairs={{0,3},{1,2},{2,1},{3,0},{4,7},{5,6},{6,5},{7,4},{8,15},{9,14},{10,... | collective-permute-start | bytes 258056 | tf_op jit(solution)/shard_map/ppermute | solution.py:107
  14.5 0.0 collective-permute-done.refs_0_
  14.5 0.0 collective-permute-start.4
  14.5 1.1 %collective-permute-done.1.refs_1_ = bf16[336,128]{1,0:T(8,128)(2,1)S(1)} collective-permute-done((bf16[336,128]{1,0:T(8,128)(2,1)S(1)}, bf16[336,128]{1,0:T(8,128)(2,1)S(1)}, u32[]{:S(2)}, u32[]{:S(2)}) %collective-permute-start.1) | collective-permute-done | bytes 86048 | tf_op jit(solution)/shard_map/ppermute | solution.py:107
  15.6 3.0 %collective-permute-start.5 = (bf16[336,128]{1,0:T(8,128)(2,1)S(1)}, bf16[336,128]{1,0:T(8,128)(2,1)S(1)}, u32[]{:S(2)}, u32[]{:S(2)}) collective-permute-start(bf16[336,128]{1,0:T(8,128)(2,1)S(1)} %get-tuple-element.21), channel_id=1, source_target_pairs={{0,2},{1,3},{2,0},{3,1},{4,6},{5,7},{6,4},{7,5},{8,13},{9,12},{10,... | collective-permute-start | bytes 258056 | tf_op jit(solution)/shard_map/ppermute | solution.py:107
  18.6 3.7 %collective-permute-done.2.refs_2_ = bf16[336,128]{1,0:T(8,128)(2,1)S(1)} collective-permute-done((bf16[336,128]{1,0:T(8,128)(2,1)S(1)}, bf16[336,128]{1,0:T(8,128)(2,1)S(1)}, u32[]{:S(2)}, u32[]{:S(2)}) %collective-permute-start.2) | collective-permute-done | bytes 86048 | tf_op jit(solution)/shard_map/ppermute | solution.py:107
  22.3 1.5 %collective-permute-start.6 = (bf16[336,128]{1,0:T(8,128)(2,1)S(1)}, bf16[336,128]{1,0:T(8,128)(2,1)S(1)}, u32[]{:S(2)}, u32[]{:S(2)}) collective-permute-start(bf16[336,128]{1,0:T(8,128)(2,1)S(1)} %get-tuple-element.22), channel_id=1, source_target_pairs={{0,1},{1,0},{2,3},{3,2},{4,5},{5,4},{6,7},{7,6},{8,12},{9,13},{10,... | collective-permute-start | bytes 258056 | tf_op jit(solution)/shard_map/ppermute | solution.py:107
  23.8 0.0 collective-permute-done.3.refs_3_
  23.8 0.0 collective-permute-done.7.refs_1_
  23.8 0.0 collective-permute-start.8
  23.8 0.5 %collective-permute-start.9 = (bf16[224,1024]{1,0:T(8,128)(2,1)S(1)}, bf16[224,1024]{1,0:T(8,128)(2,1)S(1)}, u32[]{:S(2)}, u32[]{:S(2)}) collective-permute-start(bf16[224,1024]{1,0:T(8,128)(2,1)S(1)} %collective-permute-done.7.refs_1_), channel_id=1, source_target_pairs={{0,8},{8,0},{16,24},{24,16},{1,9},{9,1},{17,25},{25,17},{2,10},{10... | collective-permute-start | bytes 1376264 | tf_op jit(solution)/shard_map/ppermute | solution.py:98
  24.3 0.0 collective-permute-done.4.refs_4_
  24.3 0.0 collective-permute-done.5.refs_5_
  24.3 2.5 %collective-permute-done.6.refs_6_ = bf16[336,128]{1,0:T(8,128)(2,1)S(1)} collective-permute-done((bf16[336,128]{1,0:T(8,128)(2,1)S(1)}, bf16[336,128]{1,0:T(8,128)(2,1)S(1)}, u32[]{:S(2)}, u32[]{:S(2)}) %collective-permute-start.6) | collective-permute-done | bytes 86048 | tf_op jit(solution)/shard_map/ppermute | solution.py:107
  26.8 1.6 %self_attention.1 = bf16[8,112,128]{2,1,0:T(8,128)(2,1)S(1)} custom-call(bf16[336,128]{1,0:T(8,128)(2,1)S(1)} %collective-permute-done.refs_0_, bf16[336,128]{1,0:T(8,128)(2,1)S(1)} %collective-permute-done.1.refs_1_, bf16[336,128]{1,0:T(8,128)(2,1)S(1)} %collective-permute-done.2.refs_2_, bf16[336,128]{1,0:T(8,128)(2,1)S(1)} %collective-permute-done.3.refs_3_, ...), custom_call_target="tpu_custom_call" | custom-call | flops 411041792 | bytes 917504 | tf_op jit(solution)/shard_map/self_attention/pallas_call | solution.py:141
  28.4 0.0 copy-start
  28.4 12.1 %all_to_all.5.o_ref = bf16[8,112,128]{2,1,0:T(8,128)(2,1)S(1)} all-to-all(bf16[8,112,128]{2,1,0:T(8,128)(2,1)S(1)} %self_attention.1), channel_id=1, replica_groups=mesh['view'=4,'ctx'=8] {'ctx'}, dimensions={0} | all-to-all | bytes 458752 | tf_op jit(solution)/shard_map/all_to_all | solution.py:154
  40.5 0.0 collective-permute-done.8.refs_2_
  40.5 0.0 collective-permute-done.9.refs_3_
  40.5 0.0 copy-done
  40.5 1.7 %cross_view.1 = bf16[112,1024]{1,0:T(8,128)(2,1)} custom-call(bf16[8,112,128]{2,1,0:T(8,128)(2,1)S(1)} %all_to_all.5.o_ref, bf16[112,1024]{1,0:T(8,128)(2,1)S(1)} %bitcast.7, bf16[224,1024]{1,0:T(8,128)(2,1)S(1)} %get-tuple-element.25.refs_0_, bf16[224,1024]{1,0:T(8,128)(2,1)S(1)} %collective-permute-done.7.refs_1_, ...), custom_call_target="tpu_custom_call" | custom-call | tf_op jit(solution)/shard_map/cross_view/pallas_call | solution.py:205
Async XLA Ops:
  1.6 22.2 %collective-permute-start.7 = (bf16[224,1024]{1,0:T(8,128)(2,1)S(1)}, bf16[224,1024]{1,0:T(8,128)(2,1)S(1)}, u32[]{:S(2)}, u32[]{:S(2)}) collective-permute-start(bf16[224,1024]{1,0:T(8,128)(2,1)S(1)} %get-tuple-element.25.refs_0_), channel_id=1, source_target_pairs={{0,16},{8,24},{16,0},{24,8},{1,17},{9,25},{17,1},{25,9},{2,18},{10... | collective-permute-start | bytes 1376264 | tf_op jit(solution)/shard_map/ppermute | solution.py:98
  4.7 9.8 %collective-permute-start = (bf16[336,128]{1,0:T(8,128)(2,1)S(1)}, bf16[336,128]{1,0:T(8,128)(2,1)S(1)}, u32[]{:S(2)}, u32[]{:S(2)}) collective-permute-start(bf16[336,128]{1,0:T(8,128)(2,1)S(1)} %get-tuple-element.16), channel_id=1, source_target_pairs={{0,7},{1,6},{2,5},{3,4},{4,3},{5,2},{6,1},{7,0},{8,11},{9,10},{10,... | collective-permute-start | bytes 258056 | tf_op jit(solution)/shard_map/ppermute | solution.py:107
  9.2 6.4 %collective-permute-start.1 = (bf16[336,128]{1,0:T(8,128)(2,1)S(1)}, bf16[336,128]{1,0:T(8,128)(2,1)S(1)}, u32[]{:S(2)}, u32[]{:S(2)}) collective-permute-start(bf16[336,128]{1,0:T(8,128)(2,1)S(1)} %get-tuple-element.17), channel_id=1, source_target_pairs={{0,6},{1,7},{2,4},{3,5},{4,2},{5,3},{6,0},{7,1},{8,10},{9,11},{10,... | collective-permute-start | bytes 258056 | tf_op jit(solution)/shard_map/ppermute | solution.py:107
  9.4 12.9 %collective-permute-start.2 = (bf16[336,128]{1,0:T(8,128)(2,1)S(1)}, bf16[336,128]{1,0:T(8,128)(2,1)S(1)}, u32[]{:S(2)}, u32[]{:S(2)}) collective-permute-start(bf16[336,128]{1,0:T(8,128)(2,1)S(1)} %get-tuple-element.18), channel_id=1, source_target_pairs={{0,5},{1,4},{2,7},{3,6},{4,1},{5,0},{6,3},{7,2},{8,9},{9,8},{10,11... | collective-permute-start | bytes 258056 | tf_op jit(solution)/shard_map/ppermute | solution.py:107
  10.2 13.6 %collective-permute-start.3 = (bf16[336,128]{1,0:T(8,128)(2,1)S(1)}, bf16[336,128]{1,0:T(8,128)(2,1)S(1)}, u32[]{:S(2)}, u32[]{:S(2)}) collective-permute-start(bf16[336,128]{1,0:T(8,128)(2,1)S(1)} %get-tuple-element.19), channel_id=1, source_target_pairs={{0,3},{1,2},{2,1},{3,0},{4,7},{5,6},{6,5},{7,4},{8,15},{9,14},{10,... | collective-permute-start | bytes 258056 | tf_op jit(solution)/shard_map/ppermute | solution.py:107
  14.5 9.9 %collective-permute-start.4 = (bf16[336,128]{1,0:T(8,128)(2,1)S(1)}, bf16[336,128]{1,0:T(8,128)(2,1)S(1)}, u32[]{:S(2)}, u32[]{:S(2)}) collective-permute-start(bf16[336,128]{1,0:T(8,128)(2,1)S(1)} %get-tuple-element.20), channel_id=1, source_target_pairs={{0,4},{1,5},{2,6},{3,7},{4,0},{5,1},{6,2},{7,3},{8,14},{9,15},{10,... | collective-permute-start | bytes 258056 | tf_op jit(solution)/shard_map/ppermute | solution.py:107
  15.6 8.7 %collective-permute-start.5 = (bf16[336,128]{1,0:T(8,128)(2,1)S(1)}, bf16[336,128]{1,0:T(8,128)(2,1)S(1)}, u32[]{:S(2)}, u32[]{:S(2)}) collective-permute-start(bf16[336,128]{1,0:T(8,128)(2,1)S(1)} %get-tuple-element.21), channel_id=1, source_target_pairs={{0,2},{1,3},{2,0},{3,1},{4,6},{5,7},{6,4},{7,5},{8,13},{9,12},{10,... | collective-permute-start | bytes 258056 | tf_op jit(solution)/shard_map/ppermute | solution.py:107
  22.3 4.5 %collective-permute-start.6 = (bf16[336,128]{1,0:T(8,128)(2,1)S(1)}, bf16[336,128]{1,0:T(8,128)(2,1)S(1)}, u32[]{:S(2)}, u32[]{:S(2)}) collective-permute-start(bf16[336,128]{1,0:T(8,128)(2,1)S(1)} %get-tuple-element.22), channel_id=1, source_target_pairs={{0,1},{1,0},{2,3},{3,2},{4,5},{5,4},{6,7},{7,6},{8,12},{9,13},{10,... | collective-permute-start | bytes 258056 | tf_op jit(solution)/shard_map/ppermute | solution.py:107
  23.8 16.6 %collective-permute-start.8 = (bf16[224,1024]{1,0:T(8,128)(2,1)S(1)}, bf16[224,1024]{1,0:T(8,128)(2,1)S(1)}, u32[]{:S(2)}, u32[]{:S(2)}) collective-permute-start(bf16[224,1024]{1,0:T(8,128)(2,1)S(1)} %get-tuple-element.25.refs_0_), channel_id=1, source_target_pairs={{0,8},{8,0},{16,24},{24,16},{1,9},{9,1},{17,25},{25,17},{2,10},{10... | collective-permute-start | bytes 1376264 | tf_op jit(solution)/shard_map/ppermute | solution.py:98
  23.8 16.6 %collective-permute-start.9 = (bf16[224,1024]{1,0:T(8,128)(2,1)S(1)}, bf16[224,1024]{1,0:T(8,128)(2,1)S(1)}, u32[]{:S(2)}, u32[]{:S(2)}) collective-permute-start(bf16[224,1024]{1,0:T(8,128)(2,1)S(1)} %collective-permute-done.7.refs_1_), channel_id=1, source_target_pairs={{0,8},{8,0},{16,24},{24,16},{1,9},{9,1},{17,25},{25,17},{2,10},{10... | collective-permute-start | bytes 1376264 | tf_op jit(solution)/shard_map/ppermute | solution.py:98
  28.4 12.1 %copy-start = (bf16[1,112,1024]{2,1,0:T(8,128)(2,1)S(1)}, bf16[1,112,1024]{2,1,0:T(8,128)(2,1)}, u32[]{:S(2)}) copy-start(bf16[1,112,1024]{2,1,0:T(8,128)(2,1)} %param.9) | copy-start | bytes 688132

commit v16 on v14

--- a/solution.py
+++ b/solution.py
@@ -63,7 +63,8 @@
 
 
 def cross_kernel(head_count, o_ref, q_ref, *refs):
-    *pair_refs, out_ref = refs
+    *pair_refs, out_hbm_ref, out_ref, sems = refs
+    copies = []
     rows = q_ref.shape[0]
     for head in range(head_count):
         lanes = slice(head * HEAD, (head + 1) * HEAD)
@@ -83,6 +84,14 @@
             mixed = term if mixed is None else mixed + term
         o_cross = mixed.astype(jnp.bfloat16).astype(jnp.float32)
         out_ref[:, lanes] = (o_self + o_cross).astype(jnp.bfloat16)
+        if head % 2:
+            done = pl.ds((head - 1) * HEAD, 2 * HEAD)
+            copies.append(
+                pltpu.make_async_copy(out_ref.at[:, done], out_hbm_ref.at[:, done], sems.at[head // 2])
+            )
+            copies[-1].start()
+    for copy in copies:
+        copy.wait()
 
 
 def kernel_params(grant=32):
@@ -106,7 +115,7 @@
 def split_attention(q, k, v, k_cross, v_cross, ctx_size):
     rows, width = q.shape
     heads = width // HEAD
-    partners = (3, 2, 1, 7, 6, 5, 4, 0)
+    partners = (3, 2, 1, 5, 4, 7, 6, 0)
     vmem = pl.BlockSpec(memory_space=pltpu.VMEM)
     hbm = pl.BlockSpec(memory_space=pltpu.HBM)
     sources = [pltpu.with_memory_space_constraint(x, pltpu.HBM) for x in (q, k, v, k_cross, v_cross)]
@@ -192,7 +201,11 @@
         functools.partial(cross_kernel, heads),
         out_shape=jax.ShapeDtypeStruct((rows, width), q_self.dtype),
         in_specs=[vmem] * (2 + view_count),
-        out_specs=vmem,
+        out_specs=pl.BlockSpec(memory_space=pl.ANY),
+        scratch_shapes=[
+            pltpu.VMEM((rows, width), q_self.dtype),
+            pltpu.SemaphoreType.DMA((heads // 2,)),
+        ],
         compiler_params=kernel_params(),
         name="cross_view",
     )(o_self, q_cross[0], *pairs)

time: 42 us -> 41.5 us (0.988)
  waiting for transfers between devices: 8.06 us -> 5.38 us
  blocking collectives: 12 us -> 13.9 us
    ppermute x10, waiting for transfers between devices: 8.06 us -> 5.38 us  [swap(): lax.ppermute(array, axis_name, [(i, i ^ partner) for i in range(axis_size)])]
    all_to_all x1, blocking collectives: 12 us -> 13.9 us  [split_attention(): back = lax.all_to_all(own, 'ctx', split_axis=0, concat_axis=0, tiled=True)]
  transfers between devices with their start and end apart: 10 -> 10, of which waited for: 3 -> 2; matrix products, arithmetic and copies ran while one was open for 0% -> 0% of each run, Pallas kernels for 4% -> 4%
where the time goes in v16:
time: 41.5 us; the launch traced here: 41.3 us
  starting transfers between devices  17.2 us (41%)
  blocking collectives  13.9 us (33%)
  waiting for transfers between devices  5.38 us (13%)
  Pallas kernels  4.83 us (12%)
    ppermute x10, starting transfers between devices, swap(): lax.ppermute(array, axis_name, [(i, i ^ partner) for i in range(axis_size)])  17.2 us
    all_to_all x1, blocking collectives, split_attention(): back = lax.all_to_all(own, 'ctx', split_axis=0, concat_axis=0, tiled=True)  13.9 us
    ppermute x10, waiting for transfers between devices, swap(): lax.ppermute(array, axis_name, [(i, i ^ partner) for i in range(axis_size)])  5.38 us
    pallas_call x1, Pallas kernels, body(): pl.pallas_call(functools.partial(cross_kernel, heads), out_shape=jax.Shap...  1.65 us
    pallas_call x1, Pallas kernels, split_attention(): pl.pallas_call(functools.partial(pack_kernel, partners), out_shape=[block...  1.61 us
    pallas_call x1, Pallas kernels, split_attention(): pl.pallas_call(functools.partial(packed_attention_kernel, partners, rows,...  1.57 us
  transfers between devices with their start and end apart: 10, of which 2 were waited for; matrix products, arithmetic and copies ran while one was open for 0% of the time, Pallas kernels for 4%

profile of v16, /device:TPU:0, one launch (start us, length us, event | category | flops | bytes accessed | tf_op | source)
XLA Modules:
  0.0 41.3 jit_solution(7273993088012921568)
XLA Ops:
  0.0 1.6 %pack_qkv.1 = (bf16[336,128]{1,0:T(8,128)(2,1)S(1)}, bf16[336,128]{1,0:T(8,128)(2,1)S(1)}, bf16[336,128]{1,0:T(8,128)(2,1)S(1)}, bf16[336,128]{1,0:T(8,128)(2,1)...) custom-call(bf16[112,1024]{1,0:T(8,128)(2,1)} %bitcast.8, ...), custom_call_target="tpu_custom_call" | custom-call | tf_op jit(solution)/shard_map/pack_qkv/pallas_call | solution.py:123
  1.6 3.0 %collective-permute-start.7 = (bf16[224,1024]{1,0:T(8,128)(2,1)S(1)}, bf16[224,1024]{1,0:T(8,128)(2,1)S(1)}, u32[]{:S(2)}, u32[]{:S(2)}) collective-permute-start(bf16[224,1024]{1,0:T(8,128)(2,1)S(1)} %get-tuple-element.25.refs_0_), channel_id=1, source_target_pairs={{0,16},{8,24},{16,0},{24,8},{1,17},{9,25},{17,1},{25,9},{2,18},{10... | collective-permute-start | bytes 1376264 | tf_op jit(solution)/shard_map/ppermute | solution.py:102
  4.7 2.5 %collective-permute-start = (bf16[336,128]{1,0:T(8,128)(2,1)S(1)}, bf16[336,128]{1,0:T(8,128)(2,1)S(1)}, u32[]{:S(2)}, u32[]{:S(2)}) collective-permute-start(bf16[336,128]{1,0:T(8,128)(2,1)S(1)} %get-tuple-element.16), channel_id=1, source_target_pairs={{0,3},{1,2},{2,1},{3,0},{4,7},{5,6},{6,5},{7,4},{8,11},{9,10},{10,... | collective-permute-start | bytes 258056 | tf_op jit(solution)/shard_map/ppermute | solution.py:102
  7.2 0.4 %collective-permute-start.1 = (bf16[336,128]{1,0:T(8,128)(2,1)S(1)}, bf16[336,128]{1,0:T(8,128)(2,1)S(1)}, u32[]{:S(2)}, u32[]{:S(2)}) collective-permute-start(bf16[336,128]{1,0:T(8,128)(2,1)S(1)} %get-tuple-element.17), channel_id=1, source_target_pairs={{0,2},{1,3},{2,0},{3,1},{4,6},{5,7},{6,4},{7,5},{8,10},{9,11},{10,... | collective-permute-start | bytes 258056 | tf_op jit(solution)/shard_map/ppermute | solution.py:102
  7.6 0.5 %collective-permute-start.2 = (bf16[336,128]{1,0:T(8,128)(2,1)S(1)}, bf16[336,128]{1,0:T(8,128)(2,1)S(1)}, u32[]{:S(2)}, u32[]{:S(2)}) collective-permute-start(bf16[336,128]{1,0:T(8,128)(2,1)S(1)} %get-tuple-element.18), channel_id=1, source_target_pairs={{0,1},{1,0},{2,3},{3,2},{4,5},{5,4},{6,7},{7,6},{8,9},{9,8},{10,11... | collective-permute-start | bytes 258056 | tf_op jit(solution)/shard_map/ppermute | solution.py:102
  8.1 3.5 %collective-permute-start.3 = (bf16[336,128]{1,0:T(8,128)(2,1)S(1)}, bf16[336,128]{1,0:T(8,128)(2,1)S(1)}, u32[]{:S(2)}, u32[]{:S(2)}) collective-permute-start(bf16[336,128]{1,0:T(8,128)(2,1)S(1)} %get-tuple-element.19), channel_id=1, source_target_pairs={{0,5},{1,4},{2,7},{3,6},{4,1},{5,0},{6,3},{7,2},{8,13},{9,12},{10,... | collective-permute-start | bytes 258056 | tf_op jit(solution)/shard_map/ppermute | solution.py:102
  11.7 0.0 collective-permute-done.refs_0_
  11.7 1.9 %collective-permute-start.4 = (bf16[336,128]{1,0:T(8,128)(2,1)S(1)}, bf16[336,128]{1,0:T(8,128)(2,1)S(1)}, u32[]{:S(2)}, u32[]{:S(2)}) collective-permute-start(bf16[336,128]{1,0:T(8,128)(2,1)S(1)} %get-tuple-element.20), channel_id=1, source_target_pairs={{0,4},{1,5},{2,6},{3,7},{4,0},{5,1},{6,2},{7,3},{8,12},{9,13},{10,... | collective-permute-start | bytes 258056 | tf_op jit(solution)/shard_map/ppermute | solution.py:102
  13.5 0.0 collective-permute-done.1.refs_1_
  13.5 2.0 %collective-permute-start.5 = (bf16[336,128]{1,0:T(8,128)(2,1)S(1)}, bf16[336,128]{1,0:T(8,128)(2,1)S(1)}, u32[]{:S(2)}, u32[]{:S(2)}) collective-permute-start(bf16[336,128]{1,0:T(8,128)(2,1)S(1)} %get-tuple-element.21), channel_id=1, source_target_pairs={{0,7},{1,6},{2,5},{3,4},{4,3},{5,2},{6,1},{7,0},{8,15},{9,14},{10,... | collective-permute-start | bytes 258056 | tf_op jit(solution)/shard_map/ppermute | solution.py:102
  15.6 0.0 collective-permute-done.2.refs_2_
  15.6 2.7 %collective-permute-start.6 = (bf16[336,128]{1,0:T(8,128)(2,1)S(1)}, bf16[336,128]{1,0:T(8,128)(2,1)S(1)}, u32[]{:S(2)}, u32[]{:S(2)}) collective-permute-start(bf16[336,128]{1,0:T(8,128)(2,1)S(1)} %get-tuple-element.22), channel_id=1, source_target_pairs={{0,6},{1,7},{2,4},{3,5},{4,2},{5,3},{6,0},{7,1},{8,14},{9,15},{10,... | collective-permute-start | bytes 258056 | tf_op jit(solution)/shard_map/ppermute | solution.py:102
  18.3 3.1 %collective-permute-done.3.refs_3_ = bf16[336,128]{1,0:T(8,128)(2,1)S(1)} collective-permute-done((bf16[336,128]{1,0:T(8,128)(2,1)S(1)}, bf16[336,128]{1,0:T(8,128)(2,1)S(1)}, u32[]{:S(2)}, u32[]{:S(2)}) %collective-permute-start.3) | collective-permute-done | bytes 86048 | tf_op jit(solution)/shard_map/ppermute | solution.py:102
  21.4 0.0 collective-permute-done.7.refs_1_
  21.4 0.0 collective-permute-start.8
  21.4 0.5 %collective-permute-start.9 = (bf16[224,1024]{1,0:T(8,128)(2,1)S(1)}, bf16[224,1024]{1,0:T(8,128)(2,1)S(1)}, u32[]{:S(2)}, u32[]{:S(2)}) collective-permute-start(bf16[224,1024]{1,0:T(8,128)(2,1)S(1)} %collective-permute-done.7.refs_1_), channel_id=1, source_target_pairs={{0,8},{8,0},{16,24},{24,16},{1,9},{9,1},{17,25},{25,17},{2,10},{10... | collective-permute-start | bytes 1376264 | tf_op jit(solution)/shard_map/ppermute | solution.py:102
  21.9 2.3 %collective-permute-done.4.refs_4_ = bf16[336,128]{1,0:T(8,128)(2,1)S(1)} collective-permute-done((bf16[336,128]{1,0:T(8,128)(2,1)S(1)}, bf16[336,128]{1,0:T(8,128)(2,1)S(1)}, u32[]{:S(2)}, u32[]{:S(2)}) %collective-permute-start.4) | collective-permute-done | bytes 86048 | tf_op jit(solution)/shard_map/ppermute | solution.py:102
  24.2 0.0 collective-permute-done.5.refs_5_
  24.2 0.0 collective-permute-done.6.refs_6_
  24.2 1.6 %self_attention.1 = bf16[8,112,128]{2,1,0:T(8,128)(2,1)S(1)} custom-call(bf16[336,128]{1,0:T(8,128)(2,1)S(1)} %collective-permute-done.refs_0_, bf16[336,128]{1,0:T(8,128)(2,1)S(1)} %collective-permute-done.1.refs_1_, bf16[336,128]{1,0:T(8,128)(2,1)S(1)} %collective-permute-done.2.refs_2_, bf16[336,128]{1,0:T(8,128)(2,1)S(1)} %collective-permute-done.3.refs_3_, ...), custom_call_target="tpu_custom_call" | custom-call | flops 411041792 | bytes 917504 | tf_op jit(solution)/shard_map/self_attention/pallas_call | solution.py:136
  25.8 0.0 copy-start
  25.8 13.9 %all_to_all.5.o_ref = bf16[8,112,128]{2,1,0:T(8,128)(2,1)S(1)} all-to-all(bf16[8,112,128]{2,1,0:T(8,128)(2,1)S(1)} %self_attention.1), channel_id=1, replica_groups=mesh['view'=4,'ctx'=8] {'ctx'}, dimensions={0} | all-to-all | bytes 458752 | tf_op jit(solution)/shard_map/all_to_all | solution.py:149
  39.7 0.0 collective-permute-done.8.refs_2_
  39.7 0.0 collective-permute-done.9.refs_3_
  39.7 0.0 copy-done
  39.7 1.6 %cross_view.1 = bf16[112,1024]{1,0:T(8,128)(2,1)} custom-call(bf16[8,112,128]{2,1,0:T(8,128)(2,1)S(1)} %all_to_all.5.o_ref, bf16[112,1024]{1,0:T(8,128)(2,1)S(1)} %bitcast.7, bf16[224,1024]{1,0:T(8,128)(2,1)S(1)} %get-tuple-element.25.refs_0_, bf16[224,1024]{1,0:T(8,128)(2,1)S(1)} %collective-permute-done.7.refs_1_, ...), custom_call_target="tpu_custom_call" | custom-call | tf_op jit(solution)/shard_map/cross_view/pallas_call | solution.py:200
Async XLA Ops:
  1.6 19.8 %collective-permute-start.7 = (bf16[224,1024]{1,0:T(8,128)(2,1)S(1)}, bf16[224,1024]{1,0:T(8,128)(2,1)S(1)}, u32[]{:S(2)}, u32[]{:S(2)}) collective-permute-start(bf16[224,1024]{1,0:T(8,128)(2,1)S(1)} %get-tuple-element.25.refs_0_), channel_id=1, source_target_pairs={{0,16},{8,24},{16,0},{24,8},{1,17},{9,25},{17,1},{25,9},{2,18},{10... | collective-permute-start | bytes 1376264 | tf_op jit(solution)/shard_map/ppermute | solution.py:102
  4.7 7.0 %collective-permute-start = (bf16[336,128]{1,0:T(8,128)(2,1)S(1)}, bf16[336,128]{1,0:T(8,128)(2,1)S(1)}, u32[]{:S(2)}, u32[]{:S(2)}) collective-permute-start(bf16[336,128]{1,0:T(8,128)(2,1)S(1)} %get-tuple-element.16), channel_id=1, source_target_pairs={{0,3},{1,2},{2,1},{3,0},{4,7},{5,6},{6,5},{7,4},{8,11},{9,10},{10,... | collective-permute-start | bytes 258056 | tf_op jit(solution)/shard_map/ppermute | solution.py:102
  7.2 6.4 %collective-permute-start.1 = (bf16[336,128]{1,0:T(8,128)(2,1)S(1)}, bf16[336,128]{1,0:T(8,128)(2,1)S(1)}, u32[]{:S(2)}, u32[]{:S(2)}) collective-permute-start(bf16[336,128]{1,0:T(8,128)(2,1)S(1)} %get-tuple-element.17), channel_id=1, source_target_pairs={{0,2},{1,3},{2,0},{3,1},{4,6},{5,7},{6,4},{7,5},{8,10},{9,11},{10,... | collective-permute-start | bytes 258056 | tf_op jit(solution)/shard_map/ppermute | solution.py:102
  7.6 8.0 %collective-permute-start.2 = (bf16[336,128]{1,0:T(8,128)(2,1)S(1)}, bf16[336,128]{1,0:T(8,128)(2,1)S(1)}, u32[]{:S(2)}, u32[]{:S(2)}) collective-permute-start(bf16[336,128]{1,0:T(8,128)(2,1)S(1)} %get-tuple-element.18), channel_id=1, source_target_pairs={{0,1},{1,0},{2,3},{3,2},{4,5},{5,4},{6,7},{7,6},{8,9},{9,8},{10,11... | collective-permute-start | bytes 258056 | tf_op jit(solution)/shard_map/ppermute | solution.py:102
  8.1 13.2 %collective-permute-start.3 = (bf16[336,128]{1,0:T(8,128)(2,1)S(1)}, bf16[336,128]{1,0:T(8,128)(2,1)S(1)}, u32[]{:S(2)}, u32[]{:S(2)}) collective-permute-start(bf16[336,128]{1,0:T(8,128)(2,1)S(1)} %get-tuple-element.19), channel_id=1, source_target_pairs={{0,5},{1,4},{2,7},{3,6},{4,1},{5,0},{6,3},{7,2},{8,13},{9,12},{10,... | collective-permute-start | bytes 258056 | tf_op jit(solution)/shard_map/ppermute | solution.py:102
  11.7 12.5 %collective-permute-start.4 = (bf16[336,128]{1,0:T(8,128)(2,1)S(1)}, bf16[336,128]{1,0:T(8,128)(2,1)S(1)}, u32[]{:S(2)}, u32[]{:S(2)}) collective-permute-start(bf16[336,128]{1,0:T(8,128)(2,1)S(1)} %get-tuple-element.20), channel_id=1, source_target_pairs={{0,4},{1,5},{2,6},{3,7},{4,0},{5,1},{6,2},{7,3},{8,12},{9,13},{10,... | collective-permute-start | bytes 258056 | tf_op jit(solution)/shard_map/ppermute | solution.py:102
  13.5 10.6 %collective-permute-start.5 = (bf16[336,128]{1,0:T(8,128)(2,1)S(1)}, bf16[336,128]{1,0:T(8,128)(2,1)S(1)}, u32[]{:S(2)}, u32[]{:S(2)}) collective-permute-start(bf16[336,128]{1,0:T(8,128)(2,1)S(1)} %get-tuple-element.21), channel_id=1, source_target_pairs={{0,7},{1,6},{2,5},{3,4},{4,3},{5,2},{6,1},{7,0},{8,15},{9,14},{10,... | collective-permute-start | bytes 258056 | tf_op jit(solution)/shard_map/ppermute | solution.py:102
  15.6 8.6 %collective-permute-start.6 = (bf16[336,128]{1,0:T(8,128)(2,1)S(1)}, bf16[336,128]{1,0:T(8,128)(2,1)S(1)}, u32[]{:S(2)}, u32[]{:S(2)}) collective-permute-start(bf16[336,128]{1,0:T(8,128)(2,1)S(1)} %get-tuple-element.22), channel_id=1, source_target_pairs={{0,6},{1,7},{2,4},{3,5},{4,2},{5,3},{6,0},{7,1},{8,14},{9,15},{10,... | collective-permute-start | bytes 258056 | tf_op jit(solution)/shard_map/ppermute | solution.py:102
  21.4 18.3 %collective-permute-start.8 = (bf16[224,1024]{1,0:T(8,128)(2,1)S(1)}, bf16[224,1024]{1,0:T(8,128)(2,1)S(1)}, u32[]{:S(2)}, u32[]{:S(2)}) collective-permute-start(bf16[224,1024]{1,0:T(8,128)(2,1)S(1)} %get-tuple-element.25.refs_0_), channel_id=1, source_target_pairs={{0,8},{8,0},{16,24},{24,16},{1,9},{9,1},{17,25},{25,17},{2,10},{10... | collective-permute-start | bytes 1376264 | tf_op jit(solution)/shard_map/ppermute | solution.py:102
  21.4 18.3 %collective-permute-start.9 = (bf16[224,1024]{1,0:T(8,128)(2,1)S(1)}, bf16[224,1024]{1,0:T(8,128)(2,1)S(1)}, u32[]{:S(2)}, u32[]{:S(2)}) collective-permute-start(bf16[224,1024]{1,0:T(8,128)(2,1)S(1)} %collective-permute-done.7.refs_1_), channel_id=1, source_target_pairs={{0,8},{8,0},{16,24},{24,16},{1,9},{9,1},{17,25},{25,17},{2,10},{10... | collective-permute-start | bytes 1376264 | tf_op jit(solution)/shard_map/ppermute | solution.py:102
  25.8 13.9 %copy-start = (bf16[1,112,1024]{2,1,0:T(8,128)(2,1)S(1)}, bf16[1,112,1024]{2,1,0:T(8,128)(2,1)}, u32[]{:S(2)}) copy-start(bf16[1,112,1024]{2,1,0:T(8,128)(2,1)} %param.9) | copy-start | bytes 688132

commit v17 on v15

--- a/solution.py
+++ b/solution.py
@@ -12,7 +12,7 @@
 SCALE = 1.0 / math.sqrt(HEAD)
 EXP2_SCALE = SCALE * math.log2(math.e)
 MIB = 1024 * 1024
-PARTNERS = tuple(zip((7, 6, 5, 3, 4, 2, 1, 0), (3, 2, 1, 7, 6, 5, 4, 0)))
+PARTNERS = tuple(zip((5, 4, 3, 2, 7, 6, 1, 0), (3, 2, 1, 5, 4, 7, 6, 0)))
 
 
 def partner_of(orders):

time: 42.3 us -> 41.7 us (0.986)
  starting transfers between devices: 17.9 us -> 21.6 us
  waiting for transfers between devices: 7.3 us -> 3.98 us
  blocking collectives: 12.1 us -> 11 us
    ppermute x7, starting transfers between devices: 14.3 us -> 18.1 us  [exchange(): return lax.ppermute(array, ('view', 'ctx'), pairs)]
    ppermute x7, waiting for transfers between devices: 7.29 us -> 3.98 us  [exchange(): return lax.ppermute(array, ('view', 'ctx'), pairs)]
    all_to_all x1, blocking collectives: 12.1 us -> 11 us  [split_attention(): back = lax.all_to_all(own, 'ctx', split_axis=0, concat_axis=0, tiled=True)]
where the time goes in v17:
time: 41.7 us; the launch traced here: 41.5 us
  starting transfers between devices  21.6 us (52%)
  blocking collectives  11 us (26%)
  Pallas kernels  4.85 us (12%)
  waiting for transfers between devices  3.98 us (10%)
    ppermute x7, starting transfers between devices, exchange(): return lax.ppermute(array, ('view', 'ctx'), pairs)  18.1 us
    all_to_all x1, blocking collectives, split_attention(): back = lax.all_to_all(own, 'ctx', split_axis=0, concat_axis=0, tiled=True)  11 us
    ppermute x7, waiting for transfers between devices, exchange(): return lax.ppermute(array, ('view', 'ctx'), pairs)  3.98 us
    ppermute x3, starting transfers between devices, swap(): lax.ppermute(array, axis_name, [(i, i ^ partner) for i in range(axis_size)])  3.54 us
    pallas_call x1, Pallas kernels, body(): pl.pallas_call(functools.partial(cross_kernel, heads), out_shape=jax.Shap...  1.68 us
    pallas_call x1, Pallas kernels, split_attention(): pl.pallas_call(functools.partial(pack_kernel, partners), out_shape=[block...  1.61 us
    pallas_call x1, Pallas kernels, split_attention(): pl.pallas_call(functools.partial(packed_attention_kernel, partners, rows,...  1.56 us
  transfers between devices with their start and end apart: 10, of which 3 were waited for; matrix products, arithmetic and copies ran while one was open for 0% of the time, Pallas kernels for 4%

profile of v17, /device:TPU:0, one launch (start us, length us, event | category | flops | bytes accessed | tf_op | source)
XLA Modules:
  0.0 41.5 jit_solution(17964516294249484443)
XLA Ops:
  0.0 1.6 %pack_qkv.1 = (bf16[336,128]{1,0:T(8,128)(2,1)S(1)}, bf16[336,128]{1,0:T(8,128)(2,1)S(1)}, bf16[336,128]{1,0:T(8,128)(2,1)S(1)}, bf16[336,128]{1,0:T(8,128)(2,1)...) custom-call(bf16[112,1024]{1,0:T(8,128)(2,1)} %bitcast.8, ...), custom_call_target="tpu_custom_call" | custom-call | tf_op jit(solution)/shard_map/pack_qkv/pallas_call | solution.py:128
  1.6 3.0 %collective-permute-start.7 = (bf16[224,1024]{1,0:T(8,128)(2,1)S(1)}, bf16[224,1024]{1,0:T(8,128)(2,1)S(1)}, u32[]{:S(2)}, u32[]{:S(2)}) collective-permute-start(bf16[224,1024]{1,0:T(8,128)(2,1)S(1)} %get-tuple-element.25.refs_0_), channel_id=1, source_target_pairs={{0,16},{8,24},{16,0},{24,8},{1,17},{9,25},{17,1},{25,9},{2,18},{10... | collective-permute-start | bytes 1376264 | tf_op jit(solution)/shard_map/ppermute | solution.py:98
  4.7 3.5 %collective-permute-start = (bf16[336,128]{1,0:T(8,128)(2,1)S(1)}, bf16[336,128]{1,0:T(8,128)(2,1)S(1)}, u32[]{:S(2)}, u32[]{:S(2)}) collective-permute-start(bf16[336,128]{1,0:T(8,128)(2,1)S(1)} %get-tuple-element.16), channel_id=1, source_target_pairs={{0,5},{1,4},{2,7},{3,6},{4,1},{5,0},{6,3},{7,2},{8,11},{9,10},{10,... | collective-permute-start | bytes 258056 | tf_op jit(solution)/shard_map/ppermute | solution.py:107
  8.2 0.3 collective-permute-start.1
  8.5 1.5 %collective-permute-start.2 = (bf16[336,128]{1,0:T(8,128)(2,1)S(1)}, bf16[336,128]{1,0:T(8,128)(2,1)S(1)}, u32[]{:S(2)}, u32[]{:S(2)}) collective-permute-start(bf16[336,128]{1,0:T(8,128)(2,1)S(1)} %get-tuple-element.18), channel_id=1, source_target_pairs={{0,3},{1,2},{2,1},{3,0},{4,7},{5,6},{6,5},{7,4},{8,9},{9,8},{10,11... | collective-permute-start | bytes 258056 | tf_op jit(solution)/shard_map/ppermute | solution.py:107
  10.1 0.4 %collective-permute-start.3 = (bf16[336,128]{1,0:T(8,128)(2,1)S(1)}, bf16[336,128]{1,0:T(8,128)(2,1)S(1)}, u32[]{:S(2)}, u32[]{:S(2)}) collective-permute-start(bf16[336,128]{1,0:T(8,128)(2,1)S(1)} %get-tuple-element.19), channel_id=1, source_target_pairs={{0,2},{1,3},{2,0},{3,1},{4,6},{5,7},{6,4},{7,5},{8,13},{9,12},{10,... | collective-permute-start | bytes 258056 | tf_op jit(solution)/shard_map/ppermute | solution.py:107
  10.5 0.5 %collective-permute-done.refs_0_ = bf16[336,128]{1,0:T(8,128)(2,1)S(1)} collective-permute-done((bf16[336,128]{1,0:T(8,128)(2,1)S(1)}, bf16[336,128]{1,0:T(8,128)(2,1)S(1)}, u32[]{:S(2)}, u32[]{:S(2)}) %collective-permute-start) | collective-permute-done | bytes 86048 | tf_op jit(solution)/shard_map/ppermute | solution.py:107
  11.0 9.4 %collective-permute-start.4 = (bf16[336,128]{1,0:T(8,128)(2,1)S(1)}, bf16[336,128]{1,0:T(8,128)(2,1)S(1)}, u32[]{:S(2)}, u32[]{:S(2)}) collective-permute-start(bf16[336,128]{1,0:T(8,128)(2,1)S(1)} %get-tuple-element.20), channel_id=1, source_target_pairs={{0,7},{1,6},{2,5},{3,4},{4,3},{5,2},{6,1},{7,0},{8,12},{9,13},{10,... | collective-permute-start | bytes 258056 | tf_op jit(solution)/shard_map/ppermute | solution.py:107
  20.4 0.0 collective-permute-done.1.refs_1_
  20.4 2.4 %collective-permute-start.5 = (bf16[336,128]{1,0:T(8,128)(2,1)S(1)}, bf16[336,128]{1,0:T(8,128)(2,1)S(1)}, u32[]{:S(2)}, u32[]{:S(2)}) collective-permute-start(bf16[336,128]{1,0:T(8,128)(2,1)S(1)} %get-tuple-element.21), channel_id=1, source_target_pairs={{0,6},{1,7},{2,4},{3,5},{4,2},{5,3},{6,0},{7,1},{8,15},{9,14},{10,... | collective-permute-start | bytes 258056 | tf_op jit(solution)/shard_map/ppermute | solution.py:107
  22.8 0.0 collective-permute-done.2.refs_2_
  22.8 0.5 %collective-permute-start.6 = (bf16[336,128]{1,0:T(8,128)(2,1)S(1)}, bf16[336,128]{1,0:T(8,128)(2,1)S(1)}, u32[]{:S(2)}, u32[]{:S(2)}) collective-permute-start(bf16[336,128]{1,0:T(8,128)(2,1)S(1)} %get-tuple-element.22), channel_id=1, source_target_pairs={{0,1},{1,0},{2,3},{3,2},{4,5},{5,4},{6,7},{7,6},{8,14},{9,15},{10,... | collective-permute-start | bytes 258056 | tf_op jit(solution)/shard_map/ppermute | solution.py:107
  23.3 0.0 collective-permute-done.3.refs_3_
  23.3 0.0 collective-permute-done.7.refs_1_
  23.3 0.0 collective-permute-start.8
  23.3 0.5 %collective-permute-start.9 = (bf16[224,1024]{1,0:T(8,128)(2,1)S(1)}, bf16[224,1024]{1,0:T(8,128)(2,1)S(1)}, u32[]{:S(2)}, u32[]{:S(2)}) collective-permute-start(bf16[224,1024]{1,0:T(8,128)(2,1)S(1)} %collective-permute-done.7.refs_1_), channel_id=1, source_target_pairs={{0,8},{8,0},{16,24},{24,16},{1,9},{9,1},{17,25},{25,17},{2,10},{10... | collective-permute-start | bytes 1376264 | tf_op jit(solution)/shard_map/ppermute | solution.py:98
  23.8 0.0 collective-permute-done.4.refs_4_
  23.8 2.9 %collective-permute-done.5.refs_5_ = bf16[336,128]{1,0:T(8,128)(2,1)S(1)} collective-permute-done((bf16[336,128]{1,0:T(8,128)(2,1)S(1)}, bf16[336,128]{1,0:T(8,128)(2,1)S(1)}, u32[]{:S(2)}, u32[]{:S(2)}) %collective-permute-start.5) | collective-permute-done | bytes 86048 | tf_op jit(solution)/shard_map/ppermute | solution.py:107
  26.7 0.6 %collective-permute-done.6.refs_6_ = bf16[336,128]{1,0:T(8,128)(2,1)S(1)} collective-permute-done((bf16[336,128]{1,0:T(8,128)(2,1)S(1)}, bf16[336,128]{1,0:T(8,128)(2,1)S(1)}, u32[]{:S(2)}, u32[]{:S(2)}) %collective-permute-start.6) | collective-permute-done | bytes 86048 | tf_op jit(solution)/shard_map/ppermute | solution.py:107
  27.2 1.6 %self_attention.1 = bf16[8,112,128]{2,1,0:T(8,128)(2,1)S(1)} custom-call(bf16[336,128]{1,0:T(8,128)(2,1)S(1)} %collective-permute-done.refs_0_, bf16[336,128]{1,0:T(8,128)(2,1)S(1)} %collective-permute-done.1.refs_1_, bf16[336,128]{1,0:T(8,128)(2,1)S(1)} %collective-permute-done.2.refs_2_, bf16[336,128]{1,0:T(8,128)(2,1)S(1)} %collective-permute-done.3.refs_3_, ...), custom_call_target="tpu_custom_call" | custom-call | flops 411041792 | bytes 917504 | tf_op jit(solution)/shard_map/self_attention/pallas_call | solution.py:141
  28.8 0.0 copy-start
  28.8 11.0 %all_to_all.5.o_ref = bf16[8,112,128]{2,1,0:T(8,128)(2,1)S(1)} all-to-all(bf16[8,112,128]{2,1,0:T(8,128)(2,1)S(1)} %self_attention.1), channel_id=1, replica_groups=mesh['view'=4,'ctx'=8] {'ctx'}, dimensions={0} | all-to-all | bytes 458752 | tf_op jit(solution)/shard_map/all_to_all | solution.py:154
  39.8 0.0 collective-permute-done.8.refs_2_
  39.8 0.0 collective-permute-done.9.refs_3_
  39.8 0.0 copy-done
  39.8 1.7 %cross_view.1 = bf16[112,1024]{1,0:T(8,128)(2,1)} custom-call(bf16[8,112,128]{2,1,0:T(8,128)(2,1)S(1)} %all_to_all.5.o_ref, bf16[112,1024]{1,0:T(8,128)(2,1)S(1)} %bitcast.7, bf16[224,1024]{1,0:T(8,128)(2,1)S(1)} %get-tuple-element.25.refs_0_, bf16[224,1024]{1,0:T(8,128)(2,1)S(1)} %collective-permute-done.7.refs_1_, ...), custom_call_target="tpu_custom_call" | custom-call | tf_op jit(solution)/shard_map/cross_view/pallas_call | solution.py:205
Async XLA Ops:
  1.6 21.7 %collective-permute-start.7 = (bf16[224,1024]{1,0:T(8,128)(2,1)S(1)}, bf16[224,1024]{1,0:T(8,128)(2,1)S(1)}, u32[]{:S(2)}, u32[]{:S(2)}) collective-permute-start(bf16[224,1024]{1,0:T(8,128)(2,1)S(1)} %get-tuple-element.25.refs_0_), channel_id=1, source_target_pairs={{0,16},{8,24},{16,0},{24,8},{1,17},{9,25},{17,1},{25,9},{2,18},{10... | collective-permute-start | bytes 1376264 | tf_op jit(solution)/shard_map/ppermute | solution.py:98
  4.7 6.4 %collective-permute-start = (bf16[336,128]{1,0:T(8,128)(2,1)S(1)}, bf16[336,128]{1,0:T(8,128)(2,1)S(1)}, u32[]{:S(2)}, u32[]{:S(2)}) collective-permute-start(bf16[336,128]{1,0:T(8,128)(2,1)S(1)} %get-tuple-element.16), channel_id=1, source_target_pairs={{0,5},{1,4},{2,7},{3,6},{4,1},{5,0},{6,3},{7,2},{8,11},{9,10},{10,... | collective-permute-start | bytes 258056 | tf_op jit(solution)/shard_map/ppermute | solution.py:107
  8.2 12.2 %collective-permute-start.1 = (bf16[336,128]{1,0:T(8,128)(2,1)S(1)}, bf16[336,128]{1,0:T(8,128)(2,1)S(1)}, u32[]{:S(2)}, u32[]{:S(2)}) collective-permute-start(bf16[336,128]{1,0:T(8,128)(2,1)S(1)} %get-tuple-element.17), channel_id=1, source_target_pairs={{0,4},{1,5},{2,6},{3,7},{4,0},{5,1},{6,2},{7,3},{8,10},{9,11},{10,... | collective-permute-start | bytes 258056 | tf_op jit(solution)/shard_map/ppermute | solution.py:107
  8.5 14.2 %collective-permute-start.2 = (bf16[336,128]{1,0:T(8,128)(2,1)S(1)}, bf16[336,128]{1,0:T(8,128)(2,1)S(1)}, u32[]{:S(2)}, u32[]{:S(2)}) collective-permute-start(bf16[336,128]{1,0:T(8,128)(2,1)S(1)} %get-tuple-element.18), channel_id=1, source_target_pairs={{0,3},{1,2},{2,1},{3,0},{4,7},{5,6},{6,5},{7,4},{8,9},{9,8},{10,11... | collective-permute-start | bytes 258056 | tf_op jit(solution)/shard_map/ppermute | solution.py:107
  10.1 13.2 %collective-permute-start.3 = (bf16[336,128]{1,0:T(8,128)(2,1)S(1)}, bf16[336,128]{1,0:T(8,128)(2,1)S(1)}, u32[]{:S(2)}, u32[]{:S(2)}) collective-permute-start(bf16[336,128]{1,0:T(8,128)(2,1)S(1)} %get-tuple-element.19), channel_id=1, source_target_pairs={{0,2},{1,3},{2,0},{3,1},{4,6},{5,7},{6,4},{7,5},{8,13},{9,12},{10,... | collective-permute-start | bytes 258056 | tf_op jit(solution)/shard_map/ppermute | solution.py:107
  11.0 12.8 %collective-permute-start.4 = (bf16[336,128]{1,0:T(8,128)(2,1)S(1)}, bf16[336,128]{1,0:T(8,128)(2,1)S(1)}, u32[]{:S(2)}, u32[]{:S(2)}) collective-permute-start(bf16[336,128]{1,0:T(8,128)(2,1)S(1)} %get-tuple-element.20), channel_id=1, source_target_pairs={{0,7},{1,6},{2,5},{3,4},{4,3},{5,2},{6,1},{7,0},{8,12},{9,13},{10,... | collective-permute-start | bytes 258056 | tf_op jit(solution)/shard_map/ppermute | solution.py:107
  20.4 6.3 %collective-permute-start.5 = (bf16[336,128]{1,0:T(8,128)(2,1)S(1)}, bf16[336,128]{1,0:T(8,128)(2,1)S(1)}, u32[]{:S(2)}, u32[]{:S(2)}) collective-permute-start(bf16[336,128]{1,0:T(8,128)(2,1)S(1)} %get-tuple-element.21), channel_id=1, source_target_pairs={{0,6},{1,7},{2,4},{3,5},{4,2},{5,3},{6,0},{7,1},{8,15},{9,14},{10,... | collective-permute-start | bytes 258056 | tf_op jit(solution)/shard_map/ppermute | solution.py:107
  22.8 4.5 %collective-permute-start.6 = (bf16[336,128]{1,0:T(8,128)(2,1)S(1)}, bf16[336,128]{1,0:T(8,128)(2,1)S(1)}, u32[]{:S(2)}, u32[]{:S(2)}) collective-permute-start(bf16[336,128]{1,0:T(8,128)(2,1)S(1)} %get-tuple-element.22), channel_id=1, source_target_pairs={{0,1},{1,0},{2,3},{3,2},{4,5},{5,4},{6,7},{7,6},{8,14},{9,15},{10,... | collective-permute-start | bytes 258056 | tf_op jit(solution)/shard_map/ppermute | solution.py:107
  23.3 16.5 %collective-permute-start.8 = (bf16[224,1024]{1,0:T(8,128)(2,1)S(1)}, bf16[224,1024]{1,0:T(8,128)(2,1)S(1)}, u32[]{:S(2)}, u32[]{:S(2)}) collective-permute-start(bf16[224,1024]{1,0:T(8,128)(2,1)S(1)} %get-tuple-element.25.refs_0_), channel_id=1, source_target_pairs={{0,8},{8,0},{16,24},{24,16},{1,9},{9,1},{17,25},{25,17},{2,10},{10... | collective-permute-start | bytes 1376264 | tf_op jit(solution)/shard_map/ppermute | solution.py:98
  23.3 16.5 %collective-permute-start.9 = (bf16[224,1024]{1,0:T(8,128)(2,1)S(1)}, bf16[224,1024]{1,0:T(8,128)(2,1)S(1)}, u32[]{:S(2)}, u32[]{:S(2)}) collective-permute-start(bf16[224,1024]{1,0:T(8,128)(2,1)S(1)} %collective-permute-done.7.refs_1_), channel_id=1, source_target_pairs={{0,8},{8,0},{16,24},{24,16},{1,9},{9,1},{17,25},{25,17},{2,10},{10... | collective-permute-start | bytes 1376264 | tf_op jit(solution)/shard_map/ppermute | solution.py:98
  28.8 11.0 %copy-start = (bf16[1,112,1024]{2,1,0:T(8,128)(2,1)S(1)}, bf16[1,112,1024]{2,1,0:T(8,128)(2,1)}, u32[]{:S(2)}) copy-start(bf16[1,112,1024]{2,1,0:T(8,128)(2,1)} %param.9) | copy-start | bytes 688132

commit v18 on v13

--- a/solution.py
+++ b/solution.py
@@ -111,7 +111,7 @@
 def split_attention(q, k, v, k_cross, v_cross, ctx_size):
     rows, width = q.shape
     heads = width // HEAD
-    far = (7, 6, 5, 4)
+    far = (5, 7, 4, 6)
     vmem = pl.BlockSpec(memory_space=pltpu.VMEM)
     hbm = pl.BlockSpec(memory_space=pltpu.HBM)
     sources = [pltpu.with_memory_space_constraint(x, pltpu.HBM) for x in (q, k, v, k_cross, v_cross)]
@@ -145,7 +145,7 @@
         name="self_attention",
     )(*moved)
     back = lax.all_to_all(own_heads, "ctx", split_axis=0, concat_axis=0, tiled=True)
-    return back, pair, (pair, moved[:2])
+    return back, pair, (pair, moved)
 
 
 def shared_attention(q, k, v, ctx_size):

time: 42.2 us -> 41.1 us (0.974)
  starting transfers between devices: 18.4 us -> 15.8 us
  waiting for transfers between devices: 7.17 us -> 7.89 us
  blocking collectives: 11.5 us -> 12.2 us
    ppermute x9, starting transfers between devices: 18.4 us -> 15.8 us  [swap(): lax.ppermute(array, axis_name, [(i, i ^ partner) for i in range(axis_size)])]
    all_to_all x1, blocking collectives: 11.5 us -> 12.2 us  [split_attention(): lax.all_to_all(own_heads, 'ctx', split_axis=0, concat_axis=0, tiled=True)]
    ppermute x9, waiting for transfers between devices: 7.17 us -> 7.89 us  [swap(): lax.ppermute(array, axis_name, [(i, i ^ partner) for i in range(axis_size)])]
where the time goes in v18:
time: 41.1 us; the launch traced here: 40.9 us
  starting transfers between devices  15.8 us (38%)
  blocking collectives  12.2 us (30%)
  waiting for transfers between devices  7.89 us (19%)
  Pallas kernels  4.87 us (12%)
    ppermute x9, starting transfers between devices, swap(): lax.ppermute(array, axis_name, [(i, i ^ partner) for i in range(axis_size)])  15.8 us
    all_to_all x1, blocking collectives, split_attention(): lax.all_to_all(own_heads, 'ctx', split_axis=0, concat_axis=0, tiled=True)  12.2 us
    ppermute x9, waiting for transfers between devices, swap(): lax.ppermute(array, axis_name, [(i, i ^ partner) for i in range(axis_size)])  7.89 us
    pallas_call x1, Pallas kernels, body(): pl.pallas_call(functools.partial(cross_kernel, heads), out_shape=jax.Shap...  1.69 us
    pallas_call x1, Pallas kernels, split_attention(): pl.pallas_call(functools.partial(pack_kernel, far), out_shape=[block] * l...  1.61 us
    pallas_call x1, Pallas kernels, split_attention(): pl.pallas_call(functools.partial(packed_attention_kernel, far, rows), out...  1.57 us
  transfers between devices with their start and end apart: 9, of which 3 were waited for; matrix products, arithmetic and copies ran while one was open for 0% of the time, Pallas kernels for 4%

profile of v18, /device:TPU:0, one launch (start us, length us, event | category | flops | bytes accessed | tf_op | source)
XLA Modules:
  0.0 40.9 jit_solution(7876982683448467316)
XLA Ops:
  0.0 1.6 %pack_qkv.1 = (bf16[336,128]{1,0:T(8,128)(2,1)S(1)}, bf16[336,128]{1,0:T(8,128)(2,1)S(1)}, bf16[336,128]{1,0:T(8,128)(2,1)S(1)}, bf16[336,128]{1,0:T(8,128)(2,1)...) custom-call(bf16[112,1024]{1,0:T(8,128)(2,1)} %bitcast.10, ...), custom_call_target="tpu_custom_call" | custom-call | tf_op jit(solution)/shard_map/pack_qkv/pallas_call | solution.py:120
  1.6 3.0 %collective-permute-start.4 = (bf16[2,336,128]{2,1,0:T(8,128)(2,1)S(1)}, bf16[2,336,128]{2,1,0:T(8,128)(2,1)S(1)}, u32[]{:S(2)}, u32[]{:S(2)}) collective-permute-start(bf16[2,336,128]{2,1,0:T(8,128)(2,1)S(1)} %get-tuple-element.19), channel_id=1, source_target_pairs={{0,1},{1,0},{2,3},{3,2},{4,5},{5,4},{6,7},{7,6},{8,9},{9,8},{10,11... | collective-permute-start | bytes 516104 | tf_op jit(solution)/shard_map/ppermute | solution.py:98
  4.6 1.5 %collective-permute-start.6 = (bf16[224,1024]{1,0:T(8,128)(2,1)S(1)}, bf16[224,1024]{1,0:T(8,128)(2,1)S(1)}, u32[]{:S(2)}, u32[]{:S(2)}) collective-permute-start(bf16[224,1024]{1,0:T(8,128)(2,1)S(1)} %get-tuple-element.23.refs_0_), channel_id=1, source_target_pairs={{0,16},{8,24},{16,0},{24,8},{1,17},{9,25},{17,1},{25,9},{2,18},{10... | collective-permute-start | bytes 1376264 | tf_op jit(solution)/shard_map/ppermute | solution.py:98
  6.1 2.6 %collective-permute-start = (bf16[336,128]{1,0:T(8,128)(2,1)S(1)}, bf16[336,128]{1,0:T(8,128)(2,1)S(1)}, u32[]{:S(2)}, u32[]{:S(2)}) collective-permute-start(bf16[336,128]{1,0:T(8,128)(2,1)S(1)} %get-tuple-element.15), channel_id=1, source_target_pairs={{0,5},{1,4},{2,7},{3,6},{4,1},{5,0},{6,3},{7,2},{8,13},{9,12},{10,... | collective-permute-start | bytes 258056 | tf_op jit(solution)/shard_map/ppermute | solution.py:98
  8.7 0.5 %collective-permute-done.4.refs_4_ = bf16[2,336,128]{2,1,0:T(8,128)(2,1)S(1)} collective-permute-done((bf16[2,336,128]{2,1,0:T(8,128)(2,1)S(1)}, bf16[2,336,128]{2,1,0:T(8,128)(2,1)S(1)}, u32[]{:S(2)}, u32[]{:S(2)}) %collective-permute-start.4) | collective-permute-done | bytes 172064 | tf_op jit(solution)/shard_map/ppermute | solution.py:98
  9.2 1.7 %collective-permute-start.5 = (bf16[2,336,128]{2,1,0:T(8,128)(2,1)S(1)}, bf16[2,336,128]{2,1,0:T(8,128)(2,1)S(1)}, u32[]{:S(2)}, u32[]{:S(2)}) collective-permute-start(bf16[2,336,128]{2,1,0:T(8,128)(2,1)S(1)} %pad_maximum_fusion), channel_id=1, source_target_pairs={{0,2},{1,3},{2,0},{3,1},{4,6},{5,7},{6,4},{7,5},{8,10},{9,11},{10,... | collective-permute-start | bytes 516104 | tf_op jit(solution)/shard_map/ppermute | solution.py:98
  10.9 4.3 %collective-permute-start.1 = (bf16[336,128]{1,0:T(8,128)(2,1)S(1)}, bf16[336,128]{1,0:T(8,128)(2,1)S(1)}, u32[]{:S(2)}, u32[]{:S(2)}) collective-permute-start(bf16[336,128]{1,0:T(8,128)(2,1)S(1)} %get-tuple-element.16), channel_id=1, source_target_pairs={{0,7},{1,6},{2,5},{3,4},{4,3},{5,2},{6,1},{7,0},{8,15},{9,14},{10,... | collective-permute-start | bytes 258056 | tf_op jit(solution)/shard_map/ppermute | solution.py:98
  15.2 0.0 collective-permute-start.2
  15.2 0.0 collective-permute-done.refs_0_
  15.2 2.2 %collective-permute-start.3 = (bf16[336,128]{1,0:T(8,128)(2,1)S(1)}, bf16[336,128]{1,0:T(8,128)(2,1)S(1)}, u32[]{:S(2)}, u32[]{:S(2)}) collective-permute-start(bf16[336,128]{1,0:T(8,128)(2,1)S(1)} %get-tuple-element.18), channel_id=1, source_target_pairs={{0,6},{1,7},{2,4},{3,5},{4,2},{5,3},{6,0},{7,1},{8,14},{9,15},{10,... | collective-permute-start | bytes 258056 | tf_op jit(solution)/shard_map/ppermute | solution.py:98
  17.4 3.8 %collective-permute-done.1.refs_1_ = bf16[336,128]{1,0:T(8,128)(2,1)S(1)} collective-permute-done((bf16[336,128]{1,0:T(8,128)(2,1)S(1)}, bf16[336,128]{1,0:T(8,128)(2,1)S(1)}, u32[]{:S(2)}, u32[]{:S(2)}) %collective-permute-start.1) | collective-permute-done | bytes 86048 | tf_op jit(solution)/shard_map/ppermute | solution.py:98
  21.2 3.5 %collective-permute-done.2.refs_2_ = bf16[336,128]{1,0:T(8,128)(2,1)S(1)} collective-permute-done((bf16[336,128]{1,0:T(8,128)(2,1)S(1)}, bf16[336,128]{1,0:T(8,128)(2,1)S(1)}, u32[]{:S(2)}, u32[]{:S(2)}) %collective-permute-start.2) | collective-permute-done | bytes 86048 | tf_op jit(solution)/shard_map/ppermute | solution.py:98
  24.8 0.0 collective-permute-done.3.refs_3_
  24.8 0.0 collective-permute-done.5.refs_5_
  24.8 0.0 collective-permute-done.6.refs_1_
  24.8 0.1 collective-permute-start.7
  24.9 0.5 %collective-permute-start.8 = (bf16[224,1024]{1,0:T(8,128)(2,1)S(1)}, bf16[224,1024]{1,0:T(8,128)(2,1)S(1)}, u32[]{:S(2)}, u32[]{:S(2)}) collective-permute-start(bf16[224,1024]{1,0:T(8,128)(2,1)S(1)} %collective-permute-done.6.refs_1_), channel_id=1, source_target_pairs={{0,8},{8,0},{16,24},{24,16},{1,9},{9,1},{17,25},{25,17},{2,10},{10... | collective-permute-start | bytes 1376264 | tf_op jit(solution)/shard_map/ppermute | solution.py:98
  25.4 1.6 %self_attention.1 = bf16[8,112,128]{2,1,0:T(8,128)(2,1)S(1)} custom-call(bf16[336,128]{1,0:T(8,128)(2,1)S(1)} %collective-permute-done.refs_0_, bf16[336,128]{1,0:T(8,128)(2,1)S(1)} %collective-permute-done.1.refs_1_, bf16[336,128]{1,0:T(8,128)(2,1)S(1)} %collective-permute-done.2.refs_2_, bf16[336,128]{1,0:T(8,128)(2,1)S(1)} %collective-permute-done.3.refs_3_, ...), custom_call_target="tpu_custom_call" | custom-call | flops 411041792 | bytes 917504 | tf_op jit(solution)/shard_map/self_attention/pallas_call | solution.py:134
  26.9 0.0 copy-start
  26.9 12.2 %all_to_all.5.o_ref = bf16[8,112,128]{2,1,0:T(8,128)(2,1)S(1)} all-to-all(bf16[8,112,128]{2,1,0:T(8,128)(2,1)S(1)} %self_attention.1), channel_id=1, replica_groups=mesh['view'=4,'ctx'=8] {'ctx'}, dimensions={0} | all-to-all | bytes 458752 | tf_op jit(solution)/shard_map/all_to_all | solution.py:147
  39.2 0.0 collective-permute-done.7.refs_2_
  39.2 0.0 collective-permute-done.8.refs_3_
  39.2 0.0 copy-done
  39.2 1.7 %cross_view.1 = bf16[112,1024]{1,0:T(8,128)(2,1)} custom-call(bf16[8,112,128]{2,1,0:T(8,128)(2,1)S(1)} %all_to_all.5.o_ref, bf16[112,1024]{1,0:T(8,128)(2,1)S(1)} %bitcast.8, bf16[224,1024]{1,0:T(8,128)(2,1)S(1)} %get-tuple-element.23.refs_0_, bf16[224,1024]{1,0:T(8,128)(2,1)S(1)} %collective-permute-done.6.refs_1_, ...), custom_call_target="tpu_custom_call" | custom-call | tf_op jit(solution)/shard_map/cross_view/pallas_call | solution.py:198
  (2 shorter events, 0.0 us)
Async XLA Ops:
  1.6 7.6 %collective-permute-start.4 = (bf16[2,336,128]{2,1,0:T(8,128)(2,1)S(1)}, bf16[2,336,128]{2,1,0:T(8,128)(2,1)S(1)}, u32[]{:S(2)}, u32[]{:S(2)}) collective-permute-start(bf16[2,336,128]{2,1,0:T(8,128)(2,1)S(1)} %get-tuple-element.19), channel_id=1, source_target_pairs={{0,1},{1,0},{2,3},{3,2},{4,5},{5,4},{6,7},{7,6},{8,9},{9,8},{10,11... | collective-permute-start | bytes 516104 | tf_op jit(solution)/shard_map/ppermute | solution.py:98
  4.6 20.2 %collective-permute-start.6 = (bf16[224,1024]{1,0:T(8,128)(2,1)S(1)}, bf16[224,1024]{1,0:T(8,128)(2,1)S(1)}, u32[]{:S(2)}, u32[]{:S(2)}) collective-permute-start(bf16[224,1024]{1,0:T(8,128)(2,1)S(1)} %get-tuple-element.23.refs_0_), channel_id=1, source_target_pairs={{0,16},{8,24},{16,0},{24,8},{1,17},{9,25},{17,1},{25,9},{2,18},{10... | collective-permute-start | bytes 1376264 | tf_op jit(solution)/shard_map/ppermute | solution.py:98
  6.1 9.1 %collective-permute-start = (bf16[336,128]{1,0:T(8,128)(2,1)S(1)}, bf16[336,128]{1,0:T(8,128)(2,1)S(1)}, u32[]{:S(2)}, u32[]{:S(2)}) collective-permute-start(bf16[336,128]{1,0:T(8,128)(2,1)S(1)} %get-tuple-element.15), channel_id=1, source_target_pairs={{0,5},{1,4},{2,7},{3,6},{4,1},{5,0},{6,3},{7,2},{8,13},{9,12},{10,... | collective-permute-start | bytes 258056 | tf_op jit(solution)/shard_map/ppermute | solution.py:98
  9.2 15.5 %collective-permute-start.5 = (bf16[2,336,128]{2,1,0:T(8,128)(2,1)S(1)}, bf16[2,336,128]{2,1,0:T(8,128)(2,1)S(1)}, u32[]{:S(2)}, u32[]{:S(2)}) collective-permute-start(bf16[2,336,128]{2,1,0:T(8,128)(2,1)S(1)} %pad_maximum_fusion), channel_id=1, source_target_pairs={{0,2},{1,3},{2,0},{3,1},{4,6},{5,7},{6,4},{7,5},{8,10},{9,11},{10,... | collective-permute-start | bytes 516104 | tf_op jit(solution)/shard_map/ppermute | solution.py:98
  10.9 10.3 %collective-permute-start.1 = (bf16[336,128]{1,0:T(8,128)(2,1)S(1)}, bf16[336,128]{1,0:T(8,128)(2,1)S(1)}, u32[]{:S(2)}, u32[]{:S(2)}) collective-permute-start(bf16[336,128]{1,0:T(8,128)(2,1)S(1)} %get-tuple-element.16), channel_id=1, source_target_pairs={{0,7},{1,6},{2,5},{3,4},{4,3},{5,2},{6,1},{7,0},{8,15},{9,14},{10,... | collective-permute-start | bytes 258056 | tf_op jit(solution)/shard_map/ppermute | solution.py:98
  15.2 9.5 %collective-permute-start.2 = (bf16[336,128]{1,0:T(8,128)(2,1)S(1)}, bf16[336,128]{1,0:T(8,128)(2,1)S(1)}, u32[]{:S(2)}, u32[]{:S(2)}) collective-permute-start(bf16[336,128]{1,0:T(8,128)(2,1)S(1)} %get-tuple-element.17), channel_id=1, source_target_pairs={{0,4},{1,5},{2,6},{3,7},{4,0},{5,1},{6,2},{7,3},{8,12},{9,13},{10,... | collective-permute-start | bytes 258056 | tf_op jit(solution)/shard_map/ppermute | solution.py:98
  15.2 9.5 %collective-permute-start.3 = (bf16[336,128]{1,0:T(8,128)(2,1)S(1)}, bf16[336,128]{1,0:T(8,128)(2,1)S(1)}, u32[]{:S(2)}, u32[]{:S(2)}) collective-permute-start(bf16[336,128]{1,0:T(8,128)(2,1)S(1)} %get-tuple-element.18), channel_id=1, source_target_pairs={{0,6},{1,7},{2,4},{3,5},{4,2},{5,3},{6,0},{7,1},{8,14},{9,15},{10,... | collective-permute-start | bytes 258056 | tf_op jit(solution)/shard_map/ppermute | solution.py:98
  24.8 14.4 %collective-permute-start.7 = (bf16[224,1024]{1,0:T(8,128)(2,1)S(1)}, bf16[224,1024]{1,0:T(8,128)(2,1)S(1)}, u32[]{:S(2)}, u32[]{:S(2)}) collective-permute-start(bf16[224,1024]{1,0:T(8,128)(2,1)S(1)} %get-tuple-element.23.refs_0_), channel_id=1, source_target_pairs={{0,8},{8,0},{16,24},{24,16},{1,9},{9,1},{17,25},{25,17},{2,10},{10... | collective-permute-start | bytes 1376264 | tf_op jit(solution)/shard_map/ppermute | solution.py:98
  24.9 14.3 %collective-permute-start.8 = (bf16[224,1024]{1,0:T(8,128)(2,1)S(1)}, bf16[224,1024]{1,0:T(8,128)(2,1)S(1)}, u32[]{:S(2)}, u32[]{:S(2)}) collective-permute-start(bf16[224,1024]{1,0:T(8,128)(2,1)S(1)} %collective-permute-done.6.refs_1_), channel_id=1, source_target_pairs={{0,8},{8,0},{16,24},{24,16},{1,9},{9,1},{17,25},{25,17},{2,10},{10... | collective-permute-start | bytes 1376264 | tf_op jit(solution)/shard_map/ppermute | solution.py:98
  26.9 12.3 %copy-start = (bf16[1,112,1024]{2,1,0:T(8,128)(2,1)S(1)}, bf16[1,112,1024]{2,1,0:T(8,128)(2,1)}, u32[]{:S(2)}) copy-start(bf16[1,112,1024]{2,1,0:T(8,128)(2,1)} %param.9) | copy-start | bytes 688132

commit v19 on v14

--- a/solution.py
+++ b/solution.py
@@ -62,6 +62,14 @@
     out_ref[...] = attend(q_ref[...], k_ref[...], v_ref[...])
 
 
+def matrix_sums(products):
+    high = products.astype(jnp.bfloat16)
+    low = (products - high.astype(jnp.float32)).astype(jnp.bfloat16)
+    halves = jnp.concatenate([high, low], axis=1)
+    ones = jnp.ones((2 * HEAD, HEAD), jnp.bfloat16)
+    return jnp.dot(halves, ones, preferred_element_type=jnp.float32)
+
+
 def cross_kernel(head_count, o_ref, q_ref, *refs):
     *pair_refs, out_ref = refs
     rows = q_ref.shape[0]
@@ -69,9 +77,10 @@
         lanes = slice(head * HEAD, (head + 1) * HEAD)
         o_self = o_ref[head].astype(jnp.float32)
         query = (q_ref[:, lanes].astype(jnp.float32) + o_self).astype(jnp.bfloat16).astype(jnp.float32)
+        products = [query * ref[0:rows, lanes].astype(jnp.float32) for ref in pair_refs]
         scores = [
-            jnp.sum(query * ref[0:rows, lanes].astype(jnp.float32), axis=-1, keepdims=True)
-            for ref in pair_refs
+            matrix_sums(product) if view % 2 else jnp.sum(product, axis=-1, keepdims=True)
+            for view, product in enumerate(products)
         ]
         top = functools.reduce(jnp.maximum, scores)
         weights = [jnp.exp2((score - top) * EXP2_SCALE) for score in scores]
@@ -106,7 +115,7 @@
 def split_attention(q, k, v, k_cross, v_cross, ctx_size):
     rows, width = q.shape
     heads = width // HEAD
-    partners = (3, 2, 1, 7, 6, 5, 4, 0)
+    partners = (3, 2, 1, 5, 7, 4, 6, 0)
     vmem = pl.BlockSpec(memory_space=pltpu.VMEM)
     hbm = pl.BlockSpec(memory_space=pltpu.HBM)
     sources = [pltpu.with_memory_space_constraint(x, pltpu.HBM) for x in (q, k, v, k_cross, v_cross)]

time: 42 us -> 41.3 us (0.983)
  starting transfers between devices: 16.8 us -> 16.3 us
    ppermute x10, starting transfers between devices: 16.8 us -> 16.3 us  [swap(): lax.ppermute(array, axis_name, [(i, i ^ partner) for i in range(axis_size)])]
  transfers between devices with their start and end apart: 10 -> 10, of which waited for: 3 -> 2; matrix products, arithmetic and copies ran while one was open for 0% -> 0% of each run, Pallas kernels for 4% -> 4%
where the time goes in v19:
time: 41.3 us; the launch traced here: 41.2 us
  starting transfers between devices  16.3 us (39%)
  blocking collectives  11.9 us (29%)
  waiting for transfers between devices  8.08 us (20%)
  Pallas kernels  4.91 us (12%)
    ppermute x10, starting transfers between devices, swap(): lax.ppermute(array, axis_name, [(i, i ^ partner) for i in range(axis_size)])  16.3 us
    all_to_all x1, blocking collectives, split_attention(): back = lax.all_to_all(own, 'ctx', split_axis=0, concat_axis=0, tiled=True)  11.9 us
    ppermute x10, waiting for transfers between devices, swap(): lax.ppermute(array, axis_name, [(i, i ^ partner) for i in range(axis_size)])  8.08 us
    pallas_call x1, Pallas kernels, body(): pl.pallas_call(functools.partial(cross_kernel, heads), out_shape=jax.Shap...  1.73 us
    pallas_call x1, Pallas kernels, split_attention(): pl.pallas_call(functools.partial(pack_kernel, partners), out_shape=[block...  1.61 us
    pallas_call x1, Pallas kernels, split_attention(): pl.pallas_call(functools.partial(packed_attention_kernel, partners, rows,...  1.57 us
  transfers between devices with their start and end apart: 10, of which 2 were waited for; matrix products, arithmetic and copies ran while one was open for 0% of the time, Pallas kernels for 4%

profile of v19, /device:TPU:0, one launch (start us, length us, event | category | flops | bytes accessed | tf_op | source)
XLA Modules:
  0.0 41.2 jit_solution(11347627187950570372)
XLA Ops:
  0.0 1.6 %pack_qkv.1 = (bf16[336,128]{1,0:T(8,128)(2,1)S(1)}, bf16[336,128]{1,0:T(8,128)(2,1)S(1)}, bf16[336,128]{1,0:T(8,128)(2,1)S(1)}, bf16[336,128]{1,0:T(8,128)(2,1)...) custom-call(bf16[112,1024]{1,0:T(8,128)(2,1)} %bitcast.8, ...), custom_call_target="tpu_custom_call" | custom-call | tf_op jit(solution)/shard_map/pack_qkv/pallas_call | solution.py:123
  1.6 3.0 %collective-permute-start.7 = (bf16[224,1024]{1,0:T(8,128)(2,1)S(1)}, bf16[224,1024]{1,0:T(8,128)(2,1)S(1)}, u32[]{:S(2)}, u32[]{:S(2)}) collective-permute-start(bf16[224,1024]{1,0:T(8,128)(2,1)S(1)} %get-tuple-element.25.refs_0_), channel_id=1, source_target_pairs={{0,16},{8,24},{16,0},{24,8},{1,17},{9,25},{17,1},{25,9},{2,18},{10... | collective-permute-start | bytes 1376264 | tf_op jit(solution)/shard_map/ppermute | solution.py:102
  4.7 2.5 %collective-permute-start = (bf16[336,128]{1,0:T(8,128)(2,1)S(1)}, bf16[336,128]{1,0:T(8,128)(2,1)S(1)}, u32[]{:S(2)}, u32[]{:S(2)}) collective-permute-start(bf16[336,128]{1,0:T(8,128)(2,1)S(1)} %get-tuple-element.16), channel_id=1, source_target_pairs={{0,3},{1,2},{2,1},{3,0},{4,7},{5,6},{6,5},{7,4},{8,11},{9,10},{10,... | collective-permute-start | bytes 258056 | tf_op jit(solution)/shard_map/ppermute | solution.py:102
  7.2 0.4 %collective-permute-start.1 = (bf16[336,128]{1,0:T(8,128)(2,1)S(1)}, bf16[336,128]{1,0:T(8,128)(2,1)S(1)}, u32[]{:S(2)}, u32[]{:S(2)}) collective-permute-start(bf16[336,128]{1,0:T(8,128)(2,1)S(1)} %get-tuple-element.17), channel_id=1, source_target_pairs={{0,2},{1,3},{2,0},{3,1},{4,6},{5,7},{6,4},{7,5},{8,10},{9,11},{10,... | collective-permute-start | bytes 258056 | tf_op jit(solution)/shard_map/ppermute | solution.py:102
  7.6 0.5 %collective-permute-start.2 = (bf16[336,128]{1,0:T(8,128)(2,1)S(1)}, bf16[336,128]{1,0:T(8,128)(2,1)S(1)}, u32[]{:S(2)}, u32[]{:S(2)}) collective-permute-start(bf16[336,128]{1,0:T(8,128)(2,1)S(1)} %get-tuple-element.18), channel_id=1, source_target_pairs={{0,1},{1,0},{2,3},{3,2},{4,5},{5,4},{6,7},{7,6},{8,9},{9,8},{10,11... | collective-permute-start | bytes 258056 | tf_op jit(solution)/shard_map/ppermute | solution.py:102
  8.1 3.5 %collective-permute-start.3 = (bf16[336,128]{1,0:T(8,128)(2,1)S(1)}, bf16[336,128]{1,0:T(8,128)(2,1)S(1)}, u32[]{:S(2)}, u32[]{:S(2)}) collective-permute-start(bf16[336,128]{1,0:T(8,128)(2,1)S(1)} %get-tuple-element.19), channel_id=1, source_target_pairs={{0,5},{1,4},{2,7},{3,6},{4,1},{5,0},{6,3},{7,2},{8,13},{9,12},{10,... | collective-permute-start | bytes 258056 | tf_op jit(solution)/shard_map/ppermute | solution.py:102
  11.7 0.0 collective-permute-done.refs_0_
  11.7 3.4 %collective-permute-start.4 = (bf16[336,128]{1,0:T(8,128)(2,1)S(1)}, bf16[336,128]{1,0:T(8,128)(2,1)S(1)}, u32[]{:S(2)}, u32[]{:S(2)}) collective-permute-start(bf16[336,128]{1,0:T(8,128)(2,1)S(1)} %get-tuple-element.20), channel_id=1, source_target_pairs={{0,7},{1,6},{2,5},{3,4},{4,3},{5,2},{6,1},{7,0},{8,15},{9,14},{10,... | collective-permute-start | bytes 258056 | tf_op jit(solution)/shard_map/ppermute | solution.py:102
  15.0 0.0 collective-permute-done.1.refs_1_
  15.0 0.4 collective-permute-start.5
  15.4 0.0 collective-permute-done.2.refs_2_
  15.4 2.0 %collective-permute-start.6 = (bf16[336,128]{1,0:T(8,128)(2,1)S(1)}, bf16[336,128]{1,0:T(8,128)(2,1)S(1)}, u32[]{:S(2)}, u32[]{:S(2)}) collective-permute-start(bf16[336,128]{1,0:T(8,128)(2,1)S(1)} %get-tuple-element.22), channel_id=1, source_target_pairs={{0,6},{1,7},{2,4},{3,5},{4,2},{5,3},{6,0},{7,1},{8,14},{9,15},{10,... | collective-permute-start | bytes 258056 | tf_op jit(solution)/shard_map/ppermute | solution.py:102
  17.4 3.4 %collective-permute-done.3.refs_3_ = bf16[336,128]{1,0:T(8,128)(2,1)S(1)} collective-permute-done((bf16[336,128]{1,0:T(8,128)(2,1)S(1)}, bf16[336,128]{1,0:T(8,128)(2,1)S(1)}, u32[]{:S(2)}, u32[]{:S(2)}) %collective-permute-start.3) | collective-permute-done | bytes 86048 | tf_op jit(solution)/shard_map/ppermute | solution.py:102
  20.8 0.0 collective-permute-done.7.refs_1_
  20.9 0.0 collective-permute-start.8
  20.9 0.5 %collective-permute-start.9 = (bf16[224,1024]{1,0:T(8,128)(2,1)S(1)}, bf16[224,1024]{1,0:T(8,128)(2,1)S(1)}, u32[]{:S(2)}, u32[]{:S(2)}) collective-permute-start(bf16[224,1024]{1,0:T(8,128)(2,1)S(1)} %collective-permute-done.7.refs_1_), channel_id=1, source_target_pairs={{0,8},{8,0},{16,24},{24,16},{1,9},{9,1},{17,25},{25,17},{2,10},{10... | collective-permute-start | bytes 1376264 | tf_op jit(solution)/shard_map/ppermute | solution.py:102
  21.4 0.0 collective-permute-done.4.refs_4_
  21.4 4.6 %collective-permute-done.5.refs_5_ = bf16[336,128]{1,0:T(8,128)(2,1)S(1)} collective-permute-done((bf16[336,128]{1,0:T(8,128)(2,1)S(1)}, bf16[336,128]{1,0:T(8,128)(2,1)S(1)}, u32[]{:S(2)}, u32[]{:S(2)}) %collective-permute-start.5) | collective-permute-done | bytes 86048 | tf_op jit(solution)/shard_map/ppermute | solution.py:102
  26.0 0.0 collective-permute-done.6.refs_6_
  26.0 1.6 %self_attention.1 = bf16[8,112,128]{2,1,0:T(8,128)(2,1)S(1)} custom-call(bf16[336,128]{1,0:T(8,128)(2,1)S(1)} %collective-permute-done.refs_0_, bf16[336,128]{1,0:T(8,128)(2,1)S(1)} %collective-permute-done.1.refs_1_, bf16[336,128]{1,0:T(8,128)(2,1)S(1)} %collective-permute-done.2.refs_2_, bf16[336,128]{1,0:T(8,128)(2,1)S(1)} %collective-permute-done.3.refs_3_, ...), custom_call_target="tpu_custom_call" | custom-call | flops 411041792 | bytes 917504 | tf_op jit(solution)/shard_map/self_attention/pallas_call | solution.py:136
  27.6 0.0 copy-start
  27.6 11.9 %all_to_all.5.o_ref = bf16[8,112,128]{2,1,0:T(8,128)(2,1)S(1)} all-to-all(bf16[8,112,128]{2,1,0:T(8,128)(2,1)S(1)} %self_attention.1), channel_id=1, replica_groups=mesh['view'=4,'ctx'=8] {'ctx'}, dimensions={0} | all-to-all | bytes 458752 | tf_op jit(solution)/shard_map/all_to_all | solution.py:149
  39.4 0.0 collective-permute-done.8.refs_2_
  39.4 0.0 collective-permute-done.9.refs_3_
  39.4 0.0 copy-done
  39.4 1.7 %cross_view.1 = bf16[112,1024]{1,0:T(8,128)(2,1)} custom-call(bf16[8,112,128]{2,1,0:T(8,128)(2,1)S(1)} %all_to_all.5.o_ref, bf16[112,1024]{1,0:T(8,128)(2,1)S(1)} %bitcast.7, bf16[224,1024]{1,0:T(8,128)(2,1)S(1)} %get-tuple-element.25.refs_0_, bf16[224,1024]{1,0:T(8,128)(2,1)S(1)} %collective-permute-done.7.refs_1_, ...), custom_call_target="tpu_custom_call" | custom-call | tf_op jit(solution)/shard_map/cross_view/pallas_call | solution.py:200
Async XLA Ops:
  1.6 19.2 %collective-permute-start.7 = (bf16[224,1024]{1,0:T(8,128)(2,1)S(1)}, bf16[224,1024]{1,0:T(8,128)(2,1)S(1)}, u32[]{:S(2)}, u32[]{:S(2)}) collective-permute-start(bf16[224,1024]{1,0:T(8,128)(2,1)S(1)} %get-tuple-element.25.refs_0_), channel_id=1, source_target_pairs={{0,16},{8,24},{16,0},{24,8},{1,17},{9,25},{17,1},{25,9},{2,18},{10... | collective-permute-start | bytes 1376264 | tf_op jit(solution)/shard_map/ppermute | solution.py:102
  4.7 7.0 %collective-permute-start = (bf16[336,128]{1,0:T(8,128)(2,1)S(1)}, bf16[336,128]{1,0:T(8,128)(2,1)S(1)}, u32[]{:S(2)}, u32[]{:S(2)}) collective-permute-start(bf16[336,128]{1,0:T(8,128)(2,1)S(1)} %get-tuple-element.16), channel_id=1, source_target_pairs={{0,3},{1,2},{2,1},{3,0},{4,7},{5,6},{6,5},{7,4},{8,11},{9,10},{10,... | collective-permute-start | bytes 258056 | tf_op jit(solution)/shard_map/ppermute | solution.py:102
  7.2 7.9 %collective-permute-start.1 = (bf16[336,128]{1,0:T(8,128)(2,1)S(1)}, bf16[336,128]{1,0:T(8,128)(2,1)S(1)}, u32[]{:S(2)}, u32[]{:S(2)}) collective-permute-start(bf16[336,128]{1,0:T(8,128)(2,1)S(1)} %get-tuple-element.17), channel_id=1, source_target_pairs={{0,2},{1,3},{2,0},{3,1},{4,6},{5,7},{6,4},{7,5},{8,10},{9,11},{10,... | collective-permute-start | bytes 258056 | tf_op jit(solution)/shard_map/ppermute | solution.py:102
  7.6 7.8 %collective-permute-start.2 = (bf16[336,128]{1,0:T(8,128)(2,1)S(1)}, bf16[336,128]{1,0:T(8,128)(2,1)S(1)}, u32[]{:S(2)}, u32[]{:S(2)}) collective-permute-start(bf16[336,128]{1,0:T(8,128)(2,1)S(1)} %get-tuple-element.18), channel_id=1, source_target_pairs={{0,1},{1,0},{2,3},{3,2},{4,5},{5,4},{6,7},{7,6},{8,9},{9,8},{10,11... | collective-permute-start | bytes 258056 | tf_op jit(solution)/shard_map/ppermute | solution.py:102
  8.1 12.7 %collective-permute-start.3 = (bf16[336,128]{1,0:T(8,128)(2,1)S(1)}, bf16[336,128]{1,0:T(8,128)(2,1)S(1)}, u32[]{:S(2)}, u32[]{:S(2)}) collective-permute-start(bf16[336,128]{1,0:T(8,128)(2,1)S(1)} %get-tuple-element.19), channel_id=1, source_target_pairs={{0,5},{1,4},{2,7},{3,6},{4,1},{5,0},{6,3},{7,2},{8,13},{9,12},{10,... | collective-permute-start | bytes 258056 | tf_op jit(solution)/shard_map/ppermute | solution.py:102
  11.7 9.7 %collective-permute-start.4 = (bf16[336,128]{1,0:T(8,128)(2,1)S(1)}, bf16[336,128]{1,0:T(8,128)(2,1)S(1)}, u32[]{:S(2)}, u32[]{:S(2)}) collective-permute-start(bf16[336,128]{1,0:T(8,128)(2,1)S(1)} %get-tuple-element.20), channel_id=1, source_target_pairs={{0,7},{1,6},{2,5},{3,4},{4,3},{5,2},{6,1},{7,0},{8,15},{9,14},{10,... | collective-permute-start | bytes 258056 | tf_op jit(solution)/shard_map/ppermute | solution.py:102
  15.0 11.0 %collective-permute-start.5 = (bf16[336,128]{1,0:T(8,128)(2,1)S(1)}, bf16[336,128]{1,0:T(8,128)(2,1)S(1)}, u32[]{:S(2)}, u32[]{:S(2)}) collective-permute-start(bf16[336,128]{1,0:T(8,128)(2,1)S(1)} %get-tuple-element.21), channel_id=1, source_target_pairs={{0,4},{1,5},{2,6},{3,7},{4,0},{5,1},{6,2},{7,3},{8,12},{9,13},{10,... | collective-permute-start | bytes 258056 | tf_op jit(solution)/shard_map/ppermute | solution.py:102
  15.4 10.6 %collective-permute-start.6 = (bf16[336,128]{1,0:T(8,128)(2,1)S(1)}, bf16[336,128]{1,0:T(8,128)(2,1)S(1)}, u32[]{:S(2)}, u32[]{:S(2)}) collective-permute-start(bf16[336,128]{1,0:T(8,128)(2,1)S(1)} %get-tuple-element.22), channel_id=1, source_target_pairs={{0,6},{1,7},{2,4},{3,5},{4,2},{5,3},{6,0},{7,1},{8,14},{9,15},{10,... | collective-permute-start | bytes 258056 | tf_op jit(solution)/shard_map/ppermute | solution.py:102
  20.9 18.6 %collective-permute-start.8 = (bf16[224,1024]{1,0:T(8,128)(2,1)S(1)}, bf16[224,1024]{1,0:T(8,128)(2,1)S(1)}, u32[]{:S(2)}, u32[]{:S(2)}) collective-permute-start(bf16[224,1024]{1,0:T(8,128)(2,1)S(1)} %get-tuple-element.25.refs_0_), channel_id=1, source_target_pairs={{0,8},{8,0},{16,24},{24,16},{1,9},{9,1},{17,25},{25,17},{2,10},{10... | collective-permute-start | bytes 1376264 | tf_op jit(solution)/shard_map/ppermute | solution.py:102
  20.9 18.6 %collective-permute-start.9 = (bf16[224,1024]{1,0:T(8,128)(2,1)S(1)}, bf16[224,1024]{1,0:T(8,128)(2,1)S(1)}, u32[]{:S(2)}, u32[]{:S(2)}) collective-permute-start(bf16[224,1024]{1,0:T(8,128)(2,1)S(1)} %collective-permute-done.7.refs_1_), channel_id=1, source_target_pairs={{0,8},{8,0},{16,24},{24,16},{1,9},{9,1},{17,25},{25,17},{2,10},{10... | collective-permute-start | bytes 1376264 | tf_op jit(solution)/shard_map/ppermute | solution.py:102
  27.6 11.9 %copy-start = (bf16[1,112,1024]{2,1,0:T(8,128)(2,1)S(1)}, bf16[1,112,1024]{2,1,0:T(8,128)(2,1)}, u32[]{:S(2)}) copy-start(bf16[1,112,1024]{2,1,0:T(8,128)(2,1)} %param.9) | copy-start | bytes 688132

commit v20 on v10

--- a/solution.py
+++ b/solution.py
@@ -65,23 +65,33 @@
 def cross_kernel(head_count, o_ref, q_ref, *refs):
     *pair_refs, out_ref = refs
     rows = q_ref.shape[0]
+    lane = lax.broadcasted_iota(jnp.int32, (rows, HEAD), 1)
+    scores = [jnp.zeros((rows, HEAD), jnp.float32) for _ in pair_refs]
     for head in range(head_count):
         lanes = slice(head * HEAD, (head + 1) * HEAD)
         o_self = o_ref[head].astype(jnp.float32)
         query = (q_ref[:, lanes].astype(jnp.float32) + o_self).astype(jnp.bfloat16).astype(jnp.float32)
-        scores = [
-            jnp.sum(query * ref[0:rows, lanes].astype(jnp.float32), axis=-1, keepdims=True)
-            for ref in pair_refs
-        ]
-        top = functools.reduce(jnp.maximum, scores)
-        weights = [jnp.exp2((score - top) * EXP2_SCALE) for score in scores]
-        inverse = 1.0 / sum(weights[1:], weights[0])
+        for view, ref in enumerate(pair_refs):
+            products = query * ref[0:rows, lanes].astype(jnp.float32)
+            summed = jnp.sum(products, axis=-1, keepdims=True)
+            scores[view] = jnp.where(lane == head, summed, scores[view])
+    top = functools.reduce(jnp.maximum, scores)
+    weights = [jnp.exp2((score - top) * EXP2_SCALE) for score in scores]
+    inverse = 1.0 / sum(weights[1:], weights[0])
+    packed = jnp.concatenate([(weight * inverse).astype(jnp.bfloat16) for weight in weights], axis=0)
+    source = lax.broadcasted_iota(jnp.int32, (HEAD, 2 * HEAD), 0)
+    target = lax.broadcasted_iota(jnp.int32, (HEAD, 2 * HEAD), 1)
+    second = jnp.where(target >= HEAD, 1, 0)
+    for head in range(0, head_count, 2):
+        lanes = slice(head * HEAD, (head + 2) * HEAD)
+        spread = jnp.where(source == second + head, 1.0, 0.0).astype(jnp.bfloat16)
+        rounded = jnp.dot(packed, spread, preferred_element_type=jnp.float32)
         mixed = None
-        for weight, ref in zip(weights, pair_refs):
-            rounded = (weight * inverse).astype(jnp.bfloat16).astype(jnp.float32)
-            term = rounded * ref[rows : 2 * rows, lanes].astype(jnp.float32)
+        for view, ref in enumerate(pair_refs):
+            term = rounded[view * rows : (view + 1) * rows] * ref[rows : 2 * rows, lanes].astype(jnp.float32)
             mixed = term if mixed is None else mixed + term
         o_cross = mixed.astype(jnp.bfloat16).astype(jnp.float32)
+        o_self = jnp.concatenate([o_ref[head], o_ref[head + 1]], axis=1).astype(jnp.float32)
         out_ref[:, lanes] = (o_self + o_cross).astype(jnp.bfloat16)
 
 

time: 40.7 us -> 40.7 us (level)
  no operation moved by 1% of the time
where the time goes in v20:
time: 40.7 us; the launch traced here: 40.5 us
  starting transfers between devices  21.3 us (52%)
  blocking collectives  11 us (27%)
  Pallas kernels  4.83 us (12%)
  waiting for transfers between devices  3.33 us (8%)
    ppermute x10, starting transfers between devices, swap(): lax.ppermute(array, axis_name, [(i, i ^ partner) for i in range(axis_size)])  21.3 us
    all_to_all x1, blocking collectives, split_attention(): back = lax.all_to_all(own, 'ctx', split_axis=0, concat_axis=0, tiled=True)  11 us
    ppermute x10, waiting for transfers between devices, swap(): lax.ppermute(array, axis_name, [(i, i ^ partner) for i in range(axis_size)])  3.33 us
    pallas_call x1, Pallas kernels, body(): pl.pallas_call(functools.partial(cross_kernel, heads), out_shape=jax.Shap...  1.65 us
    pallas_call x1, Pallas kernels, split_attention(): pl.pallas_call(functools.partial(pack_kernel, partners), out_shape=[block...  1.61 us
    pallas_call x1, Pallas kernels, split_attention(): pl.pallas_call(functools.partial(packed_attention_kernel, partners, rows,...  1.57 us
  transfers between devices with their start and end apart: 10, of which 3 were waited for; matrix products, arithmetic and copies ran while one was open for 0% of the time, Pallas kernels for 4%

profile of v20, /device:TPU:0, one launch (start us, length us, event | category | flops | bytes accessed | tf_op | source)
XLA Modules:
  0.0 40.5 jit_solution(5824014326458603081)
XLA Ops:
  0.0 1.6 %pack_qkv.1 = (bf16[336,128]{1,0:T(8,128)(2,1)S(1)}, bf16[336,128]{1,0:T(8,128)(2,1)S(1)}, bf16[336,128]{1,0:T(8,128)(2,1)S(1)}, bf16[336,128]{1,0:T(8,128)(2,1)...) custom-call(bf16[112,1024]{1,0:T(8,128)(2,1)} %bitcast.8, ...), custom_call_target="tpu_custom_call" | custom-call | tf_op jit(solution)/shard_map/pack_qkv/pallas_call | solution.py:124
  1.6 3.0 %collective-permute-start.7 = (bf16[224,1024]{1,0:T(8,128)(2,1)S(1)}, bf16[224,1024]{1,0:T(8,128)(2,1)S(1)}, u32[]{:S(2)}, u32[]{:S(2)}) collective-permute-start(bf16[224,1024]{1,0:T(8,128)(2,1)S(1)} %get-tuple-element.25.refs_0_), channel_id=1, source_target_pairs={{0,16},{8,24},{16,0},{24,8},{1,17},{9,25},{17,1},{25,9},{2,18},{10... | collective-permute-start | bytes 1376264 | tf_op jit(solution)/shard_map/ppermute | solution.py:103
  4.7 2.5 %collective-permute-start = (bf16[336,128]{1,0:T(8,128)(2,1)S(1)}, bf16[336,128]{1,0:T(8,128)(2,1)S(1)}, u32[]{:S(2)}, u32[]{:S(2)}) collective-permute-start(bf16[336,128]{1,0:T(8,128)(2,1)S(1)} %get-tuple-element.16), channel_id=1, source_target_pairs={{0,3},{1,2},{2,1},{3,0},{4,7},{5,6},{6,5},{7,4},{8,11},{9,10},{10,... | collective-permute-start | bytes 258056 | tf_op jit(solution)/shard_map/ppermute | solution.py:103
  7.2 2.4 %collective-permute-start.1 = (bf16[336,128]{1,0:T(8,128)(2,1)S(1)}, bf16[336,128]{1,0:T(8,128)(2,1)S(1)}, u32[]{:S(2)}, u32[]{:S(2)}) collective-permute-start(bf16[336,128]{1,0:T(8,128)(2,1)S(1)} %get-tuple-element.17), channel_id=1, source_target_pairs={{0,7},{1,6},{2,5},{3,4},{4,3},{5,2},{6,1},{7,0},{8,15},{9,14},{10,... | collective-permute-start | bytes 258056 | tf_op jit(solution)/shard_map/ppermute | solution.py:103
  9.6 1.3 %collective-permute-start.2 = (bf16[336,128]{1,0:T(8,128)(2,1)S(1)}, bf16[336,128]{1,0:T(8,128)(2,1)S(1)}, u32[]{:S(2)}, u32[]{:S(2)}) collective-permute-start(bf16[336,128]{1,0:T(8,128)(2,1)S(1)} %get-tuple-element.18), channel_id=1, source_target_pairs={{0,6},{1,7},{2,4},{3,5},{4,2},{5,3},{6,0},{7,1},{8,14},{9,15},{10,... | collective-permute-start | bytes 258056 | tf_op jit(solution)/shard_map/ppermute | solution.py:103
  11.0 0.0 collective-permute-start.3
  11.0 0.0 collective-permute-done.refs_0_
  11.0 4.0 %collective-permute-start.4 = (bf16[336,128]{1,0:T(8,128)(2,1)S(1)}, bf16[336,128]{1,0:T(8,128)(2,1)S(1)}, u32[]{:S(2)}, u32[]{:S(2)}) collective-permute-start(bf16[336,128]{1,0:T(8,128)(2,1)S(1)} %get-tuple-element.20), channel_id=1, source_target_pairs={{0,5},{1,4},{2,7},{3,6},{4,1},{5,0},{6,3},{7,2},{8,13},{9,12},{10,... | collective-permute-start | bytes 258056 | tf_op jit(solution)/shard_map/ppermute | solution.py:103
  14.9 0.0 collective-permute-done.1.refs_1_
  14.9 6.8 %collective-permute-start.5 = (bf16[336,128]{1,0:T(8,128)(2,1)S(1)}, bf16[336,128]{1,0:T(8,128)(2,1)S(1)}, u32[]{:S(2)}, u32[]{:S(2)}) collective-permute-start(bf16[336,128]{1,0:T(8,128)(2,1)S(1)} %get-tuple-element.21), channel_id=1, source_target_pairs={{0,4},{1,5},{2,6},{3,7},{4,0},{5,1},{6,2},{7,3},{8,12},{9,13},{10,... | collective-permute-start | bytes 258056 | tf_op jit(solution)/shard_map/ppermute | solution.py:103
  21.8 0.0 collective-permute-done.2.refs_2_
  21.8 0.7 %collective-permute-start.6 = (bf16[336,128]{1,0:T(8,128)(2,1)S(1)}, bf16[336,128]{1,0:T(8,128)(2,1)S(1)}, u32[]{:S(2)}, u32[]{:S(2)}) collective-permute-start(bf16[336,128]{1,0:T(8,128)(2,1)S(1)} %get-tuple-element.22), channel_id=1, source_target_pairs={{0,1},{1,0},{2,3},{3,2},{4,5},{5,4},{6,7},{7,6},{8,9},{9,8},{10,11... | collective-permute-start | bytes 258056 | tf_op jit(solution)/shard_map/ppermute | solution.py:103
  22.4 0.0 collective-permute-done.3.refs_3_
  22.4 0.0 collective-permute-done.7.refs_1_
  22.4 0.0 collective-permute-start.8
  22.4 0.5 %collective-permute-start.9 = (bf16[224,1024]{1,0:T(8,128)(2,1)S(1)}, bf16[224,1024]{1,0:T(8,128)(2,1)S(1)}, u32[]{:S(2)}, u32[]{:S(2)}) collective-permute-start(bf16[224,1024]{1,0:T(8,128)(2,1)S(1)} %collective-permute-done.7.refs_1_), channel_id=1, source_target_pairs={{0,8},{8,0},{16,24},{24,16},{1,9},{9,1},{17,25},{25,17},{2,10},{10... | collective-permute-start | bytes 1376264 | tf_op jit(solution)/shard_map/ppermute | solution.py:103
  22.9 1.1 %collective-permute-done.4.refs_4_ = bf16[336,128]{1,0:T(8,128)(2,1)S(1)} collective-permute-done((bf16[336,128]{1,0:T(8,128)(2,1)S(1)}, bf16[336,128]{1,0:T(8,128)(2,1)S(1)}, u32[]{:S(2)}, u32[]{:S(2)}) %collective-permute-start.4) | collective-permute-done | bytes 86048 | tf_op jit(solution)/shard_map/ppermute | solution.py:103
  24.0 0.7 %collective-permute-done.5.refs_5_ = bf16[336,128]{1,0:T(8,128)(2,1)S(1)} collective-permute-done((bf16[336,128]{1,0:T(8,128)(2,1)S(1)}, bf16[336,128]{1,0:T(8,128)(2,1)S(1)}, u32[]{:S(2)}, u32[]{:S(2)}) %collective-permute-start.5) | collective-permute-done | bytes 86048 | tf_op jit(solution)/shard_map/ppermute | solution.py:103
  24.7 1.5 %collective-permute-done.6.refs_6_ = bf16[336,128]{1,0:T(8,128)(2,1)S(1)} collective-permute-done((bf16[336,128]{1,0:T(8,128)(2,1)S(1)}, bf16[336,128]{1,0:T(8,128)(2,1)S(1)}, u32[]{:S(2)}, u32[]{:S(2)}) %collective-permute-start.6) | collective-permute-done | bytes 86048 | tf_op jit(solution)/shard_map/ppermute | solution.py:103
  26.2 1.6 %self_attention.1 = bf16[8,112,128]{2,1,0:T(8,128)(2,1)S(1)} custom-call(bf16[336,128]{1,0:T(8,128)(2,1)S(1)} %collective-permute-done.refs_0_, bf16[336,128]{1,0:T(8,128)(2,1)S(1)} %collective-permute-done.1.refs_1_, bf16[336,128]{1,0:T(8,128)(2,1)S(1)} %collective-permute-done.2.refs_2_, bf16[336,128]{1,0:T(8,128)(2,1)S(1)} %collective-permute-done.3.refs_3_, ...), custom_call_target="tpu_custom_call" | custom-call | flops 411041792 | bytes 917504 | tf_op jit(solution)/shard_map/self_attention/pallas_call | solution.py:137
  27.8 0.0 copy-start
  27.8 11.0 %all_to_all.5.o_ref = bf16[8,112,128]{2,1,0:T(8,128)(2,1)S(1)} all-to-all(bf16[8,112,128]{2,1,0:T(8,128)(2,1)S(1)} %self_attention.1), channel_id=1, replica_groups=mesh['view'=4,'ctx'=8] {'ctx'}, dimensions={0} | all-to-all | bytes 458752 | tf_op jit(solution)/shard_map/all_to_all | solution.py:150
  38.9 0.0 collective-permute-done.8.refs_2_
  38.9 0.0 collective-permute-done.9.refs_3_
  38.9 0.0 copy-done
  38.9 1.7 %cross_view.1 = bf16[112,1024]{1,0:T(8,128)(2,1)} custom-call(bf16[8,112,128]{2,1,0:T(8,128)(2,1)S(1)} %all_to_all.5.o_ref, bf16[112,1024]{1,0:T(8,128)(2,1)S(1)} %bitcast.7, bf16[224,1024]{1,0:T(8,128)(2,1)S(1)} %get-tuple-element.25.refs_0_, bf16[224,1024]{1,0:T(8,128)(2,1)S(1)} %collective-permute-done.7.refs_1_, ...), custom_call_target="tpu_custom_call" | custom-call | tf_op jit(solution)/shard_map/cross_view/pallas_call | solution.py:201
Async XLA Ops:
  1.6 20.8 %collective-permute-start.7 = (bf16[224,1024]{1,0:T(8,128)(2,1)S(1)}, bf16[224,1024]{1,0:T(8,128)(2,1)S(1)}, u32[]{:S(2)}, u32[]{:S(2)}) collective-permute-start(bf16[224,1024]{1,0:T(8,128)(2,1)S(1)} %get-tuple-element.25.refs_0_), channel_id=1, source_target_pairs={{0,16},{8,24},{16,0},{24,8},{1,17},{9,25},{17,1},{25,9},{2,18},{10... | collective-permute-start | bytes 1376264 | tf_op jit(solution)/shard_map/ppermute | solution.py:103
  4.7 6.3 %collective-permute-start = (bf16[336,128]{1,0:T(8,128)(2,1)S(1)}, bf16[336,128]{1,0:T(8,128)(2,1)S(1)}, u32[]{:S(2)}, u32[]{:S(2)}) collective-permute-start(bf16[336,128]{1,0:T(8,128)(2,1)S(1)} %get-tuple-element.16), channel_id=1, source_target_pairs={{0,3},{1,2},{2,1},{3,0},{4,7},{5,6},{6,5},{7,4},{8,11},{9,10},{10,... | collective-permute-start | bytes 258056 | tf_op jit(solution)/shard_map/ppermute | solution.py:103
  7.2 7.8 %collective-permute-start.1 = (bf16[336,128]{1,0:T(8,128)(2,1)S(1)}, bf16[336,128]{1,0:T(8,128)(2,1)S(1)}, u32[]{:S(2)}, u32[]{:S(2)}) collective-permute-start(bf16[336,128]{1,0:T(8,128)(2,1)S(1)} %get-tuple-element.17), channel_id=1, source_target_pairs={{0,7},{1,6},{2,5},{3,4},{4,3},{5,2},{6,1},{7,0},{8,15},{9,14},{10,... | collective-permute-start | bytes 258056 | tf_op jit(solution)/shard_map/ppermute | solution.py:103
  9.6 12.2 %collective-permute-start.2 = (bf16[336,128]{1,0:T(8,128)(2,1)S(1)}, bf16[336,128]{1,0:T(8,128)(2,1)S(1)}, u32[]{:S(2)}, u32[]{:S(2)}) collective-permute-start(bf16[336,128]{1,0:T(8,128)(2,1)S(1)} %get-tuple-element.18), channel_id=1, source_target_pairs={{0,6},{1,7},{2,4},{3,5},{4,2},{5,3},{6,0},{7,1},{8,14},{9,15},{10,... | collective-permute-start | bytes 258056 | tf_op jit(solution)/shard_map/ppermute | solution.py:103
  11.0 11.5 %collective-permute-start.3 = (bf16[336,128]{1,0:T(8,128)(2,1)S(1)}, bf16[336,128]{1,0:T(8,128)(2,1)S(1)}, u32[]{:S(2)}, u32[]{:S(2)}) collective-permute-start(bf16[336,128]{1,0:T(8,128)(2,1)S(1)} %get-tuple-element.19), channel_id=1, source_target_pairs={{0,2},{1,3},{2,0},{3,1},{4,6},{5,7},{6,4},{7,5},{8,10},{9,11},{10,... | collective-permute-start | bytes 258056 | tf_op jit(solution)/shard_map/ppermute | solution.py:103
  11.0 13.0 %collective-permute-start.4 = (bf16[336,128]{1,0:T(8,128)(2,1)S(1)}, bf16[336,128]{1,0:T(8,128)(2,1)S(1)}, u32[]{:S(2)}, u32[]{:S(2)}) collective-permute-start(bf16[336,128]{1,0:T(8,128)(2,1)S(1)} %get-tuple-element.20), channel_id=1, source_target_pairs={{0,5},{1,4},{2,7},{3,6},{4,1},{5,0},{6,3},{7,2},{8,13},{9,12},{10,... | collective-permute-start | bytes 258056 | tf_op jit(solution)/shard_map/ppermute | solution.py:103
  14.9 9.8 %collective-permute-start.5 = (bf16[336,128]{1,0:T(8,128)(2,1)S(1)}, bf16[336,128]{1,0:T(8,128)(2,1)S(1)}, u32[]{:S(2)}, u32[]{:S(2)}) collective-permute-start(bf16[336,128]{1,0:T(8,128)(2,1)S(1)} %get-tuple-element.21), channel_id=1, source_target_pairs={{0,4},{1,5},{2,6},{3,7},{4,0},{5,1},{6,2},{7,3},{8,12},{9,13},{10,... | collective-permute-start | bytes 258056 | tf_op jit(solution)/shard_map/ppermute | solution.py:103
  21.8 4.5 %collective-permute-start.6 = (bf16[336,128]{1,0:T(8,128)(2,1)S(1)}, bf16[336,128]{1,0:T(8,128)(2,1)S(1)}, u32[]{:S(2)}, u32[]{:S(2)}) collective-permute-start(bf16[336,128]{1,0:T(8,128)(2,1)S(1)} %get-tuple-element.22), channel_id=1, source_target_pairs={{0,1},{1,0},{2,3},{3,2},{4,5},{5,4},{6,7},{7,6},{8,9},{9,8},{10,11... | collective-permute-start | bytes 258056 | tf_op jit(solution)/shard_map/ppermute | solution.py:103
  22.4 16.5 %collective-permute-start.8 = (bf16[224,1024]{1,0:T(8,128)(2,1)S(1)}, bf16[224,1024]{1,0:T(8,128)(2,1)S(1)}, u32[]{:S(2)}, u32[]{:S(2)}) collective-permute-start(bf16[224,1024]{1,0:T(8,128)(2,1)S(1)} %get-tuple-element.25.refs_0_), channel_id=1, source_target_pairs={{0,8},{8,0},{16,24},{24,16},{1,9},{9,1},{17,25},{25,17},{2,10},{10... | collective-permute-start | bytes 1376264 | tf_op jit(solution)/shard_map/ppermute | solution.py:103
  22.4 16.5 %collective-permute-start.9 = (bf16[224,1024]{1,0:T(8,128)(2,1)S(1)}, bf16[224,1024]{1,0:T(8,128)(2,1)S(1)}, u32[]{:S(2)}, u32[]{:S(2)}) collective-permute-start(bf16[224,1024]{1,0:T(8,128)(2,1)S(1)} %collective-permute-done.7.refs_1_), channel_id=1, source_target_pairs={{0,8},{8,0},{16,24},{24,16},{1,9},{9,1},{17,25},{25,17},{2,10},{10... | collective-permute-start | bytes 1376264 | tf_op jit(solution)/shard_map/ppermute | solution.py:103
  27.8 11.1 %copy-start = (bf16[1,112,1024]{2,1,0:T(8,128)(2,1)S(1)}, bf16[1,112,1024]{2,1,0:T(8,128)(2,1)}, u32[]{:S(2)}) copy-start(bf16[1,112,1024]{2,1,0:T(8,128)(2,1)} %param.9) | copy-start | bytes 688132

commit v21 on v10

--- a/solution.py
+++ b/solution.py
@@ -65,8 +65,10 @@
 def cross_kernel(head_count, o_ref, q_ref, *refs):
     *pair_refs, out_ref = refs
     rows = q_ref.shape[0]
-    for head in range(head_count):
-        lanes = slice(head * HEAD, (head + 1) * HEAD)
+
+    @pl.loop(0, head_count)
+    def _(head):
+        lanes = pl.ds(pl.multiple_of(head * HEAD, HEAD), HEAD)
         o_self = o_ref[head].astype(jnp.float32)
         query = (q_ref[:, lanes].astype(jnp.float32) + o_self).astype(jnp.bfloat16).astype(jnp.float32)
         scores = [

time: 40.7 us -> 41.5 us (1.020)
  Pallas kernels: 4.85 us -> 5.63 us
    pallas_call x1, Pallas kernels: 1.68 us -> 2.46 us  [body(): pl.pallas_call(functools.partial(cross_kernel, heads), out_shape=jax.Shap...]
where the time goes in v21:
time: 41.5 us; the launch traced here: 41.4 us
  starting transfers between devices  21.3 us (51%)
  blocking collectives  11 us (27%)
  Pallas kernels  5.63 us (14%)
  waiting for transfers between devices  3.33 us (8%)
    ppermute x10, starting transfers between devices, swap(): lax.ppermute(array, axis_name, [(i, i ^ partner) for i in range(axis_size)])  21.3 us
    all_to_all x1, blocking collectives, split_attention(): back = lax.all_to_all(own, 'ctx', split_axis=0, concat_axis=0, tiled=True)  11 us
    ppermute x10, waiting for transfers between devices, swap(): lax.ppermute(array, axis_name, [(i, i ^ partner) for i in range(axis_size)])  3.33 us
    pallas_call x1, Pallas kernels, body(): pl.pallas_call(functools.partial(cross_kernel, heads), out_shape=jax.Shap...  2.46 us
    pallas_call x1, Pallas kernels, split_attention(): pl.pallas_call(functools.partial(pack_kernel, partners), out_shape=[block...  1.61 us
    pallas_call x1, Pallas kernels, split_attention(): pl.pallas_call(functools.partial(packed_attention_kernel, partners, rows,...  1.57 us
  transfers between devices with their start and end apart: 10, of which 3 were waited for; matrix products, arithmetic and copies ran while one was open for 0% of the time, Pallas kernels for 4%

profile of v21, /device:TPU:0, one launch (start us, length us, event | category | flops | bytes accessed | tf_op | source)
XLA Modules:
  0.0 41.4 jit_solution(11876553154723021088)
XLA Ops:
  0.0 1.6 %pack_qkv.1 = (bf16[336,128]{1,0:T(8,128)(2,1)S(1)}, bf16[336,128]{1,0:T(8,128)(2,1)S(1)}, bf16[336,128]{1,0:T(8,128)(2,1)S(1)}, bf16[336,128]{1,0:T(8,128)(2,1)...) custom-call(bf16[112,1024]{1,0:T(8,128)(2,1)} %bitcast.8, ...), custom_call_target="tpu_custom_call" | custom-call | tf_op jit(solution)/shard_map/pack_qkv/pallas_call | solution.py:116
  1.6 3.0 %collective-permute-start.7 = (bf16[224,1024]{1,0:T(8,128)(2,1)S(1)}, bf16[224,1024]{1,0:T(8,128)(2,1)S(1)}, u32[]{:S(2)}, u32[]{:S(2)}) collective-permute-start(bf16[224,1024]{1,0:T(8,128)(2,1)S(1)} %get-tuple-element.25.refs_0_), channel_id=1, source_target_pairs={{0,16},{8,24},{16,0},{24,8},{1,17},{9,25},{17,1},{25,9},{2,18},{10... | collective-permute-start | bytes 1376264 | tf_op jit(solution)/shard_map/ppermute | solution.py:95
  4.7 2.5 %collective-permute-start = (bf16[336,128]{1,0:T(8,128)(2,1)S(1)}, bf16[336,128]{1,0:T(8,128)(2,1)S(1)}, u32[]{:S(2)}, u32[]{:S(2)}) collective-permute-start(bf16[336,128]{1,0:T(8,128)(2,1)S(1)} %get-tuple-element.16), channel_id=1, source_target_pairs={{0,3},{1,2},{2,1},{3,0},{4,7},{5,6},{6,5},{7,4},{8,11},{9,10},{10,... | collective-permute-start | bytes 258056 | tf_op jit(solution)/shard_map/ppermute | solution.py:95
  7.2 2.4 %collective-permute-start.1 = (bf16[336,128]{1,0:T(8,128)(2,1)S(1)}, bf16[336,128]{1,0:T(8,128)(2,1)S(1)}, u32[]{:S(2)}, u32[]{:S(2)}) collective-permute-start(bf16[336,128]{1,0:T(8,128)(2,1)S(1)} %get-tuple-element.17), channel_id=1, source_target_pairs={{0,7},{1,6},{2,5},{3,4},{4,3},{5,2},{6,1},{7,0},{8,15},{9,14},{10,... | collective-permute-start | bytes 258056 | tf_op jit(solution)/shard_map/ppermute | solution.py:95
  9.6 1.3 %collective-permute-start.2 = (bf16[336,128]{1,0:T(8,128)(2,1)S(1)}, bf16[336,128]{1,0:T(8,128)(2,1)S(1)}, u32[]{:S(2)}, u32[]{:S(2)}) collective-permute-start(bf16[336,128]{1,0:T(8,128)(2,1)S(1)} %get-tuple-element.18), channel_id=1, source_target_pairs={{0,6},{1,7},{2,4},{3,5},{4,2},{5,3},{6,0},{7,1},{8,14},{9,15},{10,... | collective-permute-start | bytes 258056 | tf_op jit(solution)/shard_map/ppermute | solution.py:95
  11.0 0.0 collective-permute-start.3
  11.0 0.0 collective-permute-done.refs_0_
  11.0 4.0 %collective-permute-start.4 = (bf16[336,128]{1,0:T(8,128)(2,1)S(1)}, bf16[336,128]{1,0:T(8,128)(2,1)S(1)}, u32[]{:S(2)}, u32[]{:S(2)}) collective-permute-start(bf16[336,128]{1,0:T(8,128)(2,1)S(1)} %get-tuple-element.20), channel_id=1, source_target_pairs={{0,5},{1,4},{2,7},{3,6},{4,1},{5,0},{6,3},{7,2},{8,13},{9,12},{10,... | collective-permute-start | bytes 258056 | tf_op jit(solution)/shard_map/ppermute | solution.py:95
  14.9 0.0 collective-permute-done.1.refs_1_
  14.9 6.8 %collective-permute-start.5 = (bf16[336,128]{1,0:T(8,128)(2,1)S(1)}, bf16[336,128]{1,0:T(8,128)(2,1)S(1)}, u32[]{:S(2)}, u32[]{:S(2)}) collective-permute-start(bf16[336,128]{1,0:T(8,128)(2,1)S(1)} %get-tuple-element.21), channel_id=1, source_target_pairs={{0,4},{1,5},{2,6},{3,7},{4,0},{5,1},{6,2},{7,3},{8,12},{9,13},{10,... | collective-permute-start | bytes 258056 | tf_op jit(solution)/shard_map/ppermute | solution.py:95
  21.8 0.0 collective-permute-done.2.refs_2_
  21.8 0.7 %collective-permute-start.6 = (bf16[336,128]{1,0:T(8,128)(2,1)S(1)}, bf16[336,128]{1,0:T(8,128)(2,1)S(1)}, u32[]{:S(2)}, u32[]{:S(2)}) collective-permute-start(bf16[336,128]{1,0:T(8,128)(2,1)S(1)} %get-tuple-element.22), channel_id=1, source_target_pairs={{0,1},{1,0},{2,3},{3,2},{4,5},{5,4},{6,7},{7,6},{8,9},{9,8},{10,11... | collective-permute-start | bytes 258056 | tf_op jit(solution)/shard_map/ppermute | solution.py:95
  22.4 0.0 collective-permute-done.3.refs_3_
  22.4 0.0 collective-permute-done.7.refs_1_
  22.4 0.0 collective-permute-start.8
  22.4 0.5 %collective-permute-start.9 = (bf16[224,1024]{1,0:T(8,128)(2,1)S(1)}, bf16[224,1024]{1,0:T(8,128)(2,1)S(1)}, u32[]{:S(2)}, u32[]{:S(2)}) collective-permute-start(bf16[224,1024]{1,0:T(8,128)(2,1)S(1)} %collective-permute-done.7.refs_1_), channel_id=1, source_target_pairs={{0,8},{8,0},{16,24},{24,16},{1,9},{9,1},{17,25},{25,17},{2,10},{10... | collective-permute-start | bytes 1376264 | tf_op jit(solution)/shard_map/ppermute | solution.py:95
  22.9 1.1 %collective-permute-done.4.refs_4_ = bf16[336,128]{1,0:T(8,128)(2,1)S(1)} collective-permute-done((bf16[336,128]{1,0:T(8,128)(2,1)S(1)}, bf16[336,128]{1,0:T(8,128)(2,1)S(1)}, u32[]{:S(2)}, u32[]{:S(2)}) %collective-permute-start.4) | collective-permute-done | bytes 86048 | tf_op jit(solution)/shard_map/ppermute | solution.py:95
  24.0 0.7 %collective-permute-done.5.refs_5_ = bf16[336,128]{1,0:T(8,128)(2,1)S(1)} collective-permute-done((bf16[336,128]{1,0:T(8,128)(2,1)S(1)}, bf16[336,128]{1,0:T(8,128)(2,1)S(1)}, u32[]{:S(2)}, u32[]{:S(2)}) %collective-permute-start.5) | collective-permute-done | bytes 86048 | tf_op jit(solution)/shard_map/ppermute | solution.py:95
  24.7 1.5 %collective-permute-done.6.refs_6_ = bf16[336,128]{1,0:T(8,128)(2,1)S(1)} collective-permute-done((bf16[336,128]{1,0:T(8,128)(2,1)S(1)}, bf16[336,128]{1,0:T(8,128)(2,1)S(1)}, u32[]{:S(2)}, u32[]{:S(2)}) %collective-permute-start.6) | collective-permute-done | bytes 86048 | tf_op jit(solution)/shard_map/ppermute | solution.py:95
  26.2 1.6 %self_attention.1 = bf16[8,112,128]{2,1,0:T(8,128)(2,1)S(1)} custom-call(bf16[336,128]{1,0:T(8,128)(2,1)S(1)} %collective-permute-done.refs_0_, bf16[336,128]{1,0:T(8,128)(2,1)S(1)} %collective-permute-done.1.refs_1_, bf16[336,128]{1,0:T(8,128)(2,1)S(1)} %collective-permute-done.2.refs_2_, bf16[336,128]{1,0:T(8,128)(2,1)S(1)} %collective-permute-done.3.refs_3_, ...), custom_call_target="tpu_custom_call" | custom-call | flops 411041792 | bytes 917504 | tf_op jit(solution)/shard_map/self_attention/pallas_call | solution.py:129
  27.8 0.0 copy-start
  27.8 11.0 %all_to_all.5.o_ref = bf16[8,112,128]{2,1,0:T(8,128)(2,1)S(1)} all-to-all(bf16[8,112,128]{2,1,0:T(8,128)(2,1)S(1)} %self_attention.1), channel_id=1, replica_groups=mesh['view'=4,'ctx'=8] {'ctx'}, dimensions={0} | all-to-all | bytes 458752 | tf_op jit(solution)/shard_map/all_to_all | solution.py:142
  38.9 0.0 collective-permute-done.8.refs_2_
  38.9 0.0 collective-permute-done.9.refs_3_
  38.9 0.0 copy-done
  38.9 2.5 %cross_view.1 = bf16[112,1024]{1,0:T(8,128)(2,1)} custom-call(bf16[8,112,128]{2,1,0:T(8,128)(2,1)S(1)} %all_to_all.5.o_ref, bf16[112,1024]{1,0:T(8,128)(2,1)S(1)} %bitcast.7, bf16[224,1024]{1,0:T(8,128)(2,1)S(1)} %get-tuple-element.25.refs_0_, bf16[224,1024]{1,0:T(8,128)(2,1)S(1)} %collective-permute-done.7.refs_1_, ...), custom_call_target="tpu_custom_call" | custom-call | tf_op jit(solution)/shard_map/cross_view/pallas_call | solution.py:193
Async XLA Ops:
  1.6 20.8 %collective-permute-start.7 = (bf16[224,1024]{1,0:T(8,128)(2,1)S(1)}, bf16[224,1024]{1,0:T(8,128)(2,1)S(1)}, u32[]{:S(2)}, u32[]{:S(2)}) collective-permute-start(bf16[224,1024]{1,0:T(8,128)(2,1)S(1)} %get-tuple-element.25.refs_0_), channel_id=1, source_target_pairs={{0,16},{8,24},{16,0},{24,8},{1,17},{9,25},{17,1},{25,9},{2,18},{10... | collective-permute-start | bytes 1376264 | tf_op jit(solution)/shard_map/ppermute | solution.py:95
  4.7 6.3 %collective-permute-start = (bf16[336,128]{1,0:T(8,128)(2,1)S(1)}, bf16[336,128]{1,0:T(8,128)(2,1)S(1)}, u32[]{:S(2)}, u32[]{:S(2)}) collective-permute-start(bf16[336,128]{1,0:T(8,128)(2,1)S(1)} %get-tuple-element.16), channel_id=1, source_target_pairs={{0,3},{1,2},{2,1},{3,0},{4,7},{5,6},{6,5},{7,4},{8,11},{9,10},{10,... | collective-permute-start | bytes 258056 | tf_op jit(solution)/shard_map/ppermute | solution.py:95
  7.2 7.8 %collective-permute-start.1 = (bf16[336,128]{1,0:T(8,128)(2,1)S(1)}, bf16[336,128]{1,0:T(8,128)(2,1)S(1)}, u32[]{:S(2)}, u32[]{:S(2)}) collective-permute-start(bf16[336,128]{1,0:T(8,128)(2,1)S(1)} %get-tuple-element.17), channel_id=1, source_target_pairs={{0,7},{1,6},{2,5},{3,4},{4,3},{5,2},{6,1},{7,0},{8,15},{9,14},{10,... | collective-permute-start | bytes 258056 | tf_op jit(solution)/shard_map/ppermute | solution.py:95
  9.6 12.2 %collective-permute-start.2 = (bf16[336,128]{1,0:T(8,128)(2,1)S(1)}, bf16[336,128]{1,0:T(8,128)(2,1)S(1)}, u32[]{:S(2)}, u32[]{:S(2)}) collective-permute-start(bf16[336,128]{1,0:T(8,128)(2,1)S(1)} %get-tuple-element.18), channel_id=1, source_target_pairs={{0,6},{1,7},{2,4},{3,5},{4,2},{5,3},{6,0},{7,1},{8,14},{9,15},{10,... | collective-permute-start | bytes 258056 | tf_op jit(solution)/shard_map/ppermute | solution.py:95
  11.0 11.5 %collective-permute-start.3 = (bf16[336,128]{1,0:T(8,128)(2,1)S(1)}, bf16[336,128]{1,0:T(8,128)(2,1)S(1)}, u32[]{:S(2)}, u32[]{:S(2)}) collective-permute-start(bf16[336,128]{1,0:T(8,128)(2,1)S(1)} %get-tuple-element.19), channel_id=1, source_target_pairs={{0,2},{1,3},{2,0},{3,1},{4,6},{5,7},{6,4},{7,5},{8,10},{9,11},{10,... | collective-permute-start | bytes 258056 | tf_op jit(solution)/shard_map/ppermute | solution.py:95
  11.0 13.0 %collective-permute-start.4 = (bf16[336,128]{1,0:T(8,128)(2,1)S(1)}, bf16[336,128]{1,0:T(8,128)(2,1)S(1)}, u32[]{:S(2)}, u32[]{:S(2)}) collective-permute-start(bf16[336,128]{1,0:T(8,128)(2,1)S(1)} %get-tuple-element.20), channel_id=1, source_target_pairs={{0,5},{1,4},{2,7},{3,6},{4,1},{5,0},{6,3},{7,2},{8,13},{9,12},{10,... | collective-permute-start | bytes 258056 | tf_op jit(solution)/shard_map/ppermute | solution.py:95
  14.9 9.8 %collective-permute-start.5 = (bf16[336,128]{1,0:T(8,128)(2,1)S(1)}, bf16[336,128]{1,0:T(8,128)(2,1)S(1)}, u32[]{:S(2)}, u32[]{:S(2)}) collective-permute-start(bf16[336,128]{1,0:T(8,128)(2,1)S(1)} %get-tuple-element.21), channel_id=1, source_target_pairs={{0,4},{1,5},{2,6},{3,7},{4,0},{5,1},{6,2},{7,3},{8,12},{9,13},{10,... | collective-permute-start | bytes 258056 | tf_op jit(solution)/shard_map/ppermute | solution.py:95
  21.8 4.5 %collective-permute-start.6 = (bf16[336,128]{1,0:T(8,128)(2,1)S(1)}, bf16[336,128]{1,0:T(8,128)(2,1)S(1)}, u32[]{:S(2)}, u32[]{:S(2)}) collective-permute-start(bf16[336,128]{1,0:T(8,128)(2,1)S(1)} %get-tuple-element.22), channel_id=1, source_target_pairs={{0,1},{1,0},{2,3},{3,2},{4,5},{5,4},{6,7},{7,6},{8,9},{9,8},{10,11... | collective-permute-start | bytes 258056 | tf_op jit(solution)/shard_map/ppermute | solution.py:95
  22.4 16.5 %collective-permute-start.8 = (bf16[224,1024]{1,0:T(8,128)(2,1)S(1)}, bf16[224,1024]{1,0:T(8,128)(2,1)S(1)}, u32[]{:S(2)}, u32[]{:S(2)}) collective-permute-start(bf16[224,1024]{1,0:T(8,128)(2,1)S(1)} %get-tuple-element.25.refs_0_), channel_id=1, source_target_pairs={{0,8},{8,0},{16,24},{24,16},{1,9},{9,1},{17,25},{25,17},{2,10},{10... | collective-permute-start | bytes 1376264 | tf_op jit(solution)/shard_map/ppermute | solution.py:95
  22.4 16.5 %collective-permute-start.9 = (bf16[224,1024]{1,0:T(8,128)(2,1)S(1)}, bf16[224,1024]{1,0:T(8,128)(2,1)S(1)}, u32[]{:S(2)}, u32[]{:S(2)}) collective-permute-start(bf16[224,1024]{1,0:T(8,128)(2,1)S(1)} %collective-permute-done.7.refs_1_), channel_id=1, source_target_pairs={{0,8},{8,0},{16,24},{24,16},{1,9},{9,1},{17,25},{25,17},{2,10},{10... | collective-permute-start | bytes 1376264 | tf_op jit(solution)/shard_map/ppermute | solution.py:95
  27.8 11.1 %copy-start = (bf16[1,112,1024]{2,1,0:T(8,128)(2,1)S(1)}, bf16[1,112,1024]{2,1,0:T(8,128)(2,1)}, u32[]{:S(2)}) copy-start(bf16[1,112,1024]{2,1,0:T(8,128)(2,1)} %param.9) | copy-start | bytes 688132

commit v22 on v17

--- a/solution.py
+++ b/solution.py
@@ -12,7 +12,7 @@
 SCALE = 1.0 / math.sqrt(HEAD)
 EXP2_SCALE = SCALE * math.log2(math.e)
 MIB = 1024 * 1024
-PARTNERS = tuple(zip((5, 4, 3, 2, 7, 6, 1, 0), (3, 2, 1, 5, 4, 7, 6, 0)))
+PARTNERS = tuple(zip((3, 7, 6, 2, 5, 4, 1, 0), (3, 2, 1, 7, 6, 5, 4, 0)))
 
 
 def partner_of(orders):

time: 41.7 us -> 41.7 us (level)
  waiting for transfers between devices: 3.98 us -> 2.54 us
  blocking collectives: 11 us -> 12.1 us
    ppermute x7, waiting for transfers between devices: 3.98 us -> 2.53 us  [exchange(): return lax.ppermute(array, ('view', 'ctx'), pairs)]
    all_to_all x1, blocking collectives: 11 us -> 12.1 us  [split_attention(): back = lax.all_to_all(own, 'ctx', split_axis=0, concat_axis=0, tiled=True)]
  transfers between devices with their start and end apart: 10 -> 10, of which waited for: 3 -> 2; matrix products, arithmetic and copies ran while one was open for 0% -> 0% of each run, Pallas kernels for 4% -> 4%
where the time goes in v22:
time: 41.7 us; the launch traced here: 41.5 us
  starting transfers between devices  21.9 us (53%)
  blocking collectives  12.1 us (29%)
  Pallas kernels  4.85 us (12%)
  waiting for transfers between devices  2.54 us (6%)
    ppermute x7, starting transfers between devices, exchange(): return lax.ppermute(array, ('view', 'ctx'), pairs)  18.4 us
    all_to_all x1, blocking collectives, split_attention(): back = lax.all_to_all(own, 'ctx', split_axis=0, concat_axis=0, tiled=True)  12.1 us
    ppermute x3, starting transfers between devices, swap(): lax.ppermute(array, axis_name, [(i, i ^ partner) for i in range(axis_size)])  3.54 us
    ppermute x7, waiting for transfers between devices, exchange(): return lax.ppermute(array, ('view', 'ctx'), pairs)  2.53 us
    pallas_call x1, Pallas kernels, body(): pl.pallas_call(functools.partial(cross_kernel, heads), out_shape=jax.Shap...  1.68 us
    pallas_call x1, Pallas kernels, split_attention(): pl.pallas_call(functools.partial(pack_kernel, partners), out_shape=[block...  1.61 us
    pallas_call x1, Pallas kernels, split_attention(): pl.pallas_call(functools.partial(packed_attention_kernel, partners, rows,...  1.56 us
  transfers between devices with their start and end apart: 10, of which 2 were waited for; matrix products, arithmetic and copies ran while one was open for 0% of the time, Pallas kernels for 4%

profile of v22, /device:TPU:0, one launch (start us, length us, event | category | flops | bytes accessed | tf_op | source)
XLA Modules:
  0.0 41.5 jit_solution(9695514875271445382)
XLA Ops:
  0.0 1.6 %pack_qkv.1 = (bf16[336,128]{1,0:T(8,128)(2,1)S(1)}, bf16[336,128]{1,0:T(8,128)(2,1)S(1)}, bf16[336,128]{1,0:T(8,128)(2,1)S(1)}, bf16[336,128]{1,0:T(8,128)(2,1)...) custom-call(bf16[112,1024]{1,0:T(8,128)(2,1)} %bitcast.8, ...), custom_call_target="tpu_custom_call" | custom-call | tf_op jit(solution)/shard_map/pack_qkv/pallas_call | solution.py:128
  1.6 3.0 %collective-permute-start.7 = (bf16[224,1024]{1,0:T(8,128)(2,1)S(1)}, bf16[224,1024]{1,0:T(8,128)(2,1)S(1)}, u32[]{:S(2)}, u32[]{:S(2)}) collective-permute-start(bf16[224,1024]{1,0:T(8,128)(2,1)S(1)} %get-tuple-element.25.refs_0_), channel_id=1, source_target_pairs={{0,16},{8,24},{16,0},{24,8},{1,17},{9,25},{17,1},{25,9},{2,18},{10... | collective-permute-start | bytes 1376264 | tf_op jit(solution)/shard_map/ppermute | solution.py:98
  4.7 2.5 %collective-permute-start = (bf16[336,128]{1,0:T(8,128)(2,1)S(1)}, bf16[336,128]{1,0:T(8,128)(2,1)S(1)}, u32[]{:S(2)}, u32[]{:S(2)}) collective-permute-start(bf16[336,128]{1,0:T(8,128)(2,1)S(1)} %get-tuple-element.16), channel_id=1, source_target_pairs={{0,3},{1,2},{2,1},{3,0},{4,7},{5,6},{6,5},{7,4},{8,11},{9,10},{10,... | collective-permute-start | bytes 258056 | tf_op jit(solution)/shard_map/ppermute | solution.py:107
  7.2 2.4 %collective-permute-start.1 = (bf16[336,128]{1,0:T(8,128)(2,1)S(1)}, bf16[336,128]{1,0:T(8,128)(2,1)S(1)}, u32[]{:S(2)}, u32[]{:S(2)}) collective-permute-start(bf16[336,128]{1,0:T(8,128)(2,1)S(1)} %get-tuple-element.17), channel_id=1, source_target_pairs={{0,7},{1,6},{2,5},{3,4},{4,3},{5,2},{6,1},{7,0},{8,10},{9,11},{10,... | collective-permute-start | bytes 258056 | tf_op jit(solution)/shard_map/ppermute | solution.py:107
  9.6 1.3 %collective-permute-start.2 = (bf16[336,128]{1,0:T(8,128)(2,1)S(1)}, bf16[336,128]{1,0:T(8,128)(2,1)S(1)}, u32[]{:S(2)}, u32[]{:S(2)}) collective-permute-start(bf16[336,128]{1,0:T(8,128)(2,1)S(1)} %get-tuple-element.18), channel_id=1, source_target_pairs={{0,6},{1,7},{2,4},{3,5},{4,2},{5,3},{6,0},{7,1},{8,9},{9,8},{10,11... | collective-permute-start | bytes 258056 | tf_op jit(solution)/shard_map/ppermute | solution.py:107
  11.0 0.0 collective-permute-start.3
  11.0 0.0 collective-permute-done.refs_0_
  11.0 4.0 %collective-permute-start.4 = (bf16[336,128]{1,0:T(8,128)(2,1)S(1)}, bf16[336,128]{1,0:T(8,128)(2,1)S(1)}, u32[]{:S(2)}, u32[]{:S(2)}) collective-permute-start(bf16[336,128]{1,0:T(8,128)(2,1)S(1)} %get-tuple-element.20), channel_id=1, source_target_pairs={{0,5},{1,4},{2,7},{3,6},{4,1},{5,0},{6,3},{7,2},{8,14},{9,15},{10,... | collective-permute-start | bytes 258056 | tf_op jit(solution)/shard_map/ppermute | solution.py:107
  14.9 0.0 collective-permute-done.1.refs_1_
  14.9 5.5 %collective-permute-start.5 = (bf16[336,128]{1,0:T(8,128)(2,1)S(1)}, bf16[336,128]{1,0:T(8,128)(2,1)S(1)}, u32[]{:S(2)}, u32[]{:S(2)}) collective-permute-start(bf16[336,128]{1,0:T(8,128)(2,1)S(1)} %get-tuple-element.21), channel_id=1, source_target_pairs={{0,4},{1,5},{2,6},{3,7},{4,0},{5,1},{6,2},{7,3},{8,13},{9,12},{10,... | collective-permute-start | bytes 258056 | tf_op jit(solution)/shard_map/ppermute | solution.py:107
  20.4 0.0 collective-permute-done.2.refs_2_
  20.4 2.6 %collective-permute-start.6 = (bf16[336,128]{1,0:T(8,128)(2,1)S(1)}, bf16[336,128]{1,0:T(8,128)(2,1)S(1)}, u32[]{:S(2)}, u32[]{:S(2)}) collective-permute-start(bf16[336,128]{1,0:T(8,128)(2,1)S(1)} %get-tuple-element.22), channel_id=1, source_target_pairs={{0,1},{1,0},{2,3},{3,2},{4,5},{5,4},{6,7},{7,6},{8,12},{9,13},{10,... | collective-permute-start | bytes 258056 | tf_op jit(solution)/shard_map/ppermute | solution.py:107
  23.1 0.0 collective-permute-done.3.refs_3_
  23.1 0.0 collective-permute-done.7.refs_1_
  23.1 0.0 collective-permute-start.8
  23.1 0.5 %collective-permute-start.9 = (bf16[224,1024]{1,0:T(8,128)(2,1)S(1)}, bf16[224,1024]{1,0:T(8,128)(2,1)S(1)}, u32[]{:S(2)}, u32[]{:S(2)}) collective-permute-start(bf16[224,1024]{1,0:T(8,128)(2,1)S(1)} %collective-permute-done.7.refs_1_), channel_id=1, source_target_pairs={{0,8},{8,0},{16,24},{24,16},{1,9},{9,1},{17,25},{25,17},{2,10},{10... | collective-permute-start | bytes 1376264 | tf_op jit(solution)/shard_map/ppermute | solution.py:98
  23.6 1.0 %collective-permute-done.4.refs_4_ = bf16[336,128]{1,0:T(8,128)(2,1)S(1)} collective-permute-done((bf16[336,128]{1,0:T(8,128)(2,1)S(1)}, bf16[336,128]{1,0:T(8,128)(2,1)S(1)}, u32[]{:S(2)}, u32[]{:S(2)}) %collective-permute-start.4) | collective-permute-done | bytes 86048 | tf_op jit(solution)/shard_map/ppermute | solution.py:107
  24.6 1.5 %collective-permute-done.5.refs_5_ = bf16[336,128]{1,0:T(8,128)(2,1)S(1)} collective-permute-done((bf16[336,128]{1,0:T(8,128)(2,1)S(1)}, bf16[336,128]{1,0:T(8,128)(2,1)S(1)}, u32[]{:S(2)}, u32[]{:S(2)}) %collective-permute-start.5) | collective-permute-done | bytes 86048 | tf_op jit(solution)/shard_map/ppermute | solution.py:107
  26.1 0.0 collective-permute-done.6.refs_6_
  26.1 1.6 %self_attention.1 = bf16[8,112,128]{2,1,0:T(8,128)(2,1)S(1)} custom-call(bf16[336,128]{1,0:T(8,128)(2,1)S(1)} %collective-permute-done.refs_0_, bf16[336,128]{1,0:T(8,128)(2,1)S(1)} %collective-permute-done.1.refs_1_, bf16[336,128]{1,0:T(8,128)(2,1)S(1)} %collective-permute-done.2.refs_2_, bf16[336,128]{1,0:T(8,128)(2,1)S(1)} %collective-permute-done.3.refs_3_, ...), custom_call_target="tpu_custom_call" | custom-call | flops 411041792 | bytes 917504 | tf_op jit(solution)/shard_map/self_attention/pallas_call | solution.py:141
  27.7 0.0 copy-start
  27.7 12.1 %all_to_all.5.o_ref = bf16[8,112,128]{2,1,0:T(8,128)(2,1)S(1)} all-to-all(bf16[8,112,128]{2,1,0:T(8,128)(2,1)S(1)} %self_attention.1), channel_id=1, replica_groups=mesh['view'=4,'ctx'=8] {'ctx'}, dimensions={0} | all-to-all | bytes 458752 | tf_op jit(solution)/shard_map/all_to_all | solution.py:154
  39.8 0.0 collective-permute-done.8.refs_2_
  39.8 0.0 collective-permute-done.9.refs_3_
  39.8 0.0 copy-done
  39.8 1.7 %cross_view.1 = bf16[112,1024]{1,0:T(8,128)(2,1)} custom-call(bf16[8,112,128]{2,1,0:T(8,128)(2,1)S(1)} %all_to_all.5.o_ref, bf16[112,1024]{1,0:T(8,128)(2,1)S(1)} %bitcast.7, bf16[224,1024]{1,0:T(8,128)(2,1)S(1)} %get-tuple-element.25.refs_0_, bf16[224,1024]{1,0:T(8,128)(2,1)S(1)} %collective-permute-done.7.refs_1_, ...), custom_call_target="tpu_custom_call" | custom-call | tf_op jit(solution)/shard_map/cross_view/pallas_call | solution.py:205
Async XLA Ops:
  1.6 21.4 %collective-permute-start.7 = (bf16[224,1024]{1,0:T(8,128)(2,1)S(1)}, bf16[224,1024]{1,0:T(8,128)(2,1)S(1)}, u32[]{:S(2)}, u32[]{:S(2)}) collective-permute-start(bf16[224,1024]{1,0:T(8,128)(2,1)S(1)} %get-tuple-element.25.refs_0_), channel_id=1, source_target_pairs={{0,16},{8,24},{16,0},{24,8},{1,17},{9,25},{17,1},{25,9},{2,18},{10... | collective-permute-start | bytes 1376264 | tf_op jit(solution)/shard_map/ppermute | solution.py:98
  4.7 6.3 %collective-permute-start = (bf16[336,128]{1,0:T(8,128)(2,1)S(1)}, bf16[336,128]{1,0:T(8,128)(2,1)S(1)}, u32[]{:S(2)}, u32[]{:S(2)}) collective-permute-start(bf16[336,128]{1,0:T(8,128)(2,1)S(1)} %get-tuple-element.16), channel_id=1, source_target_pairs={{0,3},{1,2},{2,1},{3,0},{4,7},{5,6},{6,5},{7,4},{8,11},{9,10},{10,... | collective-permute-start | bytes 258056 | tf_op jit(solution)/shard_map/ppermute | solution.py:107
  7.2 7.8 %collective-permute-start.1 = (bf16[336,128]{1,0:T(8,128)(2,1)S(1)}, bf16[336,128]{1,0:T(8,128)(2,1)S(1)}, u32[]{:S(2)}, u32[]{:S(2)}) collective-permute-start(bf16[336,128]{1,0:T(8,128)(2,1)S(1)} %get-tuple-element.17), channel_id=1, source_target_pairs={{0,7},{1,6},{2,5},{3,4},{4,3},{5,2},{6,1},{7,0},{8,10},{9,11},{10,... | collective-permute-start | bytes 258056 | tf_op jit(solution)/shard_map/ppermute | solution.py:107
  9.6 10.8 %collective-permute-start.2 = (bf16[336,128]{1,0:T(8,128)(2,1)S(1)}, bf16[336,128]{1,0:T(8,128)(2,1)S(1)}, u32[]{:S(2)}, u32[]{:S(2)}) collective-permute-start(bf16[336,128]{1,0:T(8,128)(2,1)S(1)} %get-tuple-element.18), channel_id=1, source_target_pairs={{0,6},{1,7},{2,4},{3,5},{4,2},{5,3},{6,0},{7,1},{8,9},{9,8},{10,11... | collective-permute-start | bytes 258056 | tf_op jit(solution)/shard_map/ppermute | solution.py:107
  11.0 12.1 %collective-permute-start.3 = (bf16[336,128]{1,0:T(8,128)(2,1)S(1)}, bf16[336,128]{1,0:T(8,128)(2,1)S(1)}, u32[]{:S(2)}, u32[]{:S(2)}) collective-permute-start(bf16[336,128]{1,0:T(8,128)(2,1)S(1)} %get-tuple-element.19), channel_id=1, source_target_pairs={{0,2},{1,3},{2,0},{3,1},{4,6},{5,7},{6,4},{7,5},{8,15},{9,14},{10,... | collective-permute-start | bytes 258056 | tf_op jit(solution)/shard_map/ppermute | solution.py:107
  11.0 13.6 %collective-permute-start.4 = (bf16[336,128]{1,0:T(8,128)(2,1)S(1)}, bf16[336,128]{1,0:T(8,128)(2,1)S(1)}, u32[]{:S(2)}, u32[]{:S(2)}) collective-permute-start(bf16[336,128]{1,0:T(8,128)(2,1)S(1)} %get-tuple-element.20), channel_id=1, source_target_pairs={{0,5},{1,4},{2,7},{3,6},{4,1},{5,0},{6,3},{7,2},{8,14},{9,15},{10,... | collective-permute-start | bytes 258056 | tf_op jit(solution)/shard_map/ppermute | solution.py:107
  14.9 11.2 %collective-permute-start.5 = (bf16[336,128]{1,0:T(8,128)(2,1)S(1)}, bf16[336,128]{1,0:T(8,128)(2,1)S(1)}, u32[]{:S(2)}, u32[]{:S(2)}) collective-permute-start(bf16[336,128]{1,0:T(8,128)(2,1)S(1)} %get-tuple-element.21), channel_id=1, source_target_pairs={{0,4},{1,5},{2,6},{3,7},{4,0},{5,1},{6,2},{7,3},{8,13},{9,12},{10,... | collective-permute-start | bytes 258056 | tf_op jit(solution)/shard_map/ppermute | solution.py:107
  20.4 5.7 %collective-permute-start.6 = (bf16[336,128]{1,0:T(8,128)(2,1)S(1)}, bf16[336,128]{1,0:T(8,128)(2,1)S(1)}, u32[]{:S(2)}, u32[]{:S(2)}) collective-permute-start(bf16[336,128]{1,0:T(8,128)(2,1)S(1)} %get-tuple-element.22), channel_id=1, source_target_pairs={{0,1},{1,0},{2,3},{3,2},{4,5},{5,4},{6,7},{7,6},{8,12},{9,13},{10,... | collective-permute-start | bytes 258056 | tf_op jit(solution)/shard_map/ppermute | solution.py:107
  23.1 16.8 %collective-permute-start.8 = (bf16[224,1024]{1,0:T(8,128)(2,1)S(1)}, bf16[224,1024]{1,0:T(8,128)(2,1)S(1)}, u32[]{:S(2)}, u32[]{:S(2)}) collective-permute-start(bf16[224,1024]{1,0:T(8,128)(2,1)S(1)} %get-tuple-element.25.refs_0_), channel_id=1, source_target_pairs={{0,8},{8,0},{16,24},{24,16},{1,9},{9,1},{17,25},{25,17},{2,10},{10... | collective-permute-start | bytes 1376264 | tf_op jit(solution)/shard_map/ppermute | solution.py:98
  23.1 16.8 %collective-permute-start.9 = (bf16[224,1024]{1,0:T(8,128)(2,1)S(1)}, bf16[224,1024]{1,0:T(8,128)(2,1)S(1)}, u32[]{:S(2)}, u32[]{:S(2)}) collective-permute-start(bf16[224,1024]{1,0:T(8,128)(2,1)S(1)} %collective-permute-done.7.refs_1_), channel_id=1, source_target_pairs={{0,8},{8,0},{16,24},{24,16},{1,9},{9,1},{17,25},{25,17},{2,10},{10... | collective-permute-start | bytes 1376264 | tf_op jit(solution)/shard_map/ppermute | solution.py:98
  27.7 12.2 %copy-start = (bf16[1,112,1024]{2,1,0:T(8,128)(2,1)S(1)}, bf16[1,112,1024]{2,1,0:T(8,128)(2,1)}, u32[]{:S(2)}) copy-start(bf16[1,112,1024]{2,1,0:T(8,128)(2,1)} %param.9) | copy-start | bytes 688132

commit v23 on v14

--- a/solution.py
+++ b/solution.py
@@ -106,7 +106,7 @@
 def split_attention(q, k, v, k_cross, v_cross, ctx_size):
     rows, width = q.shape
     heads = width // HEAD
-    partners = (3, 2, 1, 7, 6, 5, 4, 0)
+    partners = (3, 5, 7, 2, 4, 6, 1, 0)
     vmem = pl.BlockSpec(memory_space=pltpu.VMEM)
     hbm = pl.BlockSpec(memory_space=pltpu.HBM)
     sources = [pltpu.with_memory_space_constraint(x, pltpu.HBM) for x in (q, k, v, k_cross, v_cross)]

time: 42 us -> 41.7 us (level)
  starting transfers between devices: 16.8 us -> 18.6 us
  waiting for transfers between devices: 8.06 us -> 7.01 us
  blocking collectives: 12 us -> 11 us
    ppermute x10, starting transfers between devices: 16.8 us -> 18.6 us  [swap(): lax.ppermute(array, axis_name, [(i, i ^ partner) for i in range(axis_size)])]
    ppermute x10, waiting for transfers between devices: 8.06 us -> 7.01 us  [swap(): lax.ppermute(array, axis_name, [(i, i ^ partner) for i in range(axis_size)])]
    all_to_all x1, blocking collectives: 12 us -> 11 us  [split_attention(): back = lax.all_to_all(own, 'ctx', split_axis=0, concat_axis=0, tiled=True)]
where the time goes in v23:
time: 41.7 us; the launch traced here: 41.5 us
  starting transfers between devices  18.6 us (45%)
  blocking collectives  11 us (26%)
  waiting for transfers between devices  7.01 us (17%)
  Pallas kernels  4.85 us (12%)
    ppermute x10, starting transfers between devices, swap(): lax.ppermute(array, axis_name, [(i, i ^ partner) for i in range(axis_size)])  18.6 us
    all_to_all x1, blocking collectives, split_attention(): back = lax.all_to_all(own, 'ctx', split_axis=0, concat_axis=0, tiled=True)  11 us
    ppermute x10, waiting for transfers between devices, swap(): lax.ppermute(array, axis_name, [(i, i ^ partner) for i in range(axis_size)])  7.01 us
    pallas_call x1, Pallas kernels, body(): pl.pallas_call(functools.partial(cross_kernel, heads), out_shape=jax.Shap...  1.68 us
    pallas_call x1, Pallas kernels, split_attention(): pl.pallas_call(functools.partial(pack_kernel, partners), out_shape=[block...  1.61 us
    pallas_call x1, Pallas kernels, split_attention(): pl.pallas_call(functools.partial(packed_attention_kernel, partners, rows,...  1.57 us
  transfers between devices with their start and end apart: 10, of which 3 were waited for; matrix products, arithmetic and copies ran while one was open for 0% of the time, Pallas kernels for 4%

profile of v23, /device:TPU:0, one launch (start us, length us, event | category | flops | bytes accessed | tf_op | source)
XLA Modules:
  0.0 41.5 jit_solution(1548597189540823000)
XLA Ops:
  0.0 1.6 %pack_qkv.1 = (bf16[336,128]{1,0:T(8,128)(2,1)S(1)}, bf16[336,128]{1,0:T(8,128)(2,1)S(1)}, bf16[336,128]{1,0:T(8,128)(2,1)S(1)}, bf16[336,128]{1,0:T(8,128)(2,1)...) custom-call(bf16[112,1024]{1,0:T(8,128)(2,1)} %bitcast.8, ...), custom_call_target="tpu_custom_call" | custom-call | tf_op jit(solution)/shard_map/pack_qkv/pallas_call | solution.py:114
  1.6 3.0 %collective-permute-start.7 = (bf16[224,1024]{1,0:T(8,128)(2,1)S(1)}, bf16[224,1024]{1,0:T(8,128)(2,1)S(1)}, u32[]{:S(2)}, u32[]{:S(2)}) collective-permute-start(bf16[224,1024]{1,0:T(8,128)(2,1)S(1)} %get-tuple-element.25.refs_0_), channel_id=1, source_target_pairs={{0,16},{8,24},{16,0},{24,8},{1,17},{9,25},{17,1},{25,9},{2,18},{10... | collective-permute-start | bytes 1376264 | tf_op jit(solution)/shard_map/ppermute | solution.py:93
  4.7 2.5 %collective-permute-start = (bf16[336,128]{1,0:T(8,128)(2,1)S(1)}, bf16[336,128]{1,0:T(8,128)(2,1)S(1)}, u32[]{:S(2)}, u32[]{:S(2)}) collective-permute-start(bf16[336,128]{1,0:T(8,128)(2,1)S(1)} %get-tuple-element.16), channel_id=1, source_target_pairs={{0,3},{1,2},{2,1},{3,0},{4,7},{5,6},{6,5},{7,4},{8,11},{9,10},{10,... | collective-permute-start | bytes 258056 | tf_op jit(solution)/shard_map/ppermute | solution.py:93
  7.2 2.6 %collective-permute-start.1 = (bf16[336,128]{1,0:T(8,128)(2,1)S(1)}, bf16[336,128]{1,0:T(8,128)(2,1)S(1)}, u32[]{:S(2)}, u32[]{:S(2)}) collective-permute-start(bf16[336,128]{1,0:T(8,128)(2,1)S(1)} %get-tuple-element.17), channel_id=1, source_target_pairs={{0,5},{1,4},{2,7},{3,6},{4,1},{5,0},{6,3},{7,2},{8,13},{9,12},{10,... | collective-permute-start | bytes 258056 | tf_op jit(solution)/shard_map/ppermute | solution.py:93
  9.7 1.1 %collective-permute-start.2 = (bf16[336,128]{1,0:T(8,128)(2,1)S(1)}, bf16[336,128]{1,0:T(8,128)(2,1)S(1)}, u32[]{:S(2)}, u32[]{:S(2)}) collective-permute-start(bf16[336,128]{1,0:T(8,128)(2,1)S(1)} %get-tuple-element.18), channel_id=1, source_target_pairs={{0,7},{1,6},{2,5},{3,4},{4,3},{5,2},{6,1},{7,0},{8,15},{9,14},{10,... | collective-permute-start | bytes 258056 | tf_op jit(solution)/shard_map/ppermute | solution.py:93
  10.9 0.7 %collective-permute-start.3 = (bf16[336,128]{1,0:T(8,128)(2,1)S(1)}, bf16[336,128]{1,0:T(8,128)(2,1)S(1)}, u32[]{:S(2)}, u32[]{:S(2)}) collective-permute-start(bf16[336,128]{1,0:T(8,128)(2,1)S(1)} %get-tuple-element.19), channel_id=1, source_target_pairs={{0,2},{1,3},{2,0},{3,1},{4,6},{5,7},{6,4},{7,5},{8,10},{9,11},{10,... | collective-permute-start | bytes 258056 | tf_op jit(solution)/shard_map/ppermute | solution.py:93
  11.5 0.0 collective-permute-done.refs_0_
  11.5 3.5 %collective-permute-start.4 = (bf16[336,128]{1,0:T(8,128)(2,1)S(1)}, bf16[336,128]{1,0:T(8,128)(2,1)S(1)}, u32[]{:S(2)}, u32[]{:S(2)}) collective-permute-start(bf16[336,128]{1,0:T(8,128)(2,1)S(1)} %get-tuple-element.20), channel_id=1, source_target_pairs={{0,4},{1,5},{2,6},{3,7},{4,0},{5,1},{6,2},{7,3},{8,12},{9,13},{10,... | collective-permute-start | bytes 258056 | tf_op jit(solution)/shard_map/ppermute | solution.py:93
  15.0 3.6 %collective-permute-done.1.refs_1_ = bf16[336,128]{1,0:T(8,128)(2,1)S(1)} collective-permute-done((bf16[336,128]{1,0:T(8,128)(2,1)S(1)}, bf16[336,128]{1,0:T(8,128)(2,1)S(1)}, u32[]{:S(2)}, u32[]{:S(2)}) %collective-permute-start.1) | collective-permute-done | bytes 86048 | tf_op jit(solution)/shard_map/ppermute | solution.py:93
  18.6 4.2 %collective-permute-start.5 = (bf16[336,128]{1,0:T(8,128)(2,1)S(1)}, bf16[336,128]{1,0:T(8,128)(2,1)S(1)}, u32[]{:S(2)}, u32[]{:S(2)}) collective-permute-start(bf16[336,128]{1,0:T(8,128)(2,1)S(1)} %get-tuple-element.21), channel_id=1, source_target_pairs={{0,6},{1,7},{2,4},{3,5},{4,2},{5,3},{6,0},{7,1},{8,14},{9,15},{10,... | collective-permute-start | bytes 258056 | tf_op jit(solution)/shard_map/ppermute | solution.py:93
  22.8 0.0 collective-permute-done.2.refs_2_
  22.8 0.5 %collective-permute-start.6 = (bf16[336,128]{1,0:T(8,128)(2,1)S(1)}, bf16[336,128]{1,0:T(8,128)(2,1)S(1)}, u32[]{:S(2)}, u32[]{:S(2)}) collective-permute-start(bf16[336,128]{1,0:T(8,128)(2,1)S(1)} %get-tuple-element.22), channel_id=1, source_target_pairs={{0,1},{1,0},{2,3},{3,2},{4,5},{5,4},{6,7},{7,6},{8,9},{9,8},{10,11... | collective-permute-start | bytes 258056 | tf_op jit(solution)/shard_map/ppermute | solution.py:93
  23.3 0.0 collective-permute-done.3.refs_3_
  23.3 0.0 collective-permute-done.7.refs_1_
  23.3 0.0 collective-permute-start.8
  23.3 0.5 %collective-permute-start.9 = (bf16[224,1024]{1,0:T(8,128)(2,1)S(1)}, bf16[224,1024]{1,0:T(8,128)(2,1)S(1)}, u32[]{:S(2)}, u32[]{:S(2)}) collective-permute-start(bf16[224,1024]{1,0:T(8,128)(2,1)S(1)} %collective-permute-done.7.refs_1_), channel_id=1, source_target_pairs={{0,8},{8,0},{16,24},{24,16},{1,9},{9,1},{17,25},{25,17},{2,10},{10... | collective-permute-start | bytes 1376264 | tf_op jit(solution)/shard_map/ppermute | solution.py:93
  23.8 0.0 collective-permute-done.4.refs_4_
  23.8 1.4 %collective-permute-done.5.refs_5_ = bf16[336,128]{1,0:T(8,128)(2,1)S(1)} collective-permute-done((bf16[336,128]{1,0:T(8,128)(2,1)S(1)}, bf16[336,128]{1,0:T(8,128)(2,1)S(1)}, u32[]{:S(2)}, u32[]{:S(2)}) %collective-permute-start.5) | collective-permute-done | bytes 86048 | tf_op jit(solution)/shard_map/ppermute | solution.py:93
  25.2 2.0 %collective-permute-done.6.refs_6_ = bf16[336,128]{1,0:T(8,128)(2,1)S(1)} collective-permute-done((bf16[336,128]{1,0:T(8,128)(2,1)S(1)}, bf16[336,128]{1,0:T(8,128)(2,1)S(1)}, u32[]{:S(2)}, u32[]{:S(2)}) %collective-permute-start.6) | collective-permute-done | bytes 86048 | tf_op jit(solution)/shard_map/ppermute | solution.py:93
  27.3 1.6 %self_attention.1 = bf16[8,112,128]{2,1,0:T(8,128)(2,1)S(1)} custom-call(bf16[336,128]{1,0:T(8,128)(2,1)S(1)} %collective-permute-done.refs_0_, bf16[336,128]{1,0:T(8,128)(2,1)S(1)} %collective-permute-done.1.refs_1_, bf16[336,128]{1,0:T(8,128)(2,1)S(1)} %collective-permute-done.2.refs_2_, bf16[336,128]{1,0:T(8,128)(2,1)S(1)} %collective-permute-done.3.refs_3_, ...), custom_call_target="tpu_custom_call" | custom-call | flops 411041792 | bytes 917504 | tf_op jit(solution)/shard_map/self_attention/pallas_call | solution.py:127
  28.8 0.0 copy-start
  28.8 11.0 %all_to_all.5.o_ref = bf16[8,112,128]{2,1,0:T(8,128)(2,1)S(1)} all-to-all(bf16[8,112,128]{2,1,0:T(8,128)(2,1)S(1)} %self_attention.1), channel_id=1, replica_groups=mesh['view'=4,'ctx'=8] {'ctx'}, dimensions={0} | all-to-all | bytes 458752 | tf_op jit(solution)/shard_map/all_to_all | solution.py:140
  39.8 0.0 collective-permute-done.8.refs_2_
  39.8 0.0 collective-permute-done.9.refs_3_
  39.9 0.0 copy-done
  39.9 1.7 %cross_view.1 = bf16[112,1024]{1,0:T(8,128)(2,1)} custom-call(bf16[8,112,128]{2,1,0:T(8,128)(2,1)S(1)} %all_to_all.5.o_ref, bf16[112,1024]{1,0:T(8,128)(2,1)S(1)} %bitcast.7, bf16[224,1024]{1,0:T(8,128)(2,1)S(1)} %get-tuple-element.25.refs_0_, bf16[224,1024]{1,0:T(8,128)(2,1)S(1)} %collective-permute-done.7.refs_1_, ...), custom_call_target="tpu_custom_call" | custom-call | tf_op jit(solution)/shard_map/cross_view/pallas_call | solution.py:191
Async XLA Ops:
  1.6 21.7 %collective-permute-start.7 = (bf16[224,1024]{1,0:T(8,128)(2,1)S(1)}, bf16[224,1024]{1,0:T(8,128)(2,1)S(1)}, u32[]{:S(2)}, u32[]{:S(2)}) collective-permute-start(bf16[224,1024]{1,0:T(8,128)(2,1)S(1)} %get-tuple-element.25.refs_0_), channel_id=1, source_target_pairs={{0,16},{8,24},{16,0},{24,8},{1,17},{9,25},{17,1},{25,9},{2,18},{10... | collective-permute-start | bytes 1376264 | tf_op jit(solution)/shard_map/ppermute | solution.py:93
  4.7 6.9 %collective-permute-start = (bf16[336,128]{1,0:T(8,128)(2,1)S(1)}, bf16[336,128]{1,0:T(8,128)(2,1)S(1)}, u32[]{:S(2)}, u32[]{:S(2)}) collective-permute-start(bf16[336,128]{1,0:T(8,128)(2,1)S(1)} %get-tuple-element.16), channel_id=1, source_target_pairs={{0,3},{1,2},{2,1},{3,0},{4,7},{5,6},{6,5},{7,4},{8,11},{9,10},{10,... | collective-permute-start | bytes 258056 | tf_op jit(solution)/shard_map/ppermute | solution.py:93
  7.2 11.4 %collective-permute-start.1 = (bf16[336,128]{1,0:T(8,128)(2,1)S(1)}, bf16[336,128]{1,0:T(8,128)(2,1)S(1)}, u32[]{:S(2)}, u32[]{:S(2)}) collective-permute-start(bf16[336,128]{1,0:T(8,128)(2,1)S(1)} %get-tuple-element.17), channel_id=1, source_target_pairs={{0,5},{1,4},{2,7},{3,6},{4,1},{5,0},{6,3},{7,2},{8,13},{9,12},{10,... | collective-permute-start | bytes 258056 | tf_op jit(solution)/shard_map/ppermute | solution.py:93
  9.7 13.1 %collective-permute-start.2 = (bf16[336,128]{1,0:T(8,128)(2,1)S(1)}, bf16[336,128]{1,0:T(8,128)(2,1)S(1)}, u32[]{:S(2)}, u32[]{:S(2)}) collective-permute-start(bf16[336,128]{1,0:T(8,128)(2,1)S(1)} %get-tuple-element.18), channel_id=1, source_target_pairs={{0,7},{1,6},{2,5},{3,4},{4,3},{5,2},{6,1},{7,0},{8,15},{9,14},{10,... | collective-permute-start | bytes 258056 | tf_op jit(solution)/shard_map/ppermute | solution.py:93
  10.9 12.4 %collective-permute-start.3 = (bf16[336,128]{1,0:T(8,128)(2,1)S(1)}, bf16[336,128]{1,0:T(8,128)(2,1)S(1)}, u32[]{:S(2)}, u32[]{:S(2)}) collective-permute-start(bf16[336,128]{1,0:T(8,128)(2,1)S(1)} %get-tuple-element.19), channel_id=1, source_target_pairs={{0,2},{1,3},{2,0},{3,1},{4,6},{5,7},{6,4},{7,5},{8,10},{9,11},{10,... | collective-permute-start | bytes 258056 | tf_op jit(solution)/shard_map/ppermute | solution.py:93
  11.5 12.3 %collective-permute-start.4 = (bf16[336,128]{1,0:T(8,128)(2,1)S(1)}, bf16[336,128]{1,0:T(8,128)(2,1)S(1)}, u32[]{:S(2)}, u32[]{:S(2)}) collective-permute-start(bf16[336,128]{1,0:T(8,128)(2,1)S(1)} %get-tuple-element.20), channel_id=1, source_target_pairs={{0,4},{1,5},{2,6},{3,7},{4,0},{5,1},{6,2},{7,3},{8,12},{9,13},{10,... | collective-permute-start | bytes 258056 | tf_op jit(solution)/shard_map/ppermute | solution.py:93
  18.6 6.6 %collective-permute-start.5 = (bf16[336,128]{1,0:T(8,128)(2,1)S(1)}, bf16[336,128]{1,0:T(8,128)(2,1)S(1)}, u32[]{:S(2)}, u32[]{:S(2)}) collective-permute-start(bf16[336,128]{1,0:T(8,128)(2,1)S(1)} %get-tuple-element.21), channel_id=1, source_target_pairs={{0,6},{1,7},{2,4},{3,5},{4,2},{5,3},{6,0},{7,1},{8,14},{9,15},{10,... | collective-permute-start | bytes 258056 | tf_op jit(solution)/shard_map/ppermute | solution.py:93
  22.8 4.5 %collective-permute-start.6 = (bf16[336,128]{1,0:T(8,128)(2,1)S(1)}, bf16[336,128]{1,0:T(8,128)(2,1)S(1)}, u32[]{:S(2)}, u32[]{:S(2)}) collective-permute-start(bf16[336,128]{1,0:T(8,128)(2,1)S(1)} %get-tuple-element.22), channel_id=1, source_target_pairs={{0,1},{1,0},{2,3},{3,2},{4,5},{5,4},{6,7},{7,6},{8,9},{9,8},{10,11... | collective-permute-start | bytes 258056 | tf_op jit(solution)/shard_map/ppermute | solution.py:93
  23.3 16.5 %collective-permute-start.8 = (bf16[224,1024]{1,0:T(8,128)(2,1)S(1)}, bf16[224,1024]{1,0:T(8,128)(2,1)S(1)}, u32[]{:S(2)}, u32[]{:S(2)}) collective-permute-start(bf16[224,1024]{1,0:T(8,128)(2,1)S(1)} %get-tuple-element.25.refs_0_), channel_id=1, source_target_pairs={{0,8},{8,0},{16,24},{24,16},{1,9},{9,1},{17,25},{25,17},{2,10},{10... | collective-permute-start | bytes 1376264 | tf_op jit(solution)/shard_map/ppermute | solution.py:93
  23.3 16.5 %collective-permute-start.9 = (bf16[224,1024]{1,0:T(8,128)(2,1)S(1)}, bf16[224,1024]{1,0:T(8,128)(2,1)S(1)}, u32[]{:S(2)}, u32[]{:S(2)}) collective-permute-start(bf16[224,1024]{1,0:T(8,128)(2,1)S(1)} %collective-permute-done.7.refs_1_), channel_id=1, source_target_pairs={{0,8},{8,0},{16,24},{24,16},{1,9},{9,1},{17,25},{25,17},{2,10},{10... | collective-permute-start | bytes 1376264 | tf_op jit(solution)/shard_map/ppermute | solution.py:93
  28.8 11.0 %copy-start = (bf16[1,112,1024]{2,1,0:T(8,128)(2,1)S(1)}, bf16[1,112,1024]{2,1,0:T(8,128)(2,1)}, u32[]{:S(2)}) copy-start(bf16[1,112,1024]{2,1,0:T(8,128)(2,1)} %param.9) | copy-start | bytes 688132

commit v24 on v10

--- a/solution.py
+++ b/solution.py
@@ -125,7 +125,7 @@
         for partner, data in zip(partners, blocks)
     ]
     own = pl.pallas_call(
-        functools.partial(packed_attention_kernel, partners, rows, max(heads // 4, 1)),
+        functools.partial(packed_attention_kernel, partners, rows, max(heads // 2, 1)),
         out_shape=jax.ShapeDtypeStruct((heads, rows, HEAD), q.dtype),
         in_specs=[vmem] * heads,
         out_specs=vmem,

time: 40.7 us -> 40.6 us (level)
  no operation moved by 1% of the time
where the time goes in v24:
time: 40.6 us; the launch traced here: 40.4 us
  starting transfers between devices  21.3 us (52%)
  blocking collectives  11.1 us (27%)
  Pallas kernels  4.72 us (12%)
  waiting for transfers between devices  3.33 us (8%)
    ppermute x10, starting transfers between devices, swap(): lax.ppermute(array, axis_name, [(i, i ^ partner) for i in range(axis_size)])  21.3 us
    all_to_all x1, blocking collectives, split_attention(): back = lax.all_to_all(own, 'ctx', split_axis=0, concat_axis=0, tiled=True)  11.1 us
    ppermute x10, waiting for transfers between devices, swap(): lax.ppermute(array, axis_name, [(i, i ^ partner) for i in range(axis_size)])  3.33 us
    pallas_call x1, Pallas kernels, body(): pl.pallas_call(functools.partial(cross_kernel, heads), out_shape=jax.Shap...  1.68 us
    pallas_call x1, Pallas kernels, split_attention(): pl.pallas_call(functools.partial(pack_kernel, partners), out_shape=[block...  1.61 us
    pallas_call x1, Pallas kernels, split_attention(): pl.pallas_call(functools.partial(packed_attention_kernel, partners, rows,...  1.44 us
  transfers between devices with their start and end apart: 10, of which 3 were waited for; matrix products, arithmetic and copies ran while one was open for 0% of the time, Pallas kernels for 4%

profile of v24, /device:TPU:0, one launch (start us, length us, event | category | flops | bytes accessed | tf_op | source)
XLA Modules:
  0.0 40.4 jit_solution(1086894938025407988)
XLA Ops:
  0.0 1.6 %pack_qkv.1 = (bf16[336,128]{1,0:T(8,128)(2,1)S(1)}, bf16[336,128]{1,0:T(8,128)(2,1)S(1)}, bf16[336,128]{1,0:T(8,128)(2,1)S(1)}, bf16[336,128]{1,0:T(8,128)(2,1)...) custom-call(bf16[112,1024]{1,0:T(8,128)(2,1)} %bitcast.8, ...), custom_call_target="tpu_custom_call" | custom-call | tf_op jit(solution)/shard_map/pack_qkv/pallas_call | solution.py:114
  1.6 3.0 %collective-permute-start.7 = (bf16[224,1024]{1,0:T(8,128)(2,1)S(1)}, bf16[224,1024]{1,0:T(8,128)(2,1)S(1)}, u32[]{:S(2)}, u32[]{:S(2)}) collective-permute-start(bf16[224,1024]{1,0:T(8,128)(2,1)S(1)} %get-tuple-element.25.refs_0_), channel_id=1, source_target_pairs={{0,16},{8,24},{16,0},{24,8},{1,17},{9,25},{17,1},{25,9},{2,18},{10... | collective-permute-start | bytes 1376264 | tf_op jit(solution)/shard_map/ppermute | solution.py:93
  4.7 2.5 %collective-permute-start = (bf16[336,128]{1,0:T(8,128)(2,1)S(1)}, bf16[336,128]{1,0:T(8,128)(2,1)S(1)}, u32[]{:S(2)}, u32[]{:S(2)}) collective-permute-start(bf16[336,128]{1,0:T(8,128)(2,1)S(1)} %get-tuple-element.16), channel_id=1, source_target_pairs={{0,3},{1,2},{2,1},{3,0},{4,7},{5,6},{6,5},{7,4},{8,11},{9,10},{10,... | collective-permute-start | bytes 258056 | tf_op jit(solution)/shard_map/ppermute | solution.py:93
  7.2 2.4 %collective-permute-start.1 = (bf16[336,128]{1,0:T(8,128)(2,1)S(1)}, bf16[336,128]{1,0:T(8,128)(2,1)S(1)}, u32[]{:S(2)}, u32[]{:S(2)}) collective-permute-start(bf16[336,128]{1,0:T(8,128)(2,1)S(1)} %get-tuple-element.17), channel_id=1, source_target_pairs={{0,7},{1,6},{2,5},{3,4},{4,3},{5,2},{6,1},{7,0},{8,15},{9,14},{10,... | collective-permute-start | bytes 258056 | tf_op jit(solution)/shard_map/ppermute | solution.py:93
  9.6 1.3 %collective-permute-start.2 = (bf16[336,128]{1,0:T(8,128)(2,1)S(1)}, bf16[336,128]{1,0:T(8,128)(2,1)S(1)}, u32[]{:S(2)}, u32[]{:S(2)}) collective-permute-start(bf16[336,128]{1,0:T(8,128)(2,1)S(1)} %get-tuple-element.18), channel_id=1, source_target_pairs={{0,6},{1,7},{2,4},{3,5},{4,2},{5,3},{6,0},{7,1},{8,14},{9,15},{10,... | collective-permute-start | bytes 258056 | tf_op jit(solution)/shard_map/ppermute | solution.py:93
  11.0 0.0 collective-permute-start.3
  11.0 0.0 collective-permute-done.refs_0_
  11.0 4.0 %collective-permute-start.4 = (bf16[336,128]{1,0:T(8,128)(2,1)S(1)}, bf16[336,128]{1,0:T(8,128)(2,1)S(1)}, u32[]{:S(2)}, u32[]{:S(2)}) collective-permute-start(bf16[336,128]{1,0:T(8,128)(2,1)S(1)} %get-tuple-element.20), channel_id=1, source_target_pairs={{0,5},{1,4},{2,7},{3,6},{4,1},{5,0},{6,3},{7,2},{8,13},{9,12},{10,... | collective-permute-start | bytes 258056 | tf_op jit(solution)/shard_map/ppermute | solution.py:93
  14.9 0.0 collective-permute-done.1.refs_1_
  14.9 6.8 %collective-permute-start.5 = (bf16[336,128]{1,0:T(8,128)(2,1)S(1)}, bf16[336,128]{1,0:T(8,128)(2,1)S(1)}, u32[]{:S(2)}, u32[]{:S(2)}) collective-permute-start(bf16[336,128]{1,0:T(8,128)(2,1)S(1)} %get-tuple-element.21), channel_id=1, source_target_pairs={{0,4},{1,5},{2,6},{3,7},{4,0},{5,1},{6,2},{7,3},{8,12},{9,13},{10,... | collective-permute-start | bytes 258056 | tf_op jit(solution)/shard_map/ppermute | solution.py:93
  21.8 0.0 collective-permute-done.2.refs_2_
  21.8 0.7 %collective-permute-start.6 = (bf16[336,128]{1,0:T(8,128)(2,1)S(1)}, bf16[336,128]{1,0:T(8,128)(2,1)S(1)}, u32[]{:S(2)}, u32[]{:S(2)}) collective-permute-start(bf16[336,128]{1,0:T(8,128)(2,1)S(1)} %get-tuple-element.22), channel_id=1, source_target_pairs={{0,1},{1,0},{2,3},{3,2},{4,5},{5,4},{6,7},{7,6},{8,9},{9,8},{10,11... | collective-permute-start | bytes 258056 | tf_op jit(solution)/shard_map/ppermute | solution.py:93
  22.4 0.0 collective-permute-done.3.refs_3_
  22.4 0.0 collective-permute-done.7.refs_1_
  22.4 0.0 collective-permute-start.8
  22.4 0.5 %collective-permute-start.9 = (bf16[224,1024]{1,0:T(8,128)(2,1)S(1)}, bf16[224,1024]{1,0:T(8,128)(2,1)S(1)}, u32[]{:S(2)}, u32[]{:S(2)}) collective-permute-start(bf16[224,1024]{1,0:T(8,128)(2,1)S(1)} %collective-permute-done.7.refs_1_), channel_id=1, source_target_pairs={{0,8},{8,0},{16,24},{24,16},{1,9},{9,1},{17,25},{25,17},{2,10},{10... | collective-permute-start | bytes 1376264 | tf_op jit(solution)/shard_map/ppermute | solution.py:93
  22.9 1.1 %collective-permute-done.4.refs_4_ = bf16[336,128]{1,0:T(8,128)(2,1)S(1)} collective-permute-done((bf16[336,128]{1,0:T(8,128)(2,1)S(1)}, bf16[336,128]{1,0:T(8,128)(2,1)S(1)}, u32[]{:S(2)}, u32[]{:S(2)}) %collective-permute-start.4) | collective-permute-done | bytes 86048 | tf_op jit(solution)/shard_map/ppermute | solution.py:93
  24.0 0.7 %collective-permute-done.5.refs_5_ = bf16[336,128]{1,0:T(8,128)(2,1)S(1)} collective-permute-done((bf16[336,128]{1,0:T(8,128)(2,1)S(1)}, bf16[336,128]{1,0:T(8,128)(2,1)S(1)}, u32[]{:S(2)}, u32[]{:S(2)}) %collective-permute-start.5) | collective-permute-done | bytes 86048 | tf_op jit(solution)/shard_map/ppermute | solution.py:93
  24.7 1.5 %collective-permute-done.6.refs_6_ = bf16[336,128]{1,0:T(8,128)(2,1)S(1)} collective-permute-done((bf16[336,128]{1,0:T(8,128)(2,1)S(1)}, bf16[336,128]{1,0:T(8,128)(2,1)S(1)}, u32[]{:S(2)}, u32[]{:S(2)}) %collective-permute-start.6) | collective-permute-done | bytes 86048 | tf_op jit(solution)/shard_map/ppermute | solution.py:93
  26.2 1.4 %self_attention.1 = bf16[8,112,128]{2,1,0:T(8,128)(2,1)S(1)} custom-call(bf16[336,128]{1,0:T(8,128)(2,1)S(1)} %collective-permute-done.refs_0_, bf16[336,128]{1,0:T(8,128)(2,1)S(1)} %collective-permute-done.1.refs_1_, bf16[336,128]{1,0:T(8,128)(2,1)S(1)} %collective-permute-done.2.refs_2_, bf16[336,128]{1,0:T(8,128)(2,1)S(1)} %collective-permute-done.3.refs_3_, ...), custom_call_target="tpu_custom_call" | custom-call | flops 411041792 | bytes 917504 | tf_op jit(solution)/shard_map/self_attention/pallas_call | solution.py:127
  27.7 0.0 copy-start
  27.7 11.1 %all_to_all.5.o_ref = bf16[8,112,128]{2,1,0:T(8,128)(2,1)S(1)} all-to-all(bf16[8,112,128]{2,1,0:T(8,128)(2,1)S(1)} %self_attention.1), channel_id=1, replica_groups=mesh['view'=4,'ctx'=8] {'ctx'}, dimensions={0} | all-to-all | bytes 458752 | tf_op jit(solution)/shard_map/all_to_all | solution.py:140
  38.8 0.0 collective-permute-done.8.refs_2_
  38.8 0.0 collective-permute-done.9.refs_3_
  38.8 0.0 copy-done
  38.8 1.7 %cross_view.1 = bf16[112,1024]{1,0:T(8,128)(2,1)} custom-call(bf16[8,112,128]{2,1,0:T(8,128)(2,1)S(1)} %all_to_all.5.o_ref, bf16[112,1024]{1,0:T(8,128)(2,1)S(1)} %bitcast.7, bf16[224,1024]{1,0:T(8,128)(2,1)S(1)} %get-tuple-element.25.refs_0_, bf16[224,1024]{1,0:T(8,128)(2,1)S(1)} %collective-permute-done.7.refs_1_, ...), custom_call_target="tpu_custom_call" | custom-call | tf_op jit(solution)/shard_map/cross_view/pallas_call | solution.py:191
Async XLA Ops:
  1.6 20.8 %collective-permute-start.7 = (bf16[224,1024]{1,0:T(8,128)(2,1)S(1)}, bf16[224,1024]{1,0:T(8,128)(2,1)S(1)}, u32[]{:S(2)}, u32[]{:S(2)}) collective-permute-start(bf16[224,1024]{1,0:T(8,128)(2,1)S(1)} %get-tuple-element.25.refs_0_), channel_id=1, source_target_pairs={{0,16},{8,24},{16,0},{24,8},{1,17},{9,25},{17,1},{25,9},{2,18},{10... | collective-permute-start | bytes 1376264 | tf_op jit(solution)/shard_map/ppermute | solution.py:93
  4.7 6.3 %collective-permute-start = (bf16[336,128]{1,0:T(8,128)(2,1)S(1)}, bf16[336,128]{1,0:T(8,128)(2,1)S(1)}, u32[]{:S(2)}, u32[]{:S(2)}) collective-permute-start(bf16[336,128]{1,0:T(8,128)(2,1)S(1)} %get-tuple-element.16), channel_id=1, source_target_pairs={{0,3},{1,2},{2,1},{3,0},{4,7},{5,6},{6,5},{7,4},{8,11},{9,10},{10,... | collective-permute-start | bytes 258056 | tf_op jit(solution)/shard_map/ppermute | solution.py:93
  7.2 7.8 %collective-permute-start.1 = (bf16[336,128]{1,0:T(8,128)(2,1)S(1)}, bf16[336,128]{1,0:T(8,128)(2,1)S(1)}, u32[]{:S(2)}, u32[]{:S(2)}) collective-permute-start(bf16[336,128]{1,0:T(8,128)(2,1)S(1)} %get-tuple-element.17), channel_id=1, source_target_pairs={{0,7},{1,6},{2,5},{3,4},{4,3},{5,2},{6,1},{7,0},{8,15},{9,14},{10,... | collective-permute-start | bytes 258056 | tf_op jit(solution)/shard_map/ppermute | solution.py:93
  9.6 12.2 %collective-permute-start.2 = (bf16[336,128]{1,0:T(8,128)(2,1)S(1)}, bf16[336,128]{1,0:T(8,128)(2,1)S(1)}, u32[]{:S(2)}, u32[]{:S(2)}) collective-permute-start(bf16[336,128]{1,0:T(8,128)(2,1)S(1)} %get-tuple-element.18), channel_id=1, source_target_pairs={{0,6},{1,7},{2,4},{3,5},{4,2},{5,3},{6,0},{7,1},{8,14},{9,15},{10,... | collective-permute-start | bytes 258056 | tf_op jit(solution)/shard_map/ppermute | solution.py:93
  11.0 11.5 %collective-permute-start.3 = (bf16[336,128]{1,0:T(8,128)(2,1)S(1)}, bf16[336,128]{1,0:T(8,128)(2,1)S(1)}, u32[]{:S(2)}, u32[]{:S(2)}) collective-permute-start(bf16[336,128]{1,0:T(8,128)(2,1)S(1)} %get-tuple-element.19), channel_id=1, source_target_pairs={{0,2},{1,3},{2,0},{3,1},{4,6},{5,7},{6,4},{7,5},{8,10},{9,11},{10,... | collective-permute-start | bytes 258056 | tf_op jit(solution)/shard_map/ppermute | solution.py:93
  11.0 13.0 %collective-permute-start.4 = (bf16[336,128]{1,0:T(8,128)(2,1)S(1)}, bf16[336,128]{1,0:T(8,128)(2,1)S(1)}, u32[]{:S(2)}, u32[]{:S(2)}) collective-permute-start(bf16[336,128]{1,0:T(8,128)(2,1)S(1)} %get-tuple-element.20), channel_id=1, source_target_pairs={{0,5},{1,4},{2,7},{3,6},{4,1},{5,0},{6,3},{7,2},{8,13},{9,12},{10,... | collective-permute-start | bytes 258056 | tf_op jit(solution)/shard_map/ppermute | solution.py:93
  14.9 9.8 %collective-permute-start.5 = (bf16[336,128]{1,0:T(8,128)(2,1)S(1)}, bf16[336,128]{1,0:T(8,128)(2,1)S(1)}, u32[]{:S(2)}, u32[]{:S(2)}) collective-permute-start(bf16[336,128]{1,0:T(8,128)(2,1)S(1)} %get-tuple-element.21), channel_id=1, source_target_pairs={{0,4},{1,5},{2,6},{3,7},{4,0},{5,1},{6,2},{7,3},{8,12},{9,13},{10,... | collective-permute-start | bytes 258056 | tf_op jit(solution)/shard_map/ppermute | solution.py:93
  21.8 4.5 %collective-permute-start.6 = (bf16[336,128]{1,0:T(8,128)(2,1)S(1)}, bf16[336,128]{1,0:T(8,128)(2,1)S(1)}, u32[]{:S(2)}, u32[]{:S(2)}) collective-permute-start(bf16[336,128]{1,0:T(8,128)(2,1)S(1)} %get-tuple-element.22), channel_id=1, source_target_pairs={{0,1},{1,0},{2,3},{3,2},{4,5},{5,4},{6,7},{7,6},{8,9},{9,8},{10,11... | collective-permute-start | bytes 258056 | tf_op jit(solution)/shard_map/ppermute | solution.py:93
  22.4 16.3 %collective-permute-start.8 = (bf16[224,1024]{1,0:T(8,128)(2,1)S(1)}, bf16[224,1024]{1,0:T(8,128)(2,1)S(1)}, u32[]{:S(2)}, u32[]{:S(2)}) collective-permute-start(bf16[224,1024]{1,0:T(8,128)(2,1)S(1)} %get-tuple-element.25.refs_0_), channel_id=1, source_target_pairs={{0,8},{8,0},{16,24},{24,16},{1,9},{9,1},{17,25},{25,17},{2,10},{10... | collective-permute-start | bytes 1376264 | tf_op jit(solution)/shard_map/ppermute | solution.py:93
  22.4 16.3 %collective-permute-start.9 = (bf16[224,1024]{1,0:T(8,128)(2,1)S(1)}, bf16[224,1024]{1,0:T(8,128)(2,1)S(1)}, u32[]{:S(2)}, u32[]{:S(2)}) collective-permute-start(bf16[224,1024]{1,0:T(8,128)(2,1)S(1)} %collective-permute-done.7.refs_1_), channel_id=1, source_target_pairs={{0,8},{8,0},{16,24},{24,16},{1,9},{9,1},{17,25},{25,17},{2,10},{10... | collective-permute-start | bytes 1376264 | tf_op jit(solution)/shard_map/ppermute | solution.py:93
  27.7 11.1 %copy-start = (bf16[1,112,1024]{2,1,0:T(8,128)(2,1)S(1)}, bf16[1,112,1024]{2,1,0:T(8,128)(2,1)}, u32[]{:S(2)}) copy-start(bf16[1,112,1024]{2,1,0:T(8,128)(2,1)} %param.9) | copy-start | bytes 688132

commit v25 on v24

--- a/solution.py
+++ b/solution.py
@@ -125,7 +125,7 @@
         for partner, data in zip(partners, blocks)
     ]
     own = pl.pallas_call(
-        functools.partial(packed_attention_kernel, partners, rows, max(heads // 2, 1)),
+        functools.partial(packed_attention_kernel, partners, rows, heads),
         out_shape=jax.ShapeDtypeStruct((heads, rows, HEAD), q.dtype),
         in_specs=[vmem] * heads,
         out_specs=vmem,

time: 40.6 us -> 41.1 us (1.012)
  Pallas kernels: 4.72 us -> 5.22 us
    pallas_call x1, Pallas kernels: 1.44 us -> 1.94 us  [split_attention(): pl.pallas_call(functools.partial(packed_attention_kernel, partners, rows,...]
  transfers between devices with their start and end apart: 10 -> 10, of which waited for: 3 -> 3; matrix products, arithmetic and copies ran while one was open for 0% -> 0% of each run, Pallas kernels for 4% -> 5%
where the time goes in v25:
time: 41.1 us; the launch traced here: 40.9 us
  starting transfers between devices  21.3 us (52%)
  blocking collectives  11 us (27%)
  Pallas kernels  5.22 us (13%)
  waiting for transfers between devices  3.33 us (8%)
    ppermute x10, starting transfers between devices, swap(): lax.ppermute(array, axis_name, [(i, i ^ partner) for i in range(axis_size)])  21.3 us
    all_to_all x1, blocking collectives, split_attention(): back = lax.all_to_all(own, 'ctx', split_axis=0, concat_axis=0, tiled=True)  11 us
    ppermute x10, waiting for transfers between devices, swap(): lax.ppermute(array, axis_name, [(i, i ^ partner) for i in range(axis_size)])  3.33 us
    pallas_call x1, Pallas kernels, split_attention(): pl.pallas_call(functools.partial(packed_attention_kernel, partners, rows,...  1.94 us
    pallas_call x1, Pallas kernels, body(): pl.pallas_call(functools.partial(cross_kernel, heads), out_shape=jax.Shap...  1.68 us
    pallas_call x1, Pallas kernels, split_attention(): pl.pallas_call(functools.partial(pack_kernel, partners), out_shape=[block...  1.61 us
  transfers between devices with their start and end apart: 10, of which 3 were waited for; matrix products, arithmetic and copies ran while one was open for 0% of the time, Pallas kernels for 5%

profile of v25, /device:TPU:0, one launch (start us, length us, event | category | flops | bytes accessed | tf_op | source)
XLA Modules:
  0.0 40.9 jit_solution(4705288177893379994)
XLA Ops:
  0.0 1.6 %pack_qkv.1 = (bf16[336,128]{1,0:T(8,128)(2,1)S(1)}, bf16[336,128]{1,0:T(8,128)(2,1)S(1)}, bf16[336,128]{1,0:T(8,128)(2,1)S(1)}, bf16[336,128]{1,0:T(8,128)(2,1)...) custom-call(bf16[112,1024]{1,0:T(8,128)(2,1)} %bitcast.8, ...), custom_call_target="tpu_custom_call" | custom-call | tf_op jit(solution)/shard_map/pack_qkv/pallas_call | solution.py:114
  1.6 3.0 %collective-permute-start.7 = (bf16[224,1024]{1,0:T(8,128)(2,1)S(1)}, bf16[224,1024]{1,0:T(8,128)(2,1)S(1)}, u32[]{:S(2)}, u32[]{:S(2)}) collective-permute-start(bf16[224,1024]{1,0:T(8,128)(2,1)S(1)} %get-tuple-element.25.refs_0_), channel_id=1, source_target_pairs={{0,16},{8,24},{16,0},{24,8},{1,17},{9,25},{17,1},{25,9},{2,18},{10... | collective-permute-start | bytes 1376264 | tf_op jit(solution)/shard_map/ppermute | solution.py:93
  4.7 2.5 %collective-permute-start = (bf16[336,128]{1,0:T(8,128)(2,1)S(1)}, bf16[336,128]{1,0:T(8,128)(2,1)S(1)}, u32[]{:S(2)}, u32[]{:S(2)}) collective-permute-start(bf16[336,128]{1,0:T(8,128)(2,1)S(1)} %get-tuple-element.16), channel_id=1, source_target_pairs={{0,3},{1,2},{2,1},{3,0},{4,7},{5,6},{6,5},{7,4},{8,11},{9,10},{10,... | collective-permute-start | bytes 258056 | tf_op jit(solution)/shard_map/ppermute | solution.py:93
  7.2 2.4 %collective-permute-start.1 = (bf16[336,128]{1,0:T(8,128)(2,1)S(1)}, bf16[336,128]{1,0:T(8,128)(2,1)S(1)}, u32[]{:S(2)}, u32[]{:S(2)}) collective-permute-start(bf16[336,128]{1,0:T(8,128)(2,1)S(1)} %get-tuple-element.17), channel_id=1, source_target_pairs={{0,7},{1,6},{2,5},{3,4},{4,3},{5,2},{6,1},{7,0},{8,15},{9,14},{10,... | collective-permute-start | bytes 258056 | tf_op jit(solution)/shard_map/ppermute | solution.py:93
  9.6 1.3 %collective-permute-start.2 = (bf16[336,128]{1,0:T(8,128)(2,1)S(1)}, bf16[336,128]{1,0:T(8,128)(2,1)S(1)}, u32[]{:S(2)}, u32[]{:S(2)}) collective-permute-start(bf16[336,128]{1,0:T(8,128)(2,1)S(1)} %get-tuple-element.18), channel_id=1, source_target_pairs={{0,6},{1,7},{2,4},{3,5},{4,2},{5,3},{6,0},{7,1},{8,14},{9,15},{10,... | collective-permute-start | bytes 258056 | tf_op jit(solution)/shard_map/ppermute | solution.py:93
  11.0 0.0 collective-permute-start.3
  11.0 0.0 collective-permute-done.refs_0_
  11.0 4.0 %collective-permute-start.4 = (bf16[336,128]{1,0:T(8,128)(2,1)S(1)}, bf16[336,128]{1,0:T(8,128)(2,1)S(1)}, u32[]{:S(2)}, u32[]{:S(2)}) collective-permute-start(bf16[336,128]{1,0:T(8,128)(2,1)S(1)} %get-tuple-element.20), channel_id=1, source_target_pairs={{0,5},{1,4},{2,7},{3,6},{4,1},{5,0},{6,3},{7,2},{8,13},{9,12},{10,... | collective-permute-start | bytes 258056 | tf_op jit(solution)/shard_map/ppermute | solution.py:93
  14.9 0.0 collective-permute-done.1.refs_1_
  14.9 6.8 %collective-permute-start.5 = (bf16[336,128]{1,0:T(8,128)(2,1)S(1)}, bf16[336,128]{1,0:T(8,128)(2,1)S(1)}, u32[]{:S(2)}, u32[]{:S(2)}) collective-permute-start(bf16[336,128]{1,0:T(8,128)(2,1)S(1)} %get-tuple-element.21), channel_id=1, source_target_pairs={{0,4},{1,5},{2,6},{3,7},{4,0},{5,1},{6,2},{7,3},{8,12},{9,13},{10,... | collective-permute-start | bytes 258056 | tf_op jit(solution)/shard_map/ppermute | solution.py:93
  21.8 0.0 collective-permute-done.2.refs_2_
  21.8 0.7 %collective-permute-start.6 = (bf16[336,128]{1,0:T(8,128)(2,1)S(1)}, bf16[336,128]{1,0:T(8,128)(2,1)S(1)}, u32[]{:S(2)}, u32[]{:S(2)}) collective-permute-start(bf16[336,128]{1,0:T(8,128)(2,1)S(1)} %get-tuple-element.22), channel_id=1, source_target_pairs={{0,1},{1,0},{2,3},{3,2},{4,5},{5,4},{6,7},{7,6},{8,9},{9,8},{10,11... | collective-permute-start | bytes 258056 | tf_op jit(solution)/shard_map/ppermute | solution.py:93
  22.4 0.0 collective-permute-done.3.refs_3_
  22.4 0.0 collective-permute-done.7.refs_1_
  22.4 0.0 collective-permute-start.8
  22.4 0.5 %collective-permute-start.9 = (bf16[224,1024]{1,0:T(8,128)(2,1)S(1)}, bf16[224,1024]{1,0:T(8,128)(2,1)S(1)}, u32[]{:S(2)}, u32[]{:S(2)}) collective-permute-start(bf16[224,1024]{1,0:T(8,128)(2,1)S(1)} %collective-permute-done.7.refs_1_), channel_id=1, source_target_pairs={{0,8},{8,0},{16,24},{24,16},{1,9},{9,1},{17,25},{25,17},{2,10},{10... | collective-permute-start | bytes 1376264 | tf_op jit(solution)/shard_map/ppermute | solution.py:93
  22.9 1.1 %collective-permute-done.4.refs_4_ = bf16[336,128]{1,0:T(8,128)(2,1)S(1)} collective-permute-done((bf16[336,128]{1,0:T(8,128)(2,1)S(1)}, bf16[336,128]{1,0:T(8,128)(2,1)S(1)}, u32[]{:S(2)}, u32[]{:S(2)}) %collective-permute-start.4) | collective-permute-done | bytes 86048 | tf_op jit(solution)/shard_map/ppermute | solution.py:93
  24.0 0.7 %collective-permute-done.5.refs_5_ = bf16[336,128]{1,0:T(8,128)(2,1)S(1)} collective-permute-done((bf16[336,128]{1,0:T(8,128)(2,1)S(1)}, bf16[336,128]{1,0:T(8,128)(2,1)S(1)}, u32[]{:S(2)}, u32[]{:S(2)}) %collective-permute-start.5) | collective-permute-done | bytes 86048 | tf_op jit(solution)/shard_map/ppermute | solution.py:93
  24.7 1.5 %collective-permute-done.6.refs_6_ = bf16[336,128]{1,0:T(8,128)(2,1)S(1)} collective-permute-done((bf16[336,128]{1,0:T(8,128)(2,1)S(1)}, bf16[336,128]{1,0:T(8,128)(2,1)S(1)}, u32[]{:S(2)}, u32[]{:S(2)}) %collective-permute-start.6) | collective-permute-done | bytes 86048 | tf_op jit(solution)/shard_map/ppermute | solution.py:93
  26.2 1.9 %self_attention.1 = bf16[8,112,128]{2,1,0:T(8,128)(2,1)S(1)} custom-call(bf16[336,128]{1,0:T(8,128)(2,1)S(1)} %collective-permute-done.refs_0_, bf16[336,128]{1,0:T(8,128)(2,1)S(1)} %collective-permute-done.1.refs_1_, bf16[336,128]{1,0:T(8,128)(2,1)S(1)} %collective-permute-done.2.refs_2_, bf16[336,128]{1,0:T(8,128)(2,1)S(1)} %collective-permute-done.3.refs_3_, ...), custom_call_target="tpu_custom_call" | custom-call | flops 411041792 | bytes 917504 | tf_op jit(solution)/shard_map/self_attention/pallas_call | solution.py:127
  28.2 0.0 copy-start
  28.2 11.0 %all_to_all.5.o_ref = bf16[8,112,128]{2,1,0:T(8,128)(2,1)S(1)} all-to-all(bf16[8,112,128]{2,1,0:T(8,128)(2,1)S(1)} %self_attention.1), channel_id=1, replica_groups=mesh['view'=4,'ctx'=8] {'ctx'}, dimensions={0} | all-to-all | bytes 458752 | tf_op jit(solution)/shard_map/all_to_all | solution.py:140
  39.2 0.0 collective-permute-done.8.refs_2_
  39.3 0.0 collective-permute-done.9.refs_3_
  39.3 0.0 copy-done
  39.3 1.7 %cross_view.1 = bf16[112,1024]{1,0:T(8,128)(2,1)} custom-call(bf16[8,112,128]{2,1,0:T(8,128)(2,1)S(1)} %all_to_all.5.o_ref, bf16[112,1024]{1,0:T(8,128)(2,1)S(1)} %bitcast.7, bf16[224,1024]{1,0:T(8,128)(2,1)S(1)} %get-tuple-element.25.refs_0_, bf16[224,1024]{1,0:T(8,128)(2,1)S(1)} %collective-permute-done.7.refs_1_, ...), custom_call_target="tpu_custom_call" | custom-call | tf_op jit(solution)/shard_map/cross_view/pallas_call | solution.py:191
Async XLA Ops:
  1.6 20.8 %collective-permute-start.7 = (bf16[224,1024]{1,0:T(8,128)(2,1)S(1)}, bf16[224,1024]{1,0:T(8,128)(2,1)S(1)}, u32[]{:S(2)}, u32[]{:S(2)}) collective-permute-start(bf16[224,1024]{1,0:T(8,128)(2,1)S(1)} %get-tuple-element.25.refs_0_), channel_id=1, source_target_pairs={{0,16},{8,24},{16,0},{24,8},{1,17},{9,25},{17,1},{25,9},{2,18},{10... | collective-permute-start | bytes 1376264 | tf_op jit(solution)/shard_map/ppermute | solution.py:93
  4.7 6.3 %collective-permute-start = (bf16[336,128]{1,0:T(8,128)(2,1)S(1)}, bf16[336,128]{1,0:T(8,128)(2,1)S(1)}, u32[]{:S(2)}, u32[]{:S(2)}) collective-permute-start(bf16[336,128]{1,0:T(8,128)(2,1)S(1)} %get-tuple-element.16), channel_id=1, source_target_pairs={{0,3},{1,2},{2,1},{3,0},{4,7},{5,6},{6,5},{7,4},{8,11},{9,10},{10,... | collective-permute-start | bytes 258056 | tf_op jit(solution)/shard_map/ppermute | solution.py:93
  7.2 7.8 %collective-permute-start.1 = (bf16[336,128]{1,0:T(8,128)(2,1)S(1)}, bf16[336,128]{1,0:T(8,128)(2,1)S(1)}, u32[]{:S(2)}, u32[]{:S(2)}) collective-permute-start(bf16[336,128]{1,0:T(8,128)(2,1)S(1)} %get-tuple-element.17), channel_id=1, source_target_pairs={{0,7},{1,6},{2,5},{3,4},{4,3},{5,2},{6,1},{7,0},{8,15},{9,14},{10,... | collective-permute-start | bytes 258056 | tf_op jit(solution)/shard_map/ppermute | solution.py:93
  9.6 12.2 %collective-permute-start.2 = (bf16[336,128]{1,0:T(8,128)(2,1)S(1)}, bf16[336,128]{1,0:T(8,128)(2,1)S(1)}, u32[]{:S(2)}, u32[]{:S(2)}) collective-permute-start(bf16[336,128]{1,0:T(8,128)(2,1)S(1)} %get-tuple-element.18), channel_id=1, source_target_pairs={{0,6},{1,7},{2,4},{3,5},{4,2},{5,3},{6,0},{7,1},{8,14},{9,15},{10,... | collective-permute-start | bytes 258056 | tf_op jit(solution)/shard_map/ppermute | solution.py:93
  11.0 11.5 %collective-permute-start.3 = (bf16[336,128]{1,0:T(8,128)(2,1)S(1)}, bf16[336,128]{1,0:T(8,128)(2,1)S(1)}, u32[]{:S(2)}, u32[]{:S(2)}) collective-permute-start(bf16[336,128]{1,0:T(8,128)(2,1)S(1)} %get-tuple-element.19), channel_id=1, source_target_pairs={{0,2},{1,3},{2,0},{3,1},{4,6},{5,7},{6,4},{7,5},{8,10},{9,11},{10,... | collective-permute-start | bytes 258056 | tf_op jit(solution)/shard_map/ppermute | solution.py:93
  11.0 13.0 %collective-permute-start.4 = (bf16[336,128]{1,0:T(8,128)(2,1)S(1)}, bf16[336,128]{1,0:T(8,128)(2,1)S(1)}, u32[]{:S(2)}, u32[]{:S(2)}) collective-permute-start(bf16[336,128]{1,0:T(8,128)(2,1)S(1)} %get-tuple-element.20), channel_id=1, source_target_pairs={{0,5},{1,4},{2,7},{3,6},{4,1},{5,0},{6,3},{7,2},{8,13},{9,12},{10,... | collective-permute-start | bytes 258056 | tf_op jit(solution)/shard_map/ppermute | solution.py:93
  14.9 9.8 %collective-permute-start.5 = (bf16[336,128]{1,0:T(8,128)(2,1)S(1)}, bf16[336,128]{1,0:T(8,128)(2,1)S(1)}, u32[]{:S(2)}, u32[]{:S(2)}) collective-permute-start(bf16[336,128]{1,0:T(8,128)(2,1)S(1)} %get-tuple-element.21), channel_id=1, source_target_pairs={{0,4},{1,5},{2,6},{3,7},{4,0},{5,1},{6,2},{7,3},{8,12},{9,13},{10,... | collective-permute-start | bytes 258056 | tf_op jit(solution)/shard_map/ppermute | solution.py:93
  21.8 4.5 %collective-permute-start.6 = (bf16[336,128]{1,0:T(8,128)(2,1)S(1)}, bf16[336,128]{1,0:T(8,128)(2,1)S(1)}, u32[]{:S(2)}, u32[]{:S(2)}) collective-permute-start(bf16[336,128]{1,0:T(8,128)(2,1)S(1)} %get-tuple-element.22), channel_id=1, source_target_pairs={{0,1},{1,0},{2,3},{3,2},{4,5},{5,4},{6,7},{7,6},{8,9},{9,8},{10,11... | collective-permute-start | bytes 258056 | tf_op jit(solution)/shard_map/ppermute | solution.py:93
  22.4 16.8 %collective-permute-start.8 = (bf16[224,1024]{1,0:T(8,128)(2,1)S(1)}, bf16[224,1024]{1,0:T(8,128)(2,1)S(1)}, u32[]{:S(2)}, u32[]{:S(2)}) collective-permute-start(bf16[224,1024]{1,0:T(8,128)(2,1)S(1)} %get-tuple-element.25.refs_0_), channel_id=1, source_target_pairs={{0,8},{8,0},{16,24},{24,16},{1,9},{9,1},{17,25},{25,17},{2,10},{10... | collective-permute-start | bytes 1376264 | tf_op jit(solution)/shard_map/ppermute | solution.py:93
  22.4 16.8 %collective-permute-start.9 = (bf16[224,1024]{1,0:T(8,128)(2,1)S(1)}, bf16[224,1024]{1,0:T(8,128)(2,1)S(1)}, u32[]{:S(2)}, u32[]{:S(2)}) collective-permute-start(bf16[224,1024]{1,0:T(8,128)(2,1)S(1)} %collective-permute-done.7.refs_1_), channel_id=1, source_target_pairs={{0,8},{8,0},{16,24},{24,16},{1,9},{9,1},{17,25},{25,17},{2,10},{10... | collective-permute-start | bytes 1376264 | tf_op jit(solution)/shard_map/ppermute | solution.py:93
  28.2 11.1 %copy-start = (bf16[1,112,1024]{2,1,0:T(8,128)(2,1)S(1)}, bf16[1,112,1024]{2,1,0:T(8,128)(2,1)}, u32[]{:S(2)}) copy-start(bf16[1,112,1024]{2,1,0:T(8,128)(2,1)} %param.9) | copy-start | bytes 688132

commit v26 on v24

--- a/solution.py
+++ b/solution.py
@@ -106,7 +106,7 @@
 def split_attention(q, k, v, k_cross, v_cross, ctx_size):
     rows, width = q.shape
     heads = width // HEAD
-    partners = (3, 7, 6, 2, 5, 4, 1, 0)
+    partners = (3, 7, 6, 2, 4, 5, 1, 0)
     vmem = pl.BlockSpec(memory_space=pltpu.VMEM)
     hbm = pl.BlockSpec(memory_space=pltpu.HBM)
     sources = [pltpu.with_memory_space_constraint(x, pltpu.HBM) for x in (q, k, v, k_cross, v_cross)]

time: 40.6 us -> 41.5 us (1.022)
  blocking collectives: 11.1 us -> 11.9 us
    all_to_all x1, blocking collectives: 11.1 us -> 11.9 us  [split_attention(): back = lax.all_to_all(own, 'ctx', split_axis=0, concat_axis=0, tiled=True)]
  transfers between devices with their start and end apart: 10 -> 10, of which waited for: 3 -> 3; matrix products, arithmetic and copies ran while one was open for 0% -> 0% of each run, Pallas kernels for 4% -> 3%
where the time goes in v26:
time: 41.5 us; the launch traced here: 41.4 us
  starting transfers between devices  21.2 us (51%)
  blocking collectives  11.9 us (29%)
  Pallas kernels  4.73 us (11%)
  waiting for transfers between devices  3.55 us (9%)
    ppermute x10, starting transfers between devices, swap(): lax.ppermute(array, axis_name, [(i, i ^ partner) for i in range(axis_size)])  21.2 us
    all_to_all x1, blocking collectives, split_attention(): back = lax.all_to_all(own, 'ctx', split_axis=0, concat_axis=0, tiled=True)  11.9 us
    ppermute x10, waiting for transfers between devices, swap(): lax.ppermute(array, axis_name, [(i, i ^ partner) for i in range(axis_size)])  3.55 us
    pallas_call x1, Pallas kernels, body(): pl.pallas_call(functools.partial(cross_kernel, heads), out_shape=jax.Shap...  1.68 us
    pallas_call x1, Pallas kernels, split_attention(): pl.pallas_call(functools.partial(pack_kernel, partners), out_shape=[block...  1.61 us
    pallas_call x1, Pallas kernels, split_attention(): pl.pallas_call(functools.partial(packed_attention_kernel, partners, rows,...  1.44 us
  transfers between devices with their start and end apart: 10, of which 3 were waited for; matrix products, arithmetic and copies ran while one was open for 0% of the time, Pallas kernels for 3%

profile of v26, /device:TPU:0, one launch (start us, length us, event | category | flops | bytes accessed | tf_op | source)
XLA Modules:
  0.0 41.4 jit_solution(9686849415028441555)
XLA Ops:
  0.0 1.6 %pack_qkv.1 = (bf16[336,128]{1,0:T(8,128)(2,1)S(1)}, bf16[336,128]{1,0:T(8,128)(2,1)S(1)}, bf16[336,128]{1,0:T(8,128)(2,1)S(1)}, bf16[336,128]{1,0:T(8,128)(2,1)...) custom-call(bf16[112,1024]{1,0:T(8,128)(2,1)} %bitcast.8, ...), custom_call_target="tpu_custom_call" | custom-call | tf_op jit(solution)/shard_map/pack_qkv/pallas_call | solution.py:114
  1.6 3.0 %collective-permute-start.7 = (bf16[224,1024]{1,0:T(8,128)(2,1)S(1)}, bf16[224,1024]{1,0:T(8,128)(2,1)S(1)}, u32[]{:S(2)}, u32[]{:S(2)}) collective-permute-start(bf16[224,1024]{1,0:T(8,128)(2,1)S(1)} %get-tuple-element.25.refs_0_), channel_id=1, source_target_pairs={{0,16},{8,24},{16,0},{24,8},{1,17},{9,25},{17,1},{25,9},{2,18},{10... | collective-permute-start | bytes 1376264 | tf_op jit(solution)/shard_map/ppermute | solution.py:93
  4.7 2.5 %collective-permute-start = (bf16[336,128]{1,0:T(8,128)(2,1)S(1)}, bf16[336,128]{1,0:T(8,128)(2,1)S(1)}, u32[]{:S(2)}, u32[]{:S(2)}) collective-permute-start(bf16[336,128]{1,0:T(8,128)(2,1)S(1)} %get-tuple-element.16), channel_id=1, source_target_pairs={{0,3},{1,2},{2,1},{3,0},{4,7},{5,6},{6,5},{7,4},{8,11},{9,10},{10,... | collective-permute-start | bytes 258056 | tf_op jit(solution)/shard_map/ppermute | solution.py:93
  7.2 2.4 %collective-permute-start.1 = (bf16[336,128]{1,0:T(8,128)(2,1)S(1)}, bf16[336,128]{1,0:T(8,128)(2,1)S(1)}, u32[]{:S(2)}, u32[]{:S(2)}) collective-permute-start(bf16[336,128]{1,0:T(8,128)(2,1)S(1)} %get-tuple-element.17), channel_id=1, source_target_pairs={{0,7},{1,6},{2,5},{3,4},{4,3},{5,2},{6,1},{7,0},{8,15},{9,14},{10,... | collective-permute-start | bytes 258056 | tf_op jit(solution)/shard_map/ppermute | solution.py:93
  9.6 1.3 %collective-permute-start.2 = (bf16[336,128]{1,0:T(8,128)(2,1)S(1)}, bf16[336,128]{1,0:T(8,128)(2,1)S(1)}, u32[]{:S(2)}, u32[]{:S(2)}) collective-permute-start(bf16[336,128]{1,0:T(8,128)(2,1)S(1)} %get-tuple-element.18), channel_id=1, source_target_pairs={{0,6},{1,7},{2,4},{3,5},{4,2},{5,3},{6,0},{7,1},{8,14},{9,15},{10,... | collective-permute-start | bytes 258056 | tf_op jit(solution)/shard_map/ppermute | solution.py:93
  11.0 0.0 collective-permute-start.3
  11.0 0.0 collective-permute-done.refs_0_
  11.0 3.0 %collective-permute-start.4 = (bf16[336,128]{1,0:T(8,128)(2,1)S(1)}, bf16[336,128]{1,0:T(8,128)(2,1)S(1)}, u32[]{:S(2)}, u32[]{:S(2)}) collective-permute-start(bf16[336,128]{1,0:T(8,128)(2,1)S(1)} %get-tuple-element.20), channel_id=1, source_target_pairs={{0,4},{1,5},{2,6},{3,7},{4,0},{5,1},{6,2},{7,3},{8,12},{9,13},{10,... | collective-permute-start | bytes 258056 | tf_op jit(solution)/shard_map/ppermute | solution.py:93
  14.0 0.9 %collective-permute-done.1.refs_1_ = bf16[336,128]{1,0:T(8,128)(2,1)S(1)} collective-permute-done((bf16[336,128]{1,0:T(8,128)(2,1)S(1)}, bf16[336,128]{1,0:T(8,128)(2,1)S(1)}, u32[]{:S(2)}, u32[]{:S(2)}) %collective-permute-start.1) | collective-permute-done | bytes 86048 | tf_op jit(solution)/shard_map/ppermute | solution.py:93
  14.9 6.9 %collective-permute-start.5 = (bf16[336,128]{1,0:T(8,128)(2,1)S(1)}, bf16[336,128]{1,0:T(8,128)(2,1)S(1)}, u32[]{:S(2)}, u32[]{:S(2)}) collective-permute-start(bf16[336,128]{1,0:T(8,128)(2,1)S(1)} %get-tuple-element.21), channel_id=1, source_target_pairs={{0,5},{1,4},{2,7},{3,6},{4,1},{5,0},{6,3},{7,2},{8,13},{9,12},{10,... | collective-permute-start | bytes 258056 | tf_op jit(solution)/shard_map/ppermute | solution.py:93
  21.8 0.0 collective-permute-done.2.refs_2_
  21.9 1.4 %collective-permute-start.6 = (bf16[336,128]{1,0:T(8,128)(2,1)S(1)}, bf16[336,128]{1,0:T(8,128)(2,1)S(1)}, u32[]{:S(2)}, u32[]{:S(2)}) collective-permute-start(bf16[336,128]{1,0:T(8,128)(2,1)S(1)} %get-tuple-element.22), channel_id=1, source_target_pairs={{0,1},{1,0},{2,3},{3,2},{4,5},{5,4},{6,7},{7,6},{8,9},{9,8},{10,11... | collective-permute-start | bytes 258056 | tf_op jit(solution)/shard_map/ppermute | solution.py:93
  23.2 0.0 collective-permute-done.3.refs_3_
  23.2 0.0 collective-permute-done.7.refs_1_
  23.2 0.0 collective-permute-start.8
  23.2 0.5 %collective-permute-start.9 = (bf16[224,1024]{1,0:T(8,128)(2,1)S(1)}, bf16[224,1024]{1,0:T(8,128)(2,1)S(1)}, u32[]{:S(2)}, u32[]{:S(2)}) collective-permute-start(bf16[224,1024]{1,0:T(8,128)(2,1)S(1)} %collective-permute-done.7.refs_1_), channel_id=1, source_target_pairs={{0,8},{8,0},{16,24},{24,16},{1,9},{9,1},{17,25},{25,17},{2,10},{10... | collective-permute-start | bytes 1376264 | tf_op jit(solution)/shard_map/ppermute | solution.py:93
  23.7 0.0 collective-permute-done.4.refs_4_
  23.8 1.5 %collective-permute-done.5.refs_5_ = bf16[336,128]{1,0:T(8,128)(2,1)S(1)} collective-permute-done((bf16[336,128]{1,0:T(8,128)(2,1)S(1)}, bf16[336,128]{1,0:T(8,128)(2,1)S(1)}, u32[]{:S(2)}, u32[]{:S(2)}) %collective-permute-start.5) | collective-permute-done | bytes 86048 | tf_op jit(solution)/shard_map/ppermute | solution.py:93
  25.3 1.0 %collective-permute-done.6.refs_6_ = bf16[336,128]{1,0:T(8,128)(2,1)S(1)} collective-permute-done((bf16[336,128]{1,0:T(8,128)(2,1)S(1)}, bf16[336,128]{1,0:T(8,128)(2,1)S(1)}, u32[]{:S(2)}, u32[]{:S(2)}) %collective-permute-start.6) | collective-permute-done | bytes 86048 | tf_op jit(solution)/shard_map/ppermute | solution.py:93
  26.3 1.4 %self_attention.1 = bf16[8,112,128]{2,1,0:T(8,128)(2,1)S(1)} custom-call(bf16[336,128]{1,0:T(8,128)(2,1)S(1)} %collective-permute-done.refs_0_, bf16[336,128]{1,0:T(8,128)(2,1)S(1)} %collective-permute-done.1.refs_1_, bf16[336,128]{1,0:T(8,128)(2,1)S(1)} %collective-permute-done.2.refs_2_, bf16[336,128]{1,0:T(8,128)(2,1)S(1)} %collective-permute-done.3.refs_3_, ...), custom_call_target="tpu_custom_call" | custom-call | flops 411041792 | bytes 917504 | tf_op jit(solution)/shard_map/self_attention/pallas_call | solution.py:127
  27.8 0.0 copy-start
  27.8 11.9 %all_to_all.5.o_ref = bf16[8,112,128]{2,1,0:T(8,128)(2,1)S(1)} all-to-all(bf16[8,112,128]{2,1,0:T(8,128)(2,1)S(1)} %self_attention.1), channel_id=1, replica_groups=mesh['view'=4,'ctx'=8] {'ctx'}, dimensions={0} | all-to-all | bytes 458752 | tf_op jit(solution)/shard_map/all_to_all | solution.py:140
  39.7 0.0 collective-permute-done.8.refs_2_
  39.7 0.0 collective-permute-done.9.refs_3_
  39.7 0.0 copy-done
  39.7 1.7 %cross_view.1 = bf16[112,1024]{1,0:T(8,128)(2,1)} custom-call(bf16[8,112,128]{2,1,0:T(8,128)(2,1)S(1)} %all_to_all.5.o_ref, bf16[112,1024]{1,0:T(8,128)(2,1)S(1)} %bitcast.7, bf16[224,1024]{1,0:T(8,128)(2,1)S(1)} %get-tuple-element.25.refs_0_, bf16[224,1024]{1,0:T(8,128)(2,1)S(1)} %collective-permute-done.7.refs_1_, ...), custom_call_target="tpu_custom_call" | custom-call | tf_op jit(solution)/shard_map/cross_view/pallas_call | solution.py:191
Async XLA Ops:
  1.6 21.6 %collective-permute-start.7 = (bf16[224,1024]{1,0:T(8,128)(2,1)S(1)}, bf16[224,1024]{1,0:T(8,128)(2,1)S(1)}, u32[]{:S(2)}, u32[]{:S(2)}) collective-permute-start(bf16[224,1024]{1,0:T(8,128)(2,1)S(1)} %get-tuple-element.25.refs_0_), channel_id=1, source_target_pairs={{0,16},{8,24},{16,0},{24,8},{1,17},{9,25},{17,1},{25,9},{2,18},{10... | collective-permute-start | bytes 1376264 | tf_op jit(solution)/shard_map/ppermute | solution.py:93
  4.7 6.3 %collective-permute-start = (bf16[336,128]{1,0:T(8,128)(2,1)S(1)}, bf16[336,128]{1,0:T(8,128)(2,1)S(1)}, u32[]{:S(2)}, u32[]{:S(2)}) collective-permute-start(bf16[336,128]{1,0:T(8,128)(2,1)S(1)} %get-tuple-element.16), channel_id=1, source_target_pairs={{0,3},{1,2},{2,1},{3,0},{4,7},{5,6},{6,5},{7,4},{8,11},{9,10},{10,... | collective-permute-start | bytes 258056 | tf_op jit(solution)/shard_map/ppermute | solution.py:93
  7.2 7.8 %collective-permute-start.1 = (bf16[336,128]{1,0:T(8,128)(2,1)S(1)}, bf16[336,128]{1,0:T(8,128)(2,1)S(1)}, u32[]{:S(2)}, u32[]{:S(2)}) collective-permute-start(bf16[336,128]{1,0:T(8,128)(2,1)S(1)} %get-tuple-element.17), channel_id=1, source_target_pairs={{0,7},{1,6},{2,5},{3,4},{4,3},{5,2},{6,1},{7,0},{8,15},{9,14},{10,... | collective-permute-start | bytes 258056 | tf_op jit(solution)/shard_map/ppermute | solution.py:93
  9.6 12.2 %collective-permute-start.2 = (bf16[336,128]{1,0:T(8,128)(2,1)S(1)}, bf16[336,128]{1,0:T(8,128)(2,1)S(1)}, u32[]{:S(2)}, u32[]{:S(2)}) collective-permute-start(bf16[336,128]{1,0:T(8,128)(2,1)S(1)} %get-tuple-element.18), channel_id=1, source_target_pairs={{0,6},{1,7},{2,4},{3,5},{4,2},{5,3},{6,0},{7,1},{8,14},{9,15},{10,... | collective-permute-start | bytes 258056 | tf_op jit(solution)/shard_map/ppermute | solution.py:93
  11.0 12.3 %collective-permute-start.3 = (bf16[336,128]{1,0:T(8,128)(2,1)S(1)}, bf16[336,128]{1,0:T(8,128)(2,1)S(1)}, u32[]{:S(2)}, u32[]{:S(2)}) collective-permute-start(bf16[336,128]{1,0:T(8,128)(2,1)S(1)} %get-tuple-element.19), channel_id=1, source_target_pairs={{0,2},{1,3},{2,0},{3,1},{4,6},{5,7},{6,4},{7,5},{8,10},{9,11},{10,... | collective-permute-start | bytes 258056 | tf_op jit(solution)/shard_map/ppermute | solution.py:93
  11.0 12.8 %collective-permute-start.4 = (bf16[336,128]{1,0:T(8,128)(2,1)S(1)}, bf16[336,128]{1,0:T(8,128)(2,1)S(1)}, u32[]{:S(2)}, u32[]{:S(2)}) collective-permute-start(bf16[336,128]{1,0:T(8,128)(2,1)S(1)} %get-tuple-element.20), channel_id=1, source_target_pairs={{0,4},{1,5},{2,6},{3,7},{4,0},{5,1},{6,2},{7,3},{8,12},{9,13},{10,... | collective-permute-start | bytes 258056 | tf_op jit(solution)/shard_map/ppermute | solution.py:93
  14.9 10.4 %collective-permute-start.5 = (bf16[336,128]{1,0:T(8,128)(2,1)S(1)}, bf16[336,128]{1,0:T(8,128)(2,1)S(1)}, u32[]{:S(2)}, u32[]{:S(2)}) collective-permute-start(bf16[336,128]{1,0:T(8,128)(2,1)S(1)} %get-tuple-element.21), channel_id=1, source_target_pairs={{0,5},{1,4},{2,7},{3,6},{4,1},{5,0},{6,3},{7,2},{8,13},{9,12},{10,... | collective-permute-start | bytes 258056 | tf_op jit(solution)/shard_map/ppermute | solution.py:93
  21.9 4.5 %collective-permute-start.6 = (bf16[336,128]{1,0:T(8,128)(2,1)S(1)}, bf16[336,128]{1,0:T(8,128)(2,1)S(1)}, u32[]{:S(2)}, u32[]{:S(2)}) collective-permute-start(bf16[336,128]{1,0:T(8,128)(2,1)S(1)} %get-tuple-element.22), channel_id=1, source_target_pairs={{0,1},{1,0},{2,3},{3,2},{4,5},{5,4},{6,7},{7,6},{8,9},{9,8},{10,11... | collective-permute-start | bytes 258056 | tf_op jit(solution)/shard_map/ppermute | solution.py:93
  23.2 16.4 %collective-permute-start.8 = (bf16[224,1024]{1,0:T(8,128)(2,1)S(1)}, bf16[224,1024]{1,0:T(8,128)(2,1)S(1)}, u32[]{:S(2)}, u32[]{:S(2)}) collective-permute-start(bf16[224,1024]{1,0:T(8,128)(2,1)S(1)} %get-tuple-element.25.refs_0_), channel_id=1, source_target_pairs={{0,8},{8,0},{16,24},{24,16},{1,9},{9,1},{17,25},{25,17},{2,10},{10... | collective-permute-start | bytes 1376264 | tf_op jit(solution)/shard_map/ppermute | solution.py:93
  23.2 16.4 %collective-permute-start.9 = (bf16[224,1024]{1,0:T(8,128)(2,1)S(1)}, bf16[224,1024]{1,0:T(8,128)(2,1)S(1)}, u32[]{:S(2)}, u32[]{:S(2)}) collective-permute-start(bf16[224,1024]{1,0:T(8,128)(2,1)S(1)} %collective-permute-done.7.refs_1_), channel_id=1, source_target_pairs={{0,8},{8,0},{16,24},{24,16},{1,9},{9,1},{17,25},{25,17},{2,10},{10... | collective-permute-start | bytes 1376264 | tf_op jit(solution)/shard_map/ppermute | solution.py:93
  27.8 11.9 %copy-start = (bf16[1,112,1024]{2,1,0:T(8,128)(2,1)S(1)}, bf16[1,112,1024]{2,1,0:T(8,128)(2,1)}, u32[]{:S(2)}) copy-start(bf16[1,112,1024]{2,1,0:T(8,128)(2,1)} %param.9) | copy-start | bytes 688132

commit v27 on v24

--- a/solution.py
+++ b/solution.py
@@ -138,7 +138,7 @@
         name="self_attention",
     )(*moved)
     back = lax.all_to_all(own, "ctx", split_axis=0, concat_axis=0, tiled=True)
-    return back, pair, (pair, moved[:4])
+    return back, pair, (pair, moved[:3])
 
 
 def shared_attention(q, k, v, ctx_size):

time: 40.6 us -> 40.6 us (level)
  no operation moved by 1% of the time
where the time goes in v27:
time: 40.6 us; the launch traced here: 40.4 us
  starting transfers between devices  21.3 us (52%)
  blocking collectives  11 us (27%)
  Pallas kernels  4.73 us (12%)
  waiting for transfers between devices  3.33 us (8%)
    ppermute x10, starting transfers between devices, swap(): lax.ppermute(array, axis_name, [(i, i ^ partner) for i in range(axis_size)])  21.3 us
    all_to_all x1, blocking collectives, split_attention(): back = lax.all_to_all(own, 'ctx', split_axis=0, concat_axis=0, tiled=True)  11 us
    ppermute x10, waiting for transfers between devices, swap(): lax.ppermute(array, axis_name, [(i, i ^ partner) for i in range(axis_size)])  3.33 us
    pallas_call x1, Pallas kernels, body(): pl.pallas_call(functools.partial(cross_kernel, heads), out_shape=jax.Shap...  1.68 us
    pallas_call x1, Pallas kernels, split_attention(): pl.pallas_call(functools.partial(pack_kernel, partners), out_shape=[block...  1.61 us
    pallas_call x1, Pallas kernels, split_attention(): pl.pallas_call(functools.partial(packed_attention_kernel, partners, rows,...  1.44 us
  transfers between devices with their start and end apart: 10, of which 3 were waited for; matrix products, arithmetic and copies ran while one was open for 0% of the time, Pallas kernels for 4%

profile of v27, /device:TPU:0, one launch (start us, length us, event | category | flops | bytes accessed | tf_op | source)
XLA Modules:
  0.0 40.4 jit_solution(14390831638615721324)
XLA Ops:
  0.0 1.6 %pack_qkv.1 = (bf16[336,128]{1,0:T(8,128)(2,1)S(1)}, bf16[336,128]{1,0:T(8,128)(2,1)S(1)}, bf16[336,128]{1,0:T(8,128)(2,1)S(1)}, bf16[336,128]{1,0:T(8,128)(2,1)...) custom-call(bf16[112,1024]{1,0:T(8,128)(2,1)} %bitcast.8, ...), custom_call_target="tpu_custom_call" | custom-call | tf_op jit(solution)/shard_map/pack_qkv/pallas_call | solution.py:114
  1.6 3.0 %collective-permute-start.7 = (bf16[224,1024]{1,0:T(8,128)(2,1)S(1)}, bf16[224,1024]{1,0:T(8,128)(2,1)S(1)}, u32[]{:S(2)}, u32[]{:S(2)}) collective-permute-start(bf16[224,1024]{1,0:T(8,128)(2,1)S(1)} %get-tuple-element.25.refs_0_), channel_id=1, source_target_pairs={{0,16},{8,24},{16,0},{24,8},{1,17},{9,25},{17,1},{25,9},{2,18},{10... | collective-permute-start | bytes 1376264 | tf_op jit(solution)/shard_map/ppermute | solution.py:93
  4.7 2.5 %collective-permute-start = (bf16[336,128]{1,0:T(8,128)(2,1)S(1)}, bf16[336,128]{1,0:T(8,128)(2,1)S(1)}, u32[]{:S(2)}, u32[]{:S(2)}) collective-permute-start(bf16[336,128]{1,0:T(8,128)(2,1)S(1)} %get-tuple-element.16), channel_id=1, source_target_pairs={{0,3},{1,2},{2,1},{3,0},{4,7},{5,6},{6,5},{7,4},{8,11},{9,10},{10,... | collective-permute-start | bytes 258056 | tf_op jit(solution)/shard_map/ppermute | solution.py:93
  7.2 2.4 %collective-permute-start.1 = (bf16[336,128]{1,0:T(8,128)(2,1)S(1)}, bf16[336,128]{1,0:T(8,128)(2,1)S(1)}, u32[]{:S(2)}, u32[]{:S(2)}) collective-permute-start(bf16[336,128]{1,0:T(8,128)(2,1)S(1)} %get-tuple-element.17), channel_id=1, source_target_pairs={{0,7},{1,6},{2,5},{3,4},{4,3},{5,2},{6,1},{7,0},{8,15},{9,14},{10,... | collective-permute-start | bytes 258056 | tf_op jit(solution)/shard_map/ppermute | solution.py:93
  9.6 1.3 %collective-permute-start.2 = (bf16[336,128]{1,0:T(8,128)(2,1)S(1)}, bf16[336,128]{1,0:T(8,128)(2,1)S(1)}, u32[]{:S(2)}, u32[]{:S(2)}) collective-permute-start(bf16[336,128]{1,0:T(8,128)(2,1)S(1)} %get-tuple-element.18), channel_id=1, source_target_pairs={{0,6},{1,7},{2,4},{3,5},{4,2},{5,3},{6,0},{7,1},{8,14},{9,15},{10,... | collective-permute-start | bytes 258056 | tf_op jit(solution)/shard_map/ppermute | solution.py:93
  11.0 0.0 collective-permute-start.3
  11.0 0.0 collective-permute-done.refs_0_
  11.0 4.0 %collective-permute-start.4 = (bf16[336,128]{1,0:T(8,128)(2,1)S(1)}, bf16[336,128]{1,0:T(8,128)(2,1)S(1)}, u32[]{:S(2)}, u32[]{:S(2)}) collective-permute-start(bf16[336,128]{1,0:T(8,128)(2,1)S(1)} %get-tuple-element.20), channel_id=1, source_target_pairs={{0,5},{1,4},{2,7},{3,6},{4,1},{5,0},{6,3},{7,2},{8,13},{9,12},{10,... | collective-permute-start | bytes 258056 | tf_op jit(solution)/shard_map/ppermute | solution.py:93
  14.9 0.0 collective-permute-done.1.refs_1_
  14.9 6.8 %collective-permute-start.5 = (bf16[336,128]{1,0:T(8,128)(2,1)S(1)}, bf16[336,128]{1,0:T(8,128)(2,1)S(1)}, u32[]{:S(2)}, u32[]{:S(2)}) collective-permute-start(bf16[336,128]{1,0:T(8,128)(2,1)S(1)} %get-tuple-element.21), channel_id=1, source_target_pairs={{0,4},{1,5},{2,6},{3,7},{4,0},{5,1},{6,2},{7,3},{8,12},{9,13},{10,... | collective-permute-start | bytes 258056 | tf_op jit(solution)/shard_map/ppermute | solution.py:93
  21.8 0.0 collective-permute-done.2.refs_2_
  21.8 0.7 %collective-permute-start.6 = (bf16[336,128]{1,0:T(8,128)(2,1)S(1)}, bf16[336,128]{1,0:T(8,128)(2,1)S(1)}, u32[]{:S(2)}, u32[]{:S(2)}) collective-permute-start(bf16[336,128]{1,0:T(8,128)(2,1)S(1)} %get-tuple-element.22), channel_id=1, source_target_pairs={{0,1},{1,0},{2,3},{3,2},{4,5},{5,4},{6,7},{7,6},{8,9},{9,8},{10,11... | collective-permute-start | bytes 258056 | tf_op jit(solution)/shard_map/ppermute | solution.py:93
  22.4 0.0 collective-permute-done.7.refs_1_
  22.4 0.0 collective-permute-start.8
  22.4 0.0 collective-permute-done.3.refs_3_
  22.4 0.5 %collective-permute-start.9 = (bf16[224,1024]{1,0:T(8,128)(2,1)S(1)}, bf16[224,1024]{1,0:T(8,128)(2,1)S(1)}, u32[]{:S(2)}, u32[]{:S(2)}) collective-permute-start(bf16[224,1024]{1,0:T(8,128)(2,1)S(1)} %collective-permute-done.7.refs_1_), channel_id=1, source_target_pairs={{0,8},{8,0},{16,24},{24,16},{1,9},{9,1},{17,25},{25,17},{2,10},{10... | collective-permute-start | bytes 1376264 | tf_op jit(solution)/shard_map/ppermute | solution.py:93
  22.9 1.1 %collective-permute-done.4.refs_4_ = bf16[336,128]{1,0:T(8,128)(2,1)S(1)} collective-permute-done((bf16[336,128]{1,0:T(8,128)(2,1)S(1)}, bf16[336,128]{1,0:T(8,128)(2,1)S(1)}, u32[]{:S(2)}, u32[]{:S(2)}) %collective-permute-start.4) | collective-permute-done | bytes 86048 | tf_op jit(solution)/shard_map/ppermute | solution.py:93
  24.0 0.7 %collective-permute-done.5.refs_5_ = bf16[336,128]{1,0:T(8,128)(2,1)S(1)} collective-permute-done((bf16[336,128]{1,0:T(8,128)(2,1)S(1)}, bf16[336,128]{1,0:T(8,128)(2,1)S(1)}, u32[]{:S(2)}, u32[]{:S(2)}) %collective-permute-start.5) | collective-permute-done | bytes 86048 | tf_op jit(solution)/shard_map/ppermute | solution.py:93
  24.7 1.5 %collective-permute-done.6.refs_6_ = bf16[336,128]{1,0:T(8,128)(2,1)S(1)} collective-permute-done((bf16[336,128]{1,0:T(8,128)(2,1)S(1)}, bf16[336,128]{1,0:T(8,128)(2,1)S(1)}, u32[]{:S(2)}, u32[]{:S(2)}) %collective-permute-start.6) | collective-permute-done | bytes 86048 | tf_op jit(solution)/shard_map/ppermute | solution.py:93
  26.2 1.4 %self_attention.1 = bf16[8,112,128]{2,1,0:T(8,128)(2,1)S(1)} custom-call(bf16[336,128]{1,0:T(8,128)(2,1)S(1)} %collective-permute-done.refs_0_, bf16[336,128]{1,0:T(8,128)(2,1)S(1)} %collective-permute-done.1.refs_1_, bf16[336,128]{1,0:T(8,128)(2,1)S(1)} %collective-permute-done.2.refs_2_, bf16[336,128]{1,0:T(8,128)(2,1)S(1)} %collective-permute-done.3.refs_3_, ...), custom_call_target="tpu_custom_call" | custom-call | flops 411041792 | bytes 917504 | tf_op jit(solution)/shard_map/self_attention/pallas_call | solution.py:127
  27.7 0.0 copy-start
  27.7 11.0 %all_to_all.5.o_ref = bf16[8,112,128]{2,1,0:T(8,128)(2,1)S(1)} all-to-all(bf16[8,112,128]{2,1,0:T(8,128)(2,1)S(1)} %self_attention.1), channel_id=1, replica_groups=mesh['view'=4,'ctx'=8] {'ctx'}, dimensions={0} | all-to-all | bytes 458752 | tf_op jit(solution)/shard_map/all_to_all | solution.py:140
  38.8 0.0 collective-permute-done.8.refs_2_
  38.8 0.0 collective-permute-done.9.refs_3_
  38.8 0.0 copy-done
  38.8 1.7 %cross_view.1 = bf16[112,1024]{1,0:T(8,128)(2,1)} custom-call(bf16[8,112,128]{2,1,0:T(8,128)(2,1)S(1)} %all_to_all.5.o_ref, bf16[112,1024]{1,0:T(8,128)(2,1)S(1)} %bitcast.7, bf16[224,1024]{1,0:T(8,128)(2,1)S(1)} %get-tuple-element.25.refs_0_, bf16[224,1024]{1,0:T(8,128)(2,1)S(1)} %collective-permute-done.7.refs_1_, ...), custom_call_target="tpu_custom_call" | custom-call | tf_op jit(solution)/shard_map/cross_view/pallas_call | solution.py:191
Async XLA Ops:
  1.6 20.8 %collective-permute-start.7 = (bf16[224,1024]{1,0:T(8,128)(2,1)S(1)}, bf16[224,1024]{1,0:T(8,128)(2,1)S(1)}, u32[]{:S(2)}, u32[]{:S(2)}) collective-permute-start(bf16[224,1024]{1,0:T(8,128)(2,1)S(1)} %get-tuple-element.25.refs_0_), channel_id=1, source_target_pairs={{0,16},{8,24},{16,0},{24,8},{1,17},{9,25},{17,1},{25,9},{2,18},{10... | collective-permute-start | bytes 1376264 | tf_op jit(solution)/shard_map/ppermute | solution.py:93
  4.7 6.3 %collective-permute-start = (bf16[336,128]{1,0:T(8,128)(2,1)S(1)}, bf16[336,128]{1,0:T(8,128)(2,1)S(1)}, u32[]{:S(2)}, u32[]{:S(2)}) collective-permute-start(bf16[336,128]{1,0:T(8,128)(2,1)S(1)} %get-tuple-element.16), channel_id=1, source_target_pairs={{0,3},{1,2},{2,1},{3,0},{4,7},{5,6},{6,5},{7,4},{8,11},{9,10},{10,... | collective-permute-start | bytes 258056 | tf_op jit(solution)/shard_map/ppermute | solution.py:93
  7.2 7.8 %collective-permute-start.1 = (bf16[336,128]{1,0:T(8,128)(2,1)S(1)}, bf16[336,128]{1,0:T(8,128)(2,1)S(1)}, u32[]{:S(2)}, u32[]{:S(2)}) collective-permute-start(bf16[336,128]{1,0:T(8,128)(2,1)S(1)} %get-tuple-element.17), channel_id=1, source_target_pairs={{0,7},{1,6},{2,5},{3,4},{4,3},{5,2},{6,1},{7,0},{8,15},{9,14},{10,... | collective-permute-start | bytes 258056 | tf_op jit(solution)/shard_map/ppermute | solution.py:93
  9.6 12.2 %collective-permute-start.2 = (bf16[336,128]{1,0:T(8,128)(2,1)S(1)}, bf16[336,128]{1,0:T(8,128)(2,1)S(1)}, u32[]{:S(2)}, u32[]{:S(2)}) collective-permute-start(bf16[336,128]{1,0:T(8,128)(2,1)S(1)} %get-tuple-element.18), channel_id=1, source_target_pairs={{0,6},{1,7},{2,4},{3,5},{4,2},{5,3},{6,0},{7,1},{8,14},{9,15},{10,... | collective-permute-start | bytes 258056 | tf_op jit(solution)/shard_map/ppermute | solution.py:93
  11.0 11.5 %collective-permute-start.3 = (bf16[336,128]{1,0:T(8,128)(2,1)S(1)}, bf16[336,128]{1,0:T(8,128)(2,1)S(1)}, u32[]{:S(2)}, u32[]{:S(2)}) collective-permute-start(bf16[336,128]{1,0:T(8,128)(2,1)S(1)} %get-tuple-element.19), channel_id=1, source_target_pairs={{0,2},{1,3},{2,0},{3,1},{4,6},{5,7},{6,4},{7,5},{8,10},{9,11},{10,... | collective-permute-start | bytes 258056 | tf_op jit(solution)/shard_map/ppermute | solution.py:93
  11.0 13.0 %collective-permute-start.4 = (bf16[336,128]{1,0:T(8,128)(2,1)S(1)}, bf16[336,128]{1,0:T(8,128)(2,1)S(1)}, u32[]{:S(2)}, u32[]{:S(2)}) collective-permute-start(bf16[336,128]{1,0:T(8,128)(2,1)S(1)} %get-tuple-element.20), channel_id=1, source_target_pairs={{0,5},{1,4},{2,7},{3,6},{4,1},{5,0},{6,3},{7,2},{8,13},{9,12},{10,... | collective-permute-start | bytes 258056 | tf_op jit(solution)/shard_map/ppermute | solution.py:93
  14.9 9.8 %collective-permute-start.5 = (bf16[336,128]{1,0:T(8,128)(2,1)S(1)}, bf16[336,128]{1,0:T(8,128)(2,1)S(1)}, u32[]{:S(2)}, u32[]{:S(2)}) collective-permute-start(bf16[336,128]{1,0:T(8,128)(2,1)S(1)} %get-tuple-element.21), channel_id=1, source_target_pairs={{0,4},{1,5},{2,6},{3,7},{4,0},{5,1},{6,2},{7,3},{8,12},{9,13},{10,... | collective-permute-start | bytes 258056 | tf_op jit(solution)/shard_map/ppermute | solution.py:93
  21.8 4.5 %collective-permute-start.6 = (bf16[336,128]{1,0:T(8,128)(2,1)S(1)}, bf16[336,128]{1,0:T(8,128)(2,1)S(1)}, u32[]{:S(2)}, u32[]{:S(2)}) collective-permute-start(bf16[336,128]{1,0:T(8,128)(2,1)S(1)} %get-tuple-element.22), channel_id=1, source_target_pairs={{0,1},{1,0},{2,3},{3,2},{4,5},{5,4},{6,7},{7,6},{8,9},{9,8},{10,11... | collective-permute-start | bytes 258056 | tf_op jit(solution)/shard_map/ppermute | solution.py:93
  22.4 16.3 %collective-permute-start.8 = (bf16[224,1024]{1,0:T(8,128)(2,1)S(1)}, bf16[224,1024]{1,0:T(8,128)(2,1)S(1)}, u32[]{:S(2)}, u32[]{:S(2)}) collective-permute-start(bf16[224,1024]{1,0:T(8,128)(2,1)S(1)} %get-tuple-element.25.refs_0_), channel_id=1, source_target_pairs={{0,8},{8,0},{16,24},{24,16},{1,9},{9,1},{17,25},{25,17},{2,10},{10... | collective-permute-start | bytes 1376264 | tf_op jit(solution)/shard_map/ppermute | solution.py:93
  22.4 16.3 %collective-permute-start.9 = (bf16[224,1024]{1,0:T(8,128)(2,1)S(1)}, bf16[224,1024]{1,0:T(8,128)(2,1)S(1)}, u32[]{:S(2)}, u32[]{:S(2)}) collective-permute-start(bf16[224,1024]{1,0:T(8,128)(2,1)S(1)} %collective-permute-done.7.refs_1_), channel_id=1, source_target_pairs={{0,8},{8,0},{16,24},{24,16},{1,9},{9,1},{17,25},{25,17},{2,10},{10... | collective-permute-start | bytes 1376264 | tf_op jit(solution)/shard_map/ppermute | solution.py:93
  27.7 11.1 %copy-start = (bf16[1,112,1024]{2,1,0:T(8,128)(2,1)S(1)}, bf16[1,112,1024]{2,1,0:T(8,128)(2,1)}, u32[]{:S(2)}) copy-start(bf16[1,112,1024]{2,1,0:T(8,128)(2,1)} %param.9) | copy-start | bytes 688132

commit v28 on v16

--- a/solution.py
+++ b/solution.py
@@ -115,7 +115,7 @@
 def split_attention(q, k, v, k_cross, v_cross, ctx_size):
     rows, width = q.shape
     heads = width // HEAD
-    partners = (3, 2, 1, 5, 4, 7, 6, 0)
+    partners = (3, 7, 6, 2, 5, 4, 1, 0)
     vmem = pl.BlockSpec(memory_space=pltpu.VMEM)
     hbm = pl.BlockSpec(memory_space=pltpu.HBM)
     sources = [pltpu.with_memory_space_constraint(x, pltpu.HBM) for x in (q, k, v, k_cross, v_cross)]
@@ -134,7 +134,7 @@
         for partner, data in zip(partners, blocks)
     ]
     own = pl.pallas_call(
-        functools.partial(packed_attention_kernel, partners, rows, max(heads // 4, 1)),
+        functools.partial(packed_attention_kernel, partners, rows, max(heads // 2, 1)),
         out_shape=jax.ShapeDtypeStruct((heads, rows, HEAD), q.dtype),
         in_specs=[vmem] * heads,
         out_specs=vmem,

time: 41.5 us -> 40.6 us (0.978)
  starting transfers between devices: 17.2 us -> 21.3 us
  blocking collectives: 13.9 us -> 11.1 us
  waiting for transfers between devices: 5.38 us -> 3.33 us
    ppermute x10, starting transfers between devices: 17.2 us -> 21.3 us  [swap(): lax.ppermute(array, axis_name, [(i, i ^ partner) for i in range(axis_size)])]
    all_to_all x1, blocking collectives: 13.9 us -> 11.1 us  [split_attention(): back = lax.all_to_all(own, 'ctx', split_axis=0, concat_axis=0, tiled=True)]
    ppermute x10, waiting for transfers between devices: 5.38 us -> 3.33 us  [swap(): lax.ppermute(array, axis_name, [(i, i ^ partner) for i in range(axis_size)])]
  transfers between devices with their start and end apart: 10 -> 10, of which waited for: 2 -> 3; matrix products, arithmetic and copies ran while one was open for 0% -> 0% of each run, Pallas kernels for 4% -> 4%
where the time goes in v28:
time: 40.6 us; the launch traced here: 40.4 us
  starting transfers between devices  21.3 us (52%)
  blocking collectives  11.1 us (27%)
  Pallas kernels  4.69 us (12%)
  waiting for transfers between devices  3.33 us (8%)
    ppermute x10, starting transfers between devices, swap(): lax.ppermute(array, axis_name, [(i, i ^ partner) for i in range(axis_size)])  21.3 us
    all_to_all x1, blocking collectives, split_attention(): back = lax.all_to_all(own, 'ctx', split_axis=0, concat_axis=0, tiled=True)  11.1 us
    ppermute x10, waiting for transfers between devices, swap(): lax.ppermute(array, axis_name, [(i, i ^ partner) for i in range(axis_size)])  3.33 us
    pallas_call x1, Pallas kernels, body(): pl.pallas_call(functools.partial(cross_kernel, heads), out_shape=jax.Shap...  1.65 us
    pallas_call x1, Pallas kernels, split_attention(): pl.pallas_call(functools.partial(pack_kernel, partners), out_shape=[block...  1.61 us
    pallas_call x1, Pallas kernels, split_attention(): pl.pallas_call(functools.partial(packed_attention_kernel, partners, rows,...  1.44 us
  transfers between devices with their start and end apart: 10, of which 3 were waited for; matrix products, arithmetic and copies ran while one was open for 0% of the time, Pallas kernels for 4%

profile of v28, /device:TPU:0, one launch (start us, length us, event | category | flops | bytes accessed | tf_op | source)
XLA Modules:
  0.0 40.4 jit_solution(4612873862859098341)
XLA Ops:
  0.0 1.6 %pack_qkv.1 = (bf16[336,128]{1,0:T(8,128)(2,1)S(1)}, bf16[336,128]{1,0:T(8,128)(2,1)S(1)}, bf16[336,128]{1,0:T(8,128)(2,1)S(1)}, bf16[336,128]{1,0:T(8,128)(2,1)...) custom-call(bf16[112,1024]{1,0:T(8,128)(2,1)} %bitcast.8, ...), custom_call_target="tpu_custom_call" | custom-call | tf_op jit(solution)/shard_map/pack_qkv/pallas_call | solution.py:123
  1.6 3.0 %collective-permute-start.7 = (bf16[224,1024]{1,0:T(8,128)(2,1)S(1)}, bf16[224,1024]{1,0:T(8,128)(2,1)S(1)}, u32[]{:S(2)}, u32[]{:S(2)}) collective-permute-start(bf16[224,1024]{1,0:T(8,128)(2,1)S(1)} %get-tuple-element.25.refs_0_), channel_id=1, source_target_pairs={{0,16},{8,24},{16,0},{24,8},{1,17},{9,25},{17,1},{25,9},{2,18},{10... | collective-permute-start | bytes 1376264 | tf_op jit(solution)/shard_map/ppermute | solution.py:102
  4.7 2.5 %collective-permute-start = (bf16[336,128]{1,0:T(8,128)(2,1)S(1)}, bf16[336,128]{1,0:T(8,128)(2,1)S(1)}, u32[]{:S(2)}, u32[]{:S(2)}) collective-permute-start(bf16[336,128]{1,0:T(8,128)(2,1)S(1)} %get-tuple-element.16), channel_id=1, source_target_pairs={{0,3},{1,2},{2,1},{3,0},{4,7},{5,6},{6,5},{7,4},{8,11},{9,10},{10,... | collective-permute-start | bytes 258056 | tf_op jit(solution)/shard_map/ppermute | solution.py:102
  7.2 2.4 %collective-permute-start.1 = (bf16[336,128]{1,0:T(8,128)(2,1)S(1)}, bf16[336,128]{1,0:T(8,128)(2,1)S(1)}, u32[]{:S(2)}, u32[]{:S(2)}) collective-permute-start(bf16[336,128]{1,0:T(8,128)(2,1)S(1)} %get-tuple-element.17), channel_id=1, source_target_pairs={{0,7},{1,6},{2,5},{3,4},{4,3},{5,2},{6,1},{7,0},{8,15},{9,14},{10,... | collective-permute-start | bytes 258056 | tf_op jit(solution)/shard_map/ppermute | solution.py:102
  9.6 1.3 %collective-permute-start.2 = (bf16[336,128]{1,0:T(8,128)(2,1)S(1)}, bf16[336,128]{1,0:T(8,128)(2,1)S(1)}, u32[]{:S(2)}, u32[]{:S(2)}) collective-permute-start(bf16[336,128]{1,0:T(8,128)(2,1)S(1)} %get-tuple-element.18), channel_id=1, source_target_pairs={{0,6},{1,7},{2,4},{3,5},{4,2},{5,3},{6,0},{7,1},{8,14},{9,15},{10,... | collective-permute-start | bytes 258056 | tf_op jit(solution)/shard_map/ppermute | solution.py:102
  11.0 0.0 collective-permute-start.3
  11.0 0.0 collective-permute-done.refs_0_
  11.0 4.0 %collective-permute-start.4 = (bf16[336,128]{1,0:T(8,128)(2,1)S(1)}, bf16[336,128]{1,0:T(8,128)(2,1)S(1)}, u32[]{:S(2)}, u32[]{:S(2)}) collective-permute-start(bf16[336,128]{1,0:T(8,128)(2,1)S(1)} %get-tuple-element.20), channel_id=1, source_target_pairs={{0,5},{1,4},{2,7},{3,6},{4,1},{5,0},{6,3},{7,2},{8,13},{9,12},{10,... | collective-permute-start | bytes 258056 | tf_op jit(solution)/shard_map/ppermute | solution.py:102
  14.9 0.0 collective-permute-done.1.refs_1_
  14.9 6.8 %collective-permute-start.5 = (bf16[336,128]{1,0:T(8,128)(2,1)S(1)}, bf16[336,128]{1,0:T(8,128)(2,1)S(1)}, u32[]{:S(2)}, u32[]{:S(2)}) collective-permute-start(bf16[336,128]{1,0:T(8,128)(2,1)S(1)} %get-tuple-element.21), channel_id=1, source_target_pairs={{0,4},{1,5},{2,6},{3,7},{4,0},{5,1},{6,2},{7,3},{8,12},{9,13},{10,... | collective-permute-start | bytes 258056 | tf_op jit(solution)/shard_map/ppermute | solution.py:102
  21.8 0.0 collective-permute-done.2.refs_2_
  21.8 0.7 %collective-permute-start.6 = (bf16[336,128]{1,0:T(8,128)(2,1)S(1)}, bf16[336,128]{1,0:T(8,128)(2,1)S(1)}, u32[]{:S(2)}, u32[]{:S(2)}) collective-permute-start(bf16[336,128]{1,0:T(8,128)(2,1)S(1)} %get-tuple-element.22), channel_id=1, source_target_pairs={{0,1},{1,0},{2,3},{3,2},{4,5},{5,4},{6,7},{7,6},{8,9},{9,8},{10,11... | collective-permute-start | bytes 258056 | tf_op jit(solution)/shard_map/ppermute | solution.py:102
  22.4 0.0 collective-permute-done.3.refs_3_
  22.4 0.0 collective-permute-done.7.refs_1_
  22.4 0.0 collective-permute-start.8
  22.4 0.5 %collective-permute-start.9 = (bf16[224,1024]{1,0:T(8,128)(2,1)S(1)}, bf16[224,1024]{1,0:T(8,128)(2,1)S(1)}, u32[]{:S(2)}, u32[]{:S(2)}) collective-permute-start(bf16[224,1024]{1,0:T(8,128)(2,1)S(1)} %collective-permute-done.7.refs_1_), channel_id=1, source_target_pairs={{0,8},{8,0},{16,24},{24,16},{1,9},{9,1},{17,25},{25,17},{2,10},{10... | collective-permute-start | bytes 1376264 | tf_op jit(solution)/shard_map/ppermute | solution.py:102
  22.9 1.1 %collective-permute-done.4.refs_4_ = bf16[336,128]{1,0:T(8,128)(2,1)S(1)} collective-permute-done((bf16[336,128]{1,0:T(8,128)(2,1)S(1)}, bf16[336,128]{1,0:T(8,128)(2,1)S(1)}, u32[]{:S(2)}, u32[]{:S(2)}) %collective-permute-start.4) | collective-permute-done | bytes 86048 | tf_op jit(solution)/shard_map/ppermute | solution.py:102
  24.0 0.7 %collective-permute-done.5.refs_5_ = bf16[336,128]{1,0:T(8,128)(2,1)S(1)} collective-permute-done((bf16[336,128]{1,0:T(8,128)(2,1)S(1)}, bf16[336,128]{1,0:T(8,128)(2,1)S(1)}, u32[]{:S(2)}, u32[]{:S(2)}) %collective-permute-start.5) | collective-permute-done | bytes 86048 | tf_op jit(solution)/shard_map/ppermute | solution.py:102
  24.7 1.5 %collective-permute-done.6.refs_6_ = bf16[336,128]{1,0:T(8,128)(2,1)S(1)} collective-permute-done((bf16[336,128]{1,0:T(8,128)(2,1)S(1)}, bf16[336,128]{1,0:T(8,128)(2,1)S(1)}, u32[]{:S(2)}, u32[]{:S(2)}) %collective-permute-start.6) | collective-permute-done | bytes 86048 | tf_op jit(solution)/shard_map/ppermute | solution.py:102
  26.2 1.4 %self_attention.1 = bf16[8,112,128]{2,1,0:T(8,128)(2,1)S(1)} custom-call(bf16[336,128]{1,0:T(8,128)(2,1)S(1)} %collective-permute-done.refs_0_, bf16[336,128]{1,0:T(8,128)(2,1)S(1)} %collective-permute-done.1.refs_1_, bf16[336,128]{1,0:T(8,128)(2,1)S(1)} %collective-permute-done.2.refs_2_, bf16[336,128]{1,0:T(8,128)(2,1)S(1)} %collective-permute-done.3.refs_3_, ...), custom_call_target="tpu_custom_call" | custom-call | flops 411041792 | bytes 917504 | tf_op jit(solution)/shard_map/self_attention/pallas_call | solution.py:136
  27.7 0.0 copy-start
  27.7 11.1 %all_to_all.5.o_ref = bf16[8,112,128]{2,1,0:T(8,128)(2,1)S(1)} all-to-all(bf16[8,112,128]{2,1,0:T(8,128)(2,1)S(1)} %self_attention.1), channel_id=1, replica_groups=mesh['view'=4,'ctx'=8] {'ctx'}, dimensions={0} | all-to-all | bytes 458752 | tf_op jit(solution)/shard_map/all_to_all | solution.py:149
  38.8 0.0 collective-permute-done.8.refs_2_
  38.8 0.0 collective-permute-done.9.refs_3_
  38.8 0.0 copy-done
  38.8 1.6 %cross_view.1 = bf16[112,1024]{1,0:T(8,128)(2,1)} custom-call(bf16[8,112,128]{2,1,0:T(8,128)(2,1)S(1)} %all_to_all.5.o_ref, bf16[112,1024]{1,0:T(8,128)(2,1)S(1)} %bitcast.7, bf16[224,1024]{1,0:T(8,128)(2,1)S(1)} %get-tuple-element.25.refs_0_, bf16[224,1024]{1,0:T(8,128)(2,1)S(1)} %collective-permute-done.7.refs_1_, ...), custom_call_target="tpu_custom_call" | custom-call | tf_op jit(solution)/shard_map/cross_view/pallas_call | solution.py:200
Async XLA Ops:
  1.6 20.8 %collective-permute-start.7 = (bf16[224,1024]{1,0:T(8,128)(2,1)S(1)}, bf16[224,1024]{1,0:T(8,128)(2,1)S(1)}, u32[]{:S(2)}, u32[]{:S(2)}) collective-permute-start(bf16[224,1024]{1,0:T(8,128)(2,1)S(1)} %get-tuple-element.25.refs_0_), channel_id=1, source_target_pairs={{0,16},{8,24},{16,0},{24,8},{1,17},{9,25},{17,1},{25,9},{2,18},{10... | collective-permute-start | bytes 1376264 | tf_op jit(solution)/shard_map/ppermute | solution.py:102
  4.7 6.3 %collective-permute-start = (bf16[336,128]{1,0:T(8,128)(2,1)S(1)}, bf16[336,128]{1,0:T(8,128)(2,1)S(1)}, u32[]{:S(2)}, u32[]{:S(2)}) collective-permute-start(bf16[336,128]{1,0:T(8,128)(2,1)S(1)} %get-tuple-element.16), channel_id=1, source_target_pairs={{0,3},{1,2},{2,1},{3,0},{4,7},{5,6},{6,5},{7,4},{8,11},{9,10},{10,... | collective-permute-start | bytes 258056 | tf_op jit(solution)/shard_map/ppermute | solution.py:102
  7.2 7.8 %collective-permute-start.1 = (bf16[336,128]{1,0:T(8,128)(2,1)S(1)}, bf16[336,128]{1,0:T(8,128)(2,1)S(1)}, u32[]{:S(2)}, u32[]{:S(2)}) collective-permute-start(bf16[336,128]{1,0:T(8,128)(2,1)S(1)} %get-tuple-element.17), channel_id=1, source_target_pairs={{0,7},{1,6},{2,5},{3,4},{4,3},{5,2},{6,1},{7,0},{8,15},{9,14},{10,... | collective-permute-start | bytes 258056 | tf_op jit(solution)/shard_map/ppermute | solution.py:102
  9.6 12.2 %collective-permute-start.2 = (bf16[336,128]{1,0:T(8,128)(2,1)S(1)}, bf16[336,128]{1,0:T(8,128)(2,1)S(1)}, u32[]{:S(2)}, u32[]{:S(2)}) collective-permute-start(bf16[336,128]{1,0:T(8,128)(2,1)S(1)} %get-tuple-element.18), channel_id=1, source_target_pairs={{0,6},{1,7},{2,4},{3,5},{4,2},{5,3},{6,0},{7,1},{8,14},{9,15},{10,... | collective-permute-start | bytes 258056 | tf_op jit(solution)/shard_map/ppermute | solution.py:102
  11.0 11.5 %collective-permute-start.3 = (bf16[336,128]{1,0:T(8,128)(2,1)S(1)}, bf16[336,128]{1,0:T(8,128)(2,1)S(1)}, u32[]{:S(2)}, u32[]{:S(2)}) collective-permute-start(bf16[336,128]{1,0:T(8,128)(2,1)S(1)} %get-tuple-element.19), channel_id=1, source_target_pairs={{0,2},{1,3},{2,0},{3,1},{4,6},{5,7},{6,4},{7,5},{8,10},{9,11},{10,... | collective-permute-start | bytes 258056 | tf_op jit(solution)/shard_map/ppermute | solution.py:102
  11.0 13.0 %collective-permute-start.4 = (bf16[336,128]{1,0:T(8,128)(2,1)S(1)}, bf16[336,128]{1,0:T(8,128)(2,1)S(1)}, u32[]{:S(2)}, u32[]{:S(2)}) collective-permute-start(bf16[336,128]{1,0:T(8,128)(2,1)S(1)} %get-tuple-element.20), channel_id=1, source_target_pairs={{0,5},{1,4},{2,7},{3,6},{4,1},{5,0},{6,3},{7,2},{8,13},{9,12},{10,... | collective-permute-start | bytes 258056 | tf_op jit(solution)/shard_map/ppermute | solution.py:102
  14.9 9.8 %collective-permute-start.5 = (bf16[336,128]{1,0:T(8,128)(2,1)S(1)}, bf16[336,128]{1,0:T(8,128)(2,1)S(1)}, u32[]{:S(2)}, u32[]{:S(2)}) collective-permute-start(bf16[336,128]{1,0:T(8,128)(2,1)S(1)} %get-tuple-element.21), channel_id=1, source_target_pairs={{0,4},{1,5},{2,6},{3,7},{4,0},{5,1},{6,2},{7,3},{8,12},{9,13},{10,... | collective-permute-start | bytes 258056 | tf_op jit(solution)/shard_map/ppermute | solution.py:102
  21.8 4.5 %collective-permute-start.6 = (bf16[336,128]{1,0:T(8,128)(2,1)S(1)}, bf16[336,128]{1,0:T(8,128)(2,1)S(1)}, u32[]{:S(2)}, u32[]{:S(2)}) collective-permute-start(bf16[336,128]{1,0:T(8,128)(2,1)S(1)} %get-tuple-element.22), channel_id=1, source_target_pairs={{0,1},{1,0},{2,3},{3,2},{4,5},{5,4},{6,7},{7,6},{8,9},{9,8},{10,11... | collective-permute-start | bytes 258056 | tf_op jit(solution)/shard_map/ppermute | solution.py:102
  22.4 16.3 %collective-permute-start.8 = (bf16[224,1024]{1,0:T(8,128)(2,1)S(1)}, bf16[224,1024]{1,0:T(8,128)(2,1)S(1)}, u32[]{:S(2)}, u32[]{:S(2)}) collective-permute-start(bf16[224,1024]{1,0:T(8,128)(2,1)S(1)} %get-tuple-element.25.refs_0_), channel_id=1, source_target_pairs={{0,8},{8,0},{16,24},{24,16},{1,9},{9,1},{17,25},{25,17},{2,10},{10... | collective-permute-start | bytes 1376264 | tf_op jit(solution)/shard_map/ppermute | solution.py:102
  22.4 16.3 %collective-permute-start.9 = (bf16[224,1024]{1,0:T(8,128)(2,1)S(1)}, bf16[224,1024]{1,0:T(8,128)(2,1)S(1)}, u32[]{:S(2)}, u32[]{:S(2)}) collective-permute-start(bf16[224,1024]{1,0:T(8,128)(2,1)S(1)} %collective-permute-done.7.refs_1_), channel_id=1, source_target_pairs={{0,8},{8,0},{16,24},{24,16},{1,9},{9,1},{17,25},{25,17},{2,10},{10... | collective-permute-start | bytes 1376264 | tf_op jit(solution)/shard_map/ppermute | solution.py:102
  27.7 11.1 %copy-start = (bf16[1,112,1024]{2,1,0:T(8,128)(2,1)S(1)}, bf16[1,112,1024]{2,1,0:T(8,128)(2,1)}, u32[]{:S(2)}) copy-start(bf16[1,112,1024]{2,1,0:T(8,128)(2,1)} %param.9) | copy-start | bytes 688132

commit v29 on v25

--- a/solution.py
+++ b/solution.py
@@ -54,7 +54,7 @@
     for first in range(0, len(in_refs), group):
         query = jnp.concatenate([ref[0:rows] for ref in in_refs[first : first + group]], axis=0)
         mixed = attend(query, keys, values)
-        for i in range(group):
+        for i in range(min(group, len(in_refs) - first)):
             out_ref[me ^ partners[first + i]] = mixed[i * rows : (i + 1) * rows]
 
 
@@ -125,7 +125,7 @@
         for partner, data in zip(partners, blocks)
     ]
     own = pl.pallas_call(
-        functools.partial(packed_attention_kernel, partners, rows, heads),
+        functools.partial(packed_attention_kernel, partners, rows, (heads + 2) // 3),
         out_shape=jax.ShapeDtypeStruct((heads, rows, HEAD), q.dtype),
         in_specs=[vmem] * heads,
         out_specs=vmem,

time: 41.1 us -> 40.6 us (0.988)
  Pallas kernels: 5.22 us -> 4.69 us
    pallas_call x1, Pallas kernels: 1.94 us -> 1.4 us  [split_attention(): pl.pallas_call(functools.partial(packed_attention_kernel, partners, rows,...]
  transfers between devices with their start and end apart: 10 -> 10, of which waited for: 3 -> 3; matrix products, arithmetic and copies ran while one was open for 0% -> 0% of each run, Pallas kernels for 5% -> 3%
where the time goes in v29:
time: 40.6 us; the launch traced here: 40.4 us
  starting transfers between devices  21.3 us (52%)
  blocking collectives  11 us (27%)
  Pallas kernels  4.69 us (12%)
  waiting for transfers between devices  3.33 us (8%)
    ppermute x10, starting transfers between devices, swap(): lax.ppermute(array, axis_name, [(i, i ^ partner) for i in range(axis_size)])  21.3 us
    all_to_all x1, blocking collectives, split_attention(): back = lax.all_to_all(own, 'ctx', split_axis=0, concat_axis=0, tiled=True)  11 us
    ppermute x10, waiting for transfers between devices, swap(): lax.ppermute(array, axis_name, [(i, i ^ partner) for i in range(axis_size)])  3.33 us
    pallas_call x1, Pallas kernels, body(): pl.pallas_call(functools.partial(cross_kernel, heads), out_shape=jax.Shap...  1.68 us
    pallas_call x1, Pallas kernels, split_attention(): pl.pallas_call(functools.partial(pack_kernel, partners), out_shape=[block...  1.61 us
    pallas_call x1, Pallas kernels, split_attention(): pl.pallas_call(functools.partial(packed_attention_kernel, partners, rows,...  1.4 us
  transfers between devices with their start and end apart: 10, of which 3 were waited for; matrix products, arithmetic and copies ran while one was open for 0% of the time, Pallas kernels for 3%

profile of v29, /device:TPU:0, one launch (start us, length us, event | category | flops | bytes accessed | tf_op | source)
XLA Modules:
  0.0 40.4 jit_solution(10316919759887514912)
XLA Ops:
  0.0 1.6 %pack_qkv.1 = (bf16[336,128]{1,0:T(8,128)(2,1)S(1)}, bf16[336,128]{1,0:T(8,128)(2,1)S(1)}, bf16[336,128]{1,0:T(8,128)(2,1)S(1)}, bf16[336,128]{1,0:T(8,128)(2,1)...) custom-call(bf16[112,1024]{1,0:T(8,128)(2,1)} %bitcast.8, ...), custom_call_target="tpu_custom_call" | custom-call | tf_op jit(solution)/shard_map/pack_qkv/pallas_call | solution.py:114
  1.6 3.0 %collective-permute-start.7 = (bf16[224,1024]{1,0:T(8,128)(2,1)S(1)}, bf16[224,1024]{1,0:T(8,128)(2,1)S(1)}, u32[]{:S(2)}, u32[]{:S(2)}) collective-permute-start(bf16[224,1024]{1,0:T(8,128)(2,1)S(1)} %get-tuple-element.25.refs_0_), channel_id=1, source_target_pairs={{0,16},{8,24},{16,0},{24,8},{1,17},{9,25},{17,1},{25,9},{2,18},{10... | collective-permute-start | bytes 1376264 | tf_op jit(solution)/shard_map/ppermute | solution.py:93
  4.7 2.5 %collective-permute-start = (bf16[336,128]{1,0:T(8,128)(2,1)S(1)}, bf16[336,128]{1,0:T(8,128)(2,1)S(1)}, u32[]{:S(2)}, u32[]{:S(2)}) collective-permute-start(bf16[336,128]{1,0:T(8,128)(2,1)S(1)} %get-tuple-element.16), channel_id=1, source_target_pairs={{0,3},{1,2},{2,1},{3,0},{4,7},{5,6},{6,5},{7,4},{8,11},{9,10},{10,... | collective-permute-start | bytes 258056 | tf_op jit(solution)/shard_map/ppermute | solution.py:93
  7.2 2.4 %collective-permute-start.1 = (bf16[336,128]{1,0:T(8,128)(2,1)S(1)}, bf16[336,128]{1,0:T(8,128)(2,1)S(1)}, u32[]{:S(2)}, u32[]{:S(2)}) collective-permute-start(bf16[336,128]{1,0:T(8,128)(2,1)S(1)} %get-tuple-element.17), channel_id=1, source_target_pairs={{0,7},{1,6},{2,5},{3,4},{4,3},{5,2},{6,1},{7,0},{8,15},{9,14},{10,... | collective-permute-start | bytes 258056 | tf_op jit(solution)/shard_map/ppermute | solution.py:93
  9.6 1.3 %collective-permute-start.2 = (bf16[336,128]{1,0:T(8,128)(2,1)S(1)}, bf16[336,128]{1,0:T(8,128)(2,1)S(1)}, u32[]{:S(2)}, u32[]{:S(2)}) collective-permute-start(bf16[336,128]{1,0:T(8,128)(2,1)S(1)} %get-tuple-element.18), channel_id=1, source_target_pairs={{0,6},{1,7},{2,4},{3,5},{4,2},{5,3},{6,0},{7,1},{8,14},{9,15},{10,... | collective-permute-start | bytes 258056 | tf_op jit(solution)/shard_map/ppermute | solution.py:93
  11.0 0.0 collective-permute-start.3
  11.0 0.0 collective-permute-done.refs_0_
  11.0 4.0 %collective-permute-start.4 = (bf16[336,128]{1,0:T(8,128)(2,1)S(1)}, bf16[336,128]{1,0:T(8,128)(2,1)S(1)}, u32[]{:S(2)}, u32[]{:S(2)}) collective-permute-start(bf16[336,128]{1,0:T(8,128)(2,1)S(1)} %get-tuple-element.20), channel_id=1, source_target_pairs={{0,5},{1,4},{2,7},{3,6},{4,1},{5,0},{6,3},{7,2},{8,13},{9,12},{10,... | collective-permute-start | bytes 258056 | tf_op jit(solution)/shard_map/ppermute | solution.py:93
  14.9 0.0 collective-permute-done.1.refs_1_
  14.9 6.8 %collective-permute-start.5 = (bf16[336,128]{1,0:T(8,128)(2,1)S(1)}, bf16[336,128]{1,0:T(8,128)(2,1)S(1)}, u32[]{:S(2)}, u32[]{:S(2)}) collective-permute-start(bf16[336,128]{1,0:T(8,128)(2,1)S(1)} %get-tuple-element.21), channel_id=1, source_target_pairs={{0,4},{1,5},{2,6},{3,7},{4,0},{5,1},{6,2},{7,3},{8,12},{9,13},{10,... | collective-permute-start | bytes 258056 | tf_op jit(solution)/shard_map/ppermute | solution.py:93
  21.8 0.0 collective-permute-done.2.refs_2_
  21.8 0.7 %collective-permute-start.6 = (bf16[336,128]{1,0:T(8,128)(2,1)S(1)}, bf16[336,128]{1,0:T(8,128)(2,1)S(1)}, u32[]{:S(2)}, u32[]{:S(2)}) collective-permute-start(bf16[336,128]{1,0:T(8,128)(2,1)S(1)} %get-tuple-element.22), channel_id=1, source_target_pairs={{0,1},{1,0},{2,3},{3,2},{4,5},{5,4},{6,7},{7,6},{8,9},{9,8},{10,11... | collective-permute-start | bytes 258056 | tf_op jit(solution)/shard_map/ppermute | solution.py:93
  22.4 0.0 collective-permute-done.3.refs_3_
  22.4 0.0 collective-permute-done.7.refs_1_
  22.4 0.0 collective-permute-start.8
  22.4 0.5 %collective-permute-start.9 = (bf16[224,1024]{1,0:T(8,128)(2,1)S(1)}, bf16[224,1024]{1,0:T(8,128)(2,1)S(1)}, u32[]{:S(2)}, u32[]{:S(2)}) collective-permute-start(bf16[224,1024]{1,0:T(8,128)(2,1)S(1)} %collective-permute-done.7.refs_1_), channel_id=1, source_target_pairs={{0,8},{8,0},{16,24},{24,16},{1,9},{9,1},{17,25},{25,17},{2,10},{10... | collective-permute-start | bytes 1376264 | tf_op jit(solution)/shard_map/ppermute | solution.py:93
  22.9 1.1 %collective-permute-done.4.refs_4_ = bf16[336,128]{1,0:T(8,128)(2,1)S(1)} collective-permute-done((bf16[336,128]{1,0:T(8,128)(2,1)S(1)}, bf16[336,128]{1,0:T(8,128)(2,1)S(1)}, u32[]{:S(2)}, u32[]{:S(2)}) %collective-permute-start.4) | collective-permute-done | bytes 86048 | tf_op jit(solution)/shard_map/ppermute | solution.py:93
  24.0 0.7 %collective-permute-done.5.refs_5_ = bf16[336,128]{1,0:T(8,128)(2,1)S(1)} collective-permute-done((bf16[336,128]{1,0:T(8,128)(2,1)S(1)}, bf16[336,128]{1,0:T(8,128)(2,1)S(1)}, u32[]{:S(2)}, u32[]{:S(2)}) %collective-permute-start.5) | collective-permute-done | bytes 86048 | tf_op jit(solution)/shard_map/ppermute | solution.py:93
  24.7 1.5 %collective-permute-done.6.refs_6_ = bf16[336,128]{1,0:T(8,128)(2,1)S(1)} collective-permute-done((bf16[336,128]{1,0:T(8,128)(2,1)S(1)}, bf16[336,128]{1,0:T(8,128)(2,1)S(1)}, u32[]{:S(2)}, u32[]{:S(2)}) %collective-permute-start.6) | collective-permute-done | bytes 86048 | tf_op jit(solution)/shard_map/ppermute | solution.py:93
  26.2 1.4 %self_attention.1 = bf16[8,112,128]{2,1,0:T(8,128)(2,1)S(1)} custom-call(bf16[336,128]{1,0:T(8,128)(2,1)S(1)} %collective-permute-done.refs_0_, bf16[336,128]{1,0:T(8,128)(2,1)S(1)} %collective-permute-done.1.refs_1_, bf16[336,128]{1,0:T(8,128)(2,1)S(1)} %collective-permute-done.2.refs_2_, bf16[336,128]{1,0:T(8,128)(2,1)S(1)} %collective-permute-done.3.refs_3_, ...), custom_call_target="tpu_custom_call" | custom-call | flops 411041792 | bytes 917504 | tf_op jit(solution)/shard_map/self_attention/pallas_call | solution.py:127
  27.7 0.0 copy-start
  27.7 11.0 %all_to_all.5.o_ref = bf16[8,112,128]{2,1,0:T(8,128)(2,1)S(1)} all-to-all(bf16[8,112,128]{2,1,0:T(8,128)(2,1)S(1)} %self_attention.1), channel_id=1, replica_groups=mesh['view'=4,'ctx'=8] {'ctx'}, dimensions={0} | all-to-all | bytes 458752 | tf_op jit(solution)/shard_map/all_to_all | solution.py:140
  38.7 0.0 collective-permute-done.8.refs_2_
  38.7 0.0 collective-permute-done.9.refs_3_
  38.7 0.0 copy-done
  38.7 1.7 %cross_view.1 = bf16[112,1024]{1,0:T(8,128)(2,1)} custom-call(bf16[8,112,128]{2,1,0:T(8,128)(2,1)S(1)} %all_to_all.5.o_ref, bf16[112,1024]{1,0:T(8,128)(2,1)S(1)} %bitcast.7, bf16[224,1024]{1,0:T(8,128)(2,1)S(1)} %get-tuple-element.25.refs_0_, bf16[224,1024]{1,0:T(8,128)(2,1)S(1)} %collective-permute-done.7.refs_1_, ...), custom_call_target="tpu_custom_call" | custom-call | tf_op jit(solution)/shard_map/cross_view/pallas_call | solution.py:191
Async XLA Ops:
  1.6 20.8 %collective-permute-start.7 = (bf16[224,1024]{1,0:T(8,128)(2,1)S(1)}, bf16[224,1024]{1,0:T(8,128)(2,1)S(1)}, u32[]{:S(2)}, u32[]{:S(2)}) collective-permute-start(bf16[224,1024]{1,0:T(8,128)(2,1)S(1)} %get-tuple-element.25.refs_0_), channel_id=1, source_target_pairs={{0,16},{8,24},{16,0},{24,8},{1,17},{9,25},{17,1},{25,9},{2,18},{10... | collective-permute-start | bytes 1376264 | tf_op jit(solution)/shard_map/ppermute | solution.py:93
  4.7 6.3 %collective-permute-start = (bf16[336,128]{1,0:T(8,128)(2,1)S(1)}, bf16[336,128]{1,0:T(8,128)(2,1)S(1)}, u32[]{:S(2)}, u32[]{:S(2)}) collective-permute-start(bf16[336,128]{1,0:T(8,128)(2,1)S(1)} %get-tuple-element.16), channel_id=1, source_target_pairs={{0,3},{1,2},{2,1},{3,0},{4,7},{5,6},{6,5},{7,4},{8,11},{9,10},{10,... | collective-permute-start | bytes 258056 | tf_op jit(solution)/shard_map/ppermute | solution.py:93
  7.2 7.8 %collective-permute-start.1 = (bf16[336,128]{1,0:T(8,128)(2,1)S(1)}, bf16[336,128]{1,0:T(8,128)(2,1)S(1)}, u32[]{:S(2)}, u32[]{:S(2)}) collective-permute-start(bf16[336,128]{1,0:T(8,128)(2,1)S(1)} %get-tuple-element.17), channel_id=1, source_target_pairs={{0,7},{1,6},{2,5},{3,4},{4,3},{5,2},{6,1},{7,0},{8,15},{9,14},{10,... | collective-permute-start | bytes 258056 | tf_op jit(solution)/shard_map/ppermute | solution.py:93
  9.6 12.2 %collective-permute-start.2 = (bf16[336,128]{1,0:T(8,128)(2,1)S(1)}, bf16[336,128]{1,0:T(8,128)(2,1)S(1)}, u32[]{:S(2)}, u32[]{:S(2)}) collective-permute-start(bf16[336,128]{1,0:T(8,128)(2,1)S(1)} %get-tuple-element.18), channel_id=1, source_target_pairs={{0,6},{1,7},{2,4},{3,5},{4,2},{5,3},{6,0},{7,1},{8,14},{9,15},{10,... | collective-permute-start | bytes 258056 | tf_op jit(solution)/shard_map/ppermute | solution.py:93
  11.0 11.5 %collective-permute-start.3 = (bf16[336,128]{1,0:T(8,128)(2,1)S(1)}, bf16[336,128]{1,0:T(8,128)(2,1)S(1)}, u32[]{:S(2)}, u32[]{:S(2)}) collective-permute-start(bf16[336,128]{1,0:T(8,128)(2,1)S(1)} %get-tuple-element.19), channel_id=1, source_target_pairs={{0,2},{1,3},{2,0},{3,1},{4,6},{5,7},{6,4},{7,5},{8,10},{9,11},{10,... | collective-permute-start | bytes 258056 | tf_op jit(solution)/shard_map/ppermute | solution.py:93
  11.0 13.0 %collective-permute-start.4 = (bf16[336,128]{1,0:T(8,128)(2,1)S(1)}, bf16[336,128]{1,0:T(8,128)(2,1)S(1)}, u32[]{:S(2)}, u32[]{:S(2)}) collective-permute-start(bf16[336,128]{1,0:T(8,128)(2,1)S(1)} %get-tuple-element.20), channel_id=1, source_target_pairs={{0,5},{1,4},{2,7},{3,6},{4,1},{5,0},{6,3},{7,2},{8,13},{9,12},{10,... | collective-permute-start | bytes 258056 | tf_op jit(solution)/shard_map/ppermute | solution.py:93
  14.9 9.8 %collective-permute-start.5 = (bf16[336,128]{1,0:T(8,128)(2,1)S(1)}, bf16[336,128]{1,0:T(8,128)(2,1)S(1)}, u32[]{:S(2)}, u32[]{:S(2)}) collective-permute-start(bf16[336,128]{1,0:T(8,128)(2,1)S(1)} %get-tuple-element.21), channel_id=1, source_target_pairs={{0,4},{1,5},{2,6},{3,7},{4,0},{5,1},{6,2},{7,3},{8,12},{9,13},{10,... | collective-permute-start | bytes 258056 | tf_op jit(solution)/shard_map/ppermute | solution.py:93
  21.8 4.5 %collective-permute-start.6 = (bf16[336,128]{1,0:T(8,128)(2,1)S(1)}, bf16[336,128]{1,0:T(8,128)(2,1)S(1)}, u32[]{:S(2)}, u32[]{:S(2)}) collective-permute-start(bf16[336,128]{1,0:T(8,128)(2,1)S(1)} %get-tuple-element.22), channel_id=1, source_target_pairs={{0,1},{1,0},{2,3},{3,2},{4,5},{5,4},{6,7},{7,6},{8,9},{9,8},{10,11... | collective-permute-start | bytes 258056 | tf_op jit(solution)/shard_map/ppermute | solution.py:93
  22.4 16.3 %collective-permute-start.8 = (bf16[224,1024]{1,0:T(8,128)(2,1)S(1)}, bf16[224,1024]{1,0:T(8,128)(2,1)S(1)}, u32[]{:S(2)}, u32[]{:S(2)}) collective-permute-start(bf16[224,1024]{1,0:T(8,128)(2,1)S(1)} %get-tuple-element.25.refs_0_), channel_id=1, source_target_pairs={{0,8},{8,0},{16,24},{24,16},{1,9},{9,1},{17,25},{25,17},{2,10},{10... | collective-permute-start | bytes 1376264 | tf_op jit(solution)/shard_map/ppermute | solution.py:93
  22.4 16.3 %collective-permute-start.9 = (bf16[224,1024]{1,0:T(8,128)(2,1)S(1)}, bf16[224,1024]{1,0:T(8,128)(2,1)S(1)}, u32[]{:S(2)}, u32[]{:S(2)}) collective-permute-start(bf16[224,1024]{1,0:T(8,128)(2,1)S(1)} %collective-permute-done.7.refs_1_), channel_id=1, source_target_pairs={{0,8},{8,0},{16,24},{24,16},{1,9},{9,1},{17,25},{25,17},{2,10},{10... | collective-permute-start | bytes 1376264 | tf_op jit(solution)/shard_map/ppermute | solution.py:93
  27.7 11.1 %copy-start = (bf16[1,112,1024]{2,1,0:T(8,128)(2,1)S(1)}, bf16[1,112,1024]{2,1,0:T(8,128)(2,1)}, u32[]{:S(2)}) copy-start(bf16[1,112,1024]{2,1,0:T(8,128)(2,1)} %param.9) | copy-start | bytes 688132
